TPU v7x, 128 devices: a whole 4x4x4 slice. The times are simulated.
128 devices in a mesh: ctx: 16 (over x, z), tab: 8 (over y, core).
Axes of the slice: x: 4, y: 4, z: 4, core: 2. Of those that a mesh axis runs over, the one named last changes fastest.
Arguments:
- table: bfloat16 [16, 8, 4096, 512], P('ctx', 'tab'), may hold values from -6 to 6
- row_ids: int32 [16, 8, 256], P('ctx', 'tab'), may hold values from 0 to 4095
- dests: int32 [16, 8, 4], P('ctx'), may hold values from 0 to 7, as said below
- slots: int32 [16, 8, 4], P('ctx'), may hold values from 0 to 3, as said below
- lengths: int32 [8, 16], P('tab'), may hold values from 1 to 2048, 4096 in all within a row
- tile_mask: int32 [8, 64, 64], P('tab'), may hold values from 0 to 1, as said below
- w_in: bfloat16 [512, 2048], replicated, may hold values from -0.25 to 0.25
- w_out: bfloat16 [512, 512], replicated, may hold values from -0.25 to 0.25
- output_gradient: bfloat16 [8, 4096, 512], P('tab', 'ctx'), may hold values from -6 to 6
Outputs:
- layer_out: bfloat16 [8, 4096, 512], P('tab', 'ctx')
- table_grad: bfloat16 [16, 8, 4096, 512], P('ctx', 'tab')
Inputs may be any that keep to these rules, and one draw needn't show every extreme that they name: `dests`: the 4 blocks of one device go to 4 different indices of tab, and every device of a ctx index receives exactly one block for each slot 0 to 3. `slots`: see dests. `lengths`: each row sums to 4096; its longest history has exactly 2048 positions. `tile_mask`: diagonal tiles are 1.
All inputs are finite; a program needn't handle non-finite values.
Results may differ from a plain program's by a relative error of at most 0.012.
Values may be sent and summed in bfloat16 or wider, within the bound.
No kernel may reach another device: no remote copies, remote signals or barrier semaphores. Data moves between devices by JAX's collectives and lax.ppermute only.
A program may use at most 192 MiB of HBM per device.

v0:
```python
import jax
import jax.numpy as jnp
from jax import lax
from jax.sharding import PartitionSpec as P

H = 4
BROWS = 64
NBLK = 4


epsilon = 1e-05


def layer_statistics(inputs):
    row_mean = jnp.mean(inputs, axis=-1, keepdims=True)
    centred = inputs - row_mean
    inverse = lax.rsqrt(jnp.mean(centred * centred, axis=-1, keepdims=True) + epsilon)
    return (centred * inverse, inverse)


def norm_backward_pass(incoming_gradient, normalized_rows, inverse):
    first = jnp.mean(incoming_gradient, axis=-1, keepdims=True)
    second = jnp.mean(incoming_gradient * normalized_rows, axis=-1, keepdims=True)
    return inverse * (incoming_gradient - first - normalized_rows * second)


def silu_slope(argument):
    sigmoid_v = jax.nn.sigmoid(argument)
    return sigmoid_v * (1.0 + argument * (1.0 - sigmoid_v))


def position_of(stored, rows_dev, chain_count):
    half = rows_dev // 2
    owner = stored // rows_dev
    local = stored % rows_dev
    early = owner * half + local
    late = (2 * chain_count - 1 - owner) * half + local - half
    return jnp.where(local < half, early, late)


def doc_index(position, doc_ends):
    return jnp.sum((position[:, None] >= doc_ends[None, :]).astype(jnp.int32), axis=1)


def pair_mask(query_pos, key_pos, doc_ends, tile_table):
    same_doc = doc_index(query_pos, doc_ends)[:, None] == doc_index(key_pos, doc_ends)[None, :]
    causal = key_pos[None, :] <= query_pos[:, None]
    tile_ids = jnp.arange(tile_table.shape[0], dtype=jnp.int32)
    query_pick = ((query_pos // BROWS)[:, None] == tile_ids[None, :]).astype(jnp.float32)
    key_pick = ((key_pos // BROWS)[None, :] == tile_ids[:, None]).astype(jnp.float32)
    picked = jnp.dot(query_pick, tile_table, precision=lax.Precision.HIGHEST)
    tile_on = jnp.dot(picked, key_pick, precision=lax.Precision.HIGHEST) > 0.5
    return (same_doc & causal & tile_on).astype(jnp.float32)


def pair_terms(query_heads, grad_heads, key_heads, value_heads, allowed, score_scale):
    scores = (
        jnp.einsum("qhd,khd->hqk", query_heads, key_heads, preferred_element_type=jnp.float32)
        * score_scale
    )
    probs = (jax.nn.silu(scores) * allowed[None]).astype(jnp.bfloat16)
    d_probs = jnp.einsum(
        "qhd,khd->hqk", grad_heads, value_heads, preferred_element_type=jnp.float32
    )
    d_scores = (d_probs * silu_slope(scores) * allowed[None] * score_scale).astype(jnp.bfloat16)
    return (probs, d_scores)


def body(table, row_ids, dests, slots, lengths, tile_mask, w_in, w_out, output_gradient):
    tab_count = lax.axis_size("tab")
    ctx_count = lax.axis_size("ctx")
    own_tab = lax.axis_index("tab")
    own_ctx = lax.axis_index("ctx")
    row_count = row_ids.shape[2]
    model_width = w_out.shape[0]
    head_dim = model_width // H
    score_scale = head_dim ** (-0.5)
    own_pos = position_of(
        own_ctx * row_count + jnp.arange(row_count, dtype=jnp.int32), row_count, ctx_count
    )
    doc_ends = jnp.cumsum(lengths[0])
    tile_table = tile_mask[0].astype(jnp.float32)
    looked_rows = jnp.take(table[0, 0], row_ids[0, 0], axis=0).reshape(NBLK, BROWS, model_width)
    route_dest = dests[0]
    route_slot = slots[0]
    own_dest = lax.dynamic_index_in_dim(route_dest, own_tab, 0, keepdims=False)
    tab_ids = jnp.arange(tab_count, dtype=jnp.int32)
    send_pick = (own_dest[None, :] == tab_ids[:, None]).astype(jnp.bfloat16)
    outgoing = jnp.einsum(
        "tp,prd->trd", send_pick, looked_rows, preferred_element_type=jnp.float32
    ).astype(jnp.bfloat16)
    arrived = lax.all_to_all(outgoing, "tab", split_axis=0, concat_axis=0, tiled=True)
    slot_ids = jnp.arange(NBLK, dtype=jnp.int32)
    slot_hits = (route_dest == own_tab)[None, :, :] & (
        route_slot[None, :, :] == slot_ids[:, None, None]
    )
    receive_pick = jnp.sum(slot_hits.astype(jnp.int32), axis=2).astype(jnp.bfloat16)
    user_sequence = jnp.einsum(
        "st,trd->srd", receive_pick, arrived, preferred_element_type=jnp.float32
    )
    user_sequence = user_sequence.astype(jnp.bfloat16).reshape(row_count, model_width)
    centred_scaled_input, inverse_deviation = layer_statistics(user_sequence.astype(jnp.float32))
    normalized_rows = centred_scaled_input.astype(jnp.bfloat16)
    pre = jnp.dot(normalized_rows, w_in, preferred_element_type=jnp.float32)
    act = jax.nn.silu(pre).astype(jnp.bfloat16)
    up_part = act[:, 0:model_width]
    value_part = act[:, model_width : 2 * model_width]
    query_part = act[:, 2 * model_width : 3 * model_width]
    key_part = act[:, 3 * model_width : 4 * model_width]
    query_heads = query_part.reshape(row_count, H, head_dim)
    zero_rows = jnp.zeros((row_count, model_width), jnp.float32)
    key_in = lax.all_gather(key_part, "ctx", axis=0, tiled=True)
    value_in = lax.all_gather(value_part, "ctx", axis=0, tiled=True)
    part_rows = key_in.shape[0]
    key_pos = position_of(jnp.arange(part_rows, dtype=jnp.int32), row_count, ctx_count)
    allowed = pair_mask(own_pos, key_pos, doc_ends, tile_table)

    def attend_compute(total):
        scores = (
            jnp.einsum(
                "qhd,khd->hqk",
                query_heads,
                key_in.reshape(part_rows, H, head_dim),
                preferred_element_type=jnp.float32,
            )
            * score_scale
        )
        probs = (jax.nn.silu(scores) * allowed[None]).astype(jnp.bfloat16)
        update = jnp.einsum(
            "hqk,khd->qhd",
            probs,
            value_in.reshape(part_rows, H, head_dim),
            preferred_element_type=jnp.float32,
        )
        return update.reshape(row_count, model_width)

    attn = lax.cond(jnp.any(allowed > 0.5), attend_compute, lambda total: total, zero_rows)
    attn_hat, attn_inverse = layer_statistics(attn)
    up_float = up_part.astype(jnp.float32)
    mixed = (attn_hat * up_float).astype(jnp.bfloat16)
    layer_out = (
        user_sequence.astype(jnp.float32)
        + jnp.dot(mixed, w_out, preferred_element_type=jnp.float32)
    ).astype(jnp.bfloat16)
    incoming_gradient = output_gradient[0]
    dmixed = jnp.dot(incoming_gradient, w_out.T, preferred_element_type=jnp.float32)
    d_up = dmixed * attn_hat
    d_attn = norm_backward_pass(dmixed * up_float, attn_hat, attn_inverse).astype(jnp.bfloat16)
    grad_heads = d_attn.reshape(row_count, H, head_dim)
    query_key_in = lax.all_gather(key_part, "ctx", axis=0, tiled=True)
    query_value_in = lax.all_gather(value_part, "ctx", axis=0, tiled=True)
    query_part_rows = query_key_in.shape[0]
    key_pos = position_of(jnp.arange(query_part_rows, dtype=jnp.int32), row_count, ctx_count)
    query_allowed = pair_mask(own_pos, key_pos, doc_ends, tile_table)

    def query_compute(total):
        key_heads = query_key_in.reshape(query_part_rows, H, head_dim)
        probs, d_scores = pair_terms(
            query_heads,
            grad_heads,
            key_heads,
            query_value_in.reshape(query_part_rows, H, head_dim),
            query_allowed,
            score_scale,
        )
        update = jnp.einsum("hqk,khd->qhd", d_scores, key_heads, preferred_element_type=jnp.float32)
        return update.reshape(row_count, model_width)

    d_query = lax.cond(jnp.any(query_allowed > 0.5), query_compute, lambda total: total, zero_rows)
    own_key_heads = key_part.reshape(row_count, H, head_dim)
    own_value_heads = value_part.reshape(row_count, H, head_dim)
    query_in = lax.all_gather(query_part, "ctx", axis=0, tiled=True)
    grad_in = lax.all_gather(d_attn, "ctx", axis=0, tiled=True)
    key_part_rows = query_in.shape[0]
    query_pos = position_of(jnp.arange(key_part_rows, dtype=jnp.int32), row_count, ctx_count)
    key_allowed = pair_mask(query_pos, own_pos, doc_ends, tile_table)

    def key_compute(totals):
        query_rows = query_in.reshape(key_part_rows, H, head_dim)
        grad_rows = grad_in.reshape(key_part_rows, H, head_dim)
        probs, d_scores = pair_terms(
            query_rows, grad_rows, own_key_heads, own_value_heads, key_allowed, score_scale
        )
        key_term = jnp.einsum(
            "hqk,qhd->khd", d_scores, query_rows, preferred_element_type=jnp.float32
        )
        value_term = jnp.einsum(
            "hqk,qhd->khd", probs, grad_rows, preferred_element_type=jnp.float32
        )
        return (
            key_term.reshape(row_count, model_width),
            value_term.reshape(row_count, model_width),
        )

    d_key, d_value = lax.cond(
        jnp.any(key_allowed > 0.5), key_compute, lambda totals: totals, (zero_rows, zero_rows)
    )
    d_act = jnp.concatenate([d_up, d_value, d_query, d_key], axis=1)
    d_pre = (d_act * silu_slope(pre)).astype(jnp.bfloat16)
    normalized_gradient = jnp.dot(d_pre, w_in.T, preferred_element_type=jnp.float32)
    sequence_gradient = (
        incoming_gradient.astype(jnp.float32)
        + norm_backward_pass(normalized_gradient, centred_scaled_input, inverse_deviation)
    ).astype(jnp.bfloat16)
    grad_blocks = sequence_gradient.reshape(NBLK, BROWS, model_width)
    returning = jnp.einsum(
        "st,srd->trd", receive_pick, grad_blocks, preferred_element_type=jnp.float32
    ).astype(jnp.bfloat16)
    came_back = lax.all_to_all(returning, "tab", split_axis=0, concat_axis=0, tiled=True)
    row_grads = jnp.einsum(
        "tp,trd->prd", send_pick, came_back, preferred_element_type=jnp.float32
    ).reshape(row_count, model_width)
    table_grad = (
        jnp.zeros((table.shape[2], model_width), jnp.float32)
        .at[row_ids[0, 0]]
        .add(row_grads)
        .astype(jnp.bfloat16)
    )
    return (
        layer_out.reshape(1, row_count, model_width),
        table_grad.reshape(1, 1, table.shape[2], model_width),
    )


def solution(mesh):
    in_specs = (
        P("ctx", "tab", None, None),
        P("ctx", "tab", None),
        P("ctx", None, None),
        P("ctx", None, None),
        P("tab", None),
        P("tab", None, None),
        P(),
        P(),
        P("tab", "ctx", None),
    )
    out_specs = (P("tab", "ctx", None), P("ctx", "tab", None, None))
    return jax.shard_map(body, mesh=mesh, in_specs=in_specs, out_specs=out_specs, check_vma=False)
```

profile of v0, /device:TPU:1, one launch (start us, length us, event | category | flops | bytes accessed | tf_op | source)
XLA Modules:
  0.0 344.5 jit_solution(9639213946264151072)
XLA Ops:
  7.2 0.8 compare_select_fusion
  8.0 0.5 broadcast.825
  8.6 1.3 reduce.10
  9.9 0.1 squeeze.17
  10.0 0.1 copy.118
  10.1 0.9 dynamic-slice_reduce_fusion
  11.0 3.9 %gather_fusion = bf16[256,512]{1,0:T(8,128)(2,1)S(1)} fusion(bf16[4096,512]{1,0:T(8,128)(2,1)} %bitcast.128, s32[1024]{0:T(1024)S(1)} %pad_clamp_fusion), kind=kCustom, calls=%fused_computation | custom fusion | bytes 525312 | tf_op jit(solution)/shard_map/jit(_take)/gather | solution.py:83
  14.9 0.5 convolution_convert_fusion
  15.4 0.9 copy.120
  16.3 6.0 %all-to-all-start = ((bf16[8,64,512]{2,1,0:T(8,128)(2,1)}), bf16[8,64,512]{2,1,0:T(8,128)(2,1)S(1)}, u32[]{:S(2)}, u32[]{:S(2)}) async-start(bf16[8,64,512]{2,1,0:T(8,128)(2,1)} %copy.120), calls=%async_computation | async-start | bytes 1048576 | tf_op jit(solution)/shard_map/all_to_all | solution.py:92
  22.4 9.4 %all-to-all-done = bf16[8,64,512]{2,1,0:T(8,128)(2,1)S(1)} async-done(((bf16[8,64,512]{2,1,0:T(8,128)(2,1)}), bf16[8,64,512]{2,1,0:T(8,128)(2,1)S(1)}, u32[]{:S(2)}, u32[]{:S(2)}) %all-to-all-start) | async-done | bytes 524320 | tf_op jit(solution)/shard_map/all_to_all | solution.py:92
  31.8 0.5 fusion.108
  32.3 0.2 copy.122
  32.5 0.3 multiply_reduce_fusion.3
  32.9 0.1 rsqrt.20
  33.1 0.1 fusion.52
  33.3 2.1 multiply_convert_fusion.5
  35.4 1.0 copy-done.8
  36.4 0.9 fusion.107
  37.4 0.7 all-gather.7.cloned.1.call-update
  38.1 0.7 all-gather.11.cloned.1.call-update
  38.9 0.1 copy.123
  39.0 0.1 reduce.6
  39.2 0.1 convert_reduce_fusion.1
  39.2 0.1 convert_reduce_fusion
  39.4 0.3 fusion.64
  39.7 5.4 %compare_reduce_fusion.1 = (pred[]{:T(512)}, f32[256,4096]{1,0:T(8,128)}) fusion(f32[256,64]{0,1:T(8,128)S(1)} %fusion.64, s32[4096]{0:T(1024)S(1)} %get-tuple-element.157, s32[256]{0:T(256)S(1)} %get-tuple-element.156, s32[4096]{0:T(1024)S(1)} %get-tuple-element.158, s32[4096]{0:T(1024)S(1)} %convert_reduce_fusion, s32[256]{0:T(256)S(1)} %convert_reduce_fusion.1), kind=kOutput, calls=%fused_computation.43 | convolution fusion | flops 813957120 | bytes 4311041 | tf_op jit(solution)/shard_map/dot_general | solution.py:52
  45.7 0.8 reshape.401
  46.5 43.2 %all-gather.5.cloned.1.call-done = bf16[4096,512]{1,0:T(8,128)(2,1)} async-done(((bf16[256,512]{1,0:T(8,128)(2,1)}), bf16[4096,512]{1,0:T(8,128)(2,1)}) %all-gather.5.cloned.1.call-update) | async-done | bytes 4194320 | tf_op jit(solution)/shard_map/all_gather | solution.py:112
  89.7 54.0 %all-gather.7.cloned.1.call-done = bf16[4096,512]{1,0:T(8,128)(2,1)} async-done(((bf16[256,512]{1,0:T(8,128)(2,1)}), bf16[4096,512]{1,0:T(8,128)(2,1)}) %all-gather.7.cloned.1.call-update) | async-done | bytes 4194320 | tf_op jit(solution)/shard_map/all_gather | solution.py:113
  143.7 21.1 %conditional.3 = (f32[256,1]{0,1:T(1,128)S(1)}, f32[256,512]{1,0:T(8,128)S(1)}) conditional(s32[]{:T(128)} %convert_element_type.116, () %tuple.32, (bf16[4096,512]{1,0:T(8,128)(2,1)}, bf16[256,4,128]{2,1,0:T(4,128)(2,1)}, f32[256,4096]{1,0:T(8,128)}, bf16[4096,512]{1,0:T(8,128)(2,1)}) %tuple.33), branch_computations={%region_7.8_spmd, %region_8.10_spmd} | conditional | flops 2176974592 | bytes 23856172 | solution.py:137
  144.0 6.5 %copy.128 = bf16[4096,512]{0,1:T(8,128)(2,1)} copy(bf16[4096,512]{1,0:T(8,128)(2,1)} %get-tuple-element.119) | data formatting | bytes 8388608 | tf_op jit(solution)/shard_map
  150.5 13.1 %fusion.102 = (f32[256]{0:T(256)S(1)}, f32[4,256,128]{1,2,0:T(8,128)}) fusion(bf16[4096,4,128]{0,2,1:T(8,128)(2,1)} %bitcast.126, f32[256,4096]{1,0:T(8,128)} %get-tuple-element.38, bf16[256,4,128]{2,1,0:T(4,128)(2,1)S(1)} %copy-done.14, bf16[4096,512]{1,0:T(8,128)(2,1)} %get-tuple-element.37), kind=kOutput, calls=%fused_computation.164 | convolution fusion | flops 2176974592 | bytes 13370368 | tf_op jit(solution)/shard_map/cond/branch_1_fun/hqk,khd->qhd/dot_general | solution.py:129
  163.5 1.2 copy.145
  164.8 0.2 multiply_reduce_fusion.2
  165.0 1.4 fusion.62
  166.5 2.0 fusion.53
  168.5 1.6 fusion.39
  170.1 5.2 %compare_reduce_fusion = (pred[]{:T(512)}, f32[4096,256]{1,0:T(8,128)}) fusion(f32[4096,64]{0,1:T(8,128)S(1)} %fusion.39, s32[256]{0:T(256)S(1)} %get-tuple-element.155, s32[4096]{0:T(1024)S(1)} %get-tuple-element.158, s32[256]{0:T(256)S(1)} %get-tuple-element.156, s32[256]{0:T(256)S(1)} %convert_reduce_fusion.1, s32[4096]{0:T(1024)S(1)} %convert_reduce_fusion), kind=kOutput, calls=%fused_computation.42 | convolution fusion | flops 813711360 | bytes 5278721 | tf_op jit(solution)/shard_map/dot_general | solution.py:52
  175.9 37.5 %conditional.5 = (f32[256,512]{1,0:T(8,128)S(1)}) conditional(s32[]{:T(128)} %convert_element_type.116, () %tuple.36, (bf16[256,512]{1,0:T(8,128)(2,1)S(1)}, bf16[4096,512]{1,0:T(8,128)(2,1)}, bf16[4096,512]{1,0:T(8,128)(2,1)}, bf16[256,4,128]{2,1,0:T(4,128)(2,1)}, f32[256,4096]{1,0:T(8,128)}) %tuple.91), branch_computations={%region_16.17_spmd, %region_17.18_spmd} | conditional | flops 3271557120 | bytes 57671716 | solution.py:169
  176.5 10.5 %fusion.22 = f32[4,256,4096]{2,1,0:T(8,128)} fusion(bf16[4096,512]{1,0:T(8,128)(2,1)} %get-tuple-element.46, bf16[256,512]{1,0:T(8,128)(2,1)S(1)} %get-tuple-element.45), kind=kOutput, calls=%fused_computation.24 | convolution fusion | flops 1073741824 | bytes 21233664 | tf_op jit(solution)/shard_map/cond/branch_1_fun/qhd,khd->hqk/dot_general | solution.py:62
  187.0 6.5 %copy.132 = bf16[4096,512]{0,1:T(8,128)(2,1)} copy(bf16[4096,512]{1,0:T(8,128)(2,1)} %get-tuple-element.127) | data formatting | bytes 8388608 | tf_op jit(solution)/shard_map
  193.5 18.6 %fusion.25 = f32[4,256,128]{1,2,0:T(8,128)} fusion(bf16[4096,4,128]{0,2,1:T(8,128)(2,1)} %bitcast.127, f32[4,256,4096]{2,1,0:T(8,128)} %fusion.22, f32[256,4096]{1,0:T(8,128)} %get-tuple-element.49, bf16[256,4,128]{2,1,0:T(4,128)(2,1)S(1)} %copy-done.15), kind=kOutput, calls=%fused_computation.27 | convolution fusion | flops 2197815296 | bytes 25952256 | tf_op jit(solution)/shard_map/cond/branch_1_fun/hqk,khd->qhd/dot_general | solution.py:166
  212.2 1.2 copy.151
  213.5 36.9 %all-gather.9.cloned.1.call-done = bf16[4096,512]{1,0:T(8,128)(2,1)} async-done(((bf16[256,512]{1,0:T(8,128)(2,1)}), bf16[4096,512]{1,0:T(8,128)(2,1)}) %all-gather.9.cloned.1.call-update) | async-done | bytes 4194320 | tf_op jit(solution)/shard_map/all_gather | solution.py:173
  250.4 54.2 %conditional.4 = (f32[256,512]{1,0:T(8,128)}, f32[256,512]{1,0:T(8,128)}) conditional(s32[]{:T(128)} %convert_element_type.125, () %tuple.34, (bf16[4096,512]{1,0:T(8,128)(2,1)}, bf16[256,512]{1,0:T(8,128)(2,1)S(1)}, bf16[4096,512]{1,0:T(8,128)(2,1)}, bf16[256,512]{1,0:T(8,128)(2,1)S(1)}, f32[4096,256]{1,0:T(8,128)}) %tuple.92), branch_computations={%region_14.15_spmd, %region_15.16_spmd} | conditional | flops 4374659072 | bytes 95944720 | solution.py:195
  250.6 6.4 %copy.131 = bf16[4096,512]{0,1:T(8,128)(2,1)} copy(bf16[4096,512]{1,0:T(8,128)(2,1)} %get-tuple-element.122) | data formatting | bytes 8388608 | tf_op jit(solution)/shard_map
  257.0 10.3 %fusion.15 = f32[4,4096,256]{2,1,0:T(8,128)} fusion(bf16[4096,4,128]{0,2,1:T(8,128)(2,1)} %bitcast.121, bf16[256,512]{1,0:T(8,128)(2,1)S(1)} %get-tuple-element.43), kind=kOutput, calls=%fused_computation.16 | convolution fusion | flops 1073741824 | bytes 21233664 | tf_op jit(solution)/shard_map/cond/branch_1_fun/qhd,khd->hqk/dot_general | solution.py:58
  267.3 6.3 %copy.130 = bf16[4096,512]{0,1:T(8,128)(2,1)} copy(bf16[4096,512]{1,0:T(8,128)(2,1)} %get-tuple-element.120) | data formatting | bytes 8388608 | tf_op jit(solution)/shard_map
  273.6 16.5 %fusion.10 = f32[4,256,128]{1,2,0:T(8,128)} fusion(bf16[4096,4,128]{0,2,1:T(8,128)(2,1)} %bitcast.122, f32[4,4096,256]{2,1,0:T(8,128)} %fusion.15, bf16[4096,4,128]{0,2,1:T(8,128)(2,1)} %bitcast.124, f32[4096,256]{1,0:T(8,128)} %get-tuple-element.44, bf16[256,512]{1,0:T(8,128)(2,1)S(1)} %get-tuple-element.41), kind=kOutput, calls=%fused_computation.13 | convolution fusion | flops 2197815296 | bytes 30146560 | tf_op jit(solution)/shard_map/cond/branch_1_fun/hqk,qhd->khd/dot_general | solution.py:184
  290.1 2.1 copy.149
  292.2 11.2 %fusion.9 = f32[4,256,128]{1,2,0:T(8,128)S(1)} fusion(bf16[4096,4,128]{0,2,1:T(8,128)(2,1)} %bitcast.125, f32[4,4096,256]{2,1,0:T(8,128)} %fusion.15, f32[4096,256]{1,0:T(8,128)} %get-tuple-element.44), kind=kOutput, calls=%fused_computation.12 | convolution fusion | flops 1103101952 | bytes 25690112 | tf_op jit(solution)/shard_map/cond/branch_1_fun/hqk,qhd->khd/dot_general | solution.py:187
  303.4 1.0 copy.147
  304.7 3.4 fusion.101
  308.1 0.2 add_convert_fusion
  308.4 0.3 convolution_convert_fusion.1
  308.7 0.9 copy.138
  309.7 5.0 %all-to-all-start.1 = ((bf16[8,64,512]{2,1,0:T(8,128)(2,1)}), bf16[8,64,512]{2,1,0:T(8,128)(2,1)}, u32[]{:S(2)}, u32[]{:S(2)}) async-start(bf16[8,64,512]{2,1,0:T(8,128)(2,1)} %copy.138), calls=%async_computation.1 | async-start | bytes 1048576 | tf_op jit(solution)/shard_map/all_to_all | solution.py:209
  314.7 2.2 fusion.42
  316.8 7.4 %all-to-all-done.1 = bf16[8,64,512]{2,1,0:T(8,128)(2,1)} async-done(((bf16[8,64,512]{2,1,0:T(8,128)(2,1)}), bf16[8,64,512]{2,1,0:T(8,128)(2,1)}, u32[]{:S(2)}, u32[]{:S(2)}) %all-to-all-start.1) | async-done | bytes 524320 | tf_op jit(solution)/shard_map/all_to_all | solution.py:209
  324.2 1.5 fusion.48
  325.7 0.2 copy.140
  325.9 5.9 %scatter_custom_fusion = f32[4096,512]{1,0:T(8,128)} fusion(s32[256]{0:T(256)} %bitcast.141, f32[256,512]{1,0:T(8,128)S(1)} %bitcast.131, f32[]{:T(128)} %constant.183.clone.1), kind=kCustom, calls=%fused_computation.40 | custom fusion | flops 131072 | bytes 8389120 | tf_op jit(solution)/shard_map/scatter-add | solution.py:216
  331.8 5.9 %convert_bitcast_fusion = bf16[1,1,4096,512]{3,2,1,0:T(8,128)(2,1)} fusion(f32[4096,512]{1,0:T(8,128)} %scatter_custom_fusion), kind=kLoop, calls=%fused_computation.39 | loop fusion | flops 2097152 | bytes 12582912 | tf_op jit(solution)/shard_map/reshape | solution.py:221
  (90 shorter events, 0.7 us)
Async XLA Ops:
  7.2 26.1 %copy-start = (bf16[512,2048]{1,0:T(8,128)(2,1)S(1)}, bf16[512,2048]{1,0:T(8,128)(2,1)}, u32[]{:S(2)}) copy-start(bf16[512,2048]{1,0:T(8,128)(2,1)} %param.21) | copy-start | bytes 6291460
  7.2 15.1 %copy-start.27 = (s32[1,8,4]{1,2,0:T(4,128)S(1)}, s32[1,8,4]{1,2,0:T(4,128)}, u32[]{:S(2)}) copy-start(s32[1,8,4]{1,2,0:T(4,128)} %param.17) | copy-start | bytes 388
  7.2 15.2 %copy-start.31 = (s32[1,8,4]{1,2,0:T(4,128)S(1)}, s32[1,8,4]{1,2,0:T(4,128)}, u32[]{:S(2)}) copy-start(s32[1,8,4]{1,2,0:T(4,128)} %param.18) | copy-start | bytes 388
  8.0 8.3 %copy-start.28 = (s32[256,1]{0,1:T(1,128)}, s32[256,1]{0,1:T(1,128)S(1)}, u32[]{:S(2)}) copy-start(s32[256,1]{0,1:T(1,128)S(1)} %compare_select_fusion) | copy-start | bytes 3076
  11.0 5.4 %copy-start.29 = (s32[4]{0:T(128)}, s32[4]{0:T(128)S(1)}, u32[]{:S(2)}) copy-start(s32[4]{0:T(128)S(1)} %dynamic-slice_reduce_fusion) | copy-start | bytes 52
  16.3 15.5 %all-to-all-start = ((bf16[8,64,512]{2,1,0:T(8,128)(2,1)}), bf16[8,64,512]{2,1,0:T(8,128)(2,1)S(1)}, u32[]{:S(2)}, u32[]{:S(2)}) async-start(bf16[8,64,512]{2,1,0:T(8,128)(2,1)} %copy.120), calls=%async_computation | async-start | bytes 1048576 | tf_op jit(solution)/shard_map/all_to_all | solution.py:92
  22.3 67.4 %all-gather.5.cloned.1.call-start = ((), (), s32[]{:S(2)}) async-start(), calls=%async_computation.2 | async-start | bytes 4456448 | tf_op jit(solution)/shard_map/all_gather | solution.py:112
  22.4 9.9 %copy-start.19 = (s32[4,8]{1,0:T(4,128)}, s32[4,8]{1,0:T(4,128)S(1)}, u32[]{:S(2)}) copy-start(s32[4,8]{1,0:T(4,128)S(1)} %convert_reduce_fusion.2) | copy-start | bytes 388
  32.5 2.9 copy-start.3
  33.0 2.4 copy-start.23
  33.1 2.3 copy-start.25
  33.3 5.6 %copy-start.32 = (s32[1,16]{1,0:T(1,128)S(1)}, s32[1,16]{1,0:T(1,128)}, u32[]{:S(2)}) copy-start(s32[1,16]{1,0:T(1,128)} %param.19) | copy-start | bytes 196
  33.3 6.1 %copy-start.16 = (s32[1,64,64]{2,1,0:T(8,128)S(1)}, s32[1,64,64]{2,1,0:T(8,128)}, u32[]{:S(2)}) copy-start(s32[1,64,64]{2,1,0:T(8,128)} %param.20) | copy-start | bytes 49156
  35.4 1.0 copy-start.8
  37.3 8.4 %copy-start.7 = (bf16[256,512]{1,0:T(8,128)(2,1)S(1)}, bf16[256,512]{1,0:T(8,128)(2,1)}, u32[]{:S(2)}) copy-start(bf16[256,512]{1,0:T(8,128)(2,1)} %get-tuple-element.143) | copy-start | bytes 786436
  37.3 106.4 %all-gather.7.cloned.1.call-start = ((), (), s32[]{:S(2)}) async-start(), calls=%async_computation.3 | async-start | bytes 4456448 | tf_op jit(solution)/shard_map/all_gather | solution.py:113
  38.1 175.4 %all-gather.11.cloned.1.call-start = ((), (), s32[]{:S(2)}) async-start(), calls=%async_computation.5 | async-start | bytes 4456448 | tf_op jit(solution)/shard_map/all_gather | solution.py:172
  38.8 211.6 %all-gather.9.cloned.1.call-start = ((), (), s32[]{:S(2)}) async-start(), calls=%async_computation.4 | async-start | bytes 4456448 | tf_op jit(solution)/shard_map/all_gather | solution.py:173
  143.7 21.3 %copy-start.9 = (bf16[512,512]{1,0:T(8,128)(2,1)S(1)}, bf16[512,512]{1,0:T(8,128)(2,1)}, u32[]{:S(2)}) copy-start(bf16[512,512]{1,0:T(8,128)(2,1)} %param.22) | copy-start | bytes 1572868
  143.7 21.3 %copy-start.11 = (bf16[1,256,512]{2,1,0:T(8,128)(2,1)S(1)}, bf16[1,256,512]{2,1,0:T(8,128)(2,1)}, u32[]{:S(2)}) copy-start(bf16[1,256,512]{2,1,0:T(8,128)(2,1)} %param.23) | copy-start | bytes 786436
  143.9 6.5 %copy-start.14 = (bf16[256,4,128]{2,1,0:T(4,128)(2,1)S(1)}, bf16[256,4,128]{2,1,0:T(4,128)(2,1)}, u32[]{:S(2)}) copy-start(bf16[256,4,128]{2,1,0:T(4,128)(2,1)} %get-tuple-element.117) | copy-start | bytes 786436 | tf_op jit(solution)/shard_map/cond
  164.7 10.6 %copy-start.1 = (f32[256,512]{1,0:T(8,128)}, f32[256,512]{1,0:T(8,128)S(1)}, u32[]{:S(2)}) copy-start(f32[256,512]{1,0:T(8,128)S(1)} %get-tuple-element.130) | copy-start | bytes 1572868
  164.8 3.7 %copy-start.17 = (f32[256,1]{0,1:T(1,128)}, f32[256,1]{0,1:T(1,128)S(1)}, u32[]{:S(2)}) copy-start(f32[256,1]{0,1:T(1,128)S(1)} %broadcast_multiply_fusion.5) | copy-start | bytes 3076
  165.0 3.5 %copy-start.21 = (f32[256]{0:T(256)}, f32[256]{0:T(256)S(1)}, u32[]{:S(2)}) copy-start(f32[256]{0:T(256)S(1)} %add_rsqrt_fusion.1) | copy-start | bytes 3076
  168.5 7.4 %copy-start.6 = (bf16[256,512]{1,0:T(8,128)(2,1)S(1)}, bf16[256,512]{1,0:T(8,128)(2,1)}, u32[]{:S(2)}) copy-start(bf16[256,512]{1,0:T(8,128)(2,1)} %get-tuple-element.141) | copy-start | bytes 786436
  175.9 74.5 %copy-start.5 = (bf16[256,512]{1,0:T(8,128)(2,1)S(1)}, bf16[256,512]{1,0:T(8,128)(2,1)}, u32[]{:S(2)}) copy-start(bf16[256,512]{1,0:T(8,128)(2,1)} %get-tuple-element.144) | copy-start | bytes 786436
  175.9 74.4 %copy-start.10 = (bf16[256,512]{1,0:T(8,128)(2,1)S(1)}, bf16[256,512]{1,0:T(8,128)(2,1)}, u32[]{:S(2)}) copy-start(bf16[256,512]{1,0:T(8,128)(2,1)} %get-tuple-element.142) | copy-start | bytes 786436
  187.0 6.6 %copy-start.15 = (bf16[256,4,128]{2,1,0:T(4,128)(2,1)S(1)}, bf16[256,4,128]{2,1,0:T(4,128)(2,1)}, u32[]{:S(2)}) copy-start(bf16[256,4,128]{2,1,0:T(4,128)(2,1)} %get-tuple-element.128) | copy-start | bytes 786436 | tf_op jit(solution)/shard_map/cond
  213.4 36.9 %copy-start.13 = (f32[256,512]{1,0:T(8,128)}, f32[256,512]{1,0:T(8,128)S(1)}, u32[]{:S(2)}) copy-start(f32[256,512]{1,0:T(8,128)S(1)} %get-tuple-element.133) | copy-start | bytes 1572868
  250.4 54.3 %copy-start.4 = (f32[4,64,512]{2,1,0:T(8,128)S(1)}, f32[4,64,512]{2,1,0:T(8,128)}, u32[]{:S(2)}) copy-start(f32[4,64,512]{2,1,0:T(8,128)} %copy-done.3) | copy-start | bytes 1572868
  250.4 54.3 %copy-start.24 = (f32[256]{0:T(256)S(1)}, f32[256]{0:T(256)}, u32[]{:S(2)}) copy-start(f32[256]{0:T(256)} %copy-done.23) | copy-start | bytes 3076
  250.4 54.3 %copy-start.26 = (f32[256]{0:T(256)S(1)}, f32[256]{0:T(256)}, u32[]{:S(2)}) copy-start(f32[256]{0:T(256)} %copy-done.25) | copy-start | bytes 3076
  304.7 3.5 %copy-start.12 = (bf16[1,256,512]{2,1,0:T(8,128)(2,1)S(1)}, bf16[1,256,512]{2,1,0:T(8,128)(2,1)}, u32[]{:S(2)}) copy-start(bf16[1,256,512]{2,1,0:T(8,128)(2,1)} %param.23) | copy-start | bytes 786436
  304.7 3.7 %copy-start.20 = (s32[4,8]{1,0:T(4,128)S(1)}, s32[4,8]{1,0:T(4,128)}, u32[]{:S(2)}) copy-start(s32[4,8]{1,0:T(4,128)} %copy-done.19) | copy-start | bytes 388
  308.1 6.6 %copy-start.2 = (f32[256,512]{1,0:T(8,128)S(1)}, f32[256,512]{1,0:T(8,128)}, u32[]{:S(2)}) copy-start(f32[256,512]{1,0:T(8,128)} %copy-done.1) | copy-start | bytes 1572868
  308.1 6.6 %copy-start.18 = (f32[256,1]{0,1:T(1,128)S(1)}, f32[256,1]{0,1:T(1,128)}, u32[]{:S(2)}) copy-start(f32[256,1]{0,1:T(1,128)} %copy-done.17) | copy-start | bytes 3076
  308.1 6.6 %copy-start.22 = (f32[256]{0:T(256)S(1)}, f32[256]{0:T(256)}, u32[]{:S(2)}) copy-start(f32[256]{0:T(256)} %copy-done.21) | copy-start | bytes 3076
  308.1 16.1 %copy-start.30 = (s32[4]{0:T(128)S(1)}, s32[4]{0:T(128)}, u32[]{:S(2)}) copy-start(s32[4]{0:T(128)} %copy-done.29) | copy-start | bytes 52
  309.7 14.5 %all-to-all-start.1 = ((bf16[8,64,512]{2,1,0:T(8,128)(2,1)}), bf16[8,64,512]{2,1,0:T(8,128)(2,1)}, u32[]{:S(2)}, u32[]{:S(2)}) async-start(bf16[8,64,512]{2,1,0:T(8,128)(2,1)} %copy.138), calls=%async_computation.1 | async-start | bytes 1048576 | tf_op jit(solution)/shard_map/all_to_all | solution.py:209
Sparse Core Ops, SparseCore 0:
  37.4 52.2 all-gather.4
  92.4 51.2 all-gather.6
  145.8 51.2 all-gather.10
  199.1 51.2 all-gather.8
where the time goes:
time: 351 us; the launch traced here: 344 us
  waiting for transfers between devices  152 us (43%)
  matrix products  105 us (30%)
  local copies, waits for them, and re-layouts  42.2 us (12%)
  other arithmetic  17.4 us (5%)
  between operations  15.7 us (4%)
  starting transfers between devices  11 us (3%)
    all_gather x1, waiting for transfers between devices, body(): value_in = lax.all_gather(value_part, 'ctx', axis=0, tiled=True)  54 us
    all_gather x1, waiting for transfers between devices, body(): key_in = lax.all_gather(key_part, 'ctx', axis=0, tiled=True)  43.2 us
    all_gather x1, waiting for transfers between devices, body(): grad_in = lax.all_gather(d_attn, 'ctx', axis=0, tiled=True)  36.9 us
    another operation x5, local copies, waits for them, and re-layouts  25.8 us
    dot_general x1, matrix products, query_compute(): jnp.einsum('hqk,khd->qhd', d_scores, key_heads, preferred_element_type=jn...  18.6 us
    dot_general x1, matrix products, key_compute(): jnp.einsum('hqk,qhd->khd', d_scores, query_rows, preferred_element_type=j...  16.5 us
    dot_general x1, matrix products, attend_compute(): jnp.einsum('hqk,khd->qhd', probs, value_in.reshape(part_rows, H, head_dim...  13.1 us
    dot_general x1, matrix products, key_compute(): jnp.einsum('hqk,qhd->khd', probs, grad_rows, preferred_element_type=jnp.f...  11.2 us
  transfers between devices with their start and end apart: 6, of which 5 were waited for; matrix products, arithmetic and copies ran while one was open for 22% of the time, Pallas kernels for 0%

commit v1 on v0

v1 whole, which is shorter than its diff:
```python
import functools

import jax
import jax.numpy as jnp
from jax import lax
from jax.experimental import pallas as pl
from jax.experimental.pallas import tpu as pltpu
from jax.sharding import Mesh, PartitionSpec as P

HEADS = 4
BROWS = 64
NBLK = 4
WIDTH = 512
HD = 128
ROWS = 256
CHUNK = 128
LENGTH = 4096
EPS = 1e-05
BF = jnp.bfloat16
F32 = jnp.float32
AXES = ("x", "z", "y", "c")
FAR = 1e9
KEY_TILE = 256
SCALE = HD ** (-0.5)


def device_id(x, z, y, c):
    return ((x * 4 + z) * 4 + y) * 2 + c


def all_coords():
    return [(x, z, y, c) for x in range(4) for z in range(4) for y in range(4) for c in range(2)]


def tab_pairs(step):
    out = []
    for x, z, y, c in all_coords():
        y2, c2 = divmod((y * 2 + c + step) % 8, 2)
        out.append((device_id(x, z, y, c), device_id(x, z, y2, c2)))
    return out


def main_pairs(j):
    return [
        (device_id(x, z, y, c), device_id((x + j) % 4, 2 * c + (z >> 1), y, z & 1))
        for x, z, y, c in all_coords()
    ]


def other_pairs(j):
    return [
        (device_id(x, z, y, c), device_id((x + j) % 4, 2 * c + 1 - (z >> 1), y, z & 1))
        for x, z, y, c in all_coords()
    ]


def core_pairs():
    return [(device_id(x, z, y, c), device_id(x, z, y, 1 - c)) for x, z, y, c in all_coords()]


def head_pairs(k):
    return [(device_id(x, z, y, c), device_id((x + k) % 4, z, y, c)) for x, z, y, c in all_coords()]


def back(pairs):
    return [(b, a) for a, b in pairs]


def send(value, pairs):
    return lax.ppermute(value, AXES, pairs)


def dot(a, b):
    return jnp.dot(a, b, preferred_element_type=F32)


def dot_nt(a, b):
    return lax.dot_general(a, b, (((1,), (1,)), ((), ())), preferred_element_type=F32)


def silu(z):
    h = 0.5 * z
    return h + h * jnp.tanh(h)


def silu_slope(z):
    h = 0.5 * z
    t = jnp.tanh(h)
    return 0.5 * (1.0 + t) * (1.0 + h * (1.0 - t))


def row_statistics(x):
    mean = jnp.mean(x, axis=-1, keepdims=True)
    centred = x - mean
    inverse = lax.rsqrt(jnp.mean(centred * centred, axis=-1, keepdims=True) + EPS)
    return centred * inverse, inverse


def norm_backward(grad, hat, inverse):
    first = jnp.mean(grad, axis=-1, keepdims=True)
    second = jnp.mean(grad * hat, axis=-1, keepdims=True)
    return inverse * (grad - first - hat * second)


def column_of(row):
    return jnp.transpose(jnp.broadcast_to(row, (CHUNK, CHUNK)))


def ds(start, size):
    return pl.ds(pl.multiple_of(start, size), size)


VMEM = pl.BlockSpec(memory_space=pltpu.VMEM)
SMEM = pl.BlockSpec(memory_space=pltpu.SMEM)


def shape(dims, dtype):
    return jax.ShapeDtypeStruct(dims, dtype)


def call(kernel, ins, specs, outs, scratch=(), flops=0, name=None):
    moved = sum(a.size * a.dtype.itemsize for a in ins)
    moved += sum(o.size * jnp.dtype(o.dtype).itemsize for o in outs)
    return pl.pallas_call(
        kernel,
        out_shape=outs,
        in_specs=specs,
        out_specs=[VMEM] * len(outs),
        scratch_shapes=list(scratch),
        compiler_params=pltpu.CompilerParams(vmem_limit_bytes=40 * 1024 * 1024),
        cost_estimate=pl.CostEstimate(flops=flops, bytes_accessed=moved, transcendentals=0),
        name=name,
    )(*ins)


def lookup_kernel(meta, dest, ids_ref, table_ref, *rest):
    outs, (total, column) = rest[:8], rest[8:]
    step = pl.program_id(0)
    tile = table_ref.shape[2]

    @pl.when(step == 0)
    def _():
        for k in range(8):
            outs[k][...] = jnp.zeros_like(outs[k])
        total[...] = jnp.zeros_like(total)
        for b in range(2):
            column[b * CHUNK : (b + 1) * CHUNK, :] = column_of(ids_ref[b : b + 1, :].astype(F32))

    lane = lax.broadcasted_iota(jnp.int32, (ROWS, CHUNK), 1).astype(F32)
    base = (step * tile).astype(F32)
    wanted = column[...] - base
    hits = [jnp.where(wanted == lane + float(n * CHUNK), 1.0, 0.0).astype(BF) for n in range(tile // CHUNK)]
    total[...] += dot(jnp.concatenate(hits, axis=1), table_ref[0, 0])

    @pl.when(step == pl.num_programs(0) - 1)
    def _():
        own = meta[2] * 2 + meta[3]
        for k in range(8):
            for p in range(NBLK):

                @pl.when(dest[own * NBLK + p] == lax.rem(own + k, 8))
                def _():
                    outs[k][...] = total[p * BROWS : (p + 1) * BROWS, :].astype(BF)


def prepare_kernel(meta, len_own, len_swap, mask_own, mask_swap, incoming, w_out, bounds, starts, key_pos, query_pos, dmixed):
    same = (meta[1] >> 1) == meta[3]
    chunk = lax.broadcasted_iota(jnp.int32, (32, CHUNK), 0)
    position = chunk * CHUNK + lax.broadcasted_iota(jnp.int32, (32, CHUNK), 1)
    lane = lax.broadcasted_iota(jnp.int32, (8, CHUNK), 1)
    row = lax.broadcasted_iota(jnp.int32, (8, CHUNK), 0)
    first, last = lane * CHUNK, lane * CHUNK + CHUNK - 1
    start = jnp.zeros((32, CHUNK), jnp.int32)
    chunk_start = jnp.zeros((8, CHUNK), jnp.int32)
    chunk_stop = jnp.full((8, CHUNK), LENGTH, jnp.int32)
    end = jnp.int32(0)
    for d in range(len_own.shape[0]):
        end = end + jnp.where(same, len_own[d], len_swap[d])
        start = jnp.where(position >= end, end, start)
        chunk_start = jnp.where(first >= end, end, chunk_start)
        chunk_stop = jnp.where(last < end, jnp.minimum(chunk_stop, end), chunk_stop)
    starts[...] = start.astype(F32)
    bounds[...] = jnp.where(row == 0, chunk_start, chunk_stop - 1)
    mask = jnp.where(same, mask_own[...], mask_swap[...]).astype(F32)
    turned = jnp.transpose(mask).astype(BF)
    mask = mask.astype(BF)
    for n in range(8):
        cols = slice(n * WIDTH, (n + 1) * WIDTH)
        spot = lax.broadcasted_iota(jnp.int32, (BROWS, WIDTH), 1) + n * WIDTH
        pick = jnp.where(
            lax.broadcasted_iota(jnp.int32, (BROWS, WIDTH), 0) == spot // BROWS, 1.0, 0.0
        ).astype(BF)
        spot = spot.astype(F32)
        key_pos[:, cols] = jnp.where(dot(mask, pick) > 0.5, spot, FAR)
        query_pos[:, cols] = jnp.where(dot(turned, pick) > 0.5, spot, -1.0)
    dmixed[...] = dot_nt(incoming[...], w_out[...])


def project_kernel(meta, dest, slot, *rest):
    blocks, (w_ref, dmixed_ref), rest = rest[:8], rest[8:10], rest[10:]
    hist, pre = rest[:2]
    main, other, extra = rest[2:6], rest[6:10], rest[10:14]
    act, grads = rest[14:]
    own = meta[2] * 2 + meta[3]
    for k in range(8):
        source = lax.rem(own - k + 8, 8)
        for p in range(NBLK):

            @pl.when(dest[source * NBLK + p] == own)
            def _():
                hist[ds(slot[source * NBLK + p] * BROWS, BROWS), :] = blocks[k][...]

    hat, _ = row_statistics(hist[...].astype(F32))
    normed = hat.astype(BF)
    for n in range(4):
        cols = slice(n * WIDTH, (n + 1) * WIDTH)
        part = dot(normed, w_ref[:, cols])
        pre[:, cols] = part
        act[:, cols] = silu(part).astype(BF)
    grads[...] = (dmixed_ref[...] * act[:, 0:WIDTH].astype(F32)).astype(BF)
    for j in range(4):
        head = lax.rem(meta[0] + j, 4) * HD
        key = act[:, ds(3 * WIDTH + head, HD)]
        value = act[:, ds(WIDTH + head, HD)]
        main[j][:, 0:HD] = key
        main[j][:, HD : 2 * HD] = value
        main[j][:, 2 * HD : 3 * HD] = act[:, ds(2 * WIDTH + head, HD)]
        other[j][:, 0:HD] = key
        other[j][:, HD : 2 * HD] = value
        extra[j][...] = grads[:, ds(head, HD)]


def place(meta):
    return meta[0], meta[1] & 1, meta[3]


def chunk_of(t, z):
    return 4 * t + jnp.where(t < 4, z, 3 - z)


def valid_keys(starts, key_pos, i, tile):
    pos = lax.broadcasted_iota(jnp.int32, (CHUNK, CHUNK), 0).astype(F32) + (i * CHUNK).astype(F32)
    start = column_of(starts[pl.ds(i, 1), :])
    repeat = KEY_TILE // CHUNK
    pos = jnp.concatenate([pos] * repeat, axis=1)
    start = jnp.concatenate([start] * repeat, axis=1)

    def at(tile):
        halves = [
            jnp.broadcast_to(key_pos[pl.ds(2 * i + n, 1), ds(tile * KEY_TILE, KEY_TILE)], (BROWS, KEY_TILE))
            for n in range(2)
        ]
        key = jnp.concatenate(halves, axis=0)
        return (key >= start) & (key <= pos)

    return at


def forward_kernel(meta, bounds, starts, key_pos, *rest):
    main, other, smain, sother, extra = (rest[4 * n : 4 * n + 4] for n in range(5))
    keys, queries, grads, attn = rest[20:24]
    returned, stats = rest[24:28], rest[28]
    head, r, core = place(meta)
    mine = 2 * r + core
    for j in range(4):
        x = lax.rem(head - j + 4, 4)
        for ref, z in (
            (main[j], mine),
            (other[j], 2 * (1 - r) + core),
            (smain[j], 2 * r + 1 - core),
            (sother[j], 2 * (1 - r) + 1 - core),
        ):
            c = 4 * x + z
            keys[ds(c * CHUNK, CHUNK), :] = ref[0:CHUNK, 0 : 2 * HD]
            keys[ds((31 - c) * CHUNK, CHUNK), :] = ref[CHUNK:ROWS, 0 : 2 * HD]
        for low, t in ((0, x), (CHUNK, 7 - x)):
            queries[ds(t * CHUNK, CHUNK), :] = main[j][low : low + CHUNK, 2 * HD : 3 * HD]
            grads[ds(t * CHUNK, CHUNK), :] = extra[j][low : low + CHUNK, :]

    def chunk(t, carry):
        i = chunk_of(t, mine)
        allowed = valid_keys(starts, key_pos, i, KEY_TILE)
        q = queries[ds(t * CHUNK, CHUNK), :]

        def step(n, total):
            rows = ds(n * KEY_TILE, KEY_TILE)
            h = dot_nt(q, keys[rows, 0:HD]) * (0.5 * SCALE)
            probs = jnp.where(allowed(n), h + h * jnp.tanh(h), 0.0).astype(BF)
            return total + dot(probs, keys[rows, HD : 2 * HD])

        first = bounds[0, i] // KEY_TILE
        last = (i * CHUNK + CHUNK - 1) // KEY_TILE
        total = lax.fori_loop(first, last + 1, step, jnp.zeros((CHUNK, HD), F32))
        rows = ds(t * CHUNK, CHUNK)
        attn[rows, :] = total
        e = grads[rows, :].astype(F32)
        mean = jnp.mean(total, axis=1, keepdims=True)
        centred = total - mean
        lane = lax.broadcasted_iota(jnp.int32, (CHUNK, CHUNK), 1)
        packed = jnp.where(lane == 0, mean, 0.0)
        packed = jnp.where(lane == 1, jnp.sum(centred * centred, axis=1, keepdims=True), packed)
        packed = jnp.where(lane == 2, jnp.sum(e, axis=1, keepdims=True), packed)
        packed = jnp.where(lane == 3, jnp.sum(e * centred, axis=1, keepdims=True), packed)
        stats[:, rows] = jnp.transpose(packed)[0:8, :]
        return carry

    lax.fori_loop(0, 8, chunk, 0)
    for j in range(4):
        x = lax.rem(head - j + 4, 4)
        for low, t in ((0, x), (CHUNK, 7 - x)):
            returned[j][low : low + CHUNK, :] = attn[ds(t * CHUNK, CHUNK), :].astype(BF)


def attn_grad_kernel(s0, s1, s2, s3, attn, grads, out):
    parts = [s[...] for s in (s0, s1, s2, s3)]
    means = [s[0:1, :] for s in parts]
    mean = (means[0] + means[1] + means[2] + means[3]) * 0.25
    spread = sum(s[1:2, :] + HD * (m - mean) * (m - mean) for s, m in zip(parts, means))
    inverse = lax.rsqrt(spread * (1.0 / WIDTH) + EPS)
    e_mean = sum(s[2:3, :] for s in parts) * (1.0 / WIDTH)
    e_on = sum(s[3:4, :] + (m - mean) * s[2:3, :] for s, m in zip(parts, means))
    e_on = e_on * inverse * (1.0 / WIDTH)
    for t in range(8):
        rows = slice(t * CHUNK, (t + 1) * CHUNK)
        cols = [column_of(v[:, rows]) for v in (mean, inverse, e_mean, e_on)]
        hat = (attn[rows, :] - cols[0]) * cols[1]
        out[rows, :] = (cols[1] * (grads[rows, :].astype(F32) - cols[2] - hat * cols[3])).astype(BF)


def query_grad_kernel(meta, bounds, starts, key_pos, keys, queries, d_attn, *rest):
    outs, total_ref = rest[:4], rest[4]
    head, r, core = place(meta)
    mine = 2 * r + core

    def chunk(t, carry):
        i = chunk_of(t, mine)
        allowed = valid_keys(starts, key_pos, i, KEY_TILE)
        rows_q = ds(t * CHUNK, CHUNK)
        q = queries[rows_q, :]
        g = d_attn[rows_q, :]

        def step(n, total):
            rows = ds(n * KEY_TILE, KEY_TILE)
            k = keys[rows, 0:HD]
            h = dot_nt(q, k) * (0.5 * SCALE)
            dp = dot_nt(g, keys[rows, HD : 2 * HD])
            th = jnp.tanh(h)
            d_scores = jnp.where(allowed(n), dp * ((1.0 + th) * (1.0 + h - h * th)), 0.0)
            return total + dot(d_scores.astype(BF), k)

        first = bounds[0, i] // KEY_TILE
        last = (i * CHUNK + CHUNK - 1) // KEY_TILE
        total = lax.fori_loop(first, last + 1, step, jnp.zeros((CHUNK, HD), F32))
        total_ref[rows_q, :] = (total * (0.5 * SCALE)).astype(BF)
        return carry

    lax.fori_loop(0, 8, chunk, 0)
    for j in range(4):
        x = lax.rem(head - j + 4, 4)
        for low, t in ((0, x), (CHUNK, 7 - x)):
            outs[j][low : low + CHUNK, :] = total_ref[ds(t * CHUNK, CHUNK), :]


def key_grad_kernel(meta, bounds, starts, query_pos, *rest):
    main, other, smain = (rest[4 * n : 4 * n + 4] for n in range(3))
    d_own, d_swap = rest[12:14]
    out_main, out_other = rest[14:18], rest[18:22]
    keys, both, sums = rest[22:25]
    head, r, core = place(meta)
    for j in range(4):
        x = lax.rem(head - j + 4, 4)
        for low, t in ((0, x), (CHUNK, 7 - x)):
            for ref, grad, half in ((main[j], d_own, core), (smain[j], d_swap, 1 - core)):
                side = half if low == 0 else 1 - half
                rows = ds((2 * t + side) * CHUNK, CHUNK)
                both[rows, 0:HD] = ref[low : low + CHUNK, 2 * HD : 3 * HD]
                both[rows, HD : 2 * HD] = grad[ds(t * CHUNK, CHUNK), :]
        keys[2 * j * CHUNK : (2 * j + 2) * CHUNK, :] = main[j][:, 0 : 2 * HD]
        keys[(8 + 2 * j) * CHUNK : (10 + 2 * j) * CHUNK, :] = other[j][...]

    def pair_chunk(t):
        return 4 * t + jnp.where(t < 4, 2 * r, 2 - 2 * r)

    def chunk(n, carry):
        x = lax.rem(head - (n // 2) % 4 + 4, 4)
        z = jnp.where(n < 8, 2 * r, 2 * (1 - r)) + core
        c = 4 * x + z
        i = jnp.where(n % 2 == 0, c, 31 - c)
        rows_k = ds(n * CHUNK, CHUNK)
        k = keys[rows_k, 0:HD]
        v = keys[rows_k, HD : 2 * HD]
        pos = lax.broadcasted_iota(jnp.int32, (CHUNK, 2 * CHUNK), 0).astype(F32) + (i * CHUNK).astype(F32)

        def step(t, totals):
            d_key, d_value = totals
            rows = ds(t * 2 * CHUNK, 2 * CHUNK)
            q = both[rows, 0:HD]
            g = both[rows, HD : 2 * HD]
            first = pair_chunk(t)
            begin = jnp.concatenate([starts[pl.ds(first, 1), :], starts[pl.ds(first + 1, 1), :]], axis=1)
            lanes = ds(first * CHUNK, 2 * CHUNK)
            halves = [
                jnp.broadcast_to(query_pos[pl.ds(2 * i + m, 1), lanes], (BROWS, 2 * CHUNK)) for m in range(2)
            ]
            allowed = (pos <= jnp.concatenate(halves, axis=0)) & (pos >= begin)
            h = dot_nt(k, q) * (0.5 * SCALE)
            dp = dot_nt(v, g)
            th = jnp.tanh(h)
            up = 1.0 + th
            probs = jnp.where(allowed, h * up, 0.0).astype(BF)
            d_scores = jnp.where(allowed, dp * (up * (1.0 + h - h * th)), 0.0).astype(BF)
            return d_key + dot(d_scores, q), d_value + dot(probs, g)

        low = i // 4
        low = jnp.where(pair_chunk(low) + 1 >= i, low, low + 1)
        last = bounds[1, i]
        high = last // (4 * CHUNK)
        high = jnp.where(pair_chunk(high) * CHUNK <= last, high, high - 1)
        zero = jnp.zeros((CHUNK, HD), F32)
        d_key, d_value = lax.fori_loop(low, high + 1, step, (zero, zero))
        sums[rows_k, 0:HD] = (d_key * (0.5 * SCALE)).astype(BF)
        sums[rows_k, HD : 2 * HD] = d_value.astype(BF)
        return carry

    lax.fori_loop(0, 16, chunk, 0)
    for j in range(4):
        out_main[j][...] = sums[2 * j * CHUNK : (2 * j + 2) * CHUNK, :]
        out_other[j][...] = sums[(8 + 2 * j) * CHUNK : (10 + 2 * j) * CHUNK, :]


def output_kernel(meta, *rest):
    parts, rest = rest[:4], rest[4:]
    pre, dmixed, hist, w_out, w_in = rest[:5]
    out, partial = rest[5:7]
    attn = rest[7]
    for j in range(4):
        attn[:, ds(lax.rem(meta[0] + j, 4) * HD, HD)] = parts[j][...].astype(F32)
    hat, _ = row_statistics(attn[...])
    u_pre = pre[:, 0:WIDTH]
    u = silu(u_pre).astype(BF).astype(F32)
    mixed = (hat * u).astype(BF)
    out[...] = (hist[...].astype(F32) + dot(mixed, w_out[...])).astype(BF)
    d_pre = (dmixed[...] * hat * silu_slope(u_pre)).astype(BF)
    partial[...] = dot_nt(d_pre, w_in[:, 0:WIDTH])


def input_grad_kernel(meta, dest, slot, *rest):
    queries, main, other = (rest[4 * n : 4 * n + 4] for n in range(3))
    pre, partial, hist, incoming, w_in = rest[12:17]
    outs = rest[17:25]
    d_act, result = rest[25:27]
    for j in range(4):
        head = lax.rem(meta[0] + j, 4) * HD
        both = main[j][...].astype(F32) + other[j][...].astype(F32)
        d_act[:, ds(head, HD)] = both[:, HD : 2 * HD]
        d_act[:, ds(WIDTH + head, HD)] = queries[j][...].astype(F32)
        d_act[:, ds(2 * WIDTH + head, HD)] = both[:, 0:HD]
    total = partial[...]
    for n in range(3):
        cols = slice((n + 1) * WIDTH, (n + 2) * WIDTH)
        d_pre = (d_act[:, n * WIDTH : (n + 1) * WIDTH] * silu_slope(pre[:, cols])).astype(BF)
        total = total + dot_nt(d_pre, w_in[:, cols])
    hat, inverse = row_statistics(hist[...].astype(F32))
    result[...] = (incoming[...].astype(F32) + norm_backward(total, hat, inverse)).astype(BF)
    own = meta[2] * 2 + meta[3]
    for k in range(8):
        outs[k][...] = jnp.zeros_like(outs[k])
        source = lax.rem(own - k + 8, 8)
        for p in range(NBLK):

            @pl.when(dest[source * NBLK + p] == own)
            def _():
                outs[k][...] = result[ds(slot[source * NBLK + p] * BROWS, BROWS), :]


def table_grad_kernel(meta, dest, ids, *rest):
    blocks, out, rows = rest[:8], rest[8], rest[9]
    step = pl.program_id(0)
    tile = out.shape[2]

    @pl.when(step == 0)
    def _():
        own = meta[2] * 2 + meta[3]
        for k in range(8):
            for p in range(NBLK):

                @pl.when(dest[own * NBLK + p] == lax.rem(own + k, 8))
                def _():
                    rows[p * BROWS : (p + 1) * BROWS, :] = blocks[k][...]

    number = lax.broadcasted_iota(jnp.int32, (tile, ROWS), 0) + step * tile
    hits = jnp.where(number == ids[...], 1.0, 0.0).astype(BF)
    out[0, 0] = dot(hits, rows[...]).astype(BF)


def body(table, row_ids, dests, slots, lengths, tile_mask, w_in, w_out, output_gradient):
    x, z, y, c = (lax.axis_index(a).astype(jnp.int32) for a in AXES)
    dest = dests.reshape(8 * NBLK)
    slot = slots.reshape(8 * NBLK)
    tab_rows = table.shape[2]

    place_info = jnp.stack([x, z, y, c])
    swap = core_pairs()
    mask = tile_mask[0]
    bounds, starts, key_pos, query_pos, dmixed = call(
        prepare_kernel,
        [place_info, lengths[0], send(lengths[0], swap), mask, send(mask, swap), output_gradient[0], w_out],
        [SMEM] * 3 + [VMEM] * 4,
        [
            shape((8, CHUNK), jnp.int32),
            shape((32, CHUNK), F32),
            shape((64, LENGTH), F32),
            shape((64, LENGTH), F32),
            shape((ROWS, WIDTH), F32),
        ],
        flops=2 * ROWS * WIDTH * WIDTH,
        name="prepare",
    )

    tiles = 8
    tile = tab_rows // tiles
    block_shape = shape((BROWS, WIDTH), BF)
    whole_block = pl.BlockSpec((BROWS, WIDTH), lambda i: (0, 0))
    outgoing = pl.pallas_call(
        lookup_kernel,
        grid=(tiles,),
        in_specs=[
            SMEM,
            SMEM,
            pl.BlockSpec((2, CHUNK), lambda i: (0, 0)),
            pl.BlockSpec((1, 1, tile, WIDTH), lambda i: (0, 0, i, 0)),
        ],
        out_specs=[whole_block] * 8,
        out_shape=[block_shape] * 8,
        scratch_shapes=[pltpu.VMEM((ROWS, WIDTH), F32), pltpu.VMEM((ROWS, CHUNK), F32)],
        name="lookup",
    )(place_info, dest, row_ids.reshape(2, CHUNK), table)
    blocks = [outgoing[0]] + [send(outgoing[k], tab_pairs(k)) for k in range(1, 8)]

    incoming = output_gradient[0]
    qkv = shape((ROWS, 3 * HD), BF)
    two = shape((ROWS, 2 * HD), BF)
    one = shape((ROWS, HD), BF)
    hist, pre, *pieces = call(
        project_kernel,
        [place_info, dest, slot, *blocks, w_in, dmixed],
        [SMEM] * 3 + [VMEM] * 10,
        [shape((ROWS, WIDTH), BF), shape((ROWS, 4 * WIDTH), F32)] + [qkv] * 4 + [two] * 4 + [one] * 4,
        [pltpu.VMEM((ROWS, 4 * WIDTH), BF), pltpu.VMEM((ROWS, WIDTH), BF)],
        flops=2 * ROWS * WIDTH * 4 * WIDTH,
        name="project",
    )
    main = [send(pieces[j], main_pairs(j)) for j in range(4)]
    other = [send(pieces[4 + j], other_pairs(j)) for j in range(4)]
    extra = [send(pieces[8 + j], main_pairs(j)) for j in range(4)]
    smain = [send(v, swap) for v in main]
    sother = [send(v, swap) for v in other]

    quarter = LENGTH // 4
    keys, queries, grads, attn, *returned = call(
        forward_kernel,
        [place_info, bounds, starts, key_pos, *main, *other, *smain, *sother, *extra],
        [SMEM] * 2 + [VMEM] * 22,
        [
            shape((LENGTH, 2 * HD), BF),
            shape((quarter, HD), BF),
            shape((quarter, HD), BF),
            shape((quarter, HD), F32),
        ]
        + [one] * 4
        + [shape((8, quarter), F32)],
        flops=10**9,
        name="forward",
    )
    stats = returned.pop()
    from_heads = [send(stats, head_pairs(k)) for k in range(1, 4)]
    attn_back = [send(returned[j], back(main_pairs(j))) for j in range(4)]

    (d_attn,) = call(
        attn_grad_kernel,
        [stats, *from_heads, attn, grads],
        [VMEM] * 6,
        [shape((quarter, HD), BF)],
        flops=10**7,
        name="attn_grad",
    )
    d_swap = send(d_attn, swap)
    d_query = call(
        query_grad_kernel,
        [place_info, bounds, starts, key_pos, keys, queries, d_attn],
        [SMEM] * 2 + [VMEM] * 5,
        [one] * 4,
        [pltpu.VMEM((quarter, HD), BF)],
        flops=2 * 10**9,
        name="query_grad",
    )
    query_back = [send(d_query[j], back(main_pairs(j))) for j in range(4)]
    d_keys = call(
        key_grad_kernel,
        [place_info, bounds, starts, query_pos, *main, *other, *smain, d_attn, d_swap],
        [SMEM] * 2 + [VMEM] * 16,
        [two] * 8,
        [
            pltpu.VMEM((LENGTH // 2, 2 * HD), BF),
            pltpu.VMEM((LENGTH // 2, 2 * HD), BF),
            pltpu.VMEM((LENGTH // 2, 2 * HD), BF),
        ],
        flops=3 * 10**9,
        name="key_grad",
    )
    main_back = [send(d_keys[j], back(main_pairs(j))) for j in range(4)]
    other_back = [send(d_keys[4 + j], back(other_pairs(j))) for j in range(4)]

    layer_out, partial = call(
        output_kernel,
        [place_info, *attn_back, pre, dmixed, hist, w_out, w_in],
        [SMEM] + [VMEM] * 9,
        [shape((ROWS, WIDTH), BF), shape((ROWS, WIDTH), F32)],
        [pltpu.VMEM((ROWS, WIDTH), F32)],
        flops=4 * ROWS * WIDTH * WIDTH,
        name="output",
    )
    returning = call(
        input_grad_kernel,
        [place_info, dest, slot, *query_back, *main_back, *other_back, pre, partial, hist, incoming, w_in],
        [SMEM] * 3 + [VMEM] * 17,
        [block_shape] * 8,
        [pltpu.VMEM((ROWS, 3 * WIDTH), F32), pltpu.VMEM((ROWS, WIDTH), BF)],
        flops=6 * ROWS * WIDTH * WIDTH,
        name="input_grad",
    )
    came_back = [returning[0]] + [send(returning[k], back(tab_pairs(k))) for k in range(1, 8)]
    table_grad = pl.pallas_call(
        table_grad_kernel,
        grid=(tiles,),
        in_specs=[SMEM, SMEM, pl.BlockSpec((1, ROWS), lambda i: (0, 0))] + [whole_block] * 8,
        out_specs=pl.BlockSpec((1, 1, tile, WIDTH), lambda i: (0, 0, i, 0)),
        out_shape=shape((1, 1, tab_rows, WIDTH), BF),
        scratch_shapes=[pltpu.VMEM((ROWS, WIDTH), BF)],
        name="table_grad",
    )(place_info, dest, row_ids.reshape(1, ROWS), *came_back)
    return layer_out.reshape(1, ROWS, WIDTH), table_grad


def solution(mesh):
    fine = Mesh(mesh.devices.reshape(4, 4, 4, 2), AXES)
    ctx, tab = ("x", "z"), ("y", "c")
    in_specs = (
        P(ctx, tab, None, None),
        P(ctx, tab, None),
        P(ctx, None, None),
        P(ctx, None, None),
        P(tab, None),
        P(tab, None, None),
        P(),
        P(),
        P(tab, ctx, None),
    )
    out_specs = (P(tab, ctx, None), P(ctx, tab, None, None))
    return jax.shard_map(body, mesh=fine, in_specs=in_specs, out_specs=out_specs, check_vma=False)
```

time: 351 us -> 180 us (0.51); the launches traced: 344 us -> 179 us
  waiting for transfers between devices: 152 us -> 34.4 us
  matrix products: 105 us -> 0 us
  starting transfers between devices: 11 us -> 81.2 us
  Pallas kernels: 0 us -> 58.4 us
  local copies, waits for them, and re-layouts: 42.2 us -> 3.71 us
  other arithmetic: 17.4 us -> 0.66 us
  between operations: 15.7 us -> 0.98 us
    all_gather x4 -> x0, waiting for transfers between devices: 134 us -> none  [the longest x1 54 us: body(): value_in = lax.all_gather(value_part, 'ctx', axis=0, tiled=True)]
    dot_general x18 -> x0, matrix products: 105 us -> none  [the longest x1 18.6 us: query_compute(): jnp.einsum('hqk,khd->qhd', d_scores, key_heads, preferred_element_type=jn...]
    ppermute x0 -> x56, starting transfers between devices: none -> 81.2 us  [send(): return lax.ppermute(value, AXES, pairs)]
    pallas_call x0 -> x10, Pallas kernels: none -> 58.4 us  [the longest x8 45 us: call(): pl.pallas_call(kernel, out_shape=outs, in_specs=specs, out_specs=[VMEM] *...]
    ppermute x0 -> x56, waiting for transfers between devices: none -> 34.4 us  [send(): return lax.ppermute(value, AXES, pairs)]
    another operation x5 -> x0, local copies, waits for them, and re-layouts: 25.8 us -> none
    all_to_all x2 -> x0, waiting for transfers between devices: 16.8 us -> none  [the longest x1 9.41 us: body(): lax.all_to_all(outgoing, 'tab', split_axis=0, concat_axis=0, tiled=True)]
    all_to_all x2 -> x0, starting transfers between devices: 10.9 us -> none  [the longest x1 5.97 us: body(): lax.all_to_all(outgoing, 'tab', split_axis=0, concat_axis=0, tiled=True)]
  transfers between devices with their start and end apart: 6 -> 56, of which waited for: 5 -> 18; matrix products, arithmetic and copies ran while one was open for 22% -> 0% of each run, Pallas kernels for 0% -> 15%
where the time goes in v1:
time: 180 us; the launch traced here: 179 us
  starting transfers between devices  81.2 us (45%)
  Pallas kernels  58.4 us (32%)
  waiting for transfers between devices  34.4 us (19%)
  local copies, waits for them, and re-layouts  3.71 us (2%)
    ppermute x56, starting transfers between devices, send(): return lax.ppermute(value, AXES, pairs)  81.2 us
    pallas_call x8, Pallas kernels, call(): pl.pallas_call(kernel, out_shape=outs, in_specs=specs, out_specs=[VMEM] *...  45 us
    ppermute x56, waiting for transfers between devices, send(): return lax.ppermute(value, AXES, pairs)  34.4 us
    pallas_call x1, Pallas kernels, body(): pl.pallas_call(lookup_kernel, grid=(tiles,), in_specs=[SMEM, SMEM, pl.Blo...  7.3 us
    pallas_call x1, Pallas kernels, body(): pl.pallas_call(table_grad_kernel, grid=(tiles,), in_specs=[SMEM, SMEM, pl...  6.1 us
  transfers between devices with their start and end apart: 56, of which 18 were waited for; matrix products, arithmetic and copies ran while one was open for 0% of the time, Pallas kernels for 15%

profile of v1, /device:TPU:1, one launch (start us, length us, event | category | flops | bytes accessed | tf_op | source)
XLA Modules:
  0.0 179.3 jit_solution(18265533208628276618)
XLA Ops:
  0.6 0.8 copy.13
  1.4 0.7 reshape.19.dest
  2.1 0.7 pad_add_fusion.meta
  2.8 7.3 %lookup.1 = (bf16[64,512]{1,0:T(8,128)(2,1)}, bf16[64,512]{1,0:T(8,128)(2,1)}, bf16[64,512]{1,0:T(8,128)(2,1)}, bf16[64,512]{1,0:T(8,128)(2,1)}, bf16[64,512]{1,...) custom-call(s32[4]{0:T(128)} %pad_add_fusion.meta, s32[32]{0:T(128)} %reshape.19.dest, ...), custom_call_target="tpu_custom_call" | custom-call | tf_op jit(solution)/shard_map/lookup/pallas_call | solution.py:524
  10.1 2.7 %collective-permute-start.2 = (bf16[64,512]{1,0:T(8,128)(2,1)}, bf16[64,512]{1,0:T(8,128)(2,1)S(1)}, u32[]{:S(2)}, u32[]{:S(2)}) collective-permute-start(bf16[64,512]{1,0:T(8,128)(2,1)} %get-tuple-element.64), channel_id=1, source_target_pairs={{0,1},{1,2},{2,3},{3,4},{4,5},{5,6},{6,7},{7,0},{8,9},{9,10},{10,1... | collective-permute-start | bytes 196616 | tf_op jit(solution)/shard_map/ppermute | solution.py:70
  12.8 1.3 collective-permute-start.3
  14.6 1.7 collective-permute-start.4
  16.3 1.3 collective-permute-start.5
  17.5 1.7 collective-permute-start.6
  19.4 2.2 %collective-permute-start.8 = (bf16[64,512]{1,0:T(8,128)(2,1)}, bf16[64,512]{1,0:T(8,128)(2,1)S(1)}, u32[]{:S(2)}, u32[]{:S(2)}) collective-permute-start(bf16[64,512]{1,0:T(8,128)(2,1)} %get-tuple-element.70), channel_id=1, source_target_pairs={{0,7},{1,0},{2,1},{3,2},{4,3},{5,4},{6,5},{7,6},{8,15},{9,8},{10,9... | collective-permute-start | bytes 196616 | tf_op jit(solution)/shard_map/ppermute | solution.py:70
  21.8 1.2 prepare.1
  23.1 0.9 collective-permute-done.7.rest_6_
  23.9 0.7 collective-permute-done.8.rest_7_
  24.6 0.8 copy-done.4
  25.5 2.4 %project.1 = (bf16[256,512]{1,0:T(8,128)(2,1)S(1)}, f32[256,2048]{1,0:T(8,128)S(1)}, bf16[256,384]{1,0:T(8,128)(2,1)S(1)}, bf16[256,384]{1,0:T(8,128)(2,1)S(1)},...) custom-call(s32[4]{0:T(128)S(1)} %copy-done.6, ...), custom_call_target="tpu_custom_call" | custom-call | flops 536870912 | bytes 7078160 | tf_op jit(solution)/shard_map/project/pallas_call | solution.py:124
  27.9 5.4 %collective-permute-start.25 = (bf16[256,128]{1,0:T(8,128)(2,1)S(1)}, bf16[256,128]{1,0:T(8,128)(2,1)S(1)}, u32[]{:S(2)}, u32[]{:S(2)}) collective-permute-start(bf16[256,128]{1,0:T(8,128)(2,1)S(1)} %get-tuple-element.80), channel_id=1, source_target_pairs={{0,0},{1,16},{2,2},{3,18},{4,4},{5,20},{6,6},{7,22},{8,1},{9,17},{... | collective-permute-start | bytes 196616 | tf_op jit(solution)/shard_map/ppermute | solution.py:70
  33.3 1.1 collective-permute-start.26
  34.4 2.4 %collective-permute-start.13 = (bf16[256,256]{1,0:T(8,128)(2,1)S(1)}, bf16[256,256]{1,0:T(8,128)(2,1)S(1)}, u32[]{:S(2)}, u32[]{:S(2)}) collective-permute-start(bf16[256,256]{1,0:T(8,128)(2,1)S(1)} %get-tuple-element.76), channel_id=1, source_target_pairs={{0,8},{1,24},{2,10},{3,26},{4,12},{5,28},{6,14},{7,30},{8,9},{9,25... | collective-permute-start | bytes 393224 | tf_op jit(solution)/shard_map/ppermute | solution.py:70
  36.8 4.3 %collective-permute-start.28 = (bf16[256,128]{1,0:T(8,128)(2,1)S(1)}, bf16[256,128]{1,0:T(8,128)(2,1)S(1)}, u32[]{:S(2)}, u32[]{:S(2)}) collective-permute-start(bf16[256,128]{1,0:T(8,128)(2,1)S(1)} %get-tuple-element.83), channel_id=1, source_target_pairs={{0,96},{1,112},{2,98},{3,114},{4,100},{5,116},{6,102},{7,118},{8,9... | collective-permute-start | bytes 196616 | tf_op jit(solution)/shard_map/ppermute | solution.py:70
  41.7 2.6 %collective-permute-start.15 = (bf16[256,256]{1,0:T(8,128)(2,1)S(1)}, bf16[256,256]{1,0:T(8,128)(2,1)S(1)}, u32[]{:S(2)}, u32[]{:S(2)}) collective-permute-start(bf16[256,256]{1,0:T(8,128)(2,1)S(1)} %get-tuple-element.78), channel_id=1, source_target_pairs={{0,72},{1,88},{2,74},{3,90},{4,76},{5,92},{6,78},{7,94},{8,73},{9,... | collective-permute-start | bytes 393224 | tf_op jit(solution)/shard_map/ppermute | solution.py:70
  44.3 3.5 %collective-permute-start.9 = (bf16[256,384]{1,0:T(8,128)(2,1)S(1)}, bf16[256,384]{1,0:T(8,128)(2,1)S(1)}, u32[]{:S(2)}, u32[]{:S(2)}) collective-permute-start(bf16[256,384]{1,0:T(8,128)(2,1)S(1)} %get-tuple-element.72), channel_id=1, source_target_pairs={{0,0},{1,16},{2,2},{3,18},{4,4},{5,20},{6,6},{7,22},{8,1},{9,17},{... | collective-permute-start | bytes 589832 | tf_op jit(solution)/shard_map/ppermute | solution.py:70
  47.9 0.9 collective-permute-start.10
  48.8 2.0 %collective-permute-start.16 = (bf16[256,256]{1,0:T(8,128)(2,1)S(1)}, bf16[256,256]{1,0:T(8,128)(2,1)S(1)}, u32[]{:S(2)}, u32[]{:S(2)}) collective-permute-start(bf16[256,256]{1,0:T(8,128)(2,1)S(1)} %get-tuple-element.79), channel_id=1, source_target_pairs={{0,104},{1,120},{2,106},{3,122},{4,108},{5,124},{6,110},{7,126},{8... | collective-permute-start | bytes 393224 | tf_op jit(solution)/shard_map/ppermute | solution.py:70
  50.8 2.4 %collective-permute-done.14.rest_5_ = bf16[256,256]{1,0:T(8,128)(2,1)S(1)} collective-permute-done((bf16[256,256]{1,0:T(8,128)(2,1)S(1)}, bf16[256,256]{1,0:T(8,128)(2,1)S(1)}, u32[]{:S(2)}, u32[]{:S(2)}) %collective-permute-start.14) | collective-permute-done | bytes 131104 | tf_op jit(solution)/shard_map/ppermute | solution.py:70
  53.2 2.3 %collective-permute-start.12 = (bf16[256,384]{1,0:T(8,128)(2,1)S(1)}, bf16[256,384]{1,0:T(8,128)(2,1)S(1)}, u32[]{:S(2)}, u32[]{:S(2)}) collective-permute-start(bf16[256,384]{1,0:T(8,128)(2,1)S(1)} %get-tuple-element.75), channel_id=1, source_target_pairs={{0,96},{1,112},{2,98},{3,114},{4,100},{5,116},{6,102},{7,118},{8,9... | collective-permute-start | bytes 589832 | tf_op jit(solution)/shard_map/ppermute | solution.py:70
  55.5 1.1 collective-permute-done.16.rest_7_
  57.2 4.3 %collective-permute-done.11.rest_2_ = bf16[256,384]{1,0:T(8,128)(2,1)S(1)} collective-permute-done((bf16[256,384]{1,0:T(8,128)(2,1)S(1)}, bf16[256,384]{1,0:T(8,128)(2,1)S(1)}, u32[]{:S(2)}, u32[]{:S(2)}) %collective-permute-start.11) | collective-permute-done | bytes 196640 | tf_op jit(solution)/shard_map/ppermute | solution.py:70
  61.8 1.6 collective-permute-done.12.rest_3_
  63.4 1.4 collective-permute-start.18
  65.6 1.1 collective-permute-done.24.rest_15_
  66.8 12.7 %forward.1 = (bf16[4096,256]{1,0:T(8,128)(2,1)S(1)}, bf16[1024,128]{1,0:T(8,128)(2,1)S(1)}, bf16[1024,128]{1,0:T(8,128)(2,1)S(1)}, f32[1024,128]{1,0:T(8,128)S(1...) custom-call(s32[4]{0:T(128)S(1)} %copy-done.6, ...), custom_call_target="tpu_custom_call" | custom-call | flops 1000000000 | bytes 7393296 | tf_op jit(solution)/shard_map/forward/pallas_call | solution.py:124
  79.5 2.4 %collective-permute-start.35 = (f32[8,1024]{1,0:T(8,128)S(1)}, f32[8,1024]{1,0:T(8,128)S(1)}, u32[]{:S(2)}, u32[]{:S(2)}) collective-permute-start(f32[8,1024]{1,0:T(8,128)S(1)} %get-tuple-element.93.s0), channel_id=1, source_target_pairs={{0,96},{1,97},{2,98},{3,99},{4,100},{5,101},{6,102},{7,103},{8,104... | collective-permute-start | bytes 98312 | tf_op jit(solution)/shard_map/ppermute | solution.py:70
  81.9 0.7 collective-permute-start.33
  82.9 3.3 %collective-permute-done.34.s2 = f32[8,1024]{1,0:T(8,128)S(1)} collective-permute-done((f32[8,1024]{1,0:T(8,128)S(1)}, f32[8,1024]{1,0:T(8,128)S(1)}, u32[]{:S(2)}, u32[]{:S(2)}) %collective-permute-start.34) | collective-permute-done | bytes 32800 | tf_op jit(solution)/shard_map/ppermute | solution.py:70
  86.8 2.7 %collective-permute-start.40 = (bf16[1024,128]{1,0:T(8,128)(2,1)S(1)}, bf16[1024,128]{1,0:T(8,128)(2,1)S(1)}, u32[]{:S(2)}, u32[]{:S(2)}) collective-permute-start(bf16[1024,128]{1,0:T(8,128)(2,1)S(1)} %attn_grad.1.d_attn.rest_12_), channel_id=1, source_target_pairs={{0,1},{1,0},{2,3},{3,2},{4,5},{5,4},{6,7},{7,6},{8,9},{9,8},{10,11... | collective-permute-start | bytes 786440 | tf_op jit(solution)/shard_map/ppermute | solution.py:70
  89.6 2.8 %collective-permute-start.29 = (bf16[256,128]{1,0:T(8,128)(2,1)S(1)}, bf16[256,128]{1,0:T(8,128)(2,1)S(1)}, u32[]{:S(2)}, u32[]{:S(2)}) collective-permute-start(bf16[256,128]{1,0:T(8,128)(2,1)S(1)} %get-tuple-element.84), channel_id=1, source_target_pairs={{0,0},{16,1},{2,2},{18,3},{4,4},{20,5},{6,6},{22,7},{1,8},{17,9},{... | collective-permute-start | bytes 196616 | tf_op jit(solution)/shard_map/ppermute | solution.py:70
  92.8 2.5 %collective-permute-start.31 = (bf16[256,128]{1,0:T(8,128)(2,1)S(1)}, bf16[256,128]{1,0:T(8,128)(2,1)S(1)}, u32[]{:S(2)}, u32[]{:S(2)}) collective-permute-start(bf16[256,128]{1,0:T(8,128)(2,1)S(1)} %get-tuple-element.86), channel_id=1, source_target_pairs={{64,0},{80,1},{66,2},{82,3},{68,4},{84,5},{70,6},{86,7},{65,8},{81... | collective-permute-start | bytes 196616 | tf_op jit(solution)/shard_map/ppermute | solution.py:70
  95.3 1.1 collective-permute-start.32
  96.4 11.4 %query_grad.1 = (bf16[256,128]{1,0:T(8,128)(2,1)S(1)}, bf16[256,128]{1,0:T(8,128)(2,1)S(1)}, bf16[256,128]{1,0:T(8,128)(2,1)S(1)}, bf16[256,128]{1,0:T(8,128)(2,1)S(1)}) custom-call(s32[4]{0:T(128)S(1)} %copy-done.6, s32[8,128]{1,0:T(8,128)S(1)} %get-tuple-element.60.bounds, f32[32,128]{1,0:T(8,128)S(1)} %get-tuple-element.61.starts, ...), custom_call_target="tpu_custom_call" | custom-call | flops 2000000000 | bytes 3952656 | tf_op jit(solution)/shard_map/query_grad/pallas_call | solution.py:124
  107.9 2.8 %collective-permute-start.36 = (bf16[256,128]{1,0:T(8,128)(2,1)S(1)}, bf16[256,128]{1,0:T(8,128)(2,1)S(1)}, u32[]{:S(2)}, u32[]{:S(2)}) collective-permute-start(bf16[256,128]{1,0:T(8,128)(2,1)S(1)} %get-tuple-element.96), channel_id=1, source_target_pairs={{0,0},{16,1},{2,2},{18,3},{4,4},{20,5},{6,6},{22,7},{1,8},{17,9},{... | collective-permute-start | bytes 196616 | tf_op jit(solution)/shard_map/ppermute | solution.py:70
  110.7 2.0 %collective-permute-start.37 = (bf16[256,128]{1,0:T(8,128)(2,1)S(1)}, bf16[256,128]{1,0:T(8,128)(2,1)S(1)}, u32[]{:S(2)}, u32[]{:S(2)}) collective-permute-start(bf16[256,128]{1,0:T(8,128)(2,1)S(1)} %get-tuple-element.97), channel_id=1, source_target_pairs={{32,0},{48,1},{34,2},{50,3},{36,4},{52,5},{38,6},{54,7},{33,8},{49... | collective-permute-start | bytes 196616 | tf_op jit(solution)/shard_map/ppermute | solution.py:70
  112.7 12.6 %key_grad.1 = (bf16[256,256]{1,0:T(8,128)(2,1)S(1)}, bf16[256,256]{1,0:T(8,128)(2,1)S(1)}, bf16[256,256]{1,0:T(8,128)(2,1)S(1)}, bf16[256,256]{1,0:T(8,128)(2,1)...) custom-call(s32[4]{0:T(128)S(1)} %copy-done.6, ...), custom_call_target="tpu_custom_call" | custom-call | flops 3000000000 | bytes 4739088 | tf_op jit(solution)/shard_map/key_grad/pallas_call | solution.py:124
  125.3 2.1 %collective-permute-start.41 = (bf16[256,256]{1,0:T(8,128)(2,1)S(1)}, bf16[256,256]{1,0:T(8,128)(2,1)S(1)}, u32[]{:S(2)}, u32[]{:S(2)}) collective-permute-start(bf16[256,256]{1,0:T(8,128)(2,1)S(1)} %get-tuple-element.101), channel_id=1, source_target_pairs={{0,0},{16,1},{2,2},{18,3},{4,4},{20,5},{6,6},{22,7},{1,8},{17,9},{... | collective-permute-start | bytes 393224 | tf_op jit(solution)/shard_map/ppermute | solution.py:70
  127.4 3.8 %collective-permute-start.42 = (bf16[256,256]{1,0:T(8,128)(2,1)S(1)}, bf16[256,256]{1,0:T(8,128)(2,1)S(1)}, u32[]{:S(2)}, u32[]{:S(2)}) collective-permute-start(bf16[256,256]{1,0:T(8,128)(2,1)S(1)} %get-tuple-element.102), channel_id=1, source_target_pairs={{32,0},{48,1},{34,2},{50,3},{36,4},{52,5},{38,6},{54,7},{33,8},{49... | collective-permute-start | bytes 393224 | tf_op jit(solution)/shard_map/ppermute | solution.py:70
  131.2 0.7 collective-permute-start.43
  131.9 2.3 %collective-permute-start.38 = (bf16[256,128]{1,0:T(8,128)(2,1)S(1)}, bf16[256,128]{1,0:T(8,128)(2,1)S(1)}, u32[]{:S(2)}, u32[]{:S(2)}) collective-permute-start(bf16[256,128]{1,0:T(8,128)(2,1)S(1)} %get-tuple-element.98), channel_id=1, source_target_pairs={{64,0},{80,1},{66,2},{82,3},{68,4},{84,5},{70,6},{86,7},{65,8},{81... | collective-permute-start | bytes 196616 | tf_op jit(solution)/shard_map/ppermute | solution.py:70
  134.3 1.9 %collective-permute-start.39 = (bf16[256,128]{1,0:T(8,128)(2,1)S(1)}, bf16[256,128]{1,0:T(8,128)(2,1)S(1)}, u32[]{:S(2)}, u32[]{:S(2)}) collective-permute-start(bf16[256,128]{1,0:T(8,128)(2,1)S(1)} %get-tuple-element.99), channel_id=1, source_target_pairs={{96,0},{112,1},{98,2},{114,3},{100,4},{116,5},{102,6},{118,7},{97,... | collective-permute-start | bytes 196616 | tf_op jit(solution)/shard_map/ppermute | solution.py:70
  136.1 6.2 %collective-permute-done.38.rest_2_ = bf16[256,128]{1,0:T(8,128)(2,1)S(1)} collective-permute-done((bf16[256,128]{1,0:T(8,128)(2,1)S(1)}, bf16[256,128]{1,0:T(8,128)(2,1)S(1)}, u32[]{:S(2)}, u32[]{:S(2)}) %collective-permute-start.38) | collective-permute-done | bytes 65568 | tf_op jit(solution)/shard_map/ppermute | solution.py:70
  142.4 1.3 collective-permute-done.39.rest_3_
  143.6 1.4 collective-permute-start.45
  145.1 1.6 collective-permute-start.46
  146.6 1.5 collective-permute-start.47
  148.1 1.1 collective-permute-start.48
  149.2 2.0 %output.1 = (bf16[256,512]{1,0:T(8,128)(2,1)}, f32[256,512]{1,0:T(8,128)S(1)}) custom-call(s32[4]{0:T(128)S(1)} %copy-done.6, bf16[256,128]{1,0:T(8,128)(2,1)S(1)} %collective-permute-done.29.rest_0_, bf16[256,128]{1,0:T(8,128)(2,1)S(1)} %collective-permute-done.30.rest_1_, bf16[256,128]{1,0:T(8,128)(2,1)S(1)} %collective-permute-done.31.rest_2_, ...), custom_call_target="tpu_custom_call" | custom-call | flops 268435456 | bytes 6553616 | tf_op jit(solution)/shard_map/output/pallas_call | solution.py:124
  151.6 0.8 collective-permute-done.46.rest_9_
  152.4 2.3 %collective-permute-done.47.rest_10_ = bf16[256,256]{1,0:T(8,128)(2,1)S(1)} collective-permute-done((bf16[256,256]{1,0:T(8,128)(2,1)S(1)}, bf16[256,256]{1,0:T(8,128)(2,1)S(1)}, u32[]{:S(2)}, u32[]{:S(2)}) %collective-permute-start.47) | collective-permute-done | bytes 131104 | tf_op jit(solution)/shard_map/ppermute | solution.py:70
  154.7 2.7 %collective-permute-done.48.rest_11_ = bf16[256,256]{1,0:T(8,128)(2,1)S(1)} collective-permute-done((bf16[256,256]{1,0:T(8,128)(2,1)S(1)}, bf16[256,256]{1,0:T(8,128)(2,1)S(1)}, u32[]{:S(2)}, u32[]{:S(2)}) %collective-permute-start.48) | collective-permute-done | bytes 131104 | tf_op jit(solution)/shard_map/ppermute | solution.py:70
  157.4 2.1 %input_grad.1 = (bf16[64,512]{1,0:T(8,128)(2,1)S(1)}, bf16[64,512]{1,0:T(8,128)(2,1)S(1)}, bf16[64,512]{1,0:T(8,128)(2,1)S(1)}, bf16[64,512]{1,0:T(8,128)(2,1)S(...) custom-call(s32[4]{0:T(128)S(1)} %copy-done.6, ...), custom_call_target="tpu_custom_call" | custom-call | flops 402653184 | bytes 7078160 | tf_op jit(solution)/shard_map/input_grad/pallas_call | solution.py:124
  160.2 2.0 %collective-permute-start.49 = (bf16[64,512]{1,0:T(8,128)(2,1)S(1)}, bf16[64,512]{1,0:T(8,128)(2,1)S(1)}, u32[]{:S(2)}, u32[]{:S(2)}) collective-permute-start(bf16[64,512]{1,0:T(8,128)(2,1)S(1)} %get-tuple-element.111), channel_id=1, source_target_pairs={{1,0},{2,1},{3,2},{4,3},{5,4},{6,5},{7,6},{0,7},{9,8},{10,9},{11,1... | collective-permute-start | bytes 196616 | tf_op jit(solution)/shard_map/ppermute | solution.py:70
  162.8 2.8 %collective-permute-start.52 = (bf16[64,512]{1,0:T(8,128)(2,1)S(1)}, bf16[64,512]{1,0:T(8,128)(2,1)S(1)}, u32[]{:S(2)}, u32[]{:S(2)}) collective-permute-start(bf16[64,512]{1,0:T(8,128)(2,1)S(1)} %get-tuple-element.114), channel_id=1, source_target_pairs={{4,0},{5,1},{6,2},{7,3},{0,4},{1,5},{2,6},{3,7},{12,8},{13,9},{14,... | collective-permute-start | bytes 196616 | tf_op jit(solution)/shard_map/ppermute | solution.py:70
  165.6 2.1 %collective-permute-start.53 = (bf16[64,512]{1,0:T(8,128)(2,1)S(1)}, bf16[64,512]{1,0:T(8,128)(2,1)S(1)}, u32[]{:S(2)}, u32[]{:S(2)}) collective-permute-start(bf16[64,512]{1,0:T(8,128)(2,1)S(1)} %get-tuple-element.115), channel_id=1, source_target_pairs={{5,0},{6,1},{7,2},{0,3},{1,4},{2,5},{3,6},{4,7},{13,8},{14,9},{15,... | collective-permute-start | bytes 196616 | tf_op jit(solution)/shard_map/ppermute | solution.py:70
  168.1 3.2 %collective-permute-done.53.rest_5_ = bf16[64,512]{1,0:T(8,128)(2,1)S(1)} collective-permute-done((bf16[64,512]{1,0:T(8,128)(2,1)S(1)}, bf16[64,512]{1,0:T(8,128)(2,1)S(1)}, u32[]{:S(2)}, u32[]{:S(2)}) %collective-permute-start.53) | collective-permute-done | bytes 65568 | tf_op jit(solution)/shard_map/ppermute | solution.py:70
  171.3 1.2 collective-permute-done.54.rest_6_
  173.2 6.1 %table_grad.1 = bf16[1,1,4096,512]{3,2,1,0:T(8,128)(2,1)} custom-call(s32[4]{0:T(128)} %pad_add_fusion.meta, s32[32]{0:T(128)} %reshape.19.dest, s32[1,256]{1,0:T(1,128)} %bitcast.17, bf16[64,512]{1,0:T(8,128)(2,1)} %copy-done.3, bf16[64,512]{1,0:T(8,128)(2,1)} %copy-done.9, bf16[64,512]{1,0:T(8,128)(2,1)} %copy-done.10, bf16[64,512]{1,0:T(8,128)(2,1)} %copy-done.11, ...), custom_call_target="tpu_custom_call" | custom-call | tf_op jit(solution)/shard_map/table_grad/pallas_call | solution.py:633
  (97 shorter events, 7.2 us)
Async XLA Ops:
  2.7 11.3 %copy-start.5 = (s32[1,64,64]{2,1,0:T(8,128)S(1)}, s32[1,64,64]{2,1,0:T(8,128)}, u32[]{:S(2)}) copy-start(s32[1,64,64]{2,1,0:T(8,128)} %param.14) | copy-start | bytes 49156
  2.7 11.4 %copy-start.8 = (s32[1,16]{1,0:T(1,128)S(1)}, s32[1,16]{1,0:T(1,128)}, u32[]{:S(2)}) copy-start(s32[1,16]{1,0:T(1,128)} %param.13) | copy-start | bytes 196
  2.7 18.9 %copy-start.16 = (s32[1,8,4]{1,2,0:T(4,128)S(1)}, s32[1,8,4]{1,2,0:T(4,128)}, u32[]{:S(2)}) copy-start(s32[1,8,4]{1,2,0:T(4,128)} %param.12) | copy-start | bytes 388
  2.7 19.1 %copy-start.1 = (bf16[512,512]{1,0:T(8,128)(2,1)S(1)}, bf16[512,512]{1,0:T(8,128)(2,1)}, u32[]{:S(2)}) copy-start(bf16[512,512]{1,0:T(8,128)(2,1)} %rest_7_.1) | copy-start | bytes 1572868
  2.7 19.0 %copy-start.2 = (bf16[1,256,512]{2,1,0:T(8,128)(2,1)S(1)}, bf16[1,256,512]{2,1,0:T(8,128)(2,1)}, u32[]{:S(2)}) copy-start(bf16[1,256,512]{2,1,0:T(8,128)(2,1)} %param.17) | copy-start | bytes 786436
  2.8 19.0 %copy-start.6 = (s32[4]{0:T(128)S(1)}, s32[4]{0:T(128)}, u32[]{:S(2)}) copy-start(s32[4]{0:T(128)} %pad_add_fusion.meta) | copy-start | bytes 52
  2.8 21.9 %copy-start = (bf16[512,2048]{1,0:T(8,128)(2,1)S(1)}, bf16[512,2048]{1,0:T(8,128)(2,1)}, u32[]{:S(2)}) copy-start(bf16[512,2048]{1,0:T(8,128)(2,1)} %rest_16_.1) | copy-start | bytes 6291460
  2.8 21.8 %copy-start.7 = (s32[32]{0:T(128)S(1)}, s32[32]{0:T(128)}, u32[]{:S(2)}) copy-start(s32[32]{0:T(128)} %reshape.19.dest) | copy-start | bytes 388
  10.1 9.2 %collective-permute-start.2 = (bf16[64,512]{1,0:T(8,128)(2,1)}, bf16[64,512]{1,0:T(8,128)(2,1)S(1)}, u32[]{:S(2)}, u32[]{:S(2)}) collective-permute-start(bf16[64,512]{1,0:T(8,128)(2,1)} %get-tuple-element.64), channel_id=1, source_target_pairs={{0,1},{1,2},{2,3},{3,4},{4,5},{5,6},{6,7},{7,0},{8,9},{9,10},{10,1... | collective-permute-start | bytes 196616 | tf_op jit(solution)/shard_map/ppermute | solution.py:70
  12.8 6.6 %collective-permute-start.3 = (bf16[64,512]{1,0:T(8,128)(2,1)}, bf16[64,512]{1,0:T(8,128)(2,1)S(1)}, u32[]{:S(2)}, u32[]{:S(2)}) collective-permute-start(bf16[64,512]{1,0:T(8,128)(2,1)} %get-tuple-element.65), channel_id=1, source_target_pairs={{0,2},{1,3},{2,4},{3,5},{4,6},{5,7},{6,0},{7,1},{8,10},{9,11},{10,... | collective-permute-start | bytes 196616 | tf_op jit(solution)/shard_map/ppermute | solution.py:70
  14.1 3.5 %collective-permute-start.1 = (s32[64,64]{1,0:T(8,128)S(1)}, s32[64,64]{1,0:T(8,128)S(1)}, u32[]{:S(2)}, u32[]{:S(2)}) collective-permute-start(s32[64,64]{1,0:T(8,128)S(1)} %bitcast.12), channel_id=1, source_target_pairs={{0,1},{1,0},{2,3},{3,2},{4,5},{5,4},{6,7},{7,6},{8,9},{9,8},{10,11... | collective-permute-start | bytes 49160 | tf_op jit(solution)/shard_map/ppermute | solution.py:70
  14.1 2.2 %collective-permute-start = (s32[16]{0:T(128)S(1)}, s32[16]{0:T(128)S(1)}, u32[]{:S(2)}, u32[]{:S(2)}) collective-permute-start(s32[16]{0:T(128)S(1)} %bitcast.14), channel_id=1, source_target_pairs={{0,1},{1,0},{2,3},{3,2},{4,5},{5,4},{6,7},{7,6},{8,9},{9,8},{10,11... | collective-permute-start | bytes 200 | tf_op jit(solution)/shard_map/ppermute | solution.py:70
  14.6 8.4 %collective-permute-start.4 = (bf16[64,512]{1,0:T(8,128)(2,1)}, bf16[64,512]{1,0:T(8,128)(2,1)S(1)}, u32[]{:S(2)}, u32[]{:S(2)}) collective-permute-start(bf16[64,512]{1,0:T(8,128)(2,1)} %get-tuple-element.66), channel_id=1, source_target_pairs={{0,3},{1,4},{2,5},{3,6},{4,7},{5,0},{6,1},{7,2},{8,11},{9,12},{10,... | collective-permute-start | bytes 196616 | tf_op jit(solution)/shard_map/ppermute | solution.py:70
  16.3 6.8 %collective-permute-start.5 = (bf16[64,512]{1,0:T(8,128)(2,1)}, bf16[64,512]{1,0:T(8,128)(2,1)S(1)}, u32[]{:S(2)}, u32[]{:S(2)}) collective-permute-start(bf16[64,512]{1,0:T(8,128)(2,1)} %get-tuple-element.67), channel_id=1, source_target_pairs={{0,4},{1,5},{2,6},{3,7},{4,0},{5,1},{6,2},{7,3},{8,12},{9,13},{10,... | collective-permute-start | bytes 196616 | tf_op jit(solution)/shard_map/ppermute | solution.py:70
  17.5 5.5 %collective-permute-start.6 = (bf16[64,512]{1,0:T(8,128)(2,1)}, bf16[64,512]{1,0:T(8,128)(2,1)S(1)}, u32[]{:S(2)}, u32[]{:S(2)}) collective-permute-start(bf16[64,512]{1,0:T(8,128)(2,1)} %get-tuple-element.68), channel_id=1, source_target_pairs={{0,5},{1,6},{2,7},{3,0},{4,1},{5,2},{6,3},{7,4},{8,13},{9,14},{10,... | collective-permute-start | bytes 196616 | tf_op jit(solution)/shard_map/ppermute | solution.py:70
  19.3 4.6 %collective-permute-start.7 = (bf16[64,512]{1,0:T(8,128)(2,1)}, bf16[64,512]{1,0:T(8,128)(2,1)S(1)}, u32[]{:S(2)}, u32[]{:S(2)}) collective-permute-start(bf16[64,512]{1,0:T(8,128)(2,1)} %get-tuple-element.69), channel_id=1, source_target_pairs={{0,6},{1,7},{2,0},{3,1},{4,2},{5,3},{6,4},{7,5},{8,14},{9,15},{10,... | collective-permute-start | bytes 196616 | tf_op jit(solution)/shard_map/ppermute | solution.py:70
  19.4 5.2 %collective-permute-start.8 = (bf16[64,512]{1,0:T(8,128)(2,1)}, bf16[64,512]{1,0:T(8,128)(2,1)S(1)}, u32[]{:S(2)}, u32[]{:S(2)}) collective-permute-start(bf16[64,512]{1,0:T(8,128)(2,1)} %get-tuple-element.70), channel_id=1, source_target_pairs={{0,7},{1,0},{2,1},{3,2},{4,3},{5,4},{6,5},{7,6},{8,15},{9,8},{10,9... | collective-permute-start | bytes 196616 | tf_op jit(solution)/shard_map/ppermute | solution.py:70
  27.9 13.2 %collective-permute-start.25 = (bf16[256,128]{1,0:T(8,128)(2,1)S(1)}, bf16[256,128]{1,0:T(8,128)(2,1)S(1)}, u32[]{:S(2)}, u32[]{:S(2)}) collective-permute-start(bf16[256,128]{1,0:T(8,128)(2,1)S(1)} %get-tuple-element.80), channel_id=1, source_target_pairs={{0,0},{1,16},{2,2},{3,18},{4,4},{5,20},{6,6},{7,22},{8,1},{9,17},{... | collective-permute-start | bytes 196616 | tf_op jit(solution)/shard_map/ppermute | solution.py:70
  33.3 8.4 %collective-permute-start.26 = (bf16[256,128]{1,0:T(8,128)(2,1)S(1)}, bf16[256,128]{1,0:T(8,128)(2,1)S(1)}, u32[]{:S(2)}, u32[]{:S(2)}) collective-permute-start(bf16[256,128]{1,0:T(8,128)(2,1)S(1)} %get-tuple-element.81), channel_id=1, source_target_pairs={{0,32},{1,48},{2,34},{3,50},{4,36},{5,52},{6,38},{7,54},{8,33},{9,... | collective-permute-start | bytes 196616 | tf_op jit(solution)/shard_map/ppermute | solution.py:70
  34.4 14.4 %collective-permute-start.13 = (bf16[256,256]{1,0:T(8,128)(2,1)S(1)}, bf16[256,256]{1,0:T(8,128)(2,1)S(1)}, u32[]{:S(2)}, u32[]{:S(2)}) collective-permute-start(bf16[256,256]{1,0:T(8,128)(2,1)S(1)} %get-tuple-element.76), channel_id=1, source_target_pairs={{0,8},{1,24},{2,10},{3,26},{4,12},{5,28},{6,14},{7,30},{8,9},{9,25... | collective-permute-start | bytes 393224 | tf_op jit(solution)/shard_map/ppermute | solution.py:70
  36.7 7.6 %collective-permute-start.27 = (bf16[256,128]{1,0:T(8,128)(2,1)S(1)}, bf16[256,128]{1,0:T(8,128)(2,1)S(1)}, u32[]{:S(2)}, u32[]{:S(2)}) collective-permute-start(bf16[256,128]{1,0:T(8,128)(2,1)S(1)} %get-tuple-element.82), channel_id=1, source_target_pairs={{0,64},{1,80},{2,66},{3,82},{4,68},{5,84},{6,70},{7,86},{8,65},{9,... | collective-permute-start | bytes 196616 | tf_op jit(solution)/shard_map/ppermute | solution.py:70
  36.8 11.1 %collective-permute-start.28 = (bf16[256,128]{1,0:T(8,128)(2,1)S(1)}, bf16[256,128]{1,0:T(8,128)(2,1)S(1)}, u32[]{:S(2)}, u32[]{:S(2)}) collective-permute-start(bf16[256,128]{1,0:T(8,128)(2,1)S(1)} %get-tuple-element.83), channel_id=1, source_target_pairs={{0,96},{1,112},{2,98},{3,114},{4,100},{5,116},{6,102},{7,118},{8,9... | collective-permute-start | bytes 196616 | tf_op jit(solution)/shard_map/ppermute | solution.py:70
  41.1 12.1 %collective-permute-start.14 = (bf16[256,256]{1,0:T(8,128)(2,1)S(1)}, bf16[256,256]{1,0:T(8,128)(2,1)S(1)}, u32[]{:S(2)}, u32[]{:S(2)}) collective-permute-start(bf16[256,256]{1,0:T(8,128)(2,1)S(1)} %get-tuple-element.77), channel_id=1, source_target_pairs={{0,40},{1,56},{2,42},{3,58},{4,44},{5,60},{6,46},{7,62},{8,41},{9,... | collective-permute-start | bytes 393224 | tf_op jit(solution)/shard_map/ppermute | solution.py:70
  41.7 11.5 %collective-permute-start.15 = (bf16[256,256]{1,0:T(8,128)(2,1)S(1)}, bf16[256,256]{1,0:T(8,128)(2,1)S(1)}, u32[]{:S(2)}, u32[]{:S(2)}) collective-permute-start(bf16[256,256]{1,0:T(8,128)(2,1)S(1)} %get-tuple-element.78), channel_id=1, source_target_pairs={{0,72},{1,88},{2,74},{3,90},{4,76},{5,92},{6,78},{7,94},{8,73},{9,... | collective-permute-start | bytes 393224 | tf_op jit(solution)/shard_map/ppermute | solution.py:70
  44.3 12.3 %collective-permute-start.9 = (bf16[256,384]{1,0:T(8,128)(2,1)S(1)}, bf16[256,384]{1,0:T(8,128)(2,1)S(1)}, u32[]{:S(2)}, u32[]{:S(2)}) collective-permute-start(bf16[256,384]{1,0:T(8,128)(2,1)S(1)} %get-tuple-element.72), channel_id=1, source_target_pairs={{0,0},{1,16},{2,2},{3,18},{4,4},{5,20},{6,6},{7,22},{8,1},{9,17},{... | collective-permute-start | bytes 589832 | tf_op jit(solution)/shard_map/ppermute | solution.py:70
  47.9 9.2 %collective-permute-start.10 = (bf16[256,384]{1,0:T(8,128)(2,1)S(1)}, bf16[256,384]{1,0:T(8,128)(2,1)S(1)}, u32[]{:S(2)}, u32[]{:S(2)}) collective-permute-start(bf16[256,384]{1,0:T(8,128)(2,1)S(1)} %get-tuple-element.73), channel_id=1, source_target_pairs={{0,32},{1,48},{2,34},{3,50},{4,36},{5,52},{6,38},{7,54},{8,33},{9,... | collective-permute-start | bytes 589832 | tf_op jit(solution)/shard_map/ppermute | solution.py:70
  48.8 7.8 %collective-permute-start.16 = (bf16[256,256]{1,0:T(8,128)(2,1)S(1)}, bf16[256,256]{1,0:T(8,128)(2,1)S(1)}, u32[]{:S(2)}, u32[]{:S(2)}) collective-permute-start(bf16[256,256]{1,0:T(8,128)(2,1)S(1)} %get-tuple-element.79), channel_id=1, source_target_pairs={{0,104},{1,120},{2,106},{3,122},{4,108},{5,124},{6,110},{7,126},{8... | collective-permute-start | bytes 393224 | tf_op jit(solution)/shard_map/ppermute | solution.py:70
  53.2 8.3 %collective-permute-start.11 = (bf16[256,384]{1,0:T(8,128)(2,1)S(1)}, bf16[256,384]{1,0:T(8,128)(2,1)S(1)}, u32[]{:S(2)}, u32[]{:S(2)}) collective-permute-start(bf16[256,384]{1,0:T(8,128)(2,1)S(1)} %get-tuple-element.74), channel_id=1, source_target_pairs={{0,64},{1,80},{2,66},{3,82},{4,68},{5,84},{6,70},{7,86},{8,65},{9,... | collective-permute-start | bytes 589832 | tf_op jit(solution)/shard_map/ppermute | solution.py:70
  53.2 10.2 %collective-permute-start.12 = (bf16[256,384]{1,0:T(8,128)(2,1)S(1)}, bf16[256,384]{1,0:T(8,128)(2,1)S(1)}, u32[]{:S(2)}, u32[]{:S(2)}) collective-permute-start(bf16[256,384]{1,0:T(8,128)(2,1)S(1)} %get-tuple-element.75), channel_id=1, source_target_pairs={{0,96},{1,112},{2,98},{3,114},{4,100},{5,116},{6,102},{7,118},{8,9... | collective-permute-start | bytes 589832 | tf_op jit(solution)/shard_map/ppermute | solution.py:70
  56.6 8.2 %collective-permute-start.21 = (bf16[256,256]{1,0:T(8,128)(2,1)S(1)}, bf16[256,256]{1,0:T(8,128)(2,1)S(1)}, u32[]{:S(2)}, u32[]{:S(2)}) collective-permute-start(bf16[256,256]{1,0:T(8,128)(2,1)S(1)} %collective-permute-done.13.rest_4_), channel_id=1, source_target_pairs={{0,1},{1,0},{2,3},{3,2},{4,5},{5,4},{6,7},{7,6},{8,9},{9,8},{10,11... | collective-permute-start | bytes 393224 | tf_op jit(solution)/shard_map/ppermute | solution.py:70
  56.6 8.2 %collective-permute-start.22 = (bf16[256,256]{1,0:T(8,128)(2,1)S(1)}, bf16[256,256]{1,0:T(8,128)(2,1)S(1)}, u32[]{:S(2)}, u32[]{:S(2)}) collective-permute-start(bf16[256,256]{1,0:T(8,128)(2,1)S(1)} %collective-permute-done.14.rest_5_), channel_id=1, source_target_pairs={{0,1},{1,0},{2,3},{3,2},{4,5},{5,4},{6,7},{7,6},{8,9},{9,8},{10,11... | collective-permute-start | bytes 393224 | tf_op jit(solution)/shard_map/ppermute | solution.py:70
  57.1 8.2 %collective-permute-start.23 = (bf16[256,256]{1,0:T(8,128)(2,1)S(1)}, bf16[256,256]{1,0:T(8,128)(2,1)S(1)}, u32[]{:S(2)}, u32[]{:S(2)}) collective-permute-start(bf16[256,256]{1,0:T(8,128)(2,1)S(1)} %collective-permute-done.15.rest_6_), channel_id=1, source_target_pairs={{0,1},{1,0},{2,3},{3,2},{4,5},{5,4},{6,7},{7,6},{8,9},{9,8},{10,11... | collective-permute-start | bytes 393224 | tf_op jit(solution)/shard_map/ppermute | solution.py:70
  61.5 5.3 %collective-permute-start.17 = (bf16[256,384]{1,0:T(8,128)(2,1)S(1)}, bf16[256,384]{1,0:T(8,128)(2,1)S(1)}, u32[]{:S(2)}, u32[]{:S(2)}) collective-permute-start(bf16[256,384]{1,0:T(8,128)(2,1)S(1)} %collective-permute-done.9.rest_0_), channel_id=1, source_target_pairs={{0,1},{1,0},{2,3},{3,2},{4,5},{5,4},{6,7},{7,6},{8,9},{9,8},{10,11... | collective-permute-start | bytes 589832 | tf_op jit(solution)/shard_map/ppermute | solution.py:70
  63.4 3.3 %collective-permute-start.18 = (bf16[256,384]{1,0:T(8,128)(2,1)S(1)}, bf16[256,384]{1,0:T(8,128)(2,1)S(1)}, u32[]{:S(2)}, u32[]{:S(2)}) collective-permute-start(bf16[256,384]{1,0:T(8,128)(2,1)S(1)} %collective-permute-done.10.rest_1_), channel_id=1, source_target_pairs={{0,1},{1,0},{2,3},{3,2},{4,5},{5,4},{6,7},{7,6},{8,9},{9,8},{10,11... | collective-permute-start | bytes 589832 | tf_op jit(solution)/shard_map/ppermute | solution.py:70
  64.8 1.9 %collective-permute-start.19 = (bf16[256,384]{1,0:T(8,128)(2,1)S(1)}, bf16[256,384]{1,0:T(8,128)(2,1)S(1)}, u32[]{:S(2)}, u32[]{:S(2)}) collective-permute-start(bf16[256,384]{1,0:T(8,128)(2,1)S(1)} %collective-permute-done.11.rest_2_), channel_id=1, source_target_pairs={{0,1},{1,0},{2,3},{3,2},{4,5},{5,4},{6,7},{7,6},{8,9},{9,8},{10,11... | collective-permute-start | bytes 589832 | tf_op jit(solution)/shard_map/ppermute | solution.py:70
  64.9 1.9 %collective-permute-start.20 = (bf16[256,384]{1,0:T(8,128)(2,1)S(1)}, bf16[256,384]{1,0:T(8,128)(2,1)S(1)}, u32[]{:S(2)}, u32[]{:S(2)}) collective-permute-start(bf16[256,384]{1,0:T(8,128)(2,1)S(1)} %collective-permute-done.12.rest_3_), channel_id=1, source_target_pairs={{0,1},{1,0},{2,3},{3,2},{4,5},{5,4},{6,7},{7,6},{8,9},{9,8},{10,11... | collective-permute-start | bytes 589832 | tf_op jit(solution)/shard_map/ppermute | solution.py:70
  65.4 1.4 collective-permute-start.24
  79.5 3.4 %collective-permute-start.35 = (f32[8,1024]{1,0:T(8,128)S(1)}, f32[8,1024]{1,0:T(8,128)S(1)}, u32[]{:S(2)}, u32[]{:S(2)}) collective-permute-start(f32[8,1024]{1,0:T(8,128)S(1)} %get-tuple-element.93.s0), channel_id=1, source_target_pairs={{0,96},{1,97},{2,98},{3,99},{4,100},{5,101},{6,102},{7,103},{8,104... | collective-permute-start | bytes 98312 | tf_op jit(solution)/shard_map/ppermute | solution.py:70
  81.9 4.3 %collective-permute-start.34 = (f32[8,1024]{1,0:T(8,128)S(1)}, f32[8,1024]{1,0:T(8,128)S(1)}, u32[]{:S(2)}, u32[]{:S(2)}) collective-permute-start(f32[8,1024]{1,0:T(8,128)S(1)} %get-tuple-element.93.s0), channel_id=1, source_target_pairs={{0,64},{1,65},{2,66},{3,67},{4,68},{5,69},{6,70},{7,71},{8,72},{9,... | collective-permute-start | bytes 98312 | tf_op jit(solution)/shard_map/ppermute | solution.py:70
  81.9 4.3 %collective-permute-start.33 = (f32[8,1024]{1,0:T(8,128)S(1)}, f32[8,1024]{1,0:T(8,128)S(1)}, u32[]{:S(2)}, u32[]{:S(2)}) collective-permute-start(f32[8,1024]{1,0:T(8,128)S(1)} %get-tuple-element.93.s0), channel_id=1, source_target_pairs={{0,32},{1,33},{2,34},{3,35},{4,36},{5,37},{6,38},{7,39},{8,40},{9,... | collective-permute-start | bytes 98312 | tf_op jit(solution)/shard_map/ppermute | solution.py:70
  86.8 23.8 %collective-permute-start.40 = (bf16[1024,128]{1,0:T(8,128)(2,1)S(1)}, bf16[1024,128]{1,0:T(8,128)(2,1)S(1)}, u32[]{:S(2)}, u32[]{:S(2)}) collective-permute-start(bf16[1024,128]{1,0:T(8,128)(2,1)S(1)} %attn_grad.1.d_attn.rest_12_), channel_id=1, source_target_pairs={{0,1},{1,0},{2,3},{3,2},{4,5},{5,4},{6,7},{7,6},{8,9},{9,8},{10,11... | collective-permute-start | bytes 786440 | tf_op jit(solution)/shard_map/ppermute | solution.py:70
  89.6 18.3 %collective-permute-start.29 = (bf16[256,128]{1,0:T(8,128)(2,1)S(1)}, bf16[256,128]{1,0:T(8,128)(2,1)S(1)}, u32[]{:S(2)}, u32[]{:S(2)}) collective-permute-start(bf16[256,128]{1,0:T(8,128)(2,1)S(1)} %get-tuple-element.84), channel_id=1, source_target_pairs={{0,0},{16,1},{2,2},{18,3},{4,4},{20,5},{6,6},{22,7},{1,8},{17,9},{... | collective-permute-start | bytes 196616 | tf_op jit(solution)/shard_map/ppermute | solution.py:70
  92.3 32.9 %collective-permute-start.30 = (bf16[256,128]{1,0:T(8,128)(2,1)S(1)}, bf16[256,128]{1,0:T(8,128)(2,1)S(1)}, u32[]{:S(2)}, u32[]{:S(2)}) collective-permute-start(bf16[256,128]{1,0:T(8,128)(2,1)S(1)} %get-tuple-element.85), channel_id=1, source_target_pairs={{32,0},{48,1},{34,2},{50,3},{36,4},{52,5},{38,6},{54,7},{33,8},{49... | collective-permute-start | bytes 196616 | tf_op jit(solution)/shard_map/ppermute | solution.py:70
  92.8 34.6 %collective-permute-start.31 = (bf16[256,128]{1,0:T(8,128)(2,1)S(1)}, bf16[256,128]{1,0:T(8,128)(2,1)S(1)}, u32[]{:S(2)}, u32[]{:S(2)}) collective-permute-start(bf16[256,128]{1,0:T(8,128)(2,1)S(1)} %get-tuple-element.86), channel_id=1, source_target_pairs={{64,0},{80,1},{66,2},{82,3},{68,4},{84,5},{70,6},{86,7},{65,8},{81... | collective-permute-start | bytes 196616 | tf_op jit(solution)/shard_map/ppermute | solution.py:70
  95.3 35.9 %collective-permute-start.32 = (bf16[256,128]{1,0:T(8,128)(2,1)S(1)}, bf16[256,128]{1,0:T(8,128)(2,1)S(1)}, u32[]{:S(2)}, u32[]{:S(2)}) collective-permute-start(bf16[256,128]{1,0:T(8,128)(2,1)S(1)} %get-tuple-element.87), channel_id=1, source_target_pairs={{96,0},{112,1},{98,2},{114,3},{100,4},{116,5},{102,6},{118,7},{97,... | collective-permute-start | bytes 196616 | tf_op jit(solution)/shard_map/ppermute | solution.py:70
  107.9 24.1 %collective-permute-start.36 = (bf16[256,128]{1,0:T(8,128)(2,1)S(1)}, bf16[256,128]{1,0:T(8,128)(2,1)S(1)}, u32[]{:S(2)}, u32[]{:S(2)}) collective-permute-start(bf16[256,128]{1,0:T(8,128)(2,1)S(1)} %get-tuple-element.96), channel_id=1, source_target_pairs={{0,0},{16,1},{2,2},{18,3},{4,4},{20,5},{6,6},{22,7},{1,8},{17,9},{... | collective-permute-start | bytes 196616 | tf_op jit(solution)/shard_map/ppermute | solution.py:70
  110.7 23.6 %collective-permute-start.37 = (bf16[256,128]{1,0:T(8,128)(2,1)S(1)}, bf16[256,128]{1,0:T(8,128)(2,1)S(1)}, u32[]{:S(2)}, u32[]{:S(2)}) collective-permute-start(bf16[256,128]{1,0:T(8,128)(2,1)S(1)} %get-tuple-element.97), channel_id=1, source_target_pairs={{32,0},{48,1},{34,2},{50,3},{36,4},{52,5},{38,6},{54,7},{33,8},{49... | collective-permute-start | bytes 196616 | tf_op jit(solution)/shard_map/ppermute | solution.py:70
  125.3 19.8 %collective-permute-start.41 = (bf16[256,256]{1,0:T(8,128)(2,1)S(1)}, bf16[256,256]{1,0:T(8,128)(2,1)S(1)}, u32[]{:S(2)}, u32[]{:S(2)}) collective-permute-start(bf16[256,256]{1,0:T(8,128)(2,1)S(1)} %get-tuple-element.101), channel_id=1, source_target_pairs={{0,0},{16,1},{2,2},{18,3},{4,4},{20,5},{6,6},{22,7},{1,8},{17,9},{... | collective-permute-start | bytes 393224 | tf_op jit(solution)/shard_map/ppermute | solution.py:70
  127.4 19.2 %collective-permute-start.42 = (bf16[256,256]{1,0:T(8,128)(2,1)S(1)}, bf16[256,256]{1,0:T(8,128)(2,1)S(1)}, u32[]{:S(2)}, u32[]{:S(2)}) collective-permute-start(bf16[256,256]{1,0:T(8,128)(2,1)S(1)} %get-tuple-element.102), channel_id=1, source_target_pairs={{32,0},{48,1},{34,2},{50,3},{36,4},{52,5},{38,6},{54,7},{33,8},{49... | collective-permute-start | bytes 393224 | tf_op jit(solution)/shard_map/ppermute | solution.py:70
  131.2 16.9 %collective-permute-start.43 = (bf16[256,256]{1,0:T(8,128)(2,1)S(1)}, bf16[256,256]{1,0:T(8,128)(2,1)S(1)}, u32[]{:S(2)}, u32[]{:S(2)}) collective-permute-start(bf16[256,256]{1,0:T(8,128)(2,1)S(1)} %get-tuple-element.103), channel_id=1, source_target_pairs={{64,0},{80,1},{66,2},{82,3},{68,4},{84,5},{70,6},{86,7},{65,8},{81... | collective-permute-start | bytes 393224 | tf_op jit(solution)/shard_map/ppermute | solution.py:70
  131.9 10.4 %collective-permute-start.38 = (bf16[256,128]{1,0:T(8,128)(2,1)S(1)}, bf16[256,128]{1,0:T(8,128)(2,1)S(1)}, u32[]{:S(2)}, u32[]{:S(2)}) collective-permute-start(bf16[256,128]{1,0:T(8,128)(2,1)S(1)} %get-tuple-element.98), channel_id=1, source_target_pairs={{64,0},{80,1},{66,2},{82,3},{68,4},{84,5},{70,6},{86,7},{65,8},{81... | collective-permute-start | bytes 196616 | tf_op jit(solution)/shard_map/ppermute | solution.py:70
  134.3 9.4 %collective-permute-start.39 = (bf16[256,128]{1,0:T(8,128)(2,1)S(1)}, bf16[256,128]{1,0:T(8,128)(2,1)S(1)}, u32[]{:S(2)}, u32[]{:S(2)}) collective-permute-start(bf16[256,128]{1,0:T(8,128)(2,1)S(1)} %get-tuple-element.99), channel_id=1, source_target_pairs={{96,0},{112,1},{98,2},{114,3},{100,4},{116,5},{102,6},{118,7},{97,... | collective-permute-start | bytes 196616 | tf_op jit(solution)/shard_map/ppermute | solution.py:70
  142.4 9.2 %collective-permute-start.44 = (bf16[256,256]{1,0:T(8,128)(2,1)S(1)}, bf16[256,256]{1,0:T(8,128)(2,1)S(1)}, u32[]{:S(2)}, u32[]{:S(2)}) collective-permute-start(bf16[256,256]{1,0:T(8,128)(2,1)S(1)} %get-tuple-element.104), channel_id=1, source_target_pairs={{96,0},{112,1},{98,2},{114,3},{100,4},{116,5},{102,6},{118,7},{97,... | collective-permute-start | bytes 393224 | tf_op jit(solution)/shard_map/ppermute | solution.py:70
  143.6 7.9 %collective-permute-start.45 = (bf16[256,256]{1,0:T(8,128)(2,1)S(1)}, bf16[256,256]{1,0:T(8,128)(2,1)S(1)}, u32[]{:S(2)}, u32[]{:S(2)}) collective-permute-start(bf16[256,256]{1,0:T(8,128)(2,1)S(1)} %get-tuple-element.105), channel_id=1, source_target_pairs={{8,0},{24,1},{10,2},{26,3},{12,4},{28,5},{14,6},{30,7},{9,8},{25,9... | collective-permute-start | bytes 393224 | tf_op jit(solution)/shard_map/ppermute | solution.py:70
  145.1 7.3 %collective-permute-start.46 = (bf16[256,256]{1,0:T(8,128)(2,1)S(1)}, bf16[256,256]{1,0:T(8,128)(2,1)S(1)}, u32[]{:S(2)}, u32[]{:S(2)}) collective-permute-start(bf16[256,256]{1,0:T(8,128)(2,1)S(1)} %get-tuple-element.106), channel_id=1, source_target_pairs={{40,0},{56,1},{42,2},{58,3},{44,4},{60,5},{46,6},{62,7},{41,8},{57... | collective-permute-start | bytes 393224 | tf_op jit(solution)/shard_map/ppermute | solution.py:70
  146.6 8.1 %collective-permute-start.47 = (bf16[256,256]{1,0:T(8,128)(2,1)S(1)}, bf16[256,256]{1,0:T(8,128)(2,1)S(1)}, u32[]{:S(2)}, u32[]{:S(2)}) collective-permute-start(bf16[256,256]{1,0:T(8,128)(2,1)S(1)} %get-tuple-element.107), channel_id=1, source_target_pairs={{72,0},{88,1},{74,2},{90,3},{76,4},{92,5},{78,6},{94,7},{73,8},{89... | collective-permute-start | bytes 393224 | tf_op jit(solution)/shard_map/ppermute | solution.py:70
  148.1 9.4 %collective-permute-start.48 = (bf16[256,256]{1,0:T(8,128)(2,1)S(1)}, bf16[256,256]{1,0:T(8,128)(2,1)S(1)}, u32[]{:S(2)}, u32[]{:S(2)}) collective-permute-start(bf16[256,256]{1,0:T(8,128)(2,1)S(1)} %get-tuple-element.108), channel_id=1, source_target_pairs={{104,0},{120,1},{106,2},{122,3},{108,4},{124,5},{110,6},{126,7},{1... | collective-permute-start | bytes 393224 | tf_op jit(solution)/shard_map/ppermute | solution.py:70
  160.2 7.5 %collective-permute-start.49 = (bf16[64,512]{1,0:T(8,128)(2,1)S(1)}, bf16[64,512]{1,0:T(8,128)(2,1)S(1)}, u32[]{:S(2)}, u32[]{:S(2)}) collective-permute-start(bf16[64,512]{1,0:T(8,128)(2,1)S(1)} %get-tuple-element.111), channel_id=1, source_target_pairs={{1,0},{2,1},{3,2},{4,3},{5,4},{6,5},{7,6},{0,7},{9,8},{10,9},{11,1... | collective-permute-start | bytes 196616 | tf_op jit(solution)/shard_map/ppermute | solution.py:70
  162.2 5.5 %collective-permute-start.50 = (bf16[64,512]{1,0:T(8,128)(2,1)S(1)}, bf16[64,512]{1,0:T(8,128)(2,1)S(1)}, u32[]{:S(2)}, u32[]{:S(2)}) collective-permute-start(bf16[64,512]{1,0:T(8,128)(2,1)S(1)} %get-tuple-element.112), channel_id=1, source_target_pairs={{2,0},{3,1},{4,2},{5,3},{6,4},{7,5},{0,6},{1,7},{10,8},{11,9},{12,... | collective-permute-start | bytes 196616 | tf_op jit(solution)/shard_map/ppermute | solution.py:70
  162.2 5.9 %collective-permute-start.51 = (bf16[64,512]{1,0:T(8,128)(2,1)S(1)}, bf16[64,512]{1,0:T(8,128)(2,1)S(1)}, u32[]{:S(2)}, u32[]{:S(2)}) collective-permute-start(bf16[64,512]{1,0:T(8,128)(2,1)S(1)} %get-tuple-element.113), channel_id=1, source_target_pairs={{3,0},{4,1},{5,2},{6,3},{7,4},{0,5},{1,6},{2,7},{11,8},{12,9},{13,... | collective-permute-start | bytes 196616 | tf_op jit(solution)/shard_map/ppermute | solution.py:70
  162.8 5.3 %collective-permute-start.52 = (bf16[64,512]{1,0:T(8,128)(2,1)S(1)}, bf16[64,512]{1,0:T(8,128)(2,1)S(1)}, u32[]{:S(2)}, u32[]{:S(2)}) collective-permute-start(bf16[64,512]{1,0:T(8,128)(2,1)S(1)} %get-tuple-element.114), channel_id=1, source_target_pairs={{4,0},{5,1},{6,2},{7,3},{0,4},{1,5},{2,6},{3,7},{12,8},{13,9},{14,... | collective-permute-start | bytes 196616 | tf_op jit(solution)/shard_map/ppermute | solution.py:70
  165.6 5.7 %collective-permute-start.53 = (bf16[64,512]{1,0:T(8,128)(2,1)S(1)}, bf16[64,512]{1,0:T(8,128)(2,1)S(1)}, u32[]{:S(2)}, u32[]{:S(2)}) collective-permute-start(bf16[64,512]{1,0:T(8,128)(2,1)S(1)} %get-tuple-element.115), channel_id=1, source_target_pairs={{5,0},{6,1},{7,2},{0,3},{1,4},{2,5},{3,6},{4,7},{13,8},{14,9},{15,... | collective-permute-start | bytes 196616 | tf_op jit(solution)/shard_map/ppermute | solution.py:70
  167.7 4.9 %collective-permute-start.54 = (bf16[64,512]{1,0:T(8,128)(2,1)S(1)}, bf16[64,512]{1,0:T(8,128)(2,1)S(1)}, u32[]{:S(2)}, u32[]{:S(2)}) collective-permute-start(bf16[64,512]{1,0:T(8,128)(2,1)S(1)} %get-tuple-element.116), channel_id=1, source_target_pairs={{6,0},{7,1},{0,2},{1,3},{2,4},{3,5},{4,6},{5,7},{14,8},{15,9},{8,1... | collective-permute-start | bytes 196616 | tf_op jit(solution)/shard_map/ppermute | solution.py:70
  167.7 4.8 %collective-permute-start.55 = (bf16[64,512]{1,0:T(8,128)(2,1)S(1)}, bf16[64,512]{1,0:T(8,128)(2,1)S(1)}, u32[]{:S(2)}, u32[]{:S(2)}) collective-permute-start(bf16[64,512]{1,0:T(8,128)(2,1)S(1)} %get-tuple-element.117), channel_id=1, source_target_pairs={{7,0},{0,1},{1,2},{2,3},{3,4},{4,5},{5,6},{6,7},{15,8},{8,9},{9,10... | collective-permute-start | bytes 196616 | tf_op jit(solution)/shard_map/ppermute | solution.py:70
  (9 other events, 22.7 us)

commit v2 on v1

--- a/solution.py
+++ b/solution.py
@@ -40,26 +40,20 @@
     return out
 
 
-def main_pairs(j):
-    return [
-        (device_id(x, z, y, c), device_id((x + j) % 4, 2 * c + (z >> 1), y, z & 1))
-        for x, z, y, c in all_coords()
-    ]
-
-
-def other_pairs(j):
-    return [
-        (device_id(x, z, y, c), device_id((x + j) % 4, 2 * c + 1 - (z >> 1), y, z & 1))
-        for x, z, y, c in all_coords()
-    ]
-
-
-def core_pairs():
-    return [(device_id(x, z, y, c), device_id(x, z, y, 1 - c)) for x, z, y, c in all_coords()]
-
-
-def head_pairs(k):
-    return [(device_id(x, z, y, c), device_id((x + k) % 4, z, y, c)) for x, z, y, c in all_coords()]
+def moved(axis, step):
+    out = []
+    for x, z, y, c in all_coords():
+        to = ((x + step) % 4, z) if axis == c else (x, (z + step) % 4)
+        out.append((device_id(x, z, y, c), device_id(*to, y, c)))
+    return out
+
+
+def head_pairs(step):
+    return moved(0, step)
+
+
+def row_pairs(step):
+    return moved(1, step)
 
 
 def back(pairs):
@@ -163,8 +157,7 @@
                     outs[k][...] = total[p * BROWS : (p + 1) * BROWS, :].astype(BF)
 
 
-def prepare_kernel(meta, len_own, len_swap, mask_own, mask_swap, incoming, w_out, bounds, starts, key_pos, query_pos, dmixed):
-    same = (meta[1] >> 1) == meta[3]
+def prepare_kernel(lengths, tile_mask, incoming, w_out, bounds, starts, key_pos, query_pos, dmixed):
     chunk = lax.broadcasted_iota(jnp.int32, (32, CHUNK), 0)
     position = chunk * CHUNK + lax.broadcasted_iota(jnp.int32, (32, CHUNK), 1)
     lane = lax.broadcasted_iota(jnp.int32, (8, CHUNK), 1)
@@ -174,14 +167,14 @@
     chunk_start = jnp.zeros((8, CHUNK), jnp.int32)
     chunk_stop = jnp.full((8, CHUNK), LENGTH, jnp.int32)
     end = jnp.int32(0)
-    for d in range(len_own.shape[0]):
-        end = end + jnp.where(same, len_own[d], len_swap[d])
+    for d in range(lengths.shape[0]):
+        end = end + lengths[d]
         start = jnp.where(position >= end, end, start)
         chunk_start = jnp.where(first >= end, end, chunk_start)
         chunk_stop = jnp.where(last < end, jnp.minimum(chunk_stop, end), chunk_stop)
     starts[...] = start.astype(F32)
     bounds[...] = jnp.where(row == 0, chunk_start, chunk_stop - 1)
-    mask = jnp.where(same, mask_own[...], mask_swap[...]).astype(F32)
+    mask = tile_mask[...].astype(F32)
     turned = jnp.transpose(mask).astype(BF)
     mask = mask.astype(BF)
     for n in range(8):
@@ -199,8 +192,8 @@
 def project_kernel(meta, dest, slot, *rest):
     blocks, (w_ref, dmixed_ref), rest = rest[:8], rest[8:10], rest[10:]
     hist, pre = rest[:2]
-    main, other, extra = rest[2:6], rest[6:10], rest[10:14]
-    act, grads = rest[14:]
+    outs = rest[2:6]
+    act, grads = rest[6:]
     own = meta[2] * 2 + meta[3]
     for k in range(8):
         source = lax.rem(own - k + 8, 8)
@@ -219,23 +212,48 @@
         act[:, cols] = silu(part).astype(BF)
     grads[...] = (dmixed_ref[...] * act[:, 0:WIDTH].astype(F32)).astype(BF)
     for j in range(4):
-        head = lax.rem(meta[0] + j, 4) * HD
-        key = act[:, ds(3 * WIDTH + head, HD)]
-        value = act[:, ds(WIDTH + head, HD)]
-        main[j][:, 0:HD] = key
-        main[j][:, HD : 2 * HD] = value
-        main[j][:, 2 * HD : 3 * HD] = act[:, ds(2 * WIDTH + head, HD)]
-        other[j][:, 0:HD] = key
-        other[j][:, HD : 2 * HD] = value
-        extra[j][...] = grads[:, ds(head, HD)]
-
-
-def place(meta):
-    return meta[0], meta[1] & 1, meta[3]
-
-
-def chunk_of(t, z):
-    return 4 * t + jnp.where(t < 4, z, 3 - z)
+        head = lax.rem(line(meta)[0] + j, 4) * HD
+        outs[j][:, 0:HD] = act[:, ds(3 * WIDTH + head, HD)]
+        outs[j][:, HD : 2 * HD] = act[:, ds(WIDTH + head, HD)]
+        outs[j][:, 2 * HD : 3 * HD] = act[:, ds(2 * WIDTH + head, HD)]
+        outs[j][:, 3 * HD : 4 * HD] = grads[:, ds(head, HD)]
+
+
+def line(meta):
+    first = meta[3] == 0
+    return jnp.where(first, meta[0], meta[1]), jnp.where(first, meta[1], meta[0])
+
+
+def chunk_of(t, row, core):
+    spread = 4 * t + jnp.where(t < 4, row, 3 - row)
+    solid = t + jnp.where(t < 4, 4 * row, 24 - 4 * row)
+    return jnp.where(core == 0, spread, solid)
+
+
+def pieces_of(meta):
+    head = line(meta)[0]
+    for j in range(4):
+        source = lax.rem(head - j + 4, 4)
+        yield j, 0, source
+        yield j, CHUNK, 7 - source
+
+
+def collect_kernel(meta, p0, p1, p2, p3, keys, queries, grads):
+    pieces = (p0, p1, p2, p3)
+    for j, low, t in pieces_of(meta):
+        rows, part = ds(t * CHUNK, CHUNK), pieces[j]
+        keys[rows, :] = part[low : low + CHUNK, 0 : 2 * HD]
+        queries[rows, :] = part[low : low + CHUNK, 2 * HD : 3 * HD]
+        grads[rows, :] = part[low : low + CHUNK, 3 * HD : 4 * HD]
+
+
+def place_rows(meta, parts, out):
+    row, core = line(meta)[1], meta[3]
+    for k in range(4):
+        other = lax.rem(row - k + 4, 4)
+        for t in range(8):
+            chunk = chunk_of(t, other, core)
+            out[ds(chunk * CHUNK, CHUNK), :] = parts[k][t * CHUNK : (t + 1) * CHUNK, :]
 
 
 def valid_keys(starts, key_pos, i, tile):
@@ -256,29 +274,13 @@
     return at
 
 
-def forward_kernel(meta, bounds, starts, key_pos, *rest):
-    main, other, smain, sother, extra = (rest[4 * n : 4 * n + 4] for n in range(5))
-    keys, queries, grads, attn = rest[20:24]
-    returned, stats = rest[24:28], rest[28]
-    head, r, core = place(meta)
-    mine = 2 * r + core
-    for j in range(4):
-        x = lax.rem(head - j + 4, 4)
-        for ref, z in (
-            (main[j], mine),
-            (other[j], 2 * (1 - r) + core),
-            (smain[j], 2 * r + 1 - core),
-            (sother[j], 2 * (1 - r) + 1 - core),
-        ):
-            c = 4 * x + z
-            keys[ds(c * CHUNK, CHUNK), :] = ref[0:CHUNK, 0 : 2 * HD]
-            keys[ds((31 - c) * CHUNK, CHUNK), :] = ref[CHUNK:ROWS, 0 : 2 * HD]
-        for low, t in ((0, x), (CHUNK, 7 - x)):
-            queries[ds(t * CHUNK, CHUNK), :] = main[j][low : low + CHUNK, 2 * HD : 3 * HD]
-            grads[ds(t * CHUNK, CHUNK), :] = extra[j][low : low + CHUNK, :]
+def forward_kernel(meta, bounds, starts, key_pos, k0, k1, k2, k3, queries, grads, keys, attn, r0, r1, r2, r3, stats):
+    returned = (r0, r1, r2, r3)
+    row, core = line(meta)[1], meta[3]
+    place_rows(meta, (k0, k1, k2, k3), keys)
 
     def chunk(t, carry):
-        i = chunk_of(t, mine)
+        i = chunk_of(t, row, core)
         allowed = valid_keys(starts, key_pos, i, KEY_TILE)
         q = queries[ds(t * CHUNK, CHUNK), :]
 
@@ -305,10 +307,8 @@
         return carry
 
     lax.fori_loop(0, 8, chunk, 0)
-    for j in range(4):
-        x = lax.rem(head - j + 4, 4)
-        for low, t in ((0, x), (CHUNK, 7 - x)):
-            returned[j][low : low + CHUNK, :] = attn[ds(t * CHUNK, CHUNK), :].astype(BF)
+    for j, low, t in pieces_of(meta):
+        returned[j][low : low + CHUNK, :] = attn[ds(t * CHUNK, CHUNK), :].astype(BF)
 
 
 def attn_grad_kernel(s0, s1, s2, s3, attn, grads, out):
@@ -329,11 +329,10 @@
 
 def query_grad_kernel(meta, bounds, starts, key_pos, keys, queries, d_attn, *rest):
     outs, total_ref = rest[:4], rest[4]
-    head, r, core = place(meta)
-    mine = 2 * r + core
+    row, core = line(meta)[1], meta[3]
 
     def chunk(t, carry):
-        i = chunk_of(t, mine)
+        i = chunk_of(t, row, core)
         allowed = valid_keys(starts, key_pos, i, KEY_TILE)
         rows_q = ds(t * CHUNK, CHUNK)
         q = queries[rows_q, :]
@@ -355,52 +354,34 @@
         return carry
 
     lax.fori_loop(0, 8, chunk, 0)
-    for j in range(4):
-        x = lax.rem(head - j + 4, 4)
-        for low, t in ((0, x), (CHUNK, 7 - x)):
-            outs[j][low : low + CHUNK, :] = total_ref[ds(t * CHUNK, CHUNK), :]
-
-
-def key_grad_kernel(meta, bounds, starts, query_pos, *rest):
-    main, other, smain = (rest[4 * n : 4 * n + 4] for n in range(3))
-    d_own, d_swap = rest[12:14]
-    out_main, out_other = rest[14:18], rest[18:22]
-    keys, both, sums = rest[22:25]
-    head, r, core = place(meta)
-    for j in range(4):
-        x = lax.rem(head - j + 4, 4)
-        for low, t in ((0, x), (CHUNK, 7 - x)):
-            for ref, grad, half in ((main[j], d_own, core), (smain[j], d_swap, 1 - core)):
-                side = half if low == 0 else 1 - half
-                rows = ds((2 * t + side) * CHUNK, CHUNK)
-                both[rows, 0:HD] = ref[low : low + CHUNK, 2 * HD : 3 * HD]
-                both[rows, HD : 2 * HD] = grad[ds(t * CHUNK, CHUNK), :]
-        keys[2 * j * CHUNK : (2 * j + 2) * CHUNK, :] = main[j][:, 0 : 2 * HD]
-        keys[(8 + 2 * j) * CHUNK : (10 + 2 * j) * CHUNK, :] = other[j][...]
-
-    def pair_chunk(t):
-        return 4 * t + jnp.where(t < 4, 2 * r, 2 - 2 * r)
-
-    def chunk(n, carry):
-        x = lax.rem(head - (n // 2) % 4 + 4, 4)
-        z = jnp.where(n < 8, 2 * r, 2 * (1 - r)) + core
-        c = 4 * x + z
-        i = jnp.where(n % 2 == 0, c, 31 - c)
-        rows_k = ds(n * CHUNK, CHUNK)
+    for j, low, t in pieces_of(meta):
+        outs[j][low : low + CHUNK, :] = total_ref[ds(t * CHUNK, CHUNK), :]
+
+
+def key_grad_kernel(meta, bounds, starts, query_pos, keys, q0, q1, q2, q3, g0, g1, g2, g3, *rest):
+    outs, (queries, grads, sums) = rest[:4], rest[4:]
+    row, core = line(meta)[1], meta[3]
+    place_rows(meta, (q0, q1, q2, q3), queries)
+    place_rows(meta, (g0, g1, g2, g3), grads)
+    tile = KEY_TILE
+
+    def chunk(t, carry):
+        i = chunk_of(t, row, core)
+        rows_k = ds(i * CHUNK, CHUNK)
         k = keys[rows_k, 0:HD]
         v = keys[rows_k, HD : 2 * HD]
-        pos = lax.broadcasted_iota(jnp.int32, (CHUNK, 2 * CHUNK), 0).astype(F32) + (i * CHUNK).astype(F32)
-
-        def step(t, totals):
+        pos = lax.broadcasted_iota(jnp.int32, (CHUNK, tile), 0).astype(F32) + (i * CHUNK).astype(F32)
+
+        def step(n, totals):
             d_key, d_value = totals
-            rows = ds(t * 2 * CHUNK, 2 * CHUNK)
-            q = both[rows, 0:HD]
-            g = both[rows, HD : 2 * HD]
-            first = pair_chunk(t)
-            begin = jnp.concatenate([starts[pl.ds(first, 1), :], starts[pl.ds(first + 1, 1), :]], axis=1)
-            lanes = ds(first * CHUNK, 2 * CHUNK)
+            rows = ds(n * tile, tile)
+            q = queries[rows, :]
+            g = grads[rows, :]
+            begin = jnp.concatenate(
+                [starts[pl.ds(n * (tile // CHUNK) + m, 1), :] for m in range(tile // CHUNK)], axis=1
+            )
             halves = [
-                jnp.broadcast_to(query_pos[pl.ds(2 * i + m, 1), lanes], (BROWS, 2 * CHUNK)) for m in range(2)
+                jnp.broadcast_to(query_pos[pl.ds(2 * i + m, 1), rows], (BROWS, tile)) for m in range(2)
             ]
             allowed = (pos <= jnp.concatenate(halves, axis=0)) & (pos >= begin)
             h = dot_nt(k, q) * (0.5 * SCALE)
@@ -411,21 +392,17 @@
             d_scores = jnp.where(allowed, dp * (up * (1.0 + h - h * th)), 0.0).astype(BF)
             return d_key + dot(d_scores, q), d_value + dot(probs, g)
 
-        low = i // 4
-        low = jnp.where(pair_chunk(low) + 1 >= i, low, low + 1)
-        last = bounds[1, i]
-        high = last // (4 * CHUNK)
-        high = jnp.where(pair_chunk(high) * CHUNK <= last, high, high - 1)
         zero = jnp.zeros((CHUNK, HD), F32)
+        low, high = (i * CHUNK) // tile, bounds[1, i] // tile
         d_key, d_value = lax.fori_loop(low, high + 1, step, (zero, zero))
-        sums[rows_k, 0:HD] = (d_key * (0.5 * SCALE)).astype(BF)
-        sums[rows_k, HD : 2 * HD] = d_value.astype(BF)
+        out = ds(t * CHUNK, CHUNK)
+        sums[out, 0:HD] = (d_key * (0.5 * SCALE)).astype(BF)
+        sums[out, HD : 2 * HD] = d_value.astype(BF)
         return carry
 
-    lax.fori_loop(0, 16, chunk, 0)
-    for j in range(4):
-        out_main[j][...] = sums[2 * j * CHUNK : (2 * j + 2) * CHUNK, :]
-        out_other[j][...] = sums[(8 + 2 * j) * CHUNK : (10 + 2 * j) * CHUNK, :]
+    lax.fori_loop(0, 8, chunk, 0)
+    for j, low, t in pieces_of(meta):
+        outs[j][low : low + CHUNK, :] = sums[ds(t * CHUNK, CHUNK), :]
 
 
 def output_kernel(meta, *rest):
@@ -434,7 +411,7 @@
     out, partial = rest[5:7]
     attn = rest[7]
     for j in range(4):
-        attn[:, ds(lax.rem(meta[0] + j, 4) * HD, HD)] = parts[j][...].astype(F32)
+        attn[:, ds(lax.rem(line(meta)[0] + j, 4) * HD, HD)] = parts[j][...].astype(F32)
     hat, _ = row_statistics(attn[...])
     u_pre = pre[:, 0:WIDTH]
     u = silu(u_pre).astype(BF).astype(F32)
@@ -445,16 +422,15 @@
 
 
 def input_grad_kernel(meta, dest, slot, *rest):
-    queries, main, other = (rest[4 * n : 4 * n + 4] for n in range(3))
-    pre, partial, hist, incoming, w_in = rest[12:17]
-    outs = rest[17:25]
-    d_act, result = rest[25:27]
+    queries, both = rest[:4], rest[4:8]
+    pre, partial, hist, incoming, w_in = rest[8:13]
+    outs = rest[13:21]
+    d_act, result = rest[21:]
     for j in range(4):
-        head = lax.rem(meta[0] + j, 4) * HD
-        both = main[j][...].astype(F32) + other[j][...].astype(F32)
-        d_act[:, ds(head, HD)] = both[:, HD : 2 * HD]
+        head = lax.rem(line(meta)[0] + j, 4) * HD
+        d_act[:, ds(head, HD)] = both[j][:, HD : 2 * HD].astype(F32)
         d_act[:, ds(WIDTH + head, HD)] = queries[j][...].astype(F32)
-        d_act[:, ds(2 * WIDTH + head, HD)] = both[:, 0:HD]
+        d_act[:, ds(2 * WIDTH + head, HD)] = both[j][:, 0:HD].astype(F32)
     total = partial[...]
     for n in range(3):
         cols = slice((n + 1) * WIDTH, (n + 2) * WIDTH)
@@ -500,12 +476,10 @@
     tab_rows = table.shape[2]
 
     place_info = jnp.stack([x, z, y, c])
-    swap = core_pairs()
-    mask = tile_mask[0]
     bounds, starts, key_pos, query_pos, dmixed = call(
         prepare_kernel,
-        [place_info, lengths[0], send(lengths[0], swap), mask, send(mask, swap), output_gradient[0], w_out],
-        [SMEM] * 3 + [VMEM] * 4,
+        [lengths[0], tile_mask[0], output_gradient[0], w_out],
+        [SMEM] + [VMEM] * 3,
         [
             shape((8, CHUNK), jnp.int32),
             shape((32, CHUNK), F32),
@@ -537,54 +511,57 @@
     )(place_info, dest, row_ids.reshape(2, CHUNK), table)
     blocks = [outgoing[0]] + [send(outgoing[k], tab_pairs(k)) for k in range(1, 8)]
 
-    incoming = output_gradient[0]
-    qkv = shape((ROWS, 3 * HD), BF)
+    four = shape((ROWS, 4 * HD), BF)
     two = shape((ROWS, 2 * HD), BF)
     one = shape((ROWS, HD), BF)
+    quarter = LENGTH // 4
+    rows_two = shape((quarter, 2 * HD), BF)
+    rows_one = shape((quarter, HD), BF)
+
+    def to_heads(values):
+        return [values[0]] + [send(values[j], head_pairs(j)) for j in range(1, 4)]
+
+    def to_owners(values):
+        return [values[0]] + [send(values[j], back(head_pairs(j))) for j in range(1, 4)]
+
+    def over_rows(value):
+        return [value] + [send(value, row_pairs(k)) for k in range(1, 4)]
+
     hist, pre, *pieces = call(
         project_kernel,
         [place_info, dest, slot, *blocks, w_in, dmixed],
         [SMEM] * 3 + [VMEM] * 10,
-        [shape((ROWS, WIDTH), BF), shape((ROWS, 4 * WIDTH), F32)] + [qkv] * 4 + [two] * 4 + [one] * 4,
+        [shape((ROWS, WIDTH), BF), shape((ROWS, 4 * WIDTH), F32)] + [four] * 4,
         [pltpu.VMEM((ROWS, 4 * WIDTH), BF), pltpu.VMEM((ROWS, WIDTH), BF)],
         flops=2 * ROWS * WIDTH * 4 * WIDTH,
         name="project",
     )
-    main = [send(pieces[j], main_pairs(j)) for j in range(4)]
-    other = [send(pieces[4 + j], other_pairs(j)) for j in range(4)]
-    extra = [send(pieces[8 + j], main_pairs(j)) for j in range(4)]
-    smain = [send(v, swap) for v in main]
-    sother = [send(v, swap) for v in other]
-
-    quarter = LENGTH // 4
-    keys, queries, grads, attn, *returned = call(
+    own_keys, queries, grads = call(
+        collect_kernel,
+        [place_info, *to_heads(pieces)],
+        [SMEM] + [VMEM] * 4,
+        [rows_two, rows_one, rows_one],
+        name="collect",
+    )
+    keys, attn, *returned = call(
         forward_kernel,
-        [place_info, bounds, starts, key_pos, *main, *other, *smain, *sother, *extra],
-        [SMEM] * 2 + [VMEM] * 22,
-        [
-            shape((LENGTH, 2 * HD), BF),
-            shape((quarter, HD), BF),
-            shape((quarter, HD), BF),
-            shape((quarter, HD), F32),
-        ]
-        + [one] * 4
-        + [shape((8, quarter), F32)],
+        [place_info, bounds, starts, key_pos, *over_rows(own_keys), queries, grads],
+        [SMEM] * 2 + [VMEM] * 8,
+        [shape((LENGTH, 2 * HD), BF), shape((quarter, HD), F32)] + [one] * 4 + [shape((8, quarter), F32)],
         flops=10**9,
         name="forward",
     )
     stats = returned.pop()
-    from_heads = [send(stats, head_pairs(k)) for k in range(1, 4)]
-    attn_back = [send(returned[j], back(main_pairs(j))) for j in range(4)]
-
+    from_heads = to_heads([stats] * 4)
+    attn_back = to_owners(returned)
     (d_attn,) = call(
         attn_grad_kernel,
-        [stats, *from_heads, attn, grads],
+        [*from_heads, attn, grads],
         [VMEM] * 6,
-        [shape((quarter, HD), BF)],
+        [rows_one],
         flops=10**7,
         name="attn_grad",
     )
-    d_swap = send(d_attn, swap)
     d_query = call(
         query_grad_kernel,
         [place_info, bounds, starts, key_pos, keys, queries, d_attn],
@@ -594,22 +571,17 @@
         flops=2 * 10**9,
         name="query_grad",
     )
-    query_back = [send(d_query[j], back(main_pairs(j))) for j in range(4)]
+    query_back = to_owners(d_query)
     d_keys = call(
         key_grad_kernel,
-        [place_info, bounds, starts, query_pos, *main, *other, *smain, d_attn, d_swap],
-        [SMEM] * 2 + [VMEM] * 16,
-        [two] * 8,
-        [
-            pltpu.VMEM((LENGTH // 2, 2 * HD), BF),
-            pltpu.VMEM((LENGTH // 2, 2 * HD), BF),
-            pltpu.VMEM((LENGTH // 2, 2 * HD), BF),
-        ],
+        [place_info, bounds, starts, query_pos, keys, *over_rows(queries), *over_rows(d_attn)],
+        [SMEM] * 2 + [VMEM] * 11,
+        [two] * 4,
+        [pltpu.VMEM((LENGTH, HD), BF), pltpu.VMEM((LENGTH, HD), BF), pltpu.VMEM((quarter, 2 * HD), BF)],
         flops=3 * 10**9,
         name="key_grad",
     )
-    main_back = [send(d_keys[j], back(main_pairs(j))) for j in range(4)]
-    other_back = [send(d_keys[4 + j], back(other_pairs(j))) for j in range(4)]
+    keys_back = to_owners(d_keys)
 
     layer_out, partial = call(
         output_kernel,
@@ -622,8 +594,8 @@
     )
     returning = call(
         input_grad_kernel,
-        [place_info, dest, slot, *query_back, *main_back, *other_back, pre, partial, hist, incoming, w_in],
-        [SMEM] * 3 + [VMEM] * 17,
+        [place_info, dest, slot, *query_back, *keys_back, pre, partial, hist, output_gradient[0], w_in],
+        [SMEM] * 3 + [VMEM] * 13,
         [block_shape] * 8,
         [pltpu.VMEM((ROWS, 3 * WIDTH), F32), pltpu.VMEM((ROWS, WIDTH), BF)],
         flops=6 * ROWS * WIDTH * WIDTH,

time: 180 us -> 151 us (0.84)
  the two profiles are of different devices: /device:TPU:1 before, /device:TPU:6 now
where the time goes in v2:
time: 151 us; the launch traced here: 150 us
  starting transfers between devices  62.3 us (41%)
  Pallas kernels  55.1 us (36%)
  waiting for transfers between devices  27.3 us (18%)
  local copies, waits for them, and re-layouts  3.67 us (2%)
    ppermute x38, starting transfers between devices, send(): return lax.ppermute(value, AXES, pairs)  62.3 us
    pallas_call x9, Pallas kernels, call(): pl.pallas_call(kernel, out_shape=outs, in_specs=specs, out_specs=[VMEM] *...  41.7 us
    ppermute x38, waiting for transfers between devices, send(): return lax.ppermute(value, AXES, pairs)  27.3 us
    pallas_call x1, Pallas kernels, body(): pl.pallas_call(lookup_kernel, grid=(tiles,), in_specs=[SMEM, SMEM, pl.Blo...  7.31 us
    pallas_call x1, Pallas kernels, body(): pl.pallas_call(table_grad_kernel, grid=(tiles,), in_specs=[SMEM, SMEM, pl...  6.11 us
  transfers between devices with their start and end apart: 38, of which 12 were waited for; matrix products, arithmetic and copies ran while one was open for 0% of the time, Pallas kernels for 24%

profile of v2, /device:TPU:6, one launch (start us, length us, event | category | flops | bytes accessed | tf_op | source)
XLA Modules:
  0.0 149.9 jit_solution(7699640851293810922)
XLA Ops:
  0.6 0.8 copy.13
  1.4 0.7 reshape.19.dest
  2.1 0.6 pad_add_fusion.meta
  2.7 0.0 copy-start.8
  2.7 7.3 %lookup.1 = (bf16[64,512]{1,0:T(8,128)(2,1)}, bf16[64,512]{1,0:T(8,128)(2,1)}, bf16[64,512]{1,0:T(8,128)(2,1)}, bf16[64,512]{1,0:T(8,128)(2,1)}, bf16[64,512]{1,...) custom-call(s32[4]{0:T(128)} %pad_add_fusion.meta, s32[32]{0:T(128)} %reshape.19.dest, ...), custom_call_target="tpu_custom_call" | custom-call | tf_op jit(solution)/shard_map/lookup/pallas_call | solution.py:498
  10.0 1.6 %collective-permute-start.1 = (bf16[64,512]{1,0:T(8,128)(2,1)}, bf16[64,512]{1,0:T(8,128)(2,1)S(1)}, u32[]{:S(2)}, u32[]{:S(2)}) collective-permute-start(bf16[64,512]{1,0:T(8,128)(2,1)} %get-tuple-element.54), channel_id=1, source_target_pairs={{0,2},{1,3},{2,4},{3,5},{4,6},{5,7},{6,0},{7,1},{8,10},{9,11},{10,... | collective-permute-start | bytes 196616 | tf_op jit(solution)/shard_map/ppermute | solution.py:64
  11.7 2.2 %collective-permute-start.2 = (bf16[64,512]{1,0:T(8,128)(2,1)}, bf16[64,512]{1,0:T(8,128)(2,1)S(1)}, u32[]{:S(2)}, u32[]{:S(2)}) collective-permute-start(bf16[64,512]{1,0:T(8,128)(2,1)} %get-tuple-element.55), channel_id=1, source_target_pairs={{0,3},{1,4},{2,5},{3,6},{4,7},{5,0},{6,1},{7,2},{8,11},{9,12},{10,... | collective-permute-start | bytes 196616 | tf_op jit(solution)/shard_map/ppermute | solution.py:64
  13.9 1.8 %collective-permute-start.3 = (bf16[64,512]{1,0:T(8,128)(2,1)}, bf16[64,512]{1,0:T(8,128)(2,1)S(1)}, u32[]{:S(2)}, u32[]{:S(2)}) collective-permute-start(bf16[64,512]{1,0:T(8,128)(2,1)} %get-tuple-element.56), channel_id=1, source_target_pairs={{0,4},{1,5},{2,6},{3,7},{4,0},{5,1},{6,2},{7,3},{8,12},{9,13},{10,... | collective-permute-start | bytes 196616 | tf_op jit(solution)/shard_map/ppermute | solution.py:64
  15.7 1.8 %collective-permute-start.4 = (bf16[64,512]{1,0:T(8,128)(2,1)}, bf16[64,512]{1,0:T(8,128)(2,1)S(1)}, u32[]{:S(2)}, u32[]{:S(2)}) collective-permute-start(bf16[64,512]{1,0:T(8,128)(2,1)} %get-tuple-element.57), channel_id=1, source_target_pairs={{0,5},{1,6},{2,7},{3,0},{4,1},{5,2},{6,3},{7,4},{8,13},{9,14},{10,... | collective-permute-start | bytes 196616 | tf_op jit(solution)/shard_map/ppermute | solution.py:64
  17.5 1.3 collective-permute-start.5
  18.9 0.1 copy.14
  19.0 0.1 reshape.20.slot
  19.1 1.2 prepare.1
  20.3 0.3 collective-permute-done.3.rest_4_
  20.6 1.4 collective-permute-done.5.rest_6_
  22.1 0.8 copy-done.4
  22.9 2.4 %project.1 = (bf16[256,512]{1,0:T(8,128)(2,1)S(1)}, f32[256,2048]{1,0:T(8,128)S(1)}, bf16[256,512]{1,0:T(8,128)(2,1)S(1)}, bf16[256,512]{1,0:T(8,128)(2,1)S(1)},...) custom-call(s32[4]{0:T(128)S(1)} %copy-done.6, s32[32]{0:T(128)S(1)} %copy-done.7, s32[32]{0:T(128)S(1)} %reshape.20.slot, ...), custom_call_target="tpu_custom_call" | custom-call | flops 536870912 | bytes 6553872 | tf_op jit(solution)/shard_map/project/pallas_call | solution.py:118
  25.3 0.6 collective-permute-start.7
  25.8 2.4 %collective-permute-start.8 = (bf16[256,512]{1,0:T(8,128)(2,1)S(1)}, bf16[256,512]{1,0:T(8,128)(2,1)S(1)}, u32[]{:S(2)}, u32[]{:S(2)}) collective-permute-start(bf16[256,512]{1,0:T(8,128)(2,1)S(1)} %get-tuple-element.63), channel_id=1, source_target_pairs={{0,64},{1,17},{2,66},{3,19},{4,68},{5,21},{6,70},{7,23},{8,72},{9,... | collective-permute-start | bytes 786440 | tf_op jit(solution)/shard_map/ppermute | solution.py:64
  28.2 3.5 %collective-permute-done.7.p1 = bf16[256,512]{1,0:T(8,128)(2,1)S(1)} collective-permute-done((bf16[256,512]{1,0:T(8,128)(2,1)S(1)}, bf16[256,512]{1,0:T(8,128)(2,1)S(1)}, u32[]{:S(2)}, u32[]{:S(2)}) %collective-permute-start.7) | collective-permute-done | bytes 262176 | tf_op jit(solution)/shard_map/ppermute | solution.py:64
  31.7 2.1 %collective-permute-done.8.p2 = bf16[256,512]{1,0:T(8,128)(2,1)S(1)} collective-permute-done((bf16[256,512]{1,0:T(8,128)(2,1)S(1)}, bf16[256,512]{1,0:T(8,128)(2,1)S(1)}, u32[]{:S(2)}, u32[]{:S(2)}) %collective-permute-start.8) | collective-permute-done | bytes 262176 | tf_op jit(solution)/shard_map/ppermute | solution.py:64
  33.8 2.7 %collective-permute-done.9.p3 = bf16[256,512]{1,0:T(8,128)(2,1)S(1)} collective-permute-done((bf16[256,512]{1,0:T(8,128)(2,1)S(1)}, bf16[256,512]{1,0:T(8,128)(2,1)S(1)}, u32[]{:S(2)}, u32[]{:S(2)}) %collective-permute-start.9) | collective-permute-done | bytes 262176 | tf_op jit(solution)/shard_map/ppermute | solution.py:64
  36.5 0.7 collect.1
  37.2 2.0 %collective-permute-start.10 = (bf16[1024,256]{1,0:T(8,128)(2,1)S(1)}, bf16[1024,256]{1,0:T(8,128)(2,1)S(1)}, u32[]{:S(2)}, u32[]{:S(2)}) collective-permute-start(bf16[1024,256]{1,0:T(8,128)(2,1)S(1)} %get-tuple-element.65.k0), channel_id=1, source_target_pairs={{0,8},{1,33},{2,10},{3,35},{4,12},{5,37},{6,14},{7,39},{8,16},{9,4... | collective-permute-start | bytes 1572872 | tf_op jit(solution)/shard_map/ppermute | solution.py:64
  39.2 3.6 %collective-permute-start.11 = (bf16[1024,256]{1,0:T(8,128)(2,1)S(1)}, bf16[1024,256]{1,0:T(8,128)(2,1)S(1)}, u32[]{:S(2)}, u32[]{:S(2)}) collective-permute-start(bf16[1024,256]{1,0:T(8,128)(2,1)S(1)} %get-tuple-element.65.k0), channel_id=1, source_target_pairs={{0,16},{1,65},{2,18},{3,67},{4,20},{5,69},{6,22},{7,71},{8,24},{9,... | collective-permute-start | bytes 1572872 | tf_op jit(solution)/shard_map/ppermute | solution.py:64
  42.7 1.0 collective-permute-start.12
  43.8 1.0 collective-permute-start.22
  44.8 3.7 %collective-permute-done.10.k1 = bf16[1024,256]{1,0:T(8,128)(2,1)S(1)} collective-permute-done((bf16[1024,256]{1,0:T(8,128)(2,1)S(1)}, bf16[1024,256]{1,0:T(8,128)(2,1)S(1)}, u32[]{:S(2)}, u32[]{:S(2)}) %collective-permute-start.10) | collective-permute-done | bytes 524320 | tf_op jit(solution)/shard_map/ppermute | solution.py:64
  48.4 7.2 %collective-permute-done.11.k2 = bf16[1024,256]{1,0:T(8,128)(2,1)S(1)} collective-permute-done((bf16[1024,256]{1,0:T(8,128)(2,1)S(1)}, bf16[1024,256]{1,0:T(8,128)(2,1)S(1)}, u32[]{:S(2)}, u32[]{:S(2)}) %collective-permute-start.11) | collective-permute-done | bytes 524320 | tf_op jit(solution)/shard_map/ppermute | solution.py:64
  55.6 11.4 %forward.1 = (bf16[4096,256]{1,0:T(8,128)(2,1)S(1)}, f32[1024,128]{1,0:T(8,128)S(1)}, bf16[256,128]{1,0:T(8,128)(2,1)S(1)}, bf16[256,128]{1,0:T(8,128)(2,1)S(1)}...) custom-call(s32[4]{0:T(128)S(1)} %copy-done.6, ...), custom_call_target="tpu_custom_call" | custom-call | flops 1000000000 | bytes 6606864 | tf_op jit(solution)/shard_map/forward/pallas_call | solution.py:118
  67.0 0.8 collective-permute-start.16
  67.8 2.3 %collective-permute-start.17 = (f32[8,1024]{1,0:T(8,128)S(1)}, f32[8,1024]{1,0:T(8,128)S(1)}, u32[]{:S(2)}, u32[]{:S(2)}) collective-permute-start(f32[8,1024]{1,0:T(8,128)S(1)} %get-tuple-element.76.s0), channel_id=1, source_target_pairs={{0,64},{1,17},{2,66},{3,19},{4,68},{5,21},{6,70},{7,23},{8,72},{9,... | collective-permute-start | bytes 98312 | tf_op jit(solution)/shard_map/ppermute | solution.py:64
  70.1 0.4 collective-permute-start.18
  70.5 2.1 %collective-permute-start.23 = (bf16[1024,128]{1,0:T(8,128)(2,1)S(1)}, bf16[1024,128]{1,0:T(8,128)(2,1)S(1)}, u32[]{:S(2)}, u32[]{:S(2)}) collective-permute-start(bf16[1024,128]{1,0:T(8,128)(2,1)S(1)} %get-tuple-element.66.queries.q0), channel_id=1, source_target_pairs={{0,16},{1,65},{2,18},{3,67},{4,20},{5,69},{6,22},{7,71},{8,24},{9,... | collective-permute-start | bytes 786440 | tf_op jit(solution)/shard_map/ppermute | solution.py:64
  72.6 3.5 %collective-permute-start.24 = (bf16[1024,128]{1,0:T(8,128)(2,1)S(1)}, bf16[1024,128]{1,0:T(8,128)(2,1)S(1)}, u32[]{:S(2)}, u32[]{:S(2)}) collective-permute-start(bf16[1024,128]{1,0:T(8,128)(2,1)S(1)} %get-tuple-element.66.queries.q0), channel_id=1, source_target_pairs={{0,24},{1,97},{2,26},{3,99},{4,28},{5,101},{6,30},{7,103},{8,0},{9... | collective-permute-start | bytes 786440 | tf_op jit(solution)/shard_map/ppermute | solution.py:64
  76.1 0.6 attn_grad.1.d_attn.g0
  76.8 0.3 collective-permute-start.25
  77.0 5.3 %collective-permute-start.26 = (bf16[1024,128]{1,0:T(8,128)(2,1)S(1)}, bf16[1024,128]{1,0:T(8,128)(2,1)S(1)}, u32[]{:S(2)}, u32[]{:S(2)}) collective-permute-start(bf16[1024,128]{1,0:T(8,128)(2,1)S(1)} %attn_grad.1.d_attn.g0), channel_id=1, source_target_pairs={{0,16},{1,65},{2,18},{3,67},{4,20},{5,69},{6,22},{7,71},{8,24},{9,... | collective-permute-start | bytes 786440 | tf_op jit(solution)/shard_map/ppermute | solution.py:64
  82.3 10.1 %query_grad.1 = (bf16[256,128]{1,0:T(8,128)(2,1)S(1)}, bf16[256,128]{1,0:T(8,128)(2,1)S(1)}, bf16[256,128]{1,0:T(8,128)(2,1)S(1)}, bf16[256,128]{1,0:T(8,128)(2,1)S(1)}) custom-call(s32[4]{0:T(128)S(1)} %copy-done.6, s32[8,128]{1,0:T(8,128)S(1)} %get-tuple-element.49.bounds, f32[32,128]{1,0:T(8,128)S(1)} %get-tuple-element.50.starts, ...), custom_call_target="tpu_custom_call" | custom-call | flops 2000000000 | bytes 3952656 | tf_op jit(solution)/shard_map/query_grad/pallas_call | solution.py:118
  92.4 0.2 collective-permute-start.13
  92.6 3.5 %collective-permute-start.14 = (bf16[256,128]{1,0:T(8,128)(2,1)S(1)}, bf16[256,128]{1,0:T(8,128)(2,1)S(1)}, u32[]{:S(2)}, u32[]{:S(2)}) collective-permute-start(bf16[256,128]{1,0:T(8,128)(2,1)S(1)} %get-tuple-element.70), channel_id=1, source_target_pairs={{64,0},{17,1},{66,2},{19,3},{68,4},{21,5},{70,6},{23,7},{72,8},{25... | collective-permute-start | bytes 196616 | tf_op jit(solution)/shard_map/ppermute | solution.py:64
  96.1 1.1 collective-permute-start.15
  97.2 1.0 collective-permute-start.19
  98.1 11.3 %key_grad.1 = (bf16[256,256]{1,0:T(8,128)(2,1)S(1)}, bf16[256,256]{1,0:T(8,128)(2,1)S(1)}, bf16[256,256]{1,0:T(8,128)(2,1)S(1)}, bf16[256,256]{1,0:T(8,128)(2,1)S(1)}) custom-call(s32[4]{0:T(128)S(1)} %copy-done.6, s32[8,128]{1,0:T(8,128)S(1)} %get-tuple-element.49.bounds, f32[32,128]{1,0:T(8,128)S(1)} %get-tuple-element.50.starts, ...), custom_call_target="tpu_custom_call" | custom-call | flops 3000000000 | bytes 5787664 | tf_op jit(solution)/shard_map/key_grad/pallas_call | solution.py:118
  109.5 0.5 collective-permute-start.28
  110.0 3.3 %collective-permute-start.29 = (bf16[256,256]{1,0:T(8,128)(2,1)S(1)}, bf16[256,256]{1,0:T(8,128)(2,1)S(1)}, u32[]{:S(2)}, u32[]{:S(2)}) collective-permute-start(bf16[256,256]{1,0:T(8,128)(2,1)S(1)} %get-tuple-element.85), channel_id=1, source_target_pairs={{64,0},{17,1},{66,2},{19,3},{68,4},{21,5},{70,6},{23,7},{72,8},{25... | collective-permute-start | bytes 393224 | tf_op jit(solution)/shard_map/ppermute | solution.py:64
  113.3 2.4 %collective-permute-start.20 = (bf16[256,128]{1,0:T(8,128)(2,1)S(1)}, bf16[256,128]{1,0:T(8,128)(2,1)S(1)}, u32[]{:S(2)}, u32[]{:S(2)}) collective-permute-start(bf16[256,128]{1,0:T(8,128)(2,1)S(1)} %get-tuple-element.80), channel_id=1, source_target_pairs={{64,0},{17,1},{66,2},{19,3},{68,4},{21,5},{70,6},{23,7},{72,8},{25... | collective-permute-start | bytes 196616 | tf_op jit(solution)/shard_map/ppermute | solution.py:64
  115.7 2.3 %collective-permute-start.21 = (bf16[256,128]{1,0:T(8,128)(2,1)S(1)}, bf16[256,128]{1,0:T(8,128)(2,1)S(1)}, u32[]{:S(2)}, u32[]{:S(2)}) collective-permute-start(bf16[256,128]{1,0:T(8,128)(2,1)S(1)} %get-tuple-element.81), channel_id=1, source_target_pairs={{96,0},{25,1},{98,2},{27,3},{100,4},{29,5},{102,6},{31,7},{104,8},... | collective-permute-start | bytes 196616 | tf_op jit(solution)/shard_map/ppermute | solution.py:64
  118.0 2.0 %output.1 = (bf16[256,512]{1,0:T(8,128)(2,1)}, f32[256,512]{1,0:T(8,128)S(1)}) custom-call(s32[4]{0:T(128)S(1)} %copy-done.6, bf16[256,128]{1,0:T(8,128)(2,1)S(1)} %get-tuple-element.68.rest_0_, bf16[256,128]{1,0:T(8,128)(2,1)S(1)} %collective-permute-done.13.rest_1_, bf16[256,128]{1,0:T(8,128)(2,1)S(1)} %collective-permute-done.14.rest_2_, ...), custom_call_target="tpu_custom_call" | custom-call | flops 268435456 | bytes 6553616 | tf_op jit(solution)/shard_map/output/pallas_call | solution.py:118
  120.0 0.0 collective-permute-done.21.rest_3_
  120.0 2.1 %input_grad.1 = (bf16[64,512]{1,0:T(8,128)(2,1)S(1)}, bf16[64,512]{1,0:T(8,128)(2,1)S(1)}, bf16[64,512]{1,0:T(8,128)(2,1)S(1)}, bf16[64,512]{1,0:T(8,128)(2,1)S(...) custom-call(s32[4]{0:T(128)S(1)} %copy-done.6, ...), custom_call_target="tpu_custom_call" | custom-call | flops 402653184 | bytes 6553872 | tf_op jit(solution)/shard_map/input_grad/pallas_call | solution.py:118
  122.1 0.6 copy-done.3
  122.7 7.0 %collective-permute-start.31 = (bf16[64,512]{1,0:T(8,128)(2,1)S(1)}, bf16[64,512]{1,0:T(8,128)(2,1)S(1)}, u32[]{:S(2)}, u32[]{:S(2)}) collective-permute-start(bf16[64,512]{1,0:T(8,128)(2,1)S(1)} %get-tuple-element.89), channel_id=1, source_target_pairs={{1,0},{2,1},{3,2},{4,3},{5,4},{6,5},{7,6},{0,7},{9,8},{10,9},{11,1... | collective-permute-start | bytes 196616 | tf_op jit(solution)/shard_map/ppermute | solution.py:64
  129.7 5.7 %collective-permute-start.34 = (bf16[64,512]{1,0:T(8,128)(2,1)S(1)}, bf16[64,512]{1,0:T(8,128)(2,1)S(1)}, u32[]{:S(2)}, u32[]{:S(2)}) collective-permute-start(bf16[64,512]{1,0:T(8,128)(2,1)S(1)} %get-tuple-element.92), channel_id=1, source_target_pairs={{4,0},{5,1},{6,2},{7,3},{0,4},{1,5},{2,6},{3,7},{12,8},{13,9},{14,... | collective-permute-start | bytes 196616 | tf_op jit(solution)/shard_map/ppermute | solution.py:64
  135.4 0.9 collective-permute-start.35
  136.3 0.4 collective-permute-start.36
  136.7 0.4 collective-permute-done.32.rest_2_
  137.2 1.3 collective-permute-done.34.rest_4_
  138.5 2.2 %collective-permute-done.35.rest_5_ = bf16[64,512]{1,0:T(8,128)(2,1)S(1)} collective-permute-done((bf16[64,512]{1,0:T(8,128)(2,1)S(1)}, bf16[64,512]{1,0:T(8,128)(2,1)S(1)}, u32[]{:S(2)}, u32[]{:S(2)}) %collective-permute-start.35) | collective-permute-done | bytes 65568 | tf_op jit(solution)/shard_map/ppermute | solution.py:64
  140.7 2.2 %collective-permute-done.36.rest_6_ = bf16[64,512]{1,0:T(8,128)(2,1)S(1)} collective-permute-done((bf16[64,512]{1,0:T(8,128)(2,1)S(1)}, bf16[64,512]{1,0:T(8,128)(2,1)S(1)}, u32[]{:S(2)}, u32[]{:S(2)}) %collective-permute-start.36) | collective-permute-done | bytes 65568 | tf_op jit(solution)/shard_map/ppermute | solution.py:64
  142.9 0.3 collective-permute-done.37.rest_7_
  143.2 0.3 copy-done.14
  143.5 0.3 copy-done.15
  143.8 6.1 %table_grad.1 = bf16[1,1,4096,512]{3,2,1,0:T(8,128)(2,1)} custom-call(s32[4]{0:T(128)} %pad_add_fusion.meta, s32[32]{0:T(128)} %reshape.19.dest, s32[1,256]{1,0:T(1,128)} %bitcast.15, bf16[64,512]{1,0:T(8,128)(2,1)} %copy-done.3, bf16[64,512]{1,0:T(8,128)(2,1)} %copy-done.9, bf16[64,512]{1,0:T(8,128)(2,1)} %copy-done.10, bf16[64,512]{1,0:T(8,128)(2,1)} %copy-done.11, ...), custom_call_target="tpu_custom_call" | custom-call | tf_op jit(solution)/shard_map/table_grad/pallas_call | solution.py:605
  (62 shorter events, 0.1 us)
Async XLA Ops:
  2.7 16.2 %copy-start.16 = (s32[1,8,4]{1,2,0:T(4,128)S(1)}, s32[1,8,4]{1,2,0:T(4,128)}, u32[]{:S(2)}) copy-start(s32[1,8,4]{1,2,0:T(4,128)} %param.12) | copy-start | bytes 388
  2.7 16.4 %copy-start.1 = (bf16[512,512]{1,0:T(8,128)(2,1)S(1)}, bf16[512,512]{1,0:T(8,128)(2,1)}, u32[]{:S(2)}) copy-start(bf16[512,512]{1,0:T(8,128)(2,1)} %rest_7_.1) | copy-start | bytes 1572868
  2.7 16.4 %copy-start.2 = (bf16[1,256,512]{2,1,0:T(8,128)(2,1)S(1)}, bf16[1,256,512]{2,1,0:T(8,128)(2,1)}, u32[]{:S(2)}) copy-start(bf16[1,256,512]{2,1,0:T(8,128)(2,1)} %param.17) | copy-start | bytes 786436
  2.7 16.4 %copy-start.5 = (s32[1,64,64]{2,1,0:T(8,128)S(1)}, s32[1,64,64]{2,1,0:T(8,128)}, u32[]{:S(2)}) copy-start(s32[1,64,64]{2,1,0:T(8,128)} %param.14) | copy-start | bytes 49156
  2.7 16.4 %copy-start.8 = (s32[1,16]{1,0:T(1,128)S(1)}, s32[1,16]{1,0:T(1,128)}, u32[]{:S(2)}) copy-start(s32[1,16]{1,0:T(1,128)} %param.13) | copy-start | bytes 196
  2.7 19.3 %copy-start = (bf16[512,2048]{1,0:T(8,128)(2,1)S(1)}, bf16[512,2048]{1,0:T(8,128)(2,1)}, u32[]{:S(2)}) copy-start(bf16[512,2048]{1,0:T(8,128)(2,1)} %rest_12_.1) | copy-start | bytes 6291460
  2.7 19.3 %copy-start.6 = (s32[4]{0:T(128)S(1)}, s32[4]{0:T(128)}, u32[]{:S(2)}) copy-start(s32[4]{0:T(128)} %pad_add_fusion.meta) | copy-start | bytes 52
  2.7 19.3 %copy-start.7 = (s32[32]{0:T(128)S(1)}, s32[32]{0:T(128)}, u32[]{:S(2)}) copy-start(s32[32]{0:T(128)} %reshape.19.dest) | copy-start | bytes 388
  10.0 7.5 %collective-permute-start = (bf16[64,512]{1,0:T(8,128)(2,1)}, bf16[64,512]{1,0:T(8,128)(2,1)S(1)}, u32[]{:S(2)}, u32[]{:S(2)}) collective-permute-start(bf16[64,512]{1,0:T(8,128)(2,1)} %get-tuple-element.53), channel_id=1, source_target_pairs={{0,1},{1,2},{2,3},{3,4},{4,5},{5,6},{6,7},{7,0},{8,9},{9,10},{10,1... | collective-permute-start | bytes 196616 | tf_op jit(solution)/shard_map/ppermute | solution.py:64
  10.0 8.9 %collective-permute-start.1 = (bf16[64,512]{1,0:T(8,128)(2,1)}, bf16[64,512]{1,0:T(8,128)(2,1)S(1)}, u32[]{:S(2)}, u32[]{:S(2)}) collective-permute-start(bf16[64,512]{1,0:T(8,128)(2,1)} %get-tuple-element.54), channel_id=1, source_target_pairs={{0,2},{1,3},{2,4},{3,5},{4,6},{5,7},{6,0},{7,1},{8,10},{9,11},{10,... | collective-permute-start | bytes 196616 | tf_op jit(solution)/shard_map/ppermute | solution.py:64
  11.7 8.6 %collective-permute-start.2 = (bf16[64,512]{1,0:T(8,128)(2,1)}, bf16[64,512]{1,0:T(8,128)(2,1)S(1)}, u32[]{:S(2)}, u32[]{:S(2)}) collective-permute-start(bf16[64,512]{1,0:T(8,128)(2,1)} %get-tuple-element.55), channel_id=1, source_target_pairs={{0,3},{1,4},{2,5},{3,6},{4,7},{5,0},{6,1},{7,2},{8,11},{9,12},{10,... | collective-permute-start | bytes 196616 | tf_op jit(solution)/shard_map/ppermute | solution.py:64
  13.9 6.7 %collective-permute-start.3 = (bf16[64,512]{1,0:T(8,128)(2,1)}, bf16[64,512]{1,0:T(8,128)(2,1)S(1)}, u32[]{:S(2)}, u32[]{:S(2)}) collective-permute-start(bf16[64,512]{1,0:T(8,128)(2,1)} %get-tuple-element.56), channel_id=1, source_target_pairs={{0,4},{1,5},{2,6},{3,7},{4,0},{5,1},{6,2},{7,3},{8,12},{9,13},{10,... | collective-permute-start | bytes 196616 | tf_op jit(solution)/shard_map/ppermute | solution.py:64
  15.7 4.8 %collective-permute-start.4 = (bf16[64,512]{1,0:T(8,128)(2,1)}, bf16[64,512]{1,0:T(8,128)(2,1)S(1)}, u32[]{:S(2)}, u32[]{:S(2)}) collective-permute-start(bf16[64,512]{1,0:T(8,128)(2,1)} %get-tuple-element.57), channel_id=1, source_target_pairs={{0,5},{1,6},{2,7},{3,0},{4,1},{5,2},{6,3},{7,4},{8,13},{9,14},{10,... | collective-permute-start | bytes 196616 | tf_op jit(solution)/shard_map/ppermute | solution.py:64
  17.5 4.5 %collective-permute-start.5 = (bf16[64,512]{1,0:T(8,128)(2,1)}, bf16[64,512]{1,0:T(8,128)(2,1)S(1)}, u32[]{:S(2)}, u32[]{:S(2)}) collective-permute-start(bf16[64,512]{1,0:T(8,128)(2,1)} %get-tuple-element.58), channel_id=1, source_target_pairs={{0,6},{1,7},{2,0},{3,1},{4,2},{5,3},{6,4},{7,5},{8,14},{9,15},{10,... | collective-permute-start | bytes 196616 | tf_op jit(solution)/shard_map/ppermute | solution.py:64
  18.9 3.1 %collective-permute-start.6 = (bf16[64,512]{1,0:T(8,128)(2,1)}, bf16[64,512]{1,0:T(8,128)(2,1)S(1)}, u32[]{:S(2)}, u32[]{:S(2)}) collective-permute-start(bf16[64,512]{1,0:T(8,128)(2,1)} %get-tuple-element.59), channel_id=1, source_target_pairs={{0,7},{1,0},{2,1},{3,2},{4,3},{5,4},{6,5},{7,6},{8,15},{9,8},{10,9... | collective-permute-start | bytes 196616 | tf_op jit(solution)/shard_map/ppermute | solution.py:64
  22.0 0.8 copy-start.4
  25.3 6.4 %collective-permute-start.7 = (bf16[256,512]{1,0:T(8,128)(2,1)S(1)}, bf16[256,512]{1,0:T(8,128)(2,1)S(1)}, u32[]{:S(2)}, u32[]{:S(2)}) collective-permute-start(bf16[256,512]{1,0:T(8,128)(2,1)S(1)} %get-tuple-element.62), channel_id=1, source_target_pairs={{0,32},{1,9},{2,34},{3,11},{4,36},{5,13},{6,38},{7,15},{8,40},{9,1... | collective-permute-start | bytes 786440 | tf_op jit(solution)/shard_map/ppermute | solution.py:64
  25.8 7.9 %collective-permute-start.8 = (bf16[256,512]{1,0:T(8,128)(2,1)S(1)}, bf16[256,512]{1,0:T(8,128)(2,1)S(1)}, u32[]{:S(2)}, u32[]{:S(2)}) collective-permute-start(bf16[256,512]{1,0:T(8,128)(2,1)S(1)} %get-tuple-element.63), channel_id=1, source_target_pairs={{0,64},{1,17},{2,66},{3,19},{4,68},{5,21},{6,70},{7,23},{8,72},{9,... | collective-permute-start | bytes 786440 | tf_op jit(solution)/shard_map/ppermute | solution.py:64
  28.2 8.3 %collective-permute-start.9 = (bf16[256,512]{1,0:T(8,128)(2,1)S(1)}, bf16[256,512]{1,0:T(8,128)(2,1)S(1)}, u32[]{:S(2)}, u32[]{:S(2)}) collective-permute-start(bf16[256,512]{1,0:T(8,128)(2,1)S(1)} %get-tuple-element.64), channel_id=1, source_target_pairs={{0,96},{1,25},{2,98},{3,27},{4,100},{5,29},{6,102},{7,31},{8,104},... | collective-permute-start | bytes 786440 | tf_op jit(solution)/shard_map/ppermute | solution.py:64
  37.2 11.3 %collective-permute-start.10 = (bf16[1024,256]{1,0:T(8,128)(2,1)S(1)}, bf16[1024,256]{1,0:T(8,128)(2,1)S(1)}, u32[]{:S(2)}, u32[]{:S(2)}) collective-permute-start(bf16[1024,256]{1,0:T(8,128)(2,1)S(1)} %get-tuple-element.65.k0), channel_id=1, source_target_pairs={{0,8},{1,33},{2,10},{3,35},{4,12},{5,37},{6,14},{7,39},{8,16},{9,4... | collective-permute-start | bytes 1572872 | tf_op jit(solution)/shard_map/ppermute | solution.py:64
  39.2 16.5 %collective-permute-start.11 = (bf16[1024,256]{1,0:T(8,128)(2,1)S(1)}, bf16[1024,256]{1,0:T(8,128)(2,1)S(1)}, u32[]{:S(2)}, u32[]{:S(2)}) collective-permute-start(bf16[1024,256]{1,0:T(8,128)(2,1)S(1)} %get-tuple-element.65.k0), channel_id=1, source_target_pairs={{0,16},{1,65},{2,18},{3,67},{4,20},{5,69},{6,22},{7,71},{8,24},{9,... | collective-permute-start | bytes 1572872 | tf_op jit(solution)/shard_map/ppermute | solution.py:64
  42.7 12.9 %collective-permute-start.12 = (bf16[1024,256]{1,0:T(8,128)(2,1)S(1)}, bf16[1024,256]{1,0:T(8,128)(2,1)S(1)}, u32[]{:S(2)}, u32[]{:S(2)}) collective-permute-start(bf16[1024,256]{1,0:T(8,128)(2,1)S(1)} %get-tuple-element.65.k0), channel_id=1, source_target_pairs={{0,24},{1,97},{2,26},{3,99},{4,28},{5,101},{6,30},{7,103},{8,0},{9... | collective-permute-start | bytes 1572872 | tf_op jit(solution)/shard_map/ppermute | solution.py:64
  43.8 38.5 %collective-permute-start.22 = (bf16[1024,128]{1,0:T(8,128)(2,1)S(1)}, bf16[1024,128]{1,0:T(8,128)(2,1)S(1)}, u32[]{:S(2)}, u32[]{:S(2)}) collective-permute-start(bf16[1024,128]{1,0:T(8,128)(2,1)S(1)} %get-tuple-element.66.queries.q0), channel_id=1, source_target_pairs={{0,8},{1,33},{2,10},{3,35},{4,12},{5,37},{6,14},{7,39},{8,16},{9,4... | collective-permute-start | bytes 786440 | tf_op jit(solution)/shard_map/ppermute | solution.py:64
  67.0 5.6 %collective-permute-start.16 = (f32[8,1024]{1,0:T(8,128)S(1)}, f32[8,1024]{1,0:T(8,128)S(1)}, u32[]{:S(2)}, u32[]{:S(2)}) collective-permute-start(f32[8,1024]{1,0:T(8,128)S(1)} %get-tuple-element.76.s0), channel_id=1, source_target_pairs={{0,32},{1,9},{2,34},{3,11},{4,36},{5,13},{6,38},{7,15},{8,40},{9,1... | collective-permute-start | bytes 98312 | tf_op jit(solution)/shard_map/ppermute | solution.py:64
  67.8 8.4 %collective-permute-start.17 = (f32[8,1024]{1,0:T(8,128)S(1)}, f32[8,1024]{1,0:T(8,128)S(1)}, u32[]{:S(2)}, u32[]{:S(2)}) collective-permute-start(f32[8,1024]{1,0:T(8,128)S(1)} %get-tuple-element.76.s0), channel_id=1, source_target_pairs={{0,64},{1,17},{2,66},{3,19},{4,68},{5,21},{6,70},{7,23},{8,72},{9,... | collective-permute-start | bytes 98312 | tf_op jit(solution)/shard_map/ppermute | solution.py:64
  70.1 6.0 %collective-permute-start.18 = (f32[8,1024]{1,0:T(8,128)S(1)}, f32[8,1024]{1,0:T(8,128)S(1)}, u32[]{:S(2)}, u32[]{:S(2)}) collective-permute-start(f32[8,1024]{1,0:T(8,128)S(1)} %get-tuple-element.76.s0), channel_id=1, source_target_pairs={{0,96},{1,25},{2,98},{3,27},{4,100},{5,29},{6,102},{7,31},{8,104},... | collective-permute-start | bytes 98312 | tf_op jit(solution)/shard_map/ppermute | solution.py:64
  70.5 21.8 %collective-permute-start.23 = (bf16[1024,128]{1,0:T(8,128)(2,1)S(1)}, bf16[1024,128]{1,0:T(8,128)(2,1)S(1)}, u32[]{:S(2)}, u32[]{:S(2)}) collective-permute-start(bf16[1024,128]{1,0:T(8,128)(2,1)S(1)} %get-tuple-element.66.queries.q0), channel_id=1, source_target_pairs={{0,16},{1,65},{2,18},{3,67},{4,20},{5,69},{6,22},{7,71},{8,24},{9,... | collective-permute-start | bytes 786440 | tf_op jit(solution)/shard_map/ppermute | solution.py:64
  72.6 19.9 %collective-permute-start.24 = (bf16[1024,128]{1,0:T(8,128)(2,1)S(1)}, bf16[1024,128]{1,0:T(8,128)(2,1)S(1)}, u32[]{:S(2)}, u32[]{:S(2)}) collective-permute-start(bf16[1024,128]{1,0:T(8,128)(2,1)S(1)} %get-tuple-element.66.queries.q0), channel_id=1, source_target_pairs={{0,24},{1,97},{2,26},{3,99},{4,28},{5,101},{6,30},{7,103},{8,0},{9... | collective-permute-start | bytes 786440 | tf_op jit(solution)/shard_map/ppermute | solution.py:64
  76.8 19.3 %collective-permute-start.25 = (bf16[1024,128]{1,0:T(8,128)(2,1)S(1)}, bf16[1024,128]{1,0:T(8,128)(2,1)S(1)}, u32[]{:S(2)}, u32[]{:S(2)}) collective-permute-start(bf16[1024,128]{1,0:T(8,128)(2,1)S(1)} %attn_grad.1.d_attn.g0), channel_id=1, source_target_pairs={{0,8},{1,33},{2,10},{3,35},{4,12},{5,37},{6,14},{7,39},{8,16},{9,4... | collective-permute-start | bytes 786440 | tf_op jit(solution)/shard_map/ppermute | solution.py:64
  77.0 20.1 %collective-permute-start.26 = (bf16[1024,128]{1,0:T(8,128)(2,1)S(1)}, bf16[1024,128]{1,0:T(8,128)(2,1)S(1)}, u32[]{:S(2)}, u32[]{:S(2)}) collective-permute-start(bf16[1024,128]{1,0:T(8,128)(2,1)S(1)} %attn_grad.1.d_attn.g0), channel_id=1, source_target_pairs={{0,16},{1,65},{2,18},{3,67},{4,20},{5,69},{6,22},{7,71},{8,24},{9,... | collective-permute-start | bytes 786440 | tf_op jit(solution)/shard_map/ppermute | solution.py:64
  82.3 15.9 %collective-permute-start.27 = (bf16[1024,128]{1,0:T(8,128)(2,1)S(1)}, bf16[1024,128]{1,0:T(8,128)(2,1)S(1)}, u32[]{:S(2)}, u32[]{:S(2)}) collective-permute-start(bf16[1024,128]{1,0:T(8,128)(2,1)S(1)} %attn_grad.1.d_attn.g0), channel_id=1, source_target_pairs={{0,24},{1,97},{2,26},{3,99},{4,28},{5,101},{6,30},{7,103},{8,0},{9... | collective-permute-start | bytes 786440 | tf_op jit(solution)/shard_map/ppermute | solution.py:64
  92.4 17.6 %collective-permute-start.13 = (bf16[256,128]{1,0:T(8,128)(2,1)S(1)}, bf16[256,128]{1,0:T(8,128)(2,1)S(1)}, u32[]{:S(2)}, u32[]{:S(2)}) collective-permute-start(bf16[256,128]{1,0:T(8,128)(2,1)S(1)} %get-tuple-element.69), channel_id=1, source_target_pairs={{32,0},{9,1},{34,2},{11,3},{36,4},{13,5},{38,6},{15,7},{40,8},{17,... | collective-permute-start | bytes 196616 | tf_op jit(solution)/shard_map/ppermute | solution.py:64
  92.6 20.7 %collective-permute-start.14 = (bf16[256,128]{1,0:T(8,128)(2,1)S(1)}, bf16[256,128]{1,0:T(8,128)(2,1)S(1)}, u32[]{:S(2)}, u32[]{:S(2)}) collective-permute-start(bf16[256,128]{1,0:T(8,128)(2,1)S(1)} %get-tuple-element.70), channel_id=1, source_target_pairs={{64,0},{17,1},{66,2},{19,3},{68,4},{21,5},{70,6},{23,7},{72,8},{25... | collective-permute-start | bytes 196616 | tf_op jit(solution)/shard_map/ppermute | solution.py:64
  96.1 17.2 %collective-permute-start.15 = (bf16[256,128]{1,0:T(8,128)(2,1)S(1)}, bf16[256,128]{1,0:T(8,128)(2,1)S(1)}, u32[]{:S(2)}, u32[]{:S(2)}) collective-permute-start(bf16[256,128]{1,0:T(8,128)(2,1)S(1)} %get-tuple-element.71), channel_id=1, source_target_pairs={{96,0},{25,1},{98,2},{27,3},{100,4},{29,5},{102,6},{31,7},{104,8},... | collective-permute-start | bytes 196616 | tf_op jit(solution)/shard_map/ppermute | solution.py:64
  97.2 18.6 %collective-permute-start.19 = (bf16[256,128]{1,0:T(8,128)(2,1)S(1)}, bf16[256,128]{1,0:T(8,128)(2,1)S(1)}, u32[]{:S(2)}, u32[]{:S(2)}) collective-permute-start(bf16[256,128]{1,0:T(8,128)(2,1)S(1)} %get-tuple-element.79), channel_id=1, source_target_pairs={{32,0},{9,1},{34,2},{11,3},{36,4},{13,5},{38,6},{15,7},{40,8},{17,... | collective-permute-start | bytes 196616 | tf_op jit(solution)/shard_map/ppermute | solution.py:64
  109.5 10.5 %collective-permute-start.28 = (bf16[256,256]{1,0:T(8,128)(2,1)S(1)}, bf16[256,256]{1,0:T(8,128)(2,1)S(1)}, u32[]{:S(2)}, u32[]{:S(2)}) collective-permute-start(bf16[256,256]{1,0:T(8,128)(2,1)S(1)} %get-tuple-element.84), channel_id=1, source_target_pairs={{32,0},{9,1},{34,2},{11,3},{36,4},{13,5},{38,6},{15,7},{40,8},{17,... | collective-permute-start | bytes 393224 | tf_op jit(solution)/shard_map/ppermute | solution.py:64
  110.0 10.0 %collective-permute-start.29 = (bf16[256,256]{1,0:T(8,128)(2,1)S(1)}, bf16[256,256]{1,0:T(8,128)(2,1)S(1)}, u32[]{:S(2)}, u32[]{:S(2)}) collective-permute-start(bf16[256,256]{1,0:T(8,128)(2,1)S(1)} %get-tuple-element.85), channel_id=1, source_target_pairs={{64,0},{17,1},{66,2},{19,3},{68,4},{21,5},{70,6},{23,7},{72,8},{25... | collective-permute-start | bytes 393224 | tf_op jit(solution)/shard_map/ppermute | solution.py:64
  113.3 6.7 %collective-permute-start.30 = (bf16[256,256]{1,0:T(8,128)(2,1)S(1)}, bf16[256,256]{1,0:T(8,128)(2,1)S(1)}, u32[]{:S(2)}, u32[]{:S(2)}) collective-permute-start(bf16[256,256]{1,0:T(8,128)(2,1)S(1)} %get-tuple-element.86), channel_id=1, source_target_pairs={{96,0},{25,1},{98,2},{27,3},{100,4},{29,5},{102,6},{31,7},{104,8},... | collective-permute-start | bytes 393224 | tf_op jit(solution)/shard_map/ppermute | solution.py:64
  113.3 6.7 %collective-permute-start.20 = (bf16[256,128]{1,0:T(8,128)(2,1)S(1)}, bf16[256,128]{1,0:T(8,128)(2,1)S(1)}, u32[]{:S(2)}, u32[]{:S(2)}) collective-permute-start(bf16[256,128]{1,0:T(8,128)(2,1)S(1)} %get-tuple-element.80), channel_id=1, source_target_pairs={{64,0},{17,1},{66,2},{19,3},{68,4},{21,5},{70,6},{23,7},{72,8},{25... | collective-permute-start | bytes 196616 | tf_op jit(solution)/shard_map/ppermute | solution.py:64
  115.7 4.3 %collective-permute-start.21 = (bf16[256,128]{1,0:T(8,128)(2,1)S(1)}, bf16[256,128]{1,0:T(8,128)(2,1)S(1)}, u32[]{:S(2)}, u32[]{:S(2)}) collective-permute-start(bf16[256,128]{1,0:T(8,128)(2,1)S(1)} %get-tuple-element.81), channel_id=1, source_target_pairs={{96,0},{25,1},{98,2},{27,3},{100,4},{29,5},{102,6},{31,7},{104,8},... | collective-permute-start | bytes 196616 | tf_op jit(solution)/shard_map/ppermute | solution.py:64
  122.1 0.6 copy-start.3
  122.7 13.6 %collective-permute-start.31 = (bf16[64,512]{1,0:T(8,128)(2,1)S(1)}, bf16[64,512]{1,0:T(8,128)(2,1)S(1)}, u32[]{:S(2)}, u32[]{:S(2)}) collective-permute-start(bf16[64,512]{1,0:T(8,128)(2,1)S(1)} %get-tuple-element.89), channel_id=1, source_target_pairs={{1,0},{2,1},{3,2},{4,3},{5,4},{6,5},{7,6},{0,7},{9,8},{10,9},{11,1... | collective-permute-start | bytes 196616 | tf_op jit(solution)/shard_map/ppermute | solution.py:64
  129.7 7.5 %collective-permute-start.32 = (bf16[64,512]{1,0:T(8,128)(2,1)S(1)}, bf16[64,512]{1,0:T(8,128)(2,1)S(1)}, u32[]{:S(2)}, u32[]{:S(2)}) collective-permute-start(bf16[64,512]{1,0:T(8,128)(2,1)S(1)} %get-tuple-element.90), channel_id=1, source_target_pairs={{2,0},{3,1},{4,2},{5,3},{6,4},{7,5},{0,6},{1,7},{10,8},{11,9},{12,... | collective-permute-start | bytes 196616 | tf_op jit(solution)/shard_map/ppermute | solution.py:64
  129.7 7.5 %collective-permute-start.33 = (bf16[64,512]{1,0:T(8,128)(2,1)S(1)}, bf16[64,512]{1,0:T(8,128)(2,1)S(1)}, u32[]{:S(2)}, u32[]{:S(2)}) collective-permute-start(bf16[64,512]{1,0:T(8,128)(2,1)S(1)} %get-tuple-element.91), channel_id=1, source_target_pairs={{3,0},{4,1},{5,2},{6,3},{7,4},{0,5},{1,6},{2,7},{11,8},{12,9},{13,... | collective-permute-start | bytes 196616 | tf_op jit(solution)/shard_map/ppermute | solution.py:64
  129.7 8.8 %collective-permute-start.34 = (bf16[64,512]{1,0:T(8,128)(2,1)S(1)}, bf16[64,512]{1,0:T(8,128)(2,1)S(1)}, u32[]{:S(2)}, u32[]{:S(2)}) collective-permute-start(bf16[64,512]{1,0:T(8,128)(2,1)S(1)} %get-tuple-element.92), channel_id=1, source_target_pairs={{4,0},{5,1},{6,2},{7,3},{0,4},{1,5},{2,6},{3,7},{12,8},{13,9},{14,... | collective-permute-start | bytes 196616 | tf_op jit(solution)/shard_map/ppermute | solution.py:64
  135.4 5.3 %collective-permute-start.35 = (bf16[64,512]{1,0:T(8,128)(2,1)S(1)}, bf16[64,512]{1,0:T(8,128)(2,1)S(1)}, u32[]{:S(2)}, u32[]{:S(2)}) collective-permute-start(bf16[64,512]{1,0:T(8,128)(2,1)S(1)} %get-tuple-element.93), channel_id=1, source_target_pairs={{5,0},{6,1},{7,2},{0,3},{1,4},{2,5},{3,6},{4,7},{13,8},{14,9},{15,... | collective-permute-start | bytes 196616 | tf_op jit(solution)/shard_map/ppermute | solution.py:64
  136.3 6.9 %copy-start.9 = (bf16[64,512]{1,0:T(8,128)(2,1)}, bf16[64,512]{1,0:T(8,128)(2,1)S(1)}, u32[]{:S(2)}) copy-start(bf16[64,512]{1,0:T(8,128)(2,1)S(1)} %collective-permute-done.31.rest_1_) | copy-start | bytes 196612
  136.3 6.6 %collective-permute-start.36 = (bf16[64,512]{1,0:T(8,128)(2,1)S(1)}, bf16[64,512]{1,0:T(8,128)(2,1)S(1)}, u32[]{:S(2)}, u32[]{:S(2)}) collective-permute-start(bf16[64,512]{1,0:T(8,128)(2,1)S(1)} %get-tuple-element.94), channel_id=1, source_target_pairs={{6,0},{7,1},{0,2},{1,3},{2,4},{3,5},{4,6},{5,7},{14,8},{15,9},{8,1... | collective-permute-start | bytes 196616 | tf_op jit(solution)/shard_map/ppermute | solution.py:64
  137.1 6.0 %copy-start.10 = (bf16[64,512]{1,0:T(8,128)(2,1)}, bf16[64,512]{1,0:T(8,128)(2,1)S(1)}, u32[]{:S(2)}) copy-start(bf16[64,512]{1,0:T(8,128)(2,1)S(1)} %collective-permute-done.32.rest_2_) | copy-start | bytes 196612
  137.1 6.0 %collective-permute-start.37 = (bf16[64,512]{1,0:T(8,128)(2,1)S(1)}, bf16[64,512]{1,0:T(8,128)(2,1)S(1)}, u32[]{:S(2)}, u32[]{:S(2)}) collective-permute-start(bf16[64,512]{1,0:T(8,128)(2,1)S(1)} %get-tuple-element.95), channel_id=1, source_target_pairs={{7,0},{0,1},{1,2},{2,3},{3,4},{4,5},{5,6},{6,7},{15,8},{8,9},{9,10... | collective-permute-start | bytes 196616 | tf_op jit(solution)/shard_map/ppermute | solution.py:64
  137.1 6.0 %copy-start.11 = (bf16[64,512]{1,0:T(8,128)(2,1)}, bf16[64,512]{1,0:T(8,128)(2,1)S(1)}, u32[]{:S(2)}) copy-start(bf16[64,512]{1,0:T(8,128)(2,1)S(1)} %collective-permute-done.33.rest_3_) | copy-start | bytes 196612
  138.5 4.7 %copy-start.12 = (bf16[64,512]{1,0:T(8,128)(2,1)}, bf16[64,512]{1,0:T(8,128)(2,1)S(1)}, u32[]{:S(2)}) copy-start(bf16[64,512]{1,0:T(8,128)(2,1)S(1)} %collective-permute-done.34.rest_4_) | copy-start | bytes 196612
  140.7 2.5 %copy-start.13 = (bf16[64,512]{1,0:T(8,128)(2,1)}, bf16[64,512]{1,0:T(8,128)(2,1)S(1)}, u32[]{:S(2)}) copy-start(bf16[64,512]{1,0:T(8,128)(2,1)S(1)} %collective-permute-done.35.rest_5_) | copy-start | bytes 196612
  142.9 0.6 copy-start.14
  143.2 0.6 copy-start.15

commit v3 on v2

v3 whole, which is shorter than its diff:
```python
import functools

import jax
import jax.numpy as jnp
from jax import lax
from jax.experimental import pallas as pl
from jax.experimental.pallas import tpu as pltpu
from jax.sharding import Mesh, PartitionSpec as P

HEADS = 4
BROWS = 64
NBLK = 4
WIDTH = 512
HD = 128
ROWS = 256
CHUNK = 128
LENGTH = 4096
EPS = 1e-05
BF = jnp.bfloat16
F32 = jnp.float32
AXES = ("x", "z", "y", "c")
FAR = 1e9
KEY_TILE = 256
GROUP = 4
KEY_GROUP = 3
SCALE = HD ** (-0.5)


def device_id(x, z, y, c):
    return ((x * 4 + z) * 4 + y) * 2 + c


def all_coords():
    return [(x, z, y, c) for x in range(4) for z in range(4) for y in range(4) for c in range(2)]


def tab_pairs(step):
    out = []
    for x, z, y, c in all_coords():
        y2, c2 = divmod((y * 2 + c + step) % 8, 2)
        out.append((device_id(x, z, y, c), device_id(x, z, y2, c2)))
    return out


def moved(axis, step):
    out = []
    for x, z, y, c in all_coords():
        to = ((x + step) % 4, z) if axis == c else (x, (z + step) % 4)
        out.append((device_id(x, z, y, c), device_id(*to, y, c)))
    return out


def head_pairs(step):
    return moved(0, step)


def row_pairs(step):
    return moved(1, step)


def back(pairs):
    return [(b, a) for a, b in pairs]


def send(value, pairs):
    return lax.ppermute(value, AXES, pairs)


def dot(a, b):
    return jnp.dot(a, b, preferred_element_type=F32)


def dot_nt(a, b):
    return lax.dot_general(a, b, (((1,), (1,)), ((), ())), preferred_element_type=F32)


def silu(z):
    h = 0.5 * z
    return h + h * jnp.tanh(h)


def silu_slope(z):
    h = 0.5 * z
    t = jnp.tanh(h)
    return 0.5 * (1.0 + t) * (1.0 + h * (1.0 - t))


def row_statistics(x):
    mean = jnp.mean(x, axis=-1, keepdims=True)
    centred = x - mean
    inverse = lax.rsqrt(jnp.mean(centred * centred, axis=-1, keepdims=True) + EPS)
    return centred * inverse, inverse


def norm_backward(grad, hat, inverse):
    first = jnp.mean(grad, axis=-1, keepdims=True)
    second = jnp.mean(grad * hat, axis=-1, keepdims=True)
    return inverse * (grad - first - hat * second)


def column_of(row):
    return jnp.transpose(jnp.broadcast_to(row, (CHUNK, CHUNK)))


def ds(start, size):
    return pl.ds(pl.multiple_of(start, size), size)


VMEM = pl.BlockSpec(memory_space=pltpu.VMEM)
SMEM = pl.BlockSpec(memory_space=pltpu.SMEM)


def shape(dims, dtype):
    return jax.ShapeDtypeStruct(dims, dtype)


def call(kernel, ins, specs, outs, scratch=(), flops=0, name=None, out_specs=None, limit=40):
    moved = sum(a.size * a.dtype.itemsize for a in ins)
    moved += sum(o.size * jnp.dtype(o.dtype).itemsize for o in outs)
    return pl.pallas_call(
        kernel,
        out_shape=outs,
        in_specs=specs,
        out_specs=out_specs or [VMEM] * len(outs),
        scratch_shapes=list(scratch),
        compiler_params=pltpu.CompilerParams(vmem_limit_bytes=limit * 1024 * 1024),
        cost_estimate=pl.CostEstimate(flops=flops, bytes_accessed=moved, transcendentals=0),
        name=name,
    )(*ins)


def lookup_kernel(meta, dest, ids_ref, table, *rest):
    outs, (buffer, total, column, arrived) = rest[:8], rest[8:]
    tile = buffer.shape[1]
    copies = [
        pltpu.make_async_copy(table.at[0, 0, pl.ds(n * tile, tile), :], buffer.at[n], arrived.at[n])
        for n in range(buffer.shape[0])
    ]
    for copy in copies:
        copy.start()
    for b in range(2):
        column[b * CHUNK : (b + 1) * CHUNK, :] = column_of(ids_ref[b : b + 1, :].astype(F32))
    lane = lax.broadcasted_iota(jnp.int32, (ROWS, CHUNK), 1).astype(F32)
    for n, copy in enumerate(copies):
        hits = [
            jnp.where(column[...] == lane + float(n * tile + m * CHUNK), 1.0, 0.0).astype(BF)
            for m in range(tile // CHUNK)
        ]
        copy.wait()
        part = dot(jnp.concatenate(hits, axis=1), buffer[n])
        if n == 0:
            total[...] = part
        else:
            total[...] += part
    own = meta[2] * 2 + meta[3]
    for k in range(8):
        outs[k][...] = jnp.zeros_like(outs[k])
        for p in range(NBLK):

            @pl.when(dest[p, own] == lax.rem(own + k, 8))
            def _():
                outs[k][...] = total[p * BROWS : (p + 1) * BROWS, :].astype(BF)


def prepare_kernel(meta, lengths, tile_mask, incoming, w_out, bounds, starts, begins, key_pos, query_pos, dmixed, turned):
    row, core = line(meta)[1], meta[3]
    lane = lax.broadcasted_iota(jnp.int32, (8, CHUNK), 1)
    first, last = lane * CHUNK, lane * CHUNK + CHUNK - 1
    ends, end = [], jnp.int32(0)
    for d in range(lengths.shape[0]):
        end = end + lengths[d]
        ends.append(end)
    chunk_start = jnp.zeros((8, CHUNK), jnp.int32)
    chunk_stop = jnp.full((8, CHUNK), LENGTH, jnp.int32)
    for end in ends:
        chunk_start = jnp.where(first >= end, end, chunk_start)
        chunk_stop = jnp.where(last < end, jnp.minimum(chunk_stop, end), chunk_stop)
    row_id = lax.broadcasted_iota(jnp.int32, (8, CHUNK), 0)
    bounds[...] = jnp.where(row_id == 0, chunk_start, chunk_stop - 1)
    turned[...] = jnp.transpose(tile_mask[...].astype(F32))
    on_keys, on_queries = [], []
    for t in range(8):
        i = chunk_of(t, row, core)
        position = lax.broadcasted_iota(jnp.int32, (CHUNK, CHUNK), 0) + i * CHUNK
        begin = jnp.zeros((CHUNK, CHUNK), jnp.int32)
        for end in ends:
            begin = jnp.where(position >= end, end, begin)
        begins[t * CHUNK : (t + 1) * CHUNK, :] = begin.astype(F32)
        for m in range(2):
            on_keys.append(tile_mask[pl.ds(2 * i + m, 1), :])
            on_queries.append(turned[pl.ds(2 * i + m, 1), :])
    on_keys = jnp.concatenate(on_keys, axis=0).astype(F32).astype(BF)
    on_queries = jnp.concatenate(on_queries, axis=0).astype(BF)
    for n in range(8):
        cols = slice(n * WIDTH, (n + 1) * WIDTH)
        spot = lax.broadcasted_iota(jnp.int32, (BROWS, WIDTH), 1) + n * WIDTH
        pick = jnp.where(
            lax.broadcasted_iota(jnp.int32, (BROWS, WIDTH), 0) == spot // BROWS, 1.0, 0.0
        ).astype(BF)
        spot = spot[0:16, :]
        place = spot.astype(F32)
        key_pos[:, cols] = jnp.where(dot(on_keys, pick) > 0.5, place, FAR)
        query_pos[:, cols] = jnp.where(dot(on_queries, pick) > 0.5, place, -1.0)
        spot = spot[0:8, :]
        begin = jnp.zeros((8, WIDTH), jnp.int32)
        for end in ends:
            begin = jnp.where(spot >= end, end, begin)
        starts[:, cols] = begin.astype(F32)
    dmixed[...] = dot_nt(incoming[...], w_out[...])


def project_kernel(meta, dest, slot, *rest):
    blocks, (w_ref, dmixed_ref), rest = rest[:8], rest[8:10], rest[10:]
    hist, pre = rest[:2]
    outs = rest[2:6]
    act, grads = rest[6:]
    own = meta[2] * 2 + meta[3]
    for k in range(8):
        source = lax.rem(own - k + 8, 8)
        for p in range(NBLK):

            @pl.when(dest[p, source] == own)
            def _():
                hist[ds(slot[p, source] * BROWS, BROWS), :] = blocks[k][...]

    hat, _ = row_statistics(hist[...].astype(F32))
    normed = hat.astype(BF)
    for n in range(4):
        cols = slice(n * WIDTH, (n + 1) * WIDTH)
        part = dot(normed, w_ref[:, cols])
        pre[:, cols] = part
        act[:, cols] = silu(part).astype(BF)
    grads[...] = (dmixed_ref[...] * act[:, 0:WIDTH].astype(F32)).astype(BF)
    for j in range(4):
        head = lax.rem(line(meta)[0] + j, 4) * HD
        outs[j][:, 0:HD] = act[:, ds(3 * WIDTH + head, HD)]
        outs[j][:, HD : 2 * HD] = act[:, ds(WIDTH + head, HD)]
        outs[j][:, 2 * HD : 3 * HD] = act[:, ds(2 * WIDTH + head, HD)]
        outs[j][:, 3 * HD : 4 * HD] = grads[:, ds(head, HD)]


def line(meta):
    first = meta[3] == 0
    return jnp.where(first, meta[0], meta[1]), jnp.where(first, meta[1], meta[0])


def chunk_of(t, row, core):
    spread = 4 * t + jnp.where(t < 4, row, 3 - row)
    solid = t + jnp.where(t < 4, 4 * row, 24 - 4 * row)
    return jnp.where(core == 0, spread, solid)


def pieces_of(meta):
    head = line(meta)[0]
    for j in range(4):
        source = lax.rem(head - j + 4, 4)
        yield j, 0, source
        yield j, CHUNK, 7 - source


def collect_kernel(meta, p0, p1, p2, p3, keys, queries, grads):
    pieces = (p0, p1, p2, p3)
    for j, low, t in pieces_of(meta):
        rows, part = ds(t * CHUNK, CHUNK), pieces[j]
        keys[rows, :] = part[low : low + CHUNK, 0 : 2 * HD]
        queries[rows, :] = part[low : low + CHUNK, 2 * HD : 3 * HD]
        grads[rows, :] = part[low : low + CHUNK, 3 * HD : 4 * HD]


def place_rows(meta, parts, out):
    row, core = line(meta)[1], meta[3]
    for k in range(4):
        other = lax.rem(row - k + 4, 4)
        for t in range(8):
            chunk = chunk_of(t, other, core)
            out[ds(chunk * CHUNK, CHUNK), :] = parts[k][t * CHUNK : (t + 1) * CHUNK, :]


def list_work(pairs, tiles, span, size):
    def one_pair(p, count):
        def one(n, count):
            pairs[count] = p
            tiles[count] = n
            return count + 1

        low, high = span(2 * p)
        low_next, high_next = span(2 * p + 1)
        count = lax.fori_loop(low, high + 1, one, count)
        return lax.fori_loop(jnp.maximum(low_next, high + 1), high_next + 1, one, count)

    count = lax.fori_loop(0, 4, one_pair, jnp.int32(0))
    for u in range(size - 1):
        pairs[count + u] = 4
        tiles[count + u] = 0
    return (count + size - 1) // size


def work_scratch():
    return [pltpu.SMEM((160,), jnp.int32), pltpu.SMEM((160,), jnp.int32)]


def pair_positions(meta, p, width):
    row, core = line(meta)[1], meta[3]
    local = lax.broadcasted_iota(jnp.int32, (CHUNK, width), 0).astype(F32)
    return jnp.concatenate(
        [local + (chunk_of(2 * p + m, row, core) * CHUNK).astype(F32) for m in range(2)], axis=0
    )


def spread_rows(table, p, cols):
    return jnp.concatenate(
        [jnp.broadcast_to(table[pl.ds(4 * p + m, 1), cols], (BROWS, KEY_TILE)) for m in range(4)], axis=0
    )


def allowed_keys(meta, begins, key_pos, p, n):
    repeat = KEY_TILE // CHUNK
    pos = jnp.concatenate([pair_positions(meta, p, CHUNK)] * repeat, axis=1)
    start = jnp.concatenate([begins[ds(p * ROWS, ROWS), :]] * repeat, axis=1)
    key = spread_rows(key_pos, p, ds(n * KEY_TILE, KEY_TILE))
    return (key >= start) & (key <= pos)


def key_span(meta, bounds):
    row, core = line(meta)[1], meta[3]

    def span(t):
        i = chunk_of(t, row, core)
        return bounds[0, i] // KEY_TILE, (i * CHUNK + CHUNK - 1) // KEY_TILE

    return span


def forward_kernel(
    meta, bounds, begins, key_pos, k0, k1, k2, k3, queries, grads,
    keys, attn, passed, stats, total, pairs, tiles,
):
    passed[...] = queries[...]
    place_rows(meta, (k0, k1, k2, k3), keys)
    total[...] = jnp.zeros_like(total)
    groups = list_work(pairs, tiles, key_span(meta, bounds), GROUP)

    def group(b, carry):
        parts = []
        for u in range(GROUP):
            slot, n = pairs[b * GROUP + u], tiles[b * GROUP + u]
            p = jnp.minimum(slot, 3)
            rows = ds(n * KEY_TILE, KEY_TILE)
            h = dot_nt(queries[ds(p * ROWS, ROWS), :], keys[rows, 0:HD]) * (0.5 * SCALE)
            allowed = allowed_keys(meta, begins, key_pos, p, n)
            probs = jnp.where(allowed, h + h * jnp.tanh(h), 0.0).astype(BF)
            parts.append((slot, dot(probs, keys[rows, HD : 2 * HD])))
        for slot, part in parts:
            total[ds(slot * ROWS, ROWS), :] += part
        return carry

    lax.fori_loop(0, groups, group, 0)
    lane = lax.broadcasted_iota(jnp.int32, (CHUNK, CHUNK), 1)
    for t in range(8):
        rows = slice(t * CHUNK, (t + 1) * CHUNK)
        x = total[rows, :]
        attn[rows, :] = x
        e = grads[rows, :].astype(F32)
        mean = jnp.mean(x, axis=1, keepdims=True)
        centred = x - mean
        packed = jnp.where(lane == 0, mean, 0.0)
        packed = jnp.where(lane == 1, jnp.sum(centred * centred, axis=1, keepdims=True), packed)
        packed = jnp.where(lane == 2, jnp.sum(e, axis=1, keepdims=True), packed)
        packed = jnp.where(lane == 3, jnp.sum(e * centred, axis=1, keepdims=True), packed)
        stats[:, rows] = jnp.transpose(packed)[0:8, :]


def attn_grad_kernel(s0, s1, s2, s3, attn, grads, q1, q2, q3, out):
    parts = [s[...] for s in (s0, s1, s2, s3)]
    means = [s[0:1, :] for s in parts]
    mean = (means[0] + means[1] + means[2] + means[3]) * 0.25
    spread = sum(s[1:2, :] + HD * (m - mean) * (m - mean) for s, m in zip(parts, means))
    inverse = lax.rsqrt(spread * (1.0 / WIDTH) + EPS)
    e_mean = sum(s[2:3, :] for s in parts) * (1.0 / WIDTH)
    e_on = sum(s[3:4, :] + (m - mean) * s[2:3, :] for s, m in zip(parts, means))
    e_on = e_on * inverse * (1.0 / WIDTH)
    for t in range(8):
        rows = slice(t * CHUNK, (t + 1) * CHUNK)
        cols = [column_of(v[:, rows]) for v in (mean, inverse, e_mean, e_on)]
        hat = (attn[rows, :] - cols[0]) * cols[1]
        out[rows, :] = (cols[1] * (grads[rows, :].astype(F32) - cols[2] - hat * cols[3])).astype(BF)


def query_grad_kernel(
    meta, bounds, begins, key_pos, keys, queries, d_attn, out, total, pairs, tiles
):
    total[...] = jnp.zeros_like(total)
    groups = list_work(pairs, tiles, key_span(meta, bounds), GROUP)

    def group(b, carry):
        parts = []
        for u in range(GROUP):
            slot, n = pairs[b * GROUP + u], tiles[b * GROUP + u]
            p = jnp.minimum(slot, 3)
            rows = ds(n * KEY_TILE, KEY_TILE)
            rows_q = ds(p * ROWS, ROWS)
            k = keys[rows, 0:HD]
            h = dot_nt(queries[rows_q, :], k) * (0.5 * SCALE)
            dp = dot_nt(d_attn[rows_q, :], keys[rows, HD : 2 * HD])
            th = jnp.tanh(h)
            allowed = allowed_keys(meta, begins, key_pos, p, n)
            d_scores = jnp.where(allowed, dp * ((1.0 + th) * (1.0 + h - h * th)), 0.0)
            parts.append((slot, dot(d_scores.astype(BF), k)))
        for slot, part in parts:
            total[ds(slot * ROWS, ROWS), :] += part
        return carry

    lax.fori_loop(0, groups, group, 0)
    out[...] = (total[0 : LENGTH // 4, :] * (0.5 * SCALE)).astype(BF)


def key_grad_kernel(
    meta, bounds, starts, query_pos, keys, q0, q1, q2, q3, g0, g1, g2, g3, d_query, attn,
    r0, r1, r2, r3, queries, grads, total, pairs, tiles,
):
    outs = (r0, r1, r2, r3)
    row, core = line(meta)[1], meta[3]
    place_rows(meta, (q0, q1, q2, q3), queries)
    place_rows(meta, (g0, g1, g2, g3), grads)
    total[...] = jnp.zeros_like(total)

    def span(t):
        i = chunk_of(t, row, core)
        return (i * CHUNK) // KEY_TILE, bounds[1, i] // KEY_TILE

    groups = list_work(pairs, tiles, span, KEY_GROUP)

    def group(b, carry):
        parts = []
        for u in range(KEY_GROUP):
            slot, n = pairs[b * KEY_GROUP + u], tiles[b * KEY_GROUP + u]
            p = jnp.minimum(slot, 3)
            rows_k = ds(p * ROWS, ROWS)
            rows = ds(n * KEY_TILE, KEY_TILE)
            q, g = queries[rows, :], grads[rows, :]
            pos = pair_positions(meta, p, KEY_TILE)
            begin = jnp.broadcast_to(starts[0:1, rows], (ROWS, KEY_TILE))
            allowed = (pos <= spread_rows(query_pos, p, rows)) & (pos >= begin)
            h = dot_nt(keys[rows_k, 0:HD], q) * (0.5 * SCALE)
            dp = dot_nt(keys[rows_k, HD : 2 * HD], g)
            th = jnp.tanh(h)
            up = 1.0 + th
            probs = jnp.where(allowed, h * up, 0.0).astype(BF)
            d_scores = jnp.where(allowed, dp * (up * (1.0 + h - h * th)), 0.0).astype(BF)
            parts.append((slot, dot(d_scores, q), dot(probs, g)))
        for slot, d_key, d_value in parts:
            rows = ds(slot * ROWS, ROWS)
            total[rows, 0:HD] += d_key
            total[rows, HD : 2 * HD] += d_value
        return carry

    lax.fori_loop(0, groups, group, 0)
    for j, low, t in pieces_of(meta):
        rows = ds(t * CHUNK, CHUNK)
        outs[j][low : low + CHUNK, 0:HD] = (total[rows, 0:HD] * (0.5 * SCALE)).astype(BF)
        outs[j][low : low + CHUNK, HD : 2 * HD] = total[rows, HD : 2 * HD].astype(BF)
        outs[j][low : low + CHUNK, 2 * HD : 3 * HD] = d_query[rows, :]
        outs[j][low : low + CHUNK, 3 * HD : 4 * HD] = attn[rows, :].astype(BF)


def input_grad_kernel(meta, dest, slot, p0, p1, p2, p3, pre, dmixed, hist, incoming, w_in, *rest):
    outs, (mixed, attn, d_act, result) = rest[:8], rest[8:]
    for j, part in enumerate((p0, p1, p2, p3)):
        head = lax.rem(line(meta)[0] + j, 4) * HD
        d_act[:, ds(2 * WIDTH + head, HD)] = part[:, 0:HD].astype(F32)
        d_act[:, ds(head, HD)] = part[:, HD : 2 * HD].astype(F32)
        d_act[:, ds(WIDTH + head, HD)] = part[:, 2 * HD : 3 * HD].astype(F32)
        attn[:, ds(head, HD)] = part[:, 3 * HD : 4 * HD].astype(F32)
    on, _ = row_statistics(attn[...])
    u_pre = pre[:, 0:WIDTH]
    mixed[...] = (on * silu(u_pre).astype(BF).astype(F32)).astype(BF)
    total = dot_nt((dmixed[...] * on * silu_slope(u_pre)).astype(BF), w_in[:, 0:WIDTH])
    for n in range(3):
        cols = slice((n + 1) * WIDTH, (n + 2) * WIDTH)
        d_pre = (d_act[:, n * WIDTH : (n + 1) * WIDTH] * silu_slope(pre[:, cols])).astype(BF)
        total = total + dot_nt(d_pre, w_in[:, cols])
    hat, inverse = row_statistics(hist[...].astype(F32))
    result[...] = (incoming[...].astype(F32) + norm_backward(total, hat, inverse)).astype(BF)
    own = meta[2] * 2 + meta[3]
    for k in range(8):
        outs[k][...] = jnp.zeros_like(outs[k])
        source = lax.rem(own - k + 8, 8)
        for p in range(NBLK):

            @pl.when(dest[p, source] == own)
            def _():
                outs[k][...] = result[ds(slot[p, source] * BROWS, BROWS), :]


def output_kernel(mixed, hist, w_out, out):
    out[...] = (hist[...].astype(F32) + dot(mixed[...], w_out[...])).astype(BF)


def table_grad_kernel(meta, dest, ids, *rest):
    blocks, out, rows, buffer, sent = rest[:8], rest[8], rest[9], rest[10], rest[11]
    tile = buffer.shape[1]
    own = meta[2] * 2 + meta[3]
    for k in range(8):
        for p in range(NBLK):

            @pl.when(dest[p, own] == lax.rem(own + k, 8))
            def _():
                rows[p * BROWS : (p + 1) * BROWS, :] = blocks[k][...]

    number = lax.broadcasted_iota(jnp.int32, (tile, ROWS), 0)
    copies = []
    for n in range(buffer.shape[0]):
        hits = jnp.where(number + n * tile == ids[...], 1.0, 0.0).astype(BF)
        buffer[n] = dot(hits, rows[...]).astype(BF)
        copy = pltpu.make_async_copy(buffer.at[n], out.at[0, 0, pl.ds(n * tile, tile), :], sent.at[n])
        copy.start()
        copies.append(copy)
    for copy in copies:
        copy.wait()


def body(table, row_ids, dests, slots, lengths, tile_mask, w_in, w_out, output_gradient):
    x, z, y, c = (lax.axis_index(a).astype(jnp.int32) for a in AXES)
    dest = dests[0].T
    slot = slots[0].T
    tab_rows = table.shape[2]

    place_info = jnp.stack([x, z, y, c])
    bounds, starts, begins, key_pos, query_pos, dmixed = call(
        prepare_kernel,
        [place_info, lengths[0], tile_mask[0], output_gradient[0], w_out],
        [SMEM] * 2 + [VMEM] * 3,
        [
            shape((8, CHUNK), jnp.int32),
            shape((8, LENGTH), F32),
            shape((LENGTH // 4, CHUNK), F32),
            shape((16, LENGTH), F32),
            shape((16, LENGTH), F32),
            shape((ROWS, WIDTH), F32),
        ],
        [pltpu.VMEM((64, 64), F32)],
        flops=2 * ROWS * WIDTH * WIDTH,
        name="prepare",
    )

    tiles = 8
    tile = tab_rows // tiles
    block_shape = shape((BROWS, WIDTH), BF)
    outgoing = call(
        lookup_kernel,
        [place_info, dest, row_ids.reshape(2, CHUNK), table],
        [SMEM, SMEM, VMEM, pl.BlockSpec(memory_space=pltpu.HBM)],
        [block_shape] * 8,
        [
            pltpu.VMEM((tiles, tile, WIDTH), BF),
            pltpu.VMEM((ROWS, WIDTH), F32),
            pltpu.VMEM((ROWS, CHUNK), F32),
            pltpu.SemaphoreType.DMA((tiles,)),
        ],
        flops=2 * ROWS * tab_rows * WIDTH,
        name="lookup",
        limit=60,
    )
    blocks = [outgoing[0]] + [send(outgoing[k], tab_pairs(k)) for k in range(1, 8)]

    four = shape((ROWS, 4 * HD), BF)
    two = shape((ROWS, 2 * HD), BF)
    one = shape((ROWS, HD), BF)
    quarter = LENGTH // 4
    rows_two = shape((quarter, 2 * HD), BF)
    rows_one = shape((quarter, HD), BF)

    def to_heads(values):
        return [values[0]] + [send(values[j], head_pairs(j)) for j in range(1, 4)]

    def to_owners(values):
        return [values[0]] + [send(values[j], back(head_pairs(j))) for j in range(1, 4)]

    def over_rows(value):
        return [value] + [send(value, row_pairs(k)) for k in range(1, 4)]

    hist, pre, *pieces = call(
        project_kernel,
        [place_info, dest, slot, *blocks, w_in, dmixed],
        [SMEM] * 3 + [VMEM] * 10,
        [shape((ROWS, WIDTH), BF), shape((ROWS, 4 * WIDTH), F32)] + [four] * 4,
        [pltpu.VMEM((ROWS, 4 * WIDTH), BF), pltpu.VMEM((ROWS, WIDTH), BF)],
        flops=2 * ROWS * WIDTH * 4 * WIDTH,
        name="project",
    )
    own_keys, queries, grads = call(
        collect_kernel,
        [place_info, *to_heads(pieces)],
        [SMEM] + [VMEM] * 4,
        [rows_two, rows_one, rows_one],
        name="collect",
    )
    keys, attn, passed, stats = call(
        forward_kernel,
        [place_info, bounds, begins, key_pos, *over_rows(own_keys), queries, grads],
        [SMEM] * 2 + [VMEM] * 8,
        [shape((LENGTH, 2 * HD), BF), shape((quarter, HD), F32), rows_one, shape((8, quarter), F32)],
        [pltpu.VMEM((quarter + ROWS, HD), F32)] + work_scratch(),
        flops=6 * 10**9,
        name="forward",
    )
    all_queries = over_rows(queries)
    (d_attn,) = call(
        attn_grad_kernel,
        [*to_heads([stats] * 4), attn, grads, *all_queries[1:]],
        [VMEM] * 6 + [pl.BlockSpec(memory_space=pl.ANY)] * 3,
        [rows_one],
        flops=10**9,
        name="attn_grad",
    )
    all_d_attn = over_rows(d_attn)
    (d_query,) = call(
        query_grad_kernel,
        [place_info, bounds, begins, key_pos, keys, queries, d_attn],
        [SMEM] * 2 + [VMEM] * 5,
        [rows_one],
        [pltpu.VMEM((quarter + ROWS, HD), F32)] + work_scratch(),
        flops=6 * 10**9,
        name="query_grad",
    )
    back_parts = call(
        key_grad_kernel,
        [place_info, bounds, starts, query_pos, own_keys, *all_queries, *all_d_attn, d_query, attn],
        [SMEM] * 2 + [VMEM] * 13,
        [four] * 4,
        [pltpu.VMEM((LENGTH, HD), BF), pltpu.VMEM((LENGTH, HD), BF), pltpu.VMEM((quarter + ROWS, 2 * HD), F32)]
        + work_scratch(),
        flops=7 * 10**9,
        name="key_grad",
    )
    incoming = output_gradient[0]
    *returning, mixed = call(
        input_grad_kernel,
        [place_info, dest, slot, *to_owners(back_parts), pre, dmixed, hist, incoming, w_in],
        [SMEM] * 3 + [VMEM] * 9,
        [block_shape] * 8 + [shape((ROWS, WIDTH), BF)],
        [
            pltpu.VMEM((ROWS, WIDTH), F32),
            pltpu.VMEM((ROWS, 3 * WIDTH), F32),
            pltpu.VMEM((ROWS, WIDTH), BF),
        ],
        flops=8 * ROWS * WIDTH * WIDTH,
        name="input_grad",
    )
    (layer_out,) = call(
        output_kernel,
        [mixed, hist, w_out],
        [VMEM] * 3,
        [shape((ROWS, WIDTH), BF)],
        flops=2 * ROWS * WIDTH * WIDTH,
        name="output",
    )
    came_back = [returning[0]] + [send(returning[k], back(tab_pairs(k))) for k in range(1, 8)]
    (table_grad,) = call(
        table_grad_kernel,
        [place_info, dest, row_ids.reshape(1, ROWS), *came_back],
        [SMEM, SMEM] + [VMEM] * 9,
        [shape((1, 1, tab_rows, WIDTH), BF)],
        [
            pltpu.VMEM((ROWS, WIDTH), BF),
            pltpu.VMEM((tiles, tile, WIDTH), BF),
            pltpu.SemaphoreType.DMA((tiles,)),
        ],
        flops=2 * ROWS * tab_rows * WIDTH,
        name="table_grad",
        out_specs=[pl.BlockSpec(memory_space=pltpu.HBM)],
    )
    return layer_out.reshape(1, ROWS, WIDTH), table_grad


def solution(mesh):
    fine = Mesh(mesh.devices.reshape(4, 4, 4, 2), AXES)
    ctx, tab = ("x", "z"), ("y", "c")
    in_specs = (
        P(ctx, tab, None, None),
        P(ctx, tab, None),
        P(ctx, None, None),
        P(ctx, None, None),
        P(tab, None),
        P(tab, None, None),
        P(),
        P(),
        P(tab, ctx, None),
    )
    out_specs = (P(tab, ctx, None), P(ctx, tab, None, None))
    return jax.shard_map(body, mesh=fine, in_specs=in_specs, out_specs=out_specs, check_vma=False)
```

time: 151 us -> 121 us (0.80)
  the two profiles are of different devices: /device:TPU:6 before, /device:TPU:1 now
where the time goes in v3:
time: 121 us; the launch traced here: 122 us
  starting transfers between devices  59.2 us (49%)
  waiting for transfers between devices  32.5 us (27%)
  Pallas kernels  28.2 us (23%)
    ppermute x32, starting transfers between devices, send(): return lax.ppermute(value, AXES, pairs)  59.2 us
    ppermute x32, waiting for transfers between devices, send(): return lax.ppermute(value, AXES, pairs)  32.5 us
    pallas_call x11, Pallas kernels, call(): pl.pallas_call(kernel, out_shape=outs, in_specs=specs, out_specs=out_spec...  28.2 us
  transfers between devices with their start and end apart: 32, of which 13 were waited for; matrix products, arithmetic and copies ran while one was open for 0% of the time, Pallas kernels for 8%

profile of v3, /device:TPU:1, one launch (start us, length us, event | category | flops | bytes accessed | tf_op | source)
XLA Modules:
  0.0 122.4 jit_solution(6858299596656180543)
XLA Ops:
  0.6 0.6 pad_add_fusion.meta
  1.3 0.0 copy-start.9
  1.3 0.0 copy-start
  1.3 0.0 copy-start.4
  1.3 0.0 copy-start.7
  1.3 4.9 %lookup.1 = (bf16[64,512]{1,0:T(8,128)(2,1)}, bf16[64,512]{1,0:T(8,128)(2,1)}, bf16[64,512]{1,0:T(8,128)(2,1)}, bf16[64,512]{1,0:T(8,128)(2,1)}, bf16[64,512]{1,...) custom-call(s32[4]{0:T(128)} %pad_add_fusion.meta, s32[4,8]{1,0:T(4,128)} %bitcast.18, ...), custom_call_target="tpu_custom_call" | custom-call | flops 1073741824 | bytes 4719760 | tf_op jit(solution)/shard_map/lookup/pallas_call | solution.py:120
  6.2 2.7 %collective-permute-start = (bf16[64,512]{1,0:T(8,128)(2,1)}, bf16[64,512]{1,0:T(8,128)(2,1)S(1)}, u32[]{:S(2)}, u32[]{:S(2)}) collective-permute-start(bf16[64,512]{1,0:T(8,128)(2,1)} %get-tuple-element.45), channel_id=1, source_target_pairs={{0,1},{1,2},{2,3},{3,4},{4,5},{5,6},{6,7},{7,0},{8,9},{9,10},{10,1... | collective-permute-start | bytes 196616 | tf_op jit(solution)/shard_map/ppermute | solution.py:66
  8.9 1.3 %collective-permute-start.1 = (bf16[64,512]{1,0:T(8,128)(2,1)}, bf16[64,512]{1,0:T(8,128)(2,1)S(1)}, u32[]{:S(2)}, u32[]{:S(2)}) collective-permute-start(bf16[64,512]{1,0:T(8,128)(2,1)} %get-tuple-element.46), channel_id=1, source_target_pairs={{0,2},{1,3},{2,4},{3,5},{4,6},{5,7},{6,0},{7,1},{8,10},{9,11},{10,... | collective-permute-start | bytes 196616 | tf_op jit(solution)/shard_map/ppermute | solution.py:66
  10.2 1.7 %collective-permute-start.2 = (bf16[64,512]{1,0:T(8,128)(2,1)}, bf16[64,512]{1,0:T(8,128)(2,1)S(1)}, u32[]{:S(2)}, u32[]{:S(2)}) collective-permute-start(bf16[64,512]{1,0:T(8,128)(2,1)} %get-tuple-element.47), channel_id=1, source_target_pairs={{0,3},{1,4},{2,5},{3,6},{4,7},{5,0},{6,1},{7,2},{8,11},{9,12},{10,... | collective-permute-start | bytes 196616 | tf_op jit(solution)/shard_map/ppermute | solution.py:66
  11.9 0.3 collective-permute-start.3
  12.3 2.0 %collective-permute-start.4 = (bf16[64,512]{1,0:T(8,128)(2,1)}, bf16[64,512]{1,0:T(8,128)(2,1)S(1)}, u32[]{:S(2)}, u32[]{:S(2)}) collective-permute-start(bf16[64,512]{1,0:T(8,128)(2,1)} %get-tuple-element.49), channel_id=1, source_target_pairs={{0,5},{1,6},{2,7},{3,0},{4,1},{5,2},{6,3},{7,4},{8,13},{9,14},{10,... | collective-permute-start | bytes 196616 | tf_op jit(solution)/shard_map/ppermute | solution.py:66
  14.2 0.8 collective-permute-start.5
  15.0 1.6 %collective-permute-start.6 = (bf16[64,512]{1,0:T(8,128)(2,1)}, bf16[64,512]{1,0:T(8,128)(2,1)S(1)}, u32[]{:S(2)}, u32[]{:S(2)}) collective-permute-start(bf16[64,512]{1,0:T(8,128)(2,1)} %get-tuple-element.51), channel_id=1, source_target_pairs={{0,7},{1,0},{2,1},{3,2},{4,3},{5,4},{6,5},{7,6},{8,15},{9,8},{10,9... | collective-permute-start | bytes 196616 | tf_op jit(solution)/shard_map/ppermute | solution.py:66
  16.7 1.7 %prepare.1 = (s32[8,128]{1,0:T(8,128)S(1)}, f32[8,4096]{1,0:T(8,128)S(1)}, f32[1024,128]{1,0:T(8,128)S(1)}, f32[16,4096]{1,0:T(8,128)S(1)}, f32[16,4096]{1,0:T(8,128)S(1)}, /*index=5*/f32[256,512]{1,0:T(8,128)S(1)}) custom-call(s32[4]{0:T(128)S(1)} %copy-done.6, s32[16]{0:T(128)S(1)} %bitcast.27, s32[64,64]{1,0:T(8,128)S(1)} %bitcast.22, ...), custom_call_target="tpu_custom_call" | custom-call | flops 134217728 | bytes 2510928 | tf_op jit(solution)/shard_map/prepare/pallas_call | solution.py:120
  18.3 0.0 collective-permute-done.2.rest_3_
  18.4 0.0 collective-permute-done.4.rest_5_
  18.4 1.4 %collective-permute-done.6.rest_7_ = bf16[64,512]{1,0:T(8,128)(2,1)S(1)} collective-permute-done((bf16[64,512]{1,0:T(8,128)(2,1)}, bf16[64,512]{1,0:T(8,128)(2,1)S(1)}, u32[]{:S(2)}, u32[]{:S(2)}) %collective-permute-start.6) | collective-permute-done | bytes 65568 | tf_op jit(solution)/shard_map/ppermute | solution.py:66
  19.8 0.0 copy-start.3
  19.8 0.8 copy-done.3
  20.6 2.4 %project.1 = (bf16[256,512]{1,0:T(8,128)(2,1)S(1)}, f32[256,2048]{1,0:T(8,128)S(1)}, bf16[256,512]{1,0:T(8,128)(2,1)S(1)}, bf16[256,512]{1,0:T(8,128)(2,1)S(1)},...) custom-call(s32[4]{0:T(128)S(1)} %copy-done.6, s32[4,8]{1,0:T(4,128)S(1)} %bitcast.19, s32[4,8]{1,0:T(4,128)S(1)} %bitcast.23, ...), custom_call_target="tpu_custom_call" | custom-call | flops 536870912 | bytes 6553872 | tf_op jit(solution)/shard_map/project/pallas_call | solution.py:120
  23.1 1.7 %collective-permute-start.7 = (bf16[256,512]{1,0:T(8,128)(2,1)S(1)}, bf16[256,512]{1,0:T(8,128)(2,1)S(1)}, u32[]{:S(2)}, u32[]{:S(2)}) collective-permute-start(bf16[256,512]{1,0:T(8,128)(2,1)S(1)} %get-tuple-element.54), channel_id=1, source_target_pairs={{0,32},{1,9},{2,34},{3,11},{4,36},{5,13},{6,38},{7,15},{8,40},{9,1... | collective-permute-start | bytes 786440 | tf_op jit(solution)/shard_map/ppermute | solution.py:66
  24.8 3.3 %collective-permute-start.8 = (bf16[256,512]{1,0:T(8,128)(2,1)S(1)}, bf16[256,512]{1,0:T(8,128)(2,1)S(1)}, u32[]{:S(2)}, u32[]{:S(2)}) collective-permute-start(bf16[256,512]{1,0:T(8,128)(2,1)S(1)} %get-tuple-element.55), channel_id=1, source_target_pairs={{0,64},{1,17},{2,66},{3,19},{4,68},{5,21},{6,70},{7,23},{8,72},{9,... | collective-permute-start | bytes 786440 | tf_op jit(solution)/shard_map/ppermute | solution.py:66
  28.1 0.7 collective-permute-start.9
  28.8 1.8 %collective-permute-done.7.p1 = bf16[256,512]{1,0:T(8,128)(2,1)S(1)} collective-permute-done((bf16[256,512]{1,0:T(8,128)(2,1)S(1)}, bf16[256,512]{1,0:T(8,128)(2,1)S(1)}, u32[]{:S(2)}, u32[]{:S(2)}) %collective-permute-start.7) | collective-permute-done | bytes 262176 | tf_op jit(solution)/shard_map/ppermute | solution.py:66
  30.7 4.0 %collective-permute-done.8.p2 = bf16[256,512]{1,0:T(8,128)(2,1)S(1)} collective-permute-done((bf16[256,512]{1,0:T(8,128)(2,1)S(1)}, bf16[256,512]{1,0:T(8,128)(2,1)S(1)}, u32[]{:S(2)}, u32[]{:S(2)}) %collective-permute-start.8) | collective-permute-done | bytes 262176 | tf_op jit(solution)/shard_map/ppermute | solution.py:66
  34.7 0.7 collect.1
  35.3 1.3 %collective-permute-start.13 = (bf16[1024,256]{1,0:T(8,128)(2,1)S(1)}, bf16[1024,256]{1,0:T(8,128)(2,1)S(1)}, u32[]{:S(2)}, u32[]{:S(2)}) collective-permute-start(bf16[1024,256]{1,0:T(8,128)(2,1)S(1)} %get-tuple-element.57.k0.keys), channel_id=1, source_target_pairs={{0,8},{1,33},{2,10},{3,35},{4,12},{5,37},{6,14},{7,39},{8,16},{9,4... | collective-permute-start | bytes 1572872 | tf_op jit(solution)/shard_map/ppermute | solution.py:66
  36.6 2.4 %collective-permute-start.14 = (bf16[1024,256]{1,0:T(8,128)(2,1)S(1)}, bf16[1024,256]{1,0:T(8,128)(2,1)S(1)}, u32[]{:S(2)}, u32[]{:S(2)}) collective-permute-start(bf16[1024,256]{1,0:T(8,128)(2,1)S(1)} %get-tuple-element.57.k0.keys), channel_id=1, source_target_pairs={{0,16},{1,65},{2,18},{3,67},{4,20},{5,69},{6,22},{7,71},{8,24},{9,... | collective-permute-start | bytes 1572872 | tf_op jit(solution)/shard_map/ppermute | solution.py:66
  39.0 1.2 collective-permute-start.15
  40.2 0.3 collective-permute-start.10
  40.5 0.9 collective-permute-start.11
  41.4 3.5 %collective-permute-done.13.k1 = bf16[1024,256]{1,0:T(8,128)(2,1)S(1)} collective-permute-done((bf16[1024,256]{1,0:T(8,128)(2,1)S(1)}, bf16[1024,256]{1,0:T(8,128)(2,1)S(1)}, u32[]{:S(2)}, u32[]{:S(2)}) %collective-permute-start.13) | collective-permute-done | bytes 524320 | tf_op jit(solution)/shard_map/ppermute | solution.py:66
  44.9 1.3 %collective-permute-start.12 = (bf16[1024,128]{1,0:T(8,128)(2,1)S(1)}, bf16[1024,128]{1,0:T(8,128)(2,1)S(1)}, u32[]{:S(2)}, u32[]{:S(2)}) collective-permute-start(bf16[1024,128]{1,0:T(8,128)(2,1)S(1)} %get-tuple-element.58.queries.q0), channel_id=1, source_target_pairs={{0,24},{1,97},{2,26},{3,99},{4,28},{5,101},{6,30},{7,103},{8,0},{9... | collective-permute-start | bytes 786440 | tf_op jit(solution)/shard_map/ppermute | solution.py:66
  46.2 5.4 %collective-permute-done.14.k2 = bf16[1024,256]{1,0:T(8,128)(2,1)S(1)} collective-permute-done((bf16[1024,256]{1,0:T(8,128)(2,1)S(1)}, bf16[1024,256]{1,0:T(8,128)(2,1)S(1)}, u32[]{:S(2)}, u32[]{:S(2)}) %collective-permute-start.14) | collective-permute-done | bytes 524320 | tf_op jit(solution)/shard_map/ppermute | solution.py:66
  51.6 4.0 %forward.1 = (bf16[4096,256]{1,0:T(8,128)(2,1)S(1)}, f32[1024,128]{1,0:T(8,128)S(1)}, bf16[1024,128]{1,0:T(8,128)(2,1)}, f32[8,1024]{1,0:T(8,128)S(1)}) custom-call(s32[4]{0:T(128)S(1)} %copy-done.6, s32[8,128]{1,0:T(8,128)S(1)} %get-tuple-element.41.bounds, f32[1024,128]{1,0:T(8,128)S(1)} %get-tuple-element.59.begins, ...), custom_call_target="tpu_custom_call" | custom-call | flops 6000000000 | bytes 6328336 | tf_op jit(solution)/shard_map/forward/pallas_call | solution.py:120
  55.6 0.7 collective-permute-start.16
  56.3 2.4 %collective-permute-start.17 = (f32[8,1024]{1,0:T(8,128)S(1)}, f32[8,1024]{1,0:T(8,128)S(1)}, u32[]{:S(2)}, u32[]{:S(2)}) collective-permute-start(f32[8,1024]{1,0:T(8,128)S(1)} %get-tuple-element.62.s0), channel_id=1, source_target_pairs={{0,64},{1,17},{2,66},{3,19},{4,68},{5,21},{6,70},{7,23},{8,72},{9,... | collective-permute-start | bytes 98312 | tf_op jit(solution)/shard_map/ppermute | solution.py:66
  58.7 1.0 collective-permute-start.18
  59.7 0.9 collective-permute-done.17.s2
  60.6 0.9 collective-permute-done.18.s3
  61.5 0.6 attn_grad.1.d_attn.g0
  62.1 1.3 %collective-permute-start.19 = (bf16[1024,128]{1,0:T(8,128)(2,1)S(1)}, bf16[1024,128]{1,0:T(8,128)(2,1)S(1)}, u32[]{:S(2)}, u32[]{:S(2)}) collective-permute-start(bf16[1024,128]{1,0:T(8,128)(2,1)S(1)} %attn_grad.1.d_attn.g0), channel_id=1, source_target_pairs={{0,8},{1,33},{2,10},{3,35},{4,12},{5,37},{6,14},{7,39},{8,16},{9,4... | collective-permute-start | bytes 786440 | tf_op jit(solution)/shard_map/ppermute | solution.py:66
  63.4 5.3 %collective-permute-start.20 = (bf16[1024,128]{1,0:T(8,128)(2,1)S(1)}, bf16[1024,128]{1,0:T(8,128)(2,1)S(1)}, u32[]{:S(2)}, u32[]{:S(2)}) collective-permute-start(bf16[1024,128]{1,0:T(8,128)(2,1)S(1)} %attn_grad.1.d_attn.g0), channel_id=1, source_target_pairs={{0,16},{1,65},{2,18},{3,67},{4,20},{5,69},{6,22},{7,71},{8,24},{9,... | collective-permute-start | bytes 786440 | tf_op jit(solution)/shard_map/ppermute | solution.py:66
  68.7 0.7 collective-permute-start.21
  69.4 3.0 %query_grad.1.d_query = bf16[1024,128]{1,0:T(8,128)(2,1)S(1)} custom-call(s32[4]{0:T(128)S(1)} %copy-done.6, s32[8,128]{1,0:T(8,128)S(1)} %get-tuple-element.41.bounds, f32[1024,128]{1,0:T(8,128)S(1)} %get-tuple-element.59.begins, f32[16,4096]{1,0:T(8,128)S(1)} %get-tuple-element.60.key_pos, bf16[4096,256]{1,0:T(8,128)(2,1)S(1)} %get-tuple-element.64.keys, ...), custom_call_target="tpu_custom_call" | custom-call | flops 6000000000 | bytes 3674128 | tf_op jit(solution)/shard_map/query_grad/pallas_call | solution.py:120
  72.4 2.8 %collective-permute-done.20.g2 = bf16[1024,128]{1,0:T(8,128)(2,1)S(1)} collective-permute-done((bf16[1024,128]{1,0:T(8,128)(2,1)S(1)}, bf16[1024,128]{1,0:T(8,128)(2,1)S(1)}, u32[]{:S(2)}, u32[]{:S(2)}) %collective-permute-start.20) | collective-permute-done | bytes 262176 | tf_op jit(solution)/shard_map/ppermute | solution.py:66
  75.3 4.0 %key_grad.1 = (bf16[256,512]{1,0:T(8,128)(2,1)S(1)}, bf16[256,512]{1,0:T(8,128)(2,1)S(1)}, bf16[256,512]{1,0:T(8,128)(2,1)S(1)}, bf16[256,512]{1,0:T(8,128)(2,1)S(1)}) custom-call(s32[4]{0:T(128)S(1)} %copy-done.6, s32[8,128]{1,0:T(8,128)S(1)} %get-tuple-element.41.bounds, f32[8,4096]{1,0:T(8,128)S(1)} %get-tuple-element.42.starts, ...), custom_call_target="tpu_custom_call" | custom-call | flops 7000000000 | bytes 4853776 | tf_op jit(solution)/shard_map/key_grad/pallas_call | solution.py:120
  79.3 1.9 %collective-permute-start.22 = (bf16[256,512]{1,0:T(8,128)(2,1)S(1)}, bf16[256,512]{1,0:T(8,128)(2,1)S(1)}, u32[]{:S(2)}, u32[]{:S(2)}) collective-permute-start(bf16[256,512]{1,0:T(8,128)(2,1)S(1)} %get-tuple-element.66), channel_id=1, source_target_pairs={{32,0},{9,1},{34,2},{11,3},{36,4},{13,5},{38,6},{15,7},{40,8},{17,... | collective-permute-start | bytes 786440 | tf_op jit(solution)/shard_map/ppermute | solution.py:66
  81.3 0.7 collective-permute-start.24
  81.9 5.5 %collective-permute-done.22.p1 = bf16[256,512]{1,0:T(8,128)(2,1)S(1)} collective-permute-done((bf16[256,512]{1,0:T(8,128)(2,1)S(1)}, bf16[256,512]{1,0:T(8,128)(2,1)S(1)}, u32[]{:S(2)}, u32[]{:S(2)}) %collective-permute-start.22) | collective-permute-done | bytes 262176 | tf_op jit(solution)/shard_map/ppermute | solution.py:66
  87.4 0.7 collective-permute-done.23.p2
  88.1 2.4 %collective-permute-done.24.p3 = bf16[256,512]{1,0:T(8,128)(2,1)S(1)} collective-permute-done((bf16[256,512]{1,0:T(8,128)(2,1)S(1)}, bf16[256,512]{1,0:T(8,128)(2,1)S(1)}, u32[]{:S(2)}, u32[]{:S(2)}) %collective-permute-start.24) | collective-permute-done | bytes 262176 | tf_op jit(solution)/shard_map/ppermute | solution.py:66
  90.5 2.6 %input_grad.1 = (bf16[64,512]{1,0:T(8,128)(2,1)S(1)}, bf16[64,512]{1,0:T(8,128)(2,1)S(1)}, bf16[64,512]{1,0:T(8,128)(2,1)S(1)}, bf16[64,512]{1,0:T(8,128)(2,1)S(...) custom-call(s32[4]{0:T(128)S(1)} %copy-done.6, ...), custom_call_target="tpu_custom_call" | custom-call | flops 536870912 | bytes 7078160 | tf_op jit(solution)/shard_map/input_grad/pallas_call | solution.py:120
  93.1 13.5 %collective-permute-start.25 = (bf16[64,512]{1,0:T(8,128)(2,1)S(1)}, bf16[64,512]{1,0:T(8,128)(2,1)S(1)}, u32[]{:S(2)}, u32[]{:S(2)}) collective-permute-start(bf16[64,512]{1,0:T(8,128)(2,1)S(1)} %get-tuple-element.73), channel_id=1, source_target_pairs={{1,0},{2,1},{3,2},{4,3},{5,4},{6,5},{7,6},{0,7},{9,8},{10,9},{11,1... | collective-permute-start | bytes 196616 | tf_op jit(solution)/shard_map/ppermute | solution.py:66
  106.6 2.7 %collective-permute-start.26 = (bf16[64,512]{1,0:T(8,128)(2,1)S(1)}, bf16[64,512]{1,0:T(8,128)(2,1)S(1)}, u32[]{:S(2)}, u32[]{:S(2)}) collective-permute-start(bf16[64,512]{1,0:T(8,128)(2,1)S(1)} %get-tuple-element.74), channel_id=1, source_target_pairs={{2,0},{3,1},{4,2},{5,3},{6,4},{7,5},{0,6},{1,7},{10,8},{11,9},{12,... | collective-permute-start | bytes 196616 | tf_op jit(solution)/shard_map/ppermute | solution.py:66
  109.4 0.0 collective-permute-start.27
  109.4 0.7 collective-permute-start.28
  110.1 3.0 %collective-permute-start.29 = (bf16[64,512]{1,0:T(8,128)(2,1)S(1)}, bf16[64,512]{1,0:T(8,128)(2,1)S(1)}, u32[]{:S(2)}, u32[]{:S(2)}) collective-permute-start(bf16[64,512]{1,0:T(8,128)(2,1)S(1)} %get-tuple-element.77), channel_id=1, source_target_pairs={{5,0},{6,1},{7,2},{0,3},{1,4},{2,5},{3,6},{4,7},{13,8},{14,9},{15,... | collective-permute-start | bytes 196616 | tf_op jit(solution)/shard_map/ppermute | solution.py:66
  113.2 0.3 collective-permute-start.30
  113.5 1.4 %collective-permute-start.31 = (bf16[64,512]{1,0:T(8,128)(2,1)S(1)}, bf16[64,512]{1,0:T(8,128)(2,1)S(1)}, u32[]{:S(2)}, u32[]{:S(2)}) collective-permute-start(bf16[64,512]{1,0:T(8,128)(2,1)S(1)} %get-tuple-element.79), channel_id=1, source_target_pairs={{7,0},{0,1},{1,2},{2,3},{3,4},{4,5},{5,6},{6,7},{15,8},{8,9},{9,10... | collective-permute-start | bytes 196616 | tf_op jit(solution)/shard_map/ppermute | solution.py:66
  114.9 1.0 output.1
  115.9 0.2 collective-permute-done.29.rest_5_
  116.2 2.9 %collective-permute-done.30.rest_6_ = bf16[64,512]{1,0:T(8,128)(2,1)S(1)} collective-permute-done((bf16[64,512]{1,0:T(8,128)(2,1)S(1)}, bf16[64,512]{1,0:T(8,128)(2,1)S(1)}, u32[]{:S(2)}, u32[]{:S(2)}) %collective-permute-start.30) | collective-permute-done | bytes 65568 | tf_op jit(solution)/shard_map/ppermute | solution.py:66
  119.1 3.2 %table_grad.1 = bf16[1,1,4096,512]{3,2,1,0:T(8,128)(2,1)} custom-call(s32[4]{0:T(128)S(1)} %copy-done.6, s32[4,8]{1,0:T(4,128)S(1)} %bitcast.21, s32[1,256]{1,0:T(1,128)S(1)} %bitcast.26, bf16[64,512]{1,0:T(8,128)(2,1)S(1)} %get-tuple-element.72.rest_0_, bf16[64,512]{1,0:T(8,128)(2,1)S(1)} %collective-permute-done.25.rest_1_, ...), custom_call_target="tpu_custom_call" | custom-call | flops 1073741824 | bytes 4719760 | tf_op jit(solution)/shard_map/table_grad/pallas_call | solution.py:120
  (32 shorter events, 0.1 us)
Async XLA Ops:
  1.2 15.4 %copy-start.1 = (bf16[512,512]{1,0:T(8,128)(2,1)S(1)}, bf16[512,512]{1,0:T(8,128)(2,1)}, u32[]{:S(2)}) copy-start(bf16[512,512]{1,0:T(8,128)(2,1)} %w_out.3) | copy-start | bytes 1572868
  1.2 15.4 %copy-start.2 = (bf16[1,256,512]{2,1,0:T(8,128)(2,1)S(1)}, bf16[1,256,512]{2,1,0:T(8,128)(2,1)}, u32[]{:S(2)}) copy-start(bf16[1,256,512]{2,1,0:T(8,128)(2,1)} %param.17) | copy-start | bytes 786436
  1.2 15.4 %copy-start.5 = (s32[1,64,64]{2,1,0:T(8,128)S(1)}, s32[1,64,64]{2,1,0:T(8,128)}, u32[]{:S(2)}) copy-start(s32[1,64,64]{2,1,0:T(8,128)} %param.14) | copy-start | bytes 49156
  1.2 15.4 %copy-start.6 = (s32[4]{0:T(128)S(1)}, s32[4]{0:T(128)}, u32[]{:S(2)}) copy-start(s32[4]{0:T(128)} %pad_add_fusion.meta) | copy-start | bytes 52
  1.3 15.4 %copy-start.9 = (s32[1,16]{1,0:T(1,128)S(1)}, s32[1,16]{1,0:T(1,128)}, u32[]{:S(2)}) copy-start(s32[1,16]{1,0:T(1,128)} %param.13) | copy-start | bytes 196
  1.3 18.5 %copy-start = (bf16[512,2048]{1,0:T(8,128)(2,1)S(1)}, bf16[512,2048]{1,0:T(8,128)(2,1)}, u32[]{:S(2)}) copy-start(bf16[512,2048]{1,0:T(8,128)(2,1)} %w_in.1) | copy-start | bytes 6291460
  1.3 18.5 %copy-start.4 = (s32[1,8,4]{1,2,0:T(4,128)S(1)}, s32[1,8,4]{1,2,0:T(4,128)}, u32[]{:S(2)}) copy-start(s32[1,8,4]{1,2,0:T(4,128)} %param.11) | copy-start | bytes 388
  1.3 18.5 %copy-start.7 = (s32[1,8,4]{1,2,0:T(4,128)S(1)}, s32[1,8,4]{1,2,0:T(4,128)}, u32[]{:S(2)}) copy-start(s32[1,8,4]{1,2,0:T(4,128)} %param.12) | copy-start | bytes 388
  6.2 8.0 %collective-permute-start = (bf16[64,512]{1,0:T(8,128)(2,1)}, bf16[64,512]{1,0:T(8,128)(2,1)S(1)}, u32[]{:S(2)}, u32[]{:S(2)}) collective-permute-start(bf16[64,512]{1,0:T(8,128)(2,1)} %get-tuple-element.45), channel_id=1, source_target_pairs={{0,1},{1,2},{2,3},{3,4},{4,5},{5,6},{6,7},{7,0},{8,9},{9,10},{10,1... | collective-permute-start | bytes 196616 | tf_op jit(solution)/shard_map/ppermute | solution.py:66
  8.9 6.1 %collective-permute-start.1 = (bf16[64,512]{1,0:T(8,128)(2,1)}, bf16[64,512]{1,0:T(8,128)(2,1)S(1)}, u32[]{:S(2)}, u32[]{:S(2)}) collective-permute-start(bf16[64,512]{1,0:T(8,128)(2,1)} %get-tuple-element.46), channel_id=1, source_target_pairs={{0,2},{1,3},{2,4},{3,5},{4,6},{5,7},{6,0},{7,1},{8,10},{9,11},{10,... | collective-permute-start | bytes 196616 | tf_op jit(solution)/shard_map/ppermute | solution.py:66
  10.2 8.1 %collective-permute-start.2 = (bf16[64,512]{1,0:T(8,128)(2,1)}, bf16[64,512]{1,0:T(8,128)(2,1)S(1)}, u32[]{:S(2)}, u32[]{:S(2)}) collective-permute-start(bf16[64,512]{1,0:T(8,128)(2,1)} %get-tuple-element.47), channel_id=1, source_target_pairs={{0,3},{1,4},{2,5},{3,6},{4,7},{5,0},{6,1},{7,2},{8,11},{9,12},{10,... | collective-permute-start | bytes 196616 | tf_op jit(solution)/shard_map/ppermute | solution.py:66
  11.9 6.4 %collective-permute-start.3 = (bf16[64,512]{1,0:T(8,128)(2,1)}, bf16[64,512]{1,0:T(8,128)(2,1)S(1)}, u32[]{:S(2)}, u32[]{:S(2)}) collective-permute-start(bf16[64,512]{1,0:T(8,128)(2,1)} %get-tuple-element.48), channel_id=1, source_target_pairs={{0,4},{1,5},{2,6},{3,7},{4,0},{5,1},{6,2},{7,3},{8,12},{9,13},{10,... | collective-permute-start | bytes 196616 | tf_op jit(solution)/shard_map/ppermute | solution.py:66
  12.3 6.1 %collective-permute-start.4 = (bf16[64,512]{1,0:T(8,128)(2,1)}, bf16[64,512]{1,0:T(8,128)(2,1)S(1)}, u32[]{:S(2)}, u32[]{:S(2)}) collective-permute-start(bf16[64,512]{1,0:T(8,128)(2,1)} %get-tuple-element.49), channel_id=1, source_target_pairs={{0,5},{1,6},{2,7},{3,0},{4,1},{5,2},{6,3},{7,4},{8,13},{9,14},{10,... | collective-permute-start | bytes 196616 | tf_op jit(solution)/shard_map/ppermute | solution.py:66
  14.2 4.2 %collective-permute-start.5 = (bf16[64,512]{1,0:T(8,128)(2,1)}, bf16[64,512]{1,0:T(8,128)(2,1)S(1)}, u32[]{:S(2)}, u32[]{:S(2)}) collective-permute-start(bf16[64,512]{1,0:T(8,128)(2,1)} %get-tuple-element.50), channel_id=1, source_target_pairs={{0,6},{1,7},{2,0},{3,1},{4,2},{5,3},{6,4},{7,5},{8,14},{9,15},{10,... | collective-permute-start | bytes 196616 | tf_op jit(solution)/shard_map/ppermute | solution.py:66
  15.0 4.7 %collective-permute-start.6 = (bf16[64,512]{1,0:T(8,128)(2,1)}, bf16[64,512]{1,0:T(8,128)(2,1)S(1)}, u32[]{:S(2)}, u32[]{:S(2)}) collective-permute-start(bf16[64,512]{1,0:T(8,128)(2,1)} %get-tuple-element.51), channel_id=1, source_target_pairs={{0,7},{1,0},{2,1},{3,2},{4,3},{5,4},{6,5},{7,6},{8,15},{9,8},{10,9... | collective-permute-start | bytes 196616 | tf_op jit(solution)/shard_map/ppermute | solution.py:66
  19.8 0.8 copy-start.3
  23.1 7.6 %collective-permute-start.7 = (bf16[256,512]{1,0:T(8,128)(2,1)S(1)}, bf16[256,512]{1,0:T(8,128)(2,1)S(1)}, u32[]{:S(2)}, u32[]{:S(2)}) collective-permute-start(bf16[256,512]{1,0:T(8,128)(2,1)S(1)} %get-tuple-element.54), channel_id=1, source_target_pairs={{0,32},{1,9},{2,34},{3,11},{4,36},{5,13},{6,38},{7,15},{8,40},{9,1... | collective-permute-start | bytes 786440 | tf_op jit(solution)/shard_map/ppermute | solution.py:66
  24.8 9.9 %collective-permute-start.8 = (bf16[256,512]{1,0:T(8,128)(2,1)S(1)}, bf16[256,512]{1,0:T(8,128)(2,1)S(1)}, u32[]{:S(2)}, u32[]{:S(2)}) collective-permute-start(bf16[256,512]{1,0:T(8,128)(2,1)S(1)} %get-tuple-element.55), channel_id=1, source_target_pairs={{0,64},{1,17},{2,66},{3,19},{4,68},{5,21},{6,70},{7,23},{8,72},{9,... | collective-permute-start | bytes 786440 | tf_op jit(solution)/shard_map/ppermute | solution.py:66
  28.1 6.6 %collective-permute-start.9 = (bf16[256,512]{1,0:T(8,128)(2,1)S(1)}, bf16[256,512]{1,0:T(8,128)(2,1)S(1)}, u32[]{:S(2)}, u32[]{:S(2)}) collective-permute-start(bf16[256,512]{1,0:T(8,128)(2,1)S(1)} %get-tuple-element.56), channel_id=1, source_target_pairs={{0,96},{1,25},{2,98},{3,27},{4,100},{5,29},{6,102},{7,31},{8,104},... | collective-permute-start | bytes 786440 | tf_op jit(solution)/shard_map/ppermute | solution.py:66
  35.3 9.6 %collective-permute-start.13 = (bf16[1024,256]{1,0:T(8,128)(2,1)S(1)}, bf16[1024,256]{1,0:T(8,128)(2,1)S(1)}, u32[]{:S(2)}, u32[]{:S(2)}) collective-permute-start(bf16[1024,256]{1,0:T(8,128)(2,1)S(1)} %get-tuple-element.57.k0.keys), channel_id=1, source_target_pairs={{0,8},{1,33},{2,10},{3,35},{4,12},{5,37},{6,14},{7,39},{8,16},{9,4... | collective-permute-start | bytes 1572872 | tf_op jit(solution)/shard_map/ppermute | solution.py:66
  36.6 15.0 %collective-permute-start.14 = (bf16[1024,256]{1,0:T(8,128)(2,1)S(1)}, bf16[1024,256]{1,0:T(8,128)(2,1)S(1)}, u32[]{:S(2)}, u32[]{:S(2)}) collective-permute-start(bf16[1024,256]{1,0:T(8,128)(2,1)S(1)} %get-tuple-element.57.k0.keys), channel_id=1, source_target_pairs={{0,16},{1,65},{2,18},{3,67},{4,20},{5,69},{6,22},{7,71},{8,24},{9,... | collective-permute-start | bytes 1572872 | tf_op jit(solution)/shard_map/ppermute | solution.py:66
  39.0 12.5 %collective-permute-start.15 = (bf16[1024,256]{1,0:T(8,128)(2,1)S(1)}, bf16[1024,256]{1,0:T(8,128)(2,1)S(1)}, u32[]{:S(2)}, u32[]{:S(2)}) collective-permute-start(bf16[1024,256]{1,0:T(8,128)(2,1)S(1)} %get-tuple-element.57.k0.keys), channel_id=1, source_target_pairs={{0,24},{1,97},{2,26},{3,99},{4,28},{5,101},{6,30},{7,103},{8,0},{9... | collective-permute-start | bytes 1572872 | tf_op jit(solution)/shard_map/ppermute | solution.py:66
  40.2 18.5 %collective-permute-start.10 = (bf16[1024,128]{1,0:T(8,128)(2,1)S(1)}, bf16[1024,128]{1,0:T(8,128)(2,1)S(1)}, u32[]{:S(2)}, u32[]{:S(2)}) collective-permute-start(bf16[1024,128]{1,0:T(8,128)(2,1)S(1)} %get-tuple-element.58.queries.q0), channel_id=1, source_target_pairs={{0,8},{1,33},{2,10},{3,35},{4,12},{5,37},{6,14},{7,39},{8,16},{9,4... | collective-permute-start | bytes 786440 | tf_op jit(solution)/shard_map/ppermute | solution.py:66
  40.5 19.2 %collective-permute-start.11 = (bf16[1024,128]{1,0:T(8,128)(2,1)S(1)}, bf16[1024,128]{1,0:T(8,128)(2,1)S(1)}, u32[]{:S(2)}, u32[]{:S(2)}) collective-permute-start(bf16[1024,128]{1,0:T(8,128)(2,1)S(1)} %get-tuple-element.58.queries.q0), channel_id=1, source_target_pairs={{0,16},{1,65},{2,18},{3,67},{4,20},{5,69},{6,22},{7,71},{8,24},{9,... | collective-permute-start | bytes 786440 | tf_op jit(solution)/shard_map/ppermute | solution.py:66
  44.9 14.8 %collective-permute-start.12 = (bf16[1024,128]{1,0:T(8,128)(2,1)S(1)}, bf16[1024,128]{1,0:T(8,128)(2,1)S(1)}, u32[]{:S(2)}, u32[]{:S(2)}) collective-permute-start(bf16[1024,128]{1,0:T(8,128)(2,1)S(1)} %get-tuple-element.58.queries.q0), channel_id=1, source_target_pairs={{0,24},{1,97},{2,26},{3,99},{4,28},{5,101},{6,30},{7,103},{8,0},{9... | collective-permute-start | bytes 786440 | tf_op jit(solution)/shard_map/ppermute | solution.py:66
  55.6 4.1 %collective-permute-start.16 = (f32[8,1024]{1,0:T(8,128)S(1)}, f32[8,1024]{1,0:T(8,128)S(1)}, u32[]{:S(2)}, u32[]{:S(2)}) collective-permute-start(f32[8,1024]{1,0:T(8,128)S(1)} %get-tuple-element.62.s0), channel_id=1, source_target_pairs={{0,32},{1,9},{2,34},{3,11},{4,36},{5,13},{6,38},{7,15},{8,40},{9,1... | collective-permute-start | bytes 98312 | tf_op jit(solution)/shard_map/ppermute | solution.py:66
  56.3 4.3 %collective-permute-start.17 = (f32[8,1024]{1,0:T(8,128)S(1)}, f32[8,1024]{1,0:T(8,128)S(1)}, u32[]{:S(2)}, u32[]{:S(2)}) collective-permute-start(f32[8,1024]{1,0:T(8,128)S(1)} %get-tuple-element.62.s0), channel_id=1, source_target_pairs={{0,64},{1,17},{2,66},{3,19},{4,68},{5,21},{6,70},{7,23},{8,72},{9,... | collective-permute-start | bytes 98312 | tf_op jit(solution)/shard_map/ppermute | solution.py:66
  58.7 2.8 %collective-permute-start.18 = (f32[8,1024]{1,0:T(8,128)S(1)}, f32[8,1024]{1,0:T(8,128)S(1)}, u32[]{:S(2)}, u32[]{:S(2)}) collective-permute-start(f32[8,1024]{1,0:T(8,128)S(1)} %get-tuple-element.62.s0), channel_id=1, source_target_pairs={{0,96},{1,25},{2,98},{3,27},{4,100},{5,29},{6,102},{7,31},{8,104},... | collective-permute-start | bytes 98312 | tf_op jit(solution)/shard_map/ppermute | solution.py:66
  62.1 10.3 %collective-permute-start.19 = (bf16[1024,128]{1,0:T(8,128)(2,1)S(1)}, bf16[1024,128]{1,0:T(8,128)(2,1)S(1)}, u32[]{:S(2)}, u32[]{:S(2)}) collective-permute-start(bf16[1024,128]{1,0:T(8,128)(2,1)S(1)} %attn_grad.1.d_attn.g0), channel_id=1, source_target_pairs={{0,8},{1,33},{2,10},{3,35},{4,12},{5,37},{6,14},{7,39},{8,16},{9,4... | collective-permute-start | bytes 786440 | tf_op jit(solution)/shard_map/ppermute | solution.py:66
  63.4 11.8 %collective-permute-start.20 = (bf16[1024,128]{1,0:T(8,128)(2,1)S(1)}, bf16[1024,128]{1,0:T(8,128)(2,1)S(1)}, u32[]{:S(2)}, u32[]{:S(2)}) collective-permute-start(bf16[1024,128]{1,0:T(8,128)(2,1)S(1)} %attn_grad.1.d_attn.g0), channel_id=1, source_target_pairs={{0,16},{1,65},{2,18},{3,67},{4,20},{5,69},{6,22},{7,71},{8,24},{9,... | collective-permute-start | bytes 786440 | tf_op jit(solution)/shard_map/ppermute | solution.py:66
  68.7 6.6 %collective-permute-start.21 = (bf16[1024,128]{1,0:T(8,128)(2,1)S(1)}, bf16[1024,128]{1,0:T(8,128)(2,1)S(1)}, u32[]{:S(2)}, u32[]{:S(2)}) collective-permute-start(bf16[1024,128]{1,0:T(8,128)(2,1)S(1)} %attn_grad.1.d_attn.g0), channel_id=1, source_target_pairs={{0,24},{1,97},{2,26},{3,99},{4,28},{5,101},{6,30},{7,103},{8,0},{9... | collective-permute-start | bytes 786440 | tf_op jit(solution)/shard_map/ppermute | solution.py:66
  79.3 8.1 %collective-permute-start.22 = (bf16[256,512]{1,0:T(8,128)(2,1)S(1)}, bf16[256,512]{1,0:T(8,128)(2,1)S(1)}, u32[]{:S(2)}, u32[]{:S(2)}) collective-permute-start(bf16[256,512]{1,0:T(8,128)(2,1)S(1)} %get-tuple-element.66), channel_id=1, source_target_pairs={{32,0},{9,1},{34,2},{11,3},{36,4},{13,5},{38,6},{15,7},{40,8},{17,... | collective-permute-start | bytes 786440 | tf_op jit(solution)/shard_map/ppermute | solution.py:66
  81.3 6.8 %collective-permute-start.23 = (bf16[256,512]{1,0:T(8,128)(2,1)S(1)}, bf16[256,512]{1,0:T(8,128)(2,1)S(1)}, u32[]{:S(2)}, u32[]{:S(2)}) collective-permute-start(bf16[256,512]{1,0:T(8,128)(2,1)S(1)} %get-tuple-element.67), channel_id=1, source_target_pairs={{64,0},{17,1},{66,2},{19,3},{68,4},{21,5},{70,6},{23,7},{72,8},{25... | collective-permute-start | bytes 786440 | tf_op jit(solution)/shard_map/ppermute | solution.py:66
  81.3 9.2 %collective-permute-start.24 = (bf16[256,512]{1,0:T(8,128)(2,1)S(1)}, bf16[256,512]{1,0:T(8,128)(2,1)S(1)}, u32[]{:S(2)}, u32[]{:S(2)}) collective-permute-start(bf16[256,512]{1,0:T(8,128)(2,1)S(1)} %get-tuple-element.68), channel_id=1, source_target_pairs={{96,0},{25,1},{98,2},{27,3},{100,4},{29,5},{102,6},{31,7},{104,8},... | collective-permute-start | bytes 786440 | tf_op jit(solution)/shard_map/ppermute | solution.py:66
  90.5 28.6 %copy-start.8 = (s32[1,1,256]{2,1,0:T(1,128)S(1)}, s32[1,1,256]{2,1,0:T(1,128)}, u32[]{:S(2)}) copy-start(s32[1,1,256]{2,1,0:T(1,128)} %param.10) | copy-start | bytes 3076
  93.1 20.1 %collective-permute-start.25 = (bf16[64,512]{1,0:T(8,128)(2,1)S(1)}, bf16[64,512]{1,0:T(8,128)(2,1)S(1)}, u32[]{:S(2)}, u32[]{:S(2)}) collective-permute-start(bf16[64,512]{1,0:T(8,128)(2,1)S(1)} %get-tuple-element.73), channel_id=1, source_target_pairs={{1,0},{2,1},{3,2},{4,3},{5,4},{6,5},{7,6},{0,7},{9,8},{10,9},{11,1... | collective-permute-start | bytes 196616 | tf_op jit(solution)/shard_map/ppermute | solution.py:66
  106.6 6.8 %collective-permute-start.26 = (bf16[64,512]{1,0:T(8,128)(2,1)S(1)}, bf16[64,512]{1,0:T(8,128)(2,1)S(1)}, u32[]{:S(2)}, u32[]{:S(2)}) collective-permute-start(bf16[64,512]{1,0:T(8,128)(2,1)S(1)} %get-tuple-element.74), channel_id=1, source_target_pairs={{2,0},{3,1},{4,2},{5,3},{6,4},{7,5},{0,6},{1,7},{10,8},{11,9},{12,... | collective-permute-start | bytes 196616 | tf_op jit(solution)/shard_map/ppermute | solution.py:66
  109.4 6.5 %collective-permute-start.27 = (bf16[64,512]{1,0:T(8,128)(2,1)S(1)}, bf16[64,512]{1,0:T(8,128)(2,1)S(1)}, u32[]{:S(2)}, u32[]{:S(2)}) collective-permute-start(bf16[64,512]{1,0:T(8,128)(2,1)S(1)} %get-tuple-element.75), channel_id=1, source_target_pairs={{3,0},{4,1},{5,2},{6,3},{7,4},{0,5},{1,6},{2,7},{11,8},{12,9},{13,... | collective-permute-start | bytes 196616 | tf_op jit(solution)/shard_map/ppermute | solution.py:66
  109.4 6.5 %collective-permute-start.28 = (bf16[64,512]{1,0:T(8,128)(2,1)S(1)}, bf16[64,512]{1,0:T(8,128)(2,1)S(1)}, u32[]{:S(2)}, u32[]{:S(2)}) collective-permute-start(bf16[64,512]{1,0:T(8,128)(2,1)S(1)} %get-tuple-element.76), channel_id=1, source_target_pairs={{4,0},{5,1},{6,2},{7,3},{0,4},{1,5},{2,6},{3,7},{12,8},{13,9},{14,... | collective-permute-start | bytes 196616 | tf_op jit(solution)/shard_map/ppermute | solution.py:66
  110.1 6.0 %collective-permute-start.29 = (bf16[64,512]{1,0:T(8,128)(2,1)S(1)}, bf16[64,512]{1,0:T(8,128)(2,1)S(1)}, u32[]{:S(2)}, u32[]{:S(2)}) collective-permute-start(bf16[64,512]{1,0:T(8,128)(2,1)S(1)} %get-tuple-element.77), channel_id=1, source_target_pairs={{5,0},{6,1},{7,2},{0,3},{1,4},{2,5},{3,6},{4,7},{13,8},{14,9},{15,... | collective-permute-start | bytes 196616 | tf_op jit(solution)/shard_map/ppermute | solution.py:66
  113.2 5.9 %collective-permute-start.30 = (bf16[64,512]{1,0:T(8,128)(2,1)S(1)}, bf16[64,512]{1,0:T(8,128)(2,1)S(1)}, u32[]{:S(2)}, u32[]{:S(2)}) collective-permute-start(bf16[64,512]{1,0:T(8,128)(2,1)S(1)} %get-tuple-element.78), channel_id=1, source_target_pairs={{6,0},{7,1},{0,2},{1,3},{2,4},{3,5},{4,6},{5,7},{14,8},{15,9},{8,1... | collective-permute-start | bytes 196616 | tf_op jit(solution)/shard_map/ppermute | solution.py:66
  113.5 5.6 %collective-permute-start.31 = (bf16[64,512]{1,0:T(8,128)(2,1)S(1)}, bf16[64,512]{1,0:T(8,128)(2,1)S(1)}, u32[]{:S(2)}, u32[]{:S(2)}) collective-permute-start(bf16[64,512]{1,0:T(8,128)(2,1)S(1)} %get-tuple-element.79), channel_id=1, source_target_pairs={{7,0},{0,1},{1,2},{2,3},{3,4},{4,5},{5,6},{6,7},{15,8},{8,9},{9,10... | collective-permute-start | bytes 196616 | tf_op jit(solution)/shard_map/ppermute | solution.py:66

commit v4 on v3

--- a/solution.py
+++ b/solution.py
@@ -23,6 +23,8 @@
 KEY_TILE = 256
 GROUP = 4
 KEY_GROUP = 3
+SINGLES = 8
+ITEMS = 128
 SCALE = HD ** (-0.5)
 
 
@@ -114,11 +116,11 @@
     return jax.ShapeDtypeStruct(dims, dtype)
 
 
-def call(kernel, ins, specs, outs, scratch=(), flops=0, name=None, out_specs=None, limit=40):
+def call(kernel, ins, specs, outs, scratch=(), flops=0, name=None, out_specs=None, limit=40, placed=True):
     moved = sum(a.size * a.dtype.itemsize for a in ins)
     moved += sum(o.size * jnp.dtype(o.dtype).itemsize for o in outs)
     return pl.pallas_call(
-        kernel,
+        with_place(kernel) if placed else kernel,
         out_shape=outs,
         in_specs=specs,
         out_specs=out_specs or [VMEM] * len(outs),
@@ -127,6 +129,13 @@
         cost_estimate=pl.CostEstimate(flops=flops, bytes_accessed=moved, transcendentals=0),
         name=name,
     )(*ins)
+
+
+def with_place(kernel):
+    def placed(*refs):
+        kernel([lax.axis_index(a) for a in AXES], *refs)
+
+    return placed
 
 
 def lookup_kernel(meta, dest, ids_ref, table, *rest):
@@ -162,21 +171,32 @@
                 outs[k][...] = total[p * BROWS : (p + 1) * BROWS, :].astype(BF)
 
 
-def prepare_kernel(meta, lengths, tile_mask, incoming, w_out, bounds, starts, begins, key_pos, query_pos, dmixed, turned):
+def prepare_kernel(meta, lengths, tile_mask, incoming, w_out, key_work, query_work, starts, begins, key_pos, query_pos, dmixed, turned, bounds):
     row, core = line(meta)[1], meta[3]
-    lane = lax.broadcasted_iota(jnp.int32, (8, CHUNK), 1)
-    first, last = lane * CHUNK, lane * CHUNK + CHUNK - 1
     ends, end = [], jnp.int32(0)
     for d in range(lengths.shape[0]):
         end = end + lengths[d]
         ends.append(end)
-    chunk_start = jnp.zeros((8, CHUNK), jnp.int32)
-    chunk_stop = jnp.full((8, CHUNK), LENGTH, jnp.int32)
-    for end in ends:
-        chunk_start = jnp.where(first >= end, end, chunk_start)
-        chunk_stop = jnp.where(last < end, jnp.minimum(chunk_stop, end), chunk_stop)
-    row_id = lax.broadcasted_iota(jnp.int32, (8, CHUNK), 0)
-    bounds[...] = jnp.where(row_id == 0, chunk_start, chunk_stop - 1)
+    for t in range(8):
+        i = chunk_of(t, row, core)
+        begin, stop = jnp.int32(0), jnp.int32(LENGTH)
+        for end in ends:
+            begin = jnp.where(i * CHUNK >= end, end, begin)
+        for end in reversed(ends):
+            stop = jnp.where(i * CHUNK + CHUNK - 1 < end, end, stop)
+        bounds[t] = begin
+        bounds[8 + t] = stop - 1
+
+    def key_span(t):
+        i = chunk_of(t, row, core)
+        return bounds[t] // KEY_TILE, (i * CHUNK + CHUNK - 1) // KEY_TILE
+
+    def query_span(t):
+        i = chunk_of(t, row, core)
+        return (i * CHUNK) // KEY_TILE, bounds[8 + t] // KEY_TILE
+
+    list_work(key_work, key_span, core)
+    list_work(query_work, query_span, core)
     turned[...] = jnp.transpose(tile_mask[...].astype(F32))
     on_keys, on_queries = [], []
     for t in range(8):
@@ -276,85 +296,98 @@
             out[ds(chunk * CHUNK, CHUNK), :] = parts[k][t * CHUNK : (t + 1) * CHUNK, :]
 
 
-def list_work(pairs, tiles, span, size):
+def list_work(work, span, core):
+    def put(unit):
+        def one(n, count):
+            work[count] = unit
+            work[ITEMS + count] = n
+            return count + 1
+
+        return one
+
     def one_pair(p, count):
-        def one(n, count):
-            pairs[count] = p
-            tiles[count] = n
-            return count + 1
-
         low, high = span(2 * p)
         low_next, high_next = span(2 * p + 1)
-        count = lax.fori_loop(low, high + 1, one, count)
-        return lax.fori_loop(jnp.maximum(low_next, high + 1), high_next + 1, one, count)
+
+        def together(count):
+            count = lax.fori_loop(low, high + 1, put(p), count)
+            return lax.fori_loop(jnp.maximum(low_next, high + 1), high_next + 1, put(p), count)
+
+        def alone(count):
+            count = lax.fori_loop(low, high + 1, put(2 * p), count)
+            return lax.fori_loop(low_next, high_next + 1, put(2 * p + 1), count)
+
+        return lax.cond(core == 0, alone, together, count)
 
     count = lax.fori_loop(0, 4, one_pair, jnp.int32(0))
-    for u in range(size - 1):
-        pairs[count + u] = 4
-        tiles[count + u] = 0
-    return (count + size - 1) // size
-
-
-def work_scratch():
-    return [pltpu.SMEM((160,), jnp.int32), pltpu.SMEM((160,), jnp.int32)]
-
-
-def pair_positions(meta, p, width):
+    for u in range(SINGLES):
+        work[count + u] = jnp.where(core == 0, 8, 4)
+        work[ITEMS + count + u] = 0
+    work[2 * ITEMS] = count
+
+
+def run_items(work, core, item, size):
+    def run(group_size, rows, last):
+        def group(b, carry):
+            done = []
+            for u in range(group_size):
+                slot, n = work[b * group_size + u], work[ITEMS + b * group_size + u]
+                done.append((slot, item(jnp.minimum(slot, last), n, rows)))
+            for slot, parts in done:
+                for ref, cols, part in parts:
+                    ref[ds(slot * rows, rows), cols] += part
+            return carry
+
+        lax.fori_loop(0, (work[2 * ITEMS] + group_size - 1) // group_size, group, 0)
+
+    @pl.when(core == 0)
+    def _():
+        run(SINGLES, CHUNK, 7)
+
+    @pl.when(core != 0)
+    def _():
+        run(size, ROWS, 3)
+
+
+def unit_positions(meta, unit, rows, width):
     row, core = line(meta)[1], meta[3]
     local = lax.broadcasted_iota(jnp.int32, (CHUNK, width), 0).astype(F32)
+    count = rows // CHUNK
     return jnp.concatenate(
-        [local + (chunk_of(2 * p + m, row, core) * CHUNK).astype(F32) for m in range(2)], axis=0
-    )
-
-
-def spread_rows(table, p, cols):
+        [local + (chunk_of(count * unit + m, row, core) * CHUNK).astype(F32) for m in range(count)], axis=0
+    )
+
+
+def spread_rows(table, unit, rows, cols):
+    count = rows // BROWS
     return jnp.concatenate(
-        [jnp.broadcast_to(table[pl.ds(4 * p + m, 1), cols], (BROWS, KEY_TILE)) for m in range(4)], axis=0
-    )
-
-
-def allowed_keys(meta, begins, key_pos, p, n):
+        [jnp.broadcast_to(table[pl.ds(count * unit + m, 1), cols], (BROWS, KEY_TILE)) for m in range(count)],
+        axis=0,
+    )
+
+
+def allowed_keys(meta, begins, key_pos, unit, n, rows):
     repeat = KEY_TILE // CHUNK
-    pos = jnp.concatenate([pair_positions(meta, p, CHUNK)] * repeat, axis=1)
-    start = jnp.concatenate([begins[ds(p * ROWS, ROWS), :]] * repeat, axis=1)
-    key = spread_rows(key_pos, p, ds(n * KEY_TILE, KEY_TILE))
+    pos = jnp.concatenate([unit_positions(meta, unit, rows, CHUNK)] * repeat, axis=1)
+    start = jnp.concatenate([begins[ds(unit * rows, rows), :]] * repeat, axis=1)
+    key = spread_rows(key_pos, unit, rows, ds(n * KEY_TILE, KEY_TILE))
     return (key >= start) & (key <= pos)
 
 
-def key_span(meta, bounds):
-    row, core = line(meta)[1], meta[3]
-
-    def span(t):
-        i = chunk_of(t, row, core)
-        return bounds[0, i] // KEY_TILE, (i * CHUNK + CHUNK - 1) // KEY_TILE
-
-    return span
-
-
 def forward_kernel(
-    meta, bounds, begins, key_pos, k0, k1, k2, k3, queries, grads,
-    keys, attn, passed, stats, total, pairs, tiles,
+    meta, work, begins, key_pos, k0, k1, k2, k3, queries, grads, keys, attn, stats, total
 ):
-    passed[...] = queries[...]
     place_rows(meta, (k0, k1, k2, k3), keys)
     total[...] = jnp.zeros_like(total)
-    groups = list_work(pairs, tiles, key_span(meta, bounds), GROUP)
-
-    def group(b, carry):
-        parts = []
-        for u in range(GROUP):
-            slot, n = pairs[b * GROUP + u], tiles[b * GROUP + u]
-            p = jnp.minimum(slot, 3)
-            rows = ds(n * KEY_TILE, KEY_TILE)
-            h = dot_nt(queries[ds(p * ROWS, ROWS), :], keys[rows, 0:HD]) * (0.5 * SCALE)
-            allowed = allowed_keys(meta, begins, key_pos, p, n)
-            probs = jnp.where(allowed, h + h * jnp.tanh(h), 0.0).astype(BF)
-            parts.append((slot, dot(probs, keys[rows, HD : 2 * HD])))
-        for slot, part in parts:
-            total[ds(slot * ROWS, ROWS), :] += part
-        return carry
-
-    lax.fori_loop(0, groups, group, 0)
+
+    def item(unit, n, rows):
+        near = ds(n * KEY_TILE, KEY_TILE)
+        h = dot_nt(queries[ds(unit * rows, rows), :], keys[near, 0:HD]) * (0.5 * SCALE)
+        allowed = allowed_keys(meta, begins, key_pos, unit, n, rows)
+        probs = jnp.where(allowed, h + h * jnp.tanh(h), 0.0).astype(BF)
+        return [(total, slice(None), dot(probs, keys[near, HD : 2 * HD]))]
+
+    run_items(work, meta[3], item, GROUP)
     lane = lax.broadcasted_iota(jnp.int32, (CHUNK, CHUNK), 1)
     for t in range(8):
         rows = slice(t * CHUNK, (t + 1) * CHUNK)
@@ -386,75 +419,52 @@
         out[rows, :] = (cols[1] * (grads[rows, :].astype(F32) - cols[2] - hat * cols[3])).astype(BF)
 
 
-def query_grad_kernel(
-    meta, bounds, begins, key_pos, keys, queries, d_attn, out, total, pairs, tiles
-):
+def query_grad_kernel(meta, work, begins, key_pos, keys, queries, d_attn, out, total):
     total[...] = jnp.zeros_like(total)
-    groups = list_work(pairs, tiles, key_span(meta, bounds), GROUP)
-
-    def group(b, carry):
-        parts = []
-        for u in range(GROUP):
-            slot, n = pairs[b * GROUP + u], tiles[b * GROUP + u]
-            p = jnp.minimum(slot, 3)
-            rows = ds(n * KEY_TILE, KEY_TILE)
-            rows_q = ds(p * ROWS, ROWS)
-            k = keys[rows, 0:HD]
-            h = dot_nt(queries[rows_q, :], k) * (0.5 * SCALE)
-            dp = dot_nt(d_attn[rows_q, :], keys[rows, HD : 2 * HD])
-            th = jnp.tanh(h)
-            allowed = allowed_keys(meta, begins, key_pos, p, n)
-            d_scores = jnp.where(allowed, dp * ((1.0 + th) * (1.0 + h - h * th)), 0.0)
-            parts.append((slot, dot(d_scores.astype(BF), k)))
-        for slot, part in parts:
-            total[ds(slot * ROWS, ROWS), :] += part
-        return carry
-
-    lax.fori_loop(0, groups, group, 0)
+
+    def item(unit, n, rows):
+        near = ds(n * KEY_TILE, KEY_TILE)
+        own = ds(unit * rows, rows)
+        k = keys[near, 0:HD]
+        h = dot_nt(queries[own, :], k) * (0.5 * SCALE)
+        dp = dot_nt(d_attn[own, :], keys[near, HD : 2 * HD])
+        th = jnp.tanh(h)
+        allowed = allowed_keys(meta, begins, key_pos, unit, n, rows)
+        d_scores = jnp.where(allowed, dp * ((1.0 + th) * (1.0 + h - h * th)), 0.0)
+        return [(total, slice(None), dot(d_scores.astype(BF), k))]
+
+    run_items(work, meta[3], item, GROUP)
     out[...] = (total[0 : LENGTH // 4, :] * (0.5 * SCALE)).astype(BF)
 
 
 def key_grad_kernel(
-    meta, bounds, starts, query_pos, keys, q0, q1, q2, q3, g0, g1, g2, g3, d_query, attn,
-    r0, r1, r2, r3, queries, grads, total, pairs, tiles,
+    meta, work, starts, query_pos, keys, q0, q1, q2, q3, g0, g1, g2, g3, d_query, attn,
+    r0, r1, r2, r3, queries, grads, total,
 ):
     outs = (r0, r1, r2, r3)
-    row, core = line(meta)[1], meta[3]
     place_rows(meta, (q0, q1, q2, q3), queries)
     place_rows(meta, (g0, g1, g2, g3), grads)
     total[...] = jnp.zeros_like(total)
 
-    def span(t):
-        i = chunk_of(t, row, core)
-        return (i * CHUNK) // KEY_TILE, bounds[1, i] // KEY_TILE
-
-    groups = list_work(pairs, tiles, span, KEY_GROUP)
-
-    def group(b, carry):
-        parts = []
-        for u in range(KEY_GROUP):
-            slot, n = pairs[b * KEY_GROUP + u], tiles[b * KEY_GROUP + u]
-            p = jnp.minimum(slot, 3)
-            rows_k = ds(p * ROWS, ROWS)
-            rows = ds(n * KEY_TILE, KEY_TILE)
-            q, g = queries[rows, :], grads[rows, :]
-            pos = pair_positions(meta, p, KEY_TILE)
-            begin = jnp.broadcast_to(starts[0:1, rows], (ROWS, KEY_TILE))
-            allowed = (pos <= spread_rows(query_pos, p, rows)) & (pos >= begin)
-            h = dot_nt(keys[rows_k, 0:HD], q) * (0.5 * SCALE)
-            dp = dot_nt(keys[rows_k, HD : 2 * HD], g)
-            th = jnp.tanh(h)
-            up = 1.0 + th
-            probs = jnp.where(allowed, h * up, 0.0).astype(BF)
-            d_scores = jnp.where(allowed, dp * (up * (1.0 + h - h * th)), 0.0).astype(BF)
-            parts.append((slot, dot(d_scores, q), dot(probs, g)))
-        for slot, d_key, d_value in parts:
-            rows = ds(slot * ROWS, ROWS)
-            total[rows, 0:HD] += d_key
-            total[rows, HD : 2 * HD] += d_value
-        return carry
-
-    lax.fori_loop(0, groups, group, 0)
+    def item(unit, n, rows):
+        own = ds(unit * rows, rows)
+        near = ds(n * KEY_TILE, KEY_TILE)
+        q, g = queries[near, :], grads[near, :]
+        pos = unit_positions(meta, unit, rows, KEY_TILE)
+        begin = jnp.broadcast_to(starts[0:1, near], (rows, KEY_TILE))
+        allowed = (pos <= spread_rows(query_pos, unit, rows, near)) & (pos >= begin)
+        h = dot_nt(keys[own, 0:HD], q) * (0.5 * SCALE)
+        dp = dot_nt(keys[own, HD : 2 * HD], g)
+        th = jnp.tanh(h)
+        up = 1.0 + th
+        probs = jnp.where(allowed, h * up, 0.0).astype(BF)
+        d_scores = jnp.where(allowed, dp * (up * (1.0 + h - h * th)), 0.0).astype(BF)
+        return [
+            (total, slice(0, HD), dot(d_scores, q)),
+            (total, slice(HD, 2 * HD), dot(probs, g)),
+        ]
+
+    run_items(work, meta[3], item, KEY_GROUP)
     for j, low, t in pieces_of(meta):
         rows = ds(t * CHUNK, CHUNK)
         outs[j][low : low + CHUNK, 0:HD] = (total[rows, 0:HD] * (0.5 * SCALE)).astype(BF)
@@ -520,27 +530,27 @@
 
 
 def body(table, row_ids, dests, slots, lengths, tile_mask, w_in, w_out, output_gradient):
-    x, z, y, c = (lax.axis_index(a).astype(jnp.int32) for a in AXES)
     dest = dests[0].T
     slot = slots[0].T
     tab_rows = table.shape[2]
 
-    place_info = jnp.stack([x, z, y, c])
-    bounds, starts, begins, key_pos, query_pos, dmixed = call(
+    key_work, query_work, starts, begins, key_pos, query_pos, dmixed = call(
         prepare_kernel,
-        [place_info, lengths[0], tile_mask[0], output_gradient[0], w_out],
-        [SMEM] * 2 + [VMEM] * 3,
+        [lengths[0], tile_mask[0], output_gradient[0], w_out],
+        [SMEM] + [VMEM] * 3,
         [
-            shape((8, CHUNK), jnp.int32),
+            shape((2 * ITEMS + 1,), jnp.int32),
+            shape((2 * ITEMS + 1,), jnp.int32),
             shape((8, LENGTH), F32),
             shape((LENGTH // 4, CHUNK), F32),
             shape((16, LENGTH), F32),
             shape((16, LENGTH), F32),
             shape((ROWS, WIDTH), F32),
         ],
-        [pltpu.VMEM((64, 64), F32)],
+        [pltpu.VMEM((64, 64), F32), pltpu.SMEM((16,), jnp.int32)],
         flops=2 * ROWS * WIDTH * WIDTH,
         name="prepare",
+        out_specs=[SMEM] * 2 + [VMEM] * 5,
     )
 
     tiles = 8
@@ -548,8 +558,8 @@
     block_shape = shape((BROWS, WIDTH), BF)
     outgoing = call(
         lookup_kernel,
-        [place_info, dest, row_ids.reshape(2, CHUNK), table],
-        [SMEM, SMEM, VMEM, pl.BlockSpec(memory_space=pltpu.HBM)],
+        [dest, row_ids.reshape(2, CHUNK), table],
+        [SMEM, VMEM, pl.BlockSpec(memory_space=pltpu.HBM)],
         [block_shape] * 8,
         [
             pltpu.VMEM((tiles, tile, WIDTH), BF),
@@ -581,8 +591,8 @@
 
     hist, pre, *pieces = call(
         project_kernel,
-        [place_info, dest, slot, *blocks, w_in, dmixed],
-        [SMEM] * 3 + [VMEM] * 10,
+        [dest, slot, *blocks, w_in, dmixed],
+        [SMEM] * 2 + [VMEM] * 10,
         [shape((ROWS, WIDTH), BF), shape((ROWS, 4 * WIDTH), F32)] + [four] * 4,
         [pltpu.VMEM((ROWS, 4 * WIDTH), BF), pltpu.VMEM((ROWS, WIDTH), BF)],
         flops=2 * ROWS * WIDTH * 4 * WIDTH,
@@ -590,17 +600,17 @@
     )
     own_keys, queries, grads = call(
         collect_kernel,
-        [place_info, *to_heads(pieces)],
-        [SMEM] + [VMEM] * 4,
+        [*to_heads(pieces)],
+        [VMEM] * 4,
         [rows_two, rows_one, rows_one],
         name="collect",
     )
-    keys, attn, passed, stats = call(
+    keys, attn, stats = call(
         forward_kernel,
-        [place_info, bounds, begins, key_pos, *over_rows(own_keys), queries, grads],
-        [SMEM] * 2 + [VMEM] * 8,
-        [shape((LENGTH, 2 * HD), BF), shape((quarter, HD), F32), rows_one, shape((8, quarter), F32)],
-        [pltpu.VMEM((quarter + ROWS, HD), F32)] + work_scratch(),
+        [key_work, begins, key_pos, *over_rows(own_keys), queries, grads],
+        [SMEM] + [VMEM] * 8,
+        [shape((LENGTH, 2 * HD), BF), shape((quarter, HD), F32), shape((8, quarter), F32)],
+        [pltpu.VMEM((quarter + ROWS, HD), F32)],
         flops=6 * 10**9,
         name="forward",
     )
@@ -612,32 +622,33 @@
         [rows_one],
         flops=10**9,
         name="attn_grad",
+        placed=False,
     )
     all_d_attn = over_rows(d_attn)
     (d_query,) = call(
         query_grad_kernel,
-        [place_info, bounds, begins, key_pos, keys, queries, d_attn],
-        [SMEM] * 2 + [VMEM] * 5,
+        [key_work, begins, key_pos, keys, queries, d_attn],
+        [SMEM] + [VMEM] * 5,
         [rows_one],
-        [pltpu.VMEM((quarter + ROWS, HD), F32)] + work_scratch(),
+        [pltpu.VMEM((quarter + ROWS, HD), F32)],
         flops=6 * 10**9,
         name="query_grad",
     )
     back_parts = call(
         key_grad_kernel,
-        [place_info, bounds, starts, query_pos, own_keys, *all_queries, *all_d_attn, d_query, attn],
-        [SMEM] * 2 + [VMEM] * 13,
+        [query_work, starts, query_pos, own_keys, *all_queries, *all_d_attn, d_query, attn],
+        [SMEM] + [VMEM] * 13,
         [four] * 4,
         [pltpu.VMEM((LENGTH, HD), BF), pltpu.VMEM((LENGTH, HD), BF), pltpu.VMEM((quarter + ROWS, 2 * HD), F32)]
-        + work_scratch(),
+       ,
         flops=7 * 10**9,
         name="key_grad",
     )
     incoming = output_gradient[0]
     *returning, mixed = call(
         input_grad_kernel,
-        [place_info, dest, slot, *to_owners(back_parts), pre, dmixed, hist, incoming, w_in],
-        [SMEM] * 3 + [VMEM] * 9,
+        [dest, slot, *to_owners(back_parts), pre, dmixed, hist, incoming, w_in],
+        [SMEM] * 2 + [VMEM] * 9,
         [block_shape] * 8 + [shape((ROWS, WIDTH), BF)],
         [
             pltpu.VMEM((ROWS, WIDTH), F32),
@@ -654,12 +665,13 @@
         [shape((ROWS, WIDTH), BF)],
         flops=2 * ROWS * WIDTH * WIDTH,
         name="output",
+        placed=False,
     )
     came_back = [returning[0]] + [send(returning[k], back(tab_pairs(k))) for k in range(1, 8)]
     (table_grad,) = call(
         table_grad_kernel,
-        [place_info, dest, row_ids.reshape(1, ROWS), *came_back],
-        [SMEM, SMEM] + [VMEM] * 9,
+        [dest, row_ids.reshape(1, ROWS), *came_back],
+        [SMEM] + [VMEM] * 9,
         [shape((1, 1, tab_rows, WIDTH), BF)],
         [
             pltpu.VMEM((ROWS, WIDTH), BF),

time: 121 us -> 116 us (0.959); the launches traced: 122 us -> 115 us
  starting transfers between devices: 59.2 us -> 52.6 us
    ppermute x32, starting transfers between devices: 59.2 us -> 52.6 us  [send(): return lax.ppermute(value, AXES, pairs)]
  transfers between devices with their start and end apart: 32 -> 32, of which waited for: 13 -> 13; matrix products, arithmetic and copies ran while one was open for 0% -> 0% of each run, Pallas kernels for 8% -> 9%
where the time goes in v4:
time: 116 us; the launch traced here: 115 us
  starting transfers between devices  52.6 us (45%)
  waiting for transfers between devices  32.8 us (28%)
  Pallas kernels  27.9 us (24%)
    ppermute x32, starting transfers between devices, send(): return lax.ppermute(value, AXES, pairs)  52.6 us
    ppermute x32, waiting for transfers between devices, send(): return lax.ppermute(value, AXES, pairs)  32.8 us
    pallas_call x11, Pallas kernels, call(): pl.pallas_call(with_place(kernel) if placed else kernel, out_shape=outs,...  27.9 us
  transfers between devices with their start and end apart: 32, of which 13 were waited for; matrix products, arithmetic and copies ran while one was open for 0% of the time, Pallas kernels for 9%

profile of v4, /device:TPU:1, one launch (start us, length us, event | category | flops | bytes accessed | tf_op | source)
XLA Modules:
  0.0 115.1 jit_solution(18188688781447991595)
XLA Ops:
  0.7 4.9 %lookup.1 = (bf16[64,512]{1,0:T(8,128)(2,1)}, bf16[64,512]{1,0:T(8,128)(2,1)}, bf16[64,512]{1,0:T(8,128)(2,1)}, bf16[64,512]{1,0:T(8,128)(2,1)}, bf16[64,512]{1,...) custom-call(s32[4,8]{1,0:T(4,128)} %bitcast.14, s32[2,128]{1,0:T(2,128)} %bitcast.21, ...), custom_call_target="tpu_custom_call" | custom-call | flops 1073741824 | bytes 4719744 | tf_op jit(solution)/shard_map/lookup/pallas_call | solution.py:122
  5.6 2.7 %collective-permute-start = (bf16[64,512]{1,0:T(8,128)(2,1)}, bf16[64,512]{1,0:T(8,128)(2,1)S(1)}, u32[]{:S(2)}, u32[]{:S(2)}) collective-permute-start(bf16[64,512]{1,0:T(8,128)(2,1)} %get-tuple-element.46), channel_id=1, source_target_pairs={{0,1},{1,2},{2,3},{3,4},{4,5},{5,6},{6,7},{7,0},{8,9},{9,10},{10,1... | collective-permute-start | bytes 196616 | tf_op jit(solution)/shard_map/ppermute | solution.py:68
  8.3 1.3 %collective-permute-start.1 = (bf16[64,512]{1,0:T(8,128)(2,1)}, bf16[64,512]{1,0:T(8,128)(2,1)S(1)}, u32[]{:S(2)}, u32[]{:S(2)}) collective-permute-start(bf16[64,512]{1,0:T(8,128)(2,1)} %get-tuple-element.47), channel_id=1, source_target_pairs={{0,2},{1,3},{2,4},{3,5},{4,6},{5,7},{6,0},{7,1},{8,10},{9,11},{10,... | collective-permute-start | bytes 196616 | tf_op jit(solution)/shard_map/ppermute | solution.py:68
  9.6 1.7 %collective-permute-start.2 = (bf16[64,512]{1,0:T(8,128)(2,1)}, bf16[64,512]{1,0:T(8,128)(2,1)S(1)}, u32[]{:S(2)}, u32[]{:S(2)}) collective-permute-start(bf16[64,512]{1,0:T(8,128)(2,1)} %get-tuple-element.48), channel_id=1, source_target_pairs={{0,3},{1,4},{2,5},{3,6},{4,7},{5,0},{6,1},{7,2},{8,11},{9,12},{10,... | collective-permute-start | bytes 196616 | tf_op jit(solution)/shard_map/ppermute | solution.py:68
  11.3 0.3 collective-permute-start.3
  11.6 2.0 %collective-permute-start.4 = (bf16[64,512]{1,0:T(8,128)(2,1)}, bf16[64,512]{1,0:T(8,128)(2,1)S(1)}, u32[]{:S(2)}, u32[]{:S(2)}) collective-permute-start(bf16[64,512]{1,0:T(8,128)(2,1)} %get-tuple-element.50), channel_id=1, source_target_pairs={{0,5},{1,6},{2,7},{3,0},{4,1},{5,2},{6,3},{7,4},{8,13},{9,14},{10,... | collective-permute-start | bytes 196616 | tf_op jit(solution)/shard_map/ppermute | solution.py:68
  13.6 0.0 collective-permute-done.refs_3_
  13.6 0.8 collective-permute-start.5
  14.4 0.0 collective-permute-done.1.refs_4_
  14.4 1.6 %collective-permute-start.6 = (bf16[64,512]{1,0:T(8,128)(2,1)}, bf16[64,512]{1,0:T(8,128)(2,1)S(1)}, u32[]{:S(2)}, u32[]{:S(2)}) collective-permute-start(bf16[64,512]{1,0:T(8,128)(2,1)} %get-tuple-element.52), channel_id=1, source_target_pairs={{0,7},{1,0},{2,1},{3,2},{4,3},{5,4},{6,5},{7,6},{8,15},{9,8},{10,9... | collective-permute-start | bytes 196616 | tf_op jit(solution)/shard_map/ppermute | solution.py:68
  16.0 2.8 %prepare.1 = (s32[257]{0:T(512)S(1)}, s32[257]{0:T(512)S(1)}, f32[8,4096]{1,0:T(8,128)S(1)}, f32[1024,128]{1,0:T(8,128)S(1)}, f32[16,4096]{1,0:T(8,128)S(1)}, /*...) custom-call(s32[16]{0:T(128)S(1)} %bitcast.23, s32[64,64]{1,0:T(8,128)S(1)} %bitcast.18, bf16[256,512]{1,0:T(8,128)(2,1)S(1)} %bitcast.12, ...), custom_call_target="tpu_custom_call" | custom-call | flops 134217728 | bytes 2508872 | tf_op jit(solution)/shard_map/prepare/pallas_call | solution.py:122
  18.8 0.0 collective-permute-done.2.refs_5_
  18.8 0.0 collective-permute-done.4.refs_7_
  18.8 0.0 collective-permute-done.5.refs_8_
  18.8 0.3 collective-permute-done.6.refs_9_
  19.2 0.0 copy-start.3
  19.2 0.8 copy-done.3
  20.0 2.4 %project.1 = (bf16[256,512]{1,0:T(8,128)(2,1)S(1)}, f32[256,2048]{1,0:T(8,128)S(1)}, bf16[256,512]{1,0:T(8,128)(2,1)S(1)}, bf16[256,512]{1,0:T(8,128)(2,1)S(1)},...) custom-call(s32[4,8]{1,0:T(4,128)S(1)} %bitcast.15, s32[4,8]{1,0:T(4,128)S(1)} %bitcast.19, ...), custom_call_target="tpu_custom_call" | custom-call | flops 536870912 | bytes 6553856 | tf_op jit(solution)/shard_map/project/pallas_call | solution.py:122
  22.4 1.7 %collective-permute-start.7 = (bf16[256,512]{1,0:T(8,128)(2,1)S(1)}, bf16[256,512]{1,0:T(8,128)(2,1)S(1)}, u32[]{:S(2)}, u32[]{:S(2)}) collective-permute-start(bf16[256,512]{1,0:T(8,128)(2,1)S(1)} %get-tuple-element.55), channel_id=1, source_target_pairs={{0,32},{1,9},{2,34},{3,11},{4,36},{5,13},{6,38},{7,15},{8,40},{9,1... | collective-permute-start | bytes 786440 | tf_op jit(solution)/shard_map/ppermute | solution.py:68
  24.2 3.3 %collective-permute-start.8 = (bf16[256,512]{1,0:T(8,128)(2,1)S(1)}, bf16[256,512]{1,0:T(8,128)(2,1)S(1)}, u32[]{:S(2)}, u32[]{:S(2)}) collective-permute-start(bf16[256,512]{1,0:T(8,128)(2,1)S(1)} %get-tuple-element.56), channel_id=1, source_target_pairs={{0,64},{1,17},{2,66},{3,19},{4,68},{5,21},{6,70},{7,23},{8,72},{9,... | collective-permute-start | bytes 786440 | tf_op jit(solution)/shard_map/ppermute | solution.py:68
  27.5 0.7 collective-permute-start.9
  28.2 1.9 %collective-permute-done.7.refs_1_ = bf16[256,512]{1,0:T(8,128)(2,1)S(1)} collective-permute-done((bf16[256,512]{1,0:T(8,128)(2,1)S(1)}, bf16[256,512]{1,0:T(8,128)(2,1)S(1)}, u32[]{:S(2)}, u32[]{:S(2)}) %collective-permute-start.7) | collective-permute-done | bytes 262176 | tf_op jit(solution)/shard_map/ppermute | solution.py:68
  30.0 4.0 %collective-permute-done.8.refs_2_ = bf16[256,512]{1,0:T(8,128)(2,1)S(1)} collective-permute-done((bf16[256,512]{1,0:T(8,128)(2,1)S(1)}, bf16[256,512]{1,0:T(8,128)(2,1)S(1)}, u32[]{:S(2)}, u32[]{:S(2)}) %collective-permute-start.8) | collective-permute-done | bytes 262176 | tf_op jit(solution)/shard_map/ppermute | solution.py:68
  34.0 0.0 collective-permute-done.9.refs_3_
  34.0 0.1 collect.1
  34.2 1.3 %collective-permute-start.13 = (bf16[1024,256]{1,0:T(8,128)(2,1)S(1)}, bf16[1024,256]{1,0:T(8,128)(2,1)S(1)}, u32[]{:S(2)}, u32[]{:S(2)}) collective-permute-start(bf16[1024,256]{1,0:T(8,128)(2,1)S(1)} %get-tuple-element.58.refs_3_), channel_id=1, source_target_pairs={{0,8},{1,33},{2,10},{3,35},{4,12},{5,37},{6,14},{7,39},{8,16},{9,4... | collective-permute-start | bytes 1572872 | tf_op jit(solution)/shard_map/ppermute | solution.py:68
  35.4 2.4 %collective-permute-start.14 = (bf16[1024,256]{1,0:T(8,128)(2,1)S(1)}, bf16[1024,256]{1,0:T(8,128)(2,1)S(1)}, u32[]{:S(2)}, u32[]{:S(2)}) collective-permute-start(bf16[1024,256]{1,0:T(8,128)(2,1)S(1)} %get-tuple-element.58.refs_3_), channel_id=1, source_target_pairs={{0,16},{1,65},{2,18},{3,67},{4,20},{5,69},{6,22},{7,71},{8,24},{9,... | collective-permute-start | bytes 1572872 | tf_op jit(solution)/shard_map/ppermute | solution.py:68
  37.9 1.2 %collective-permute-start.15 = (bf16[1024,256]{1,0:T(8,128)(2,1)S(1)}, bf16[1024,256]{1,0:T(8,128)(2,1)S(1)}, u32[]{:S(2)}, u32[]{:S(2)}) collective-permute-start(bf16[1024,256]{1,0:T(8,128)(2,1)S(1)} %get-tuple-element.58.refs_3_), channel_id=1, source_target_pairs={{0,24},{1,97},{2,26},{3,99},{4,28},{5,101},{6,30},{7,103},{8,0},{9... | collective-permute-start | bytes 1572872 | tf_op jit(solution)/shard_map/ppermute | solution.py:68
  39.0 0.3 collective-permute-start.10
  39.4 0.9 collective-permute-start.11
  40.2 3.5 %collective-permute-done.13.refs_4_ = bf16[1024,256]{1,0:T(8,128)(2,1)S(1)} collective-permute-done((bf16[1024,256]{1,0:T(8,128)(2,1)S(1)}, bf16[1024,256]{1,0:T(8,128)(2,1)S(1)}, u32[]{:S(2)}, u32[]{:S(2)}) %collective-permute-start.13) | collective-permute-done | bytes 524320 | tf_op jit(solution)/shard_map/ppermute | solution.py:68
  43.8 1.3 %collective-permute-start.12 = (bf16[1024,128]{1,0:T(8,128)(2,1)S(1)}, bf16[1024,128]{1,0:T(8,128)(2,1)S(1)}, u32[]{:S(2)}, u32[]{:S(2)}) collective-permute-start(bf16[1024,128]{1,0:T(8,128)(2,1)S(1)} %get-tuple-element.59.refs_7_.refs_4_), channel_id=1, source_target_pairs={{0,24},{1,97},{2,26},{3,99},{4,28},{5,101},{6,30},{7,103},{8,0},{9... | collective-permute-start | bytes 786440 | tf_op jit(solution)/shard_map/ppermute | solution.py:68
  45.0 5.4 %collective-permute-done.14.refs_5_ = bf16[1024,256]{1,0:T(8,128)(2,1)S(1)} collective-permute-done((bf16[1024,256]{1,0:T(8,128)(2,1)S(1)}, bf16[1024,256]{1,0:T(8,128)(2,1)S(1)}, u32[]{:S(2)}, u32[]{:S(2)}) %collective-permute-start.14) | collective-permute-done | bytes 524320 | tf_op jit(solution)/shard_map/ppermute | solution.py:68
  50.4 0.0 collective-permute-done.15.refs_6_
  50.4 3.6 %forward.1 = (bf16[4096,256]{1,0:T(8,128)(2,1)S(1)}, f32[1024,128]{1,0:T(8,128)S(1)}, f32[8,1024]{1,0:T(8,128)S(1)}) custom-call(s32[257]{0:T(512)S(1)} %get-tuple-element.60.refs_0_, f32[1024,128]{1,0:T(8,128)S(1)} %get-tuple-element.61.refs_1_, f32[16,4096]{1,0:T(8,128)S(1)} %get-tuple-element.62.refs_2_, bf16[1024,256]{1,0:T(8,128)(2,1)S(1)} %get-tuple-element.58.refs_3_, ...), custom_call_target="tpu_custom_call" | custom-call | flops 6000000000 | bytes 6063108 | tf_op jit(solution)/shard_map/forward/pallas_call | solution.py:122
  54.0 0.8 collective-permute-start.16
  54.8 2.4 %collective-permute-start.17 = (f32[8,1024]{1,0:T(8,128)S(1)}, f32[8,1024]{1,0:T(8,128)S(1)}, u32[]{:S(2)}, u32[]{:S(2)}) collective-permute-start(f32[8,1024]{1,0:T(8,128)S(1)} %get-tuple-element.64.s0), channel_id=1, source_target_pairs={{0,64},{1,17},{2,66},{3,19},{4,68},{5,21},{6,70},{7,23},{8,72},{9,... | collective-permute-start | bytes 98312 | tf_op jit(solution)/shard_map/ppermute | solution.py:68
  57.2 1.0 collective-permute-start.18
  58.1 0.0 collective-permute-done.11.q2.refs_6_
  58.1 0.9 collective-permute-done.17.s2
  59.0 0.9 collective-permute-done.18.s3
  59.9 0.6 attn_grad.1.refs_5_.refs_8_
  60.6 2.0 %collective-permute-start.19 = (bf16[1024,128]{1,0:T(8,128)(2,1)S(1)}, bf16[1024,128]{1,0:T(8,128)(2,1)S(1)}, u32[]{:S(2)}, u32[]{:S(2)}) collective-permute-start(bf16[1024,128]{1,0:T(8,128)(2,1)S(1)} %attn_grad.1.refs_5_.refs_8_), channel_id=1, source_target_pairs={{0,8},{1,33},{2,10},{3,35},{4,12},{5,37},{6,14},{7,39},{8,16},{9,4... | collective-permute-start | bytes 786440 | tf_op jit(solution)/shard_map/ppermute | solution.py:68
  62.6 4.9 %collective-permute-start.20 = (bf16[1024,128]{1,0:T(8,128)(2,1)S(1)}, bf16[1024,128]{1,0:T(8,128)(2,1)S(1)}, u32[]{:S(2)}, u32[]{:S(2)}) collective-permute-start(bf16[1024,128]{1,0:T(8,128)(2,1)S(1)} %attn_grad.1.refs_5_.refs_8_), channel_id=1, source_target_pairs={{0,16},{1,65},{2,18},{3,67},{4,20},{5,69},{6,22},{7,71},{8,24},{9,... | collective-permute-start | bytes 786440 | tf_op jit(solution)/shard_map/ppermute | solution.py:68
  67.5 2.8 %query_grad.1.refs_12_ = bf16[1024,128]{1,0:T(8,128)(2,1)S(1)} custom-call(s32[257]{0:T(512)S(1)} %get-tuple-element.60.refs_0_, f32[1024,128]{1,0:T(8,128)S(1)} %get-tuple-element.61.refs_1_, f32[16,4096]{1,0:T(8,128)S(1)} %get-tuple-element.62.refs_2_, bf16[4096,256]{1,0:T(8,128)(2,1)S(1)} %get-tuple-element.66.refs_3_, ...), custom_call_target="tpu_custom_call" | custom-call | flops 6000000000 | bytes 3671044 | tf_op jit(solution)/shard_map/query_grad/pallas_call | solution.py:122
  70.3 4.0 %collective-permute-done.20.refs_10_ = bf16[1024,128]{1,0:T(8,128)(2,1)S(1)} collective-permute-done((bf16[1024,128]{1,0:T(8,128)(2,1)S(1)}, bf16[1024,128]{1,0:T(8,128)(2,1)S(1)}, u32[]{:S(2)}, u32[]{:S(2)}) %collective-permute-start.20) | collective-permute-done | bytes 262176 | tf_op jit(solution)/shard_map/ppermute | solution.py:68
  74.3 3.8 %key_grad.1 = (bf16[256,512]{1,0:T(8,128)(2,1)S(1)}, bf16[256,512]{1,0:T(8,128)(2,1)S(1)}, bf16[256,512]{1,0:T(8,128)(2,1)S(1)}, bf16[256,512]{1,0:T(8,128)(2,1)S(1)}) custom-call(s32[257]{0:T(512)S(1)} %get-tuple-element.42.refs_0_, f32[8,4096]{1,0:T(8,128)S(1)} %get-tuple-element.43.refs_1_, f32[16,4096]{1,0:T(8,128)S(1)} %get-tuple-element.44.refs_2_, ...), custom_call_target="tpu_custom_call" | custom-call | flops 7000000000 | bytes 4850692 | tf_op jit(solution)/shard_map/key_grad/pallas_call | solution.py:122
  78.2 1.9 %collective-permute-start.22 = (bf16[256,512]{1,0:T(8,128)(2,1)S(1)}, bf16[256,512]{1,0:T(8,128)(2,1)S(1)}, u32[]{:S(2)}, u32[]{:S(2)}) collective-permute-start(bf16[256,512]{1,0:T(8,128)(2,1)S(1)} %get-tuple-element.68), channel_id=1, source_target_pairs={{32,0},{9,1},{34,2},{11,3},{36,4},{13,5},{38,6},{15,7},{40,8},{17,... | collective-permute-start | bytes 786440 | tf_op jit(solution)/shard_map/ppermute | solution.py:68
  80.1 0.0 collective-permute-start.23
  80.1 0.6 collective-permute-start.24
  80.8 5.5 %collective-permute-done.22.refs_3_ = bf16[256,512]{1,0:T(8,128)(2,1)S(1)} collective-permute-done((bf16[256,512]{1,0:T(8,128)(2,1)S(1)}, bf16[256,512]{1,0:T(8,128)(2,1)S(1)}, u32[]{:S(2)}, u32[]{:S(2)}) %collective-permute-start.22) | collective-permute-done | bytes 262176 | tf_op jit(solution)/shard_map/ppermute | solution.py:68
  86.2 0.7 collective-permute-done.23.refs_4_
  86.9 2.4 %collective-permute-done.24.refs_5_ = bf16[256,512]{1,0:T(8,128)(2,1)S(1)} collective-permute-done((bf16[256,512]{1,0:T(8,128)(2,1)S(1)}, bf16[256,512]{1,0:T(8,128)(2,1)S(1)}, u32[]{:S(2)}, u32[]{:S(2)}) %collective-permute-start.24) | collective-permute-done | bytes 262176 | tf_op jit(solution)/shard_map/ppermute | solution.py:68
  89.4 2.7 %input_grad.1 = (bf16[64,512]{1,0:T(8,128)(2,1)S(1)}, bf16[64,512]{1,0:T(8,128)(2,1)S(1)}, bf16[64,512]{1,0:T(8,128)(2,1)S(1)}, bf16[64,512]{1,0:T(8,128)(2,1)S(...) custom-call(s32[4,8]{1,0:T(4,128)S(1)} %bitcast.16, ...), custom_call_target="tpu_custom_call" | custom-call | flops 536870912 | bytes 7078144 | tf_op jit(solution)/shard_map/input_grad/pallas_call | solution.py:122
  92.1 7.9 %collective-permute-start.25 = (bf16[64,512]{1,0:T(8,128)(2,1)S(1)}, bf16[64,512]{1,0:T(8,128)(2,1)S(1)}, u32[]{:S(2)}, u32[]{:S(2)}) collective-permute-start(bf16[64,512]{1,0:T(8,128)(2,1)S(1)} %get-tuple-element.75), channel_id=1, source_target_pairs={{1,0},{2,1},{3,2},{4,3},{5,4},{6,5},{7,6},{0,7},{9,8},{10,9},{11,1... | collective-permute-start | bytes 196616 | tf_op jit(solution)/shard_map/ppermute | solution.py:68
  99.9 2.1 %collective-permute-start.26 = (bf16[64,512]{1,0:T(8,128)(2,1)S(1)}, bf16[64,512]{1,0:T(8,128)(2,1)S(1)}, u32[]{:S(2)}, u32[]{:S(2)}) collective-permute-start(bf16[64,512]{1,0:T(8,128)(2,1)S(1)} %get-tuple-element.76), channel_id=1, source_target_pairs={{2,0},{3,1},{4,2},{5,3},{6,4},{7,5},{0,6},{1,7},{10,8},{11,9},{12,... | collective-permute-start | bytes 196616 | tf_op jit(solution)/shard_map/ppermute | solution.py:68
  102.0 1.3 %collective-permute-start.27 = (bf16[64,512]{1,0:T(8,128)(2,1)S(1)}, bf16[64,512]{1,0:T(8,128)(2,1)S(1)}, u32[]{:S(2)}, u32[]{:S(2)}) collective-permute-start(bf16[64,512]{1,0:T(8,128)(2,1)S(1)} %get-tuple-element.77), channel_id=1, source_target_pairs={{3,0},{4,1},{5,2},{6,3},{7,4},{0,5},{1,6},{2,7},{11,8},{12,9},{13,... | collective-permute-start | bytes 196616 | tf_op jit(solution)/shard_map/ppermute | solution.py:68
  103.3 0.6 collective-permute-start.28
  103.9 3.5 %collective-permute-start.29 = (bf16[64,512]{1,0:T(8,128)(2,1)S(1)}, bf16[64,512]{1,0:T(8,128)(2,1)S(1)}, u32[]{:S(2)}, u32[]{:S(2)}) collective-permute-start(bf16[64,512]{1,0:T(8,128)(2,1)S(1)} %get-tuple-element.79), channel_id=1, source_target_pairs={{5,0},{6,1},{7,2},{0,3},{1,4},{2,5},{3,6},{4,7},{13,8},{14,9},{15,... | collective-permute-start | bytes 196616 | tf_op jit(solution)/shard_map/ppermute | solution.py:68
  107.4 0.1 collective-permute-start.31
  107.5 1.0 output.1
  108.5 1.4 %collective-permute-done.29.refs_7_ = bf16[64,512]{1,0:T(8,128)(2,1)S(1)} collective-permute-done((bf16[64,512]{1,0:T(8,128)(2,1)S(1)}, bf16[64,512]{1,0:T(8,128)(2,1)S(1)}, u32[]{:S(2)}, u32[]{:S(2)}) %collective-permute-start.29) | collective-permute-done | bytes 65568 | tf_op jit(solution)/shard_map/ppermute | solution.py:68
  109.9 1.8 %collective-permute-done.30.refs_8_ = bf16[64,512]{1,0:T(8,128)(2,1)S(1)} collective-permute-done((bf16[64,512]{1,0:T(8,128)(2,1)S(1)}, bf16[64,512]{1,0:T(8,128)(2,1)S(1)}, u32[]{:S(2)}, u32[]{:S(2)}) %collective-permute-start.30) | collective-permute-done | bytes 65568 | tf_op jit(solution)/shard_map/ppermute | solution.py:68
  111.8 3.2 %table_grad.1 = bf16[1,1,4096,512]{3,2,1,0:T(8,128)(2,1)} custom-call(s32[4,8]{1,0:T(4,128)S(1)} %bitcast.17, s32[1,256]{1,0:T(1,128)S(1)} %bitcast.22, bf16[64,512]{1,0:T(8,128)(2,1)S(1)} %get-tuple-element.74.refs_2_, bf16[64,512]{1,0:T(8,128)(2,1)S(1)} %collective-permute-done.25.refs_3_, bf16[64,512]{1,0:T(8,128)(2,1)S(1)} %collective-permute-done.26.refs_4_, ...), custom_call_target="tpu_custom_call" | custom-call | flops 1073741824 | bytes 4719744 | tf_op jit(solution)/shard_map/table_grad/pallas_call | solution.py:122
  (29 shorter events, 0.1 us)
Async XLA Ops:
  0.6 15.4 %copy-start.1 = (bf16[512,512]{1,0:T(8,128)(2,1)S(1)}, bf16[512,512]{1,0:T(8,128)(2,1)}, u32[]{:S(2)}) copy-start(bf16[512,512]{1,0:T(8,128)(2,1)} %w_out.1) | copy-start | bytes 1572868
  0.6 15.4 %copy-start.2 = (bf16[1,256,512]{2,1,0:T(8,128)(2,1)S(1)}, bf16[1,256,512]{2,1,0:T(8,128)(2,1)}, u32[]{:S(2)}) copy-start(bf16[1,256,512]{2,1,0:T(8,128)(2,1)} %param.17) | copy-start | bytes 786436
  0.7 15.4 %copy-start.5 = (s32[1,64,64]{2,1,0:T(8,128)S(1)}, s32[1,64,64]{2,1,0:T(8,128)}, u32[]{:S(2)}) copy-start(s32[1,64,64]{2,1,0:T(8,128)} %param.14) | copy-start | bytes 49156
  0.7 15.4 %copy-start.8 = (s32[1,16]{1,0:T(1,128)S(1)}, s32[1,16]{1,0:T(1,128)}, u32[]{:S(2)}) copy-start(s32[1,16]{1,0:T(1,128)} %param.13) | copy-start | bytes 196
  0.7 18.5 %copy-start = (bf16[512,2048]{1,0:T(8,128)(2,1)S(1)}, bf16[512,2048]{1,0:T(8,128)(2,1)}, u32[]{:S(2)}) copy-start(bf16[512,2048]{1,0:T(8,128)(2,1)} %refs_10_.3) | copy-start | bytes 6291460
  0.7 18.5 %copy-start.4 = (s32[1,8,4]{1,2,0:T(4,128)S(1)}, s32[1,8,4]{1,2,0:T(4,128)}, u32[]{:S(2)}) copy-start(s32[1,8,4]{1,2,0:T(4,128)} %param.11) | copy-start | bytes 388
  0.7 18.5 %copy-start.6 = (s32[1,8,4]{1,2,0:T(4,128)S(1)}, s32[1,8,4]{1,2,0:T(4,128)}, u32[]{:S(2)}) copy-start(s32[1,8,4]{1,2,0:T(4,128)} %param.12) | copy-start | bytes 388
  5.6 8.0 %collective-permute-start = (bf16[64,512]{1,0:T(8,128)(2,1)}, bf16[64,512]{1,0:T(8,128)(2,1)S(1)}, u32[]{:S(2)}, u32[]{:S(2)}) collective-permute-start(bf16[64,512]{1,0:T(8,128)(2,1)} %get-tuple-element.46), channel_id=1, source_target_pairs={{0,1},{1,2},{2,3},{3,4},{4,5},{5,6},{6,7},{7,0},{8,9},{9,10},{10,1... | collective-permute-start | bytes 196616 | tf_op jit(solution)/shard_map/ppermute | solution.py:68
  8.3 6.1 %collective-permute-start.1 = (bf16[64,512]{1,0:T(8,128)(2,1)}, bf16[64,512]{1,0:T(8,128)(2,1)S(1)}, u32[]{:S(2)}, u32[]{:S(2)}) collective-permute-start(bf16[64,512]{1,0:T(8,128)(2,1)} %get-tuple-element.47), channel_id=1, source_target_pairs={{0,2},{1,3},{2,4},{3,5},{4,6},{5,7},{6,0},{7,1},{8,10},{9,11},{10,... | collective-permute-start | bytes 196616 | tf_op jit(solution)/shard_map/ppermute | solution.py:68
  9.6 9.2 %collective-permute-start.2 = (bf16[64,512]{1,0:T(8,128)(2,1)}, bf16[64,512]{1,0:T(8,128)(2,1)S(1)}, u32[]{:S(2)}, u32[]{:S(2)}) collective-permute-start(bf16[64,512]{1,0:T(8,128)(2,1)} %get-tuple-element.48), channel_id=1, source_target_pairs={{0,3},{1,4},{2,5},{3,6},{4,7},{5,0},{6,1},{7,2},{8,11},{9,12},{10,... | collective-permute-start | bytes 196616 | tf_op jit(solution)/shard_map/ppermute | solution.py:68
  11.3 7.5 %collective-permute-start.3 = (bf16[64,512]{1,0:T(8,128)(2,1)}, bf16[64,512]{1,0:T(8,128)(2,1)S(1)}, u32[]{:S(2)}, u32[]{:S(2)}) collective-permute-start(bf16[64,512]{1,0:T(8,128)(2,1)} %get-tuple-element.49), channel_id=1, source_target_pairs={{0,4},{1,5},{2,6},{3,7},{4,0},{5,1},{6,2},{7,3},{8,12},{9,13},{10,... | collective-permute-start | bytes 196616 | tf_op jit(solution)/shard_map/ppermute | solution.py:68
  11.6 7.2 %collective-permute-start.4 = (bf16[64,512]{1,0:T(8,128)(2,1)}, bf16[64,512]{1,0:T(8,128)(2,1)S(1)}, u32[]{:S(2)}, u32[]{:S(2)}) collective-permute-start(bf16[64,512]{1,0:T(8,128)(2,1)} %get-tuple-element.50), channel_id=1, source_target_pairs={{0,5},{1,6},{2,7},{3,0},{4,1},{5,2},{6,3},{7,4},{8,13},{9,14},{10,... | collective-permute-start | bytes 196616 | tf_op jit(solution)/shard_map/ppermute | solution.py:68
  13.6 5.2 %collective-permute-start.5 = (bf16[64,512]{1,0:T(8,128)(2,1)}, bf16[64,512]{1,0:T(8,128)(2,1)S(1)}, u32[]{:S(2)}, u32[]{:S(2)}) collective-permute-start(bf16[64,512]{1,0:T(8,128)(2,1)} %get-tuple-element.51), channel_id=1, source_target_pairs={{0,6},{1,7},{2,0},{3,1},{4,2},{5,3},{6,4},{7,5},{8,14},{9,15},{10,... | collective-permute-start | bytes 196616 | tf_op jit(solution)/shard_map/ppermute | solution.py:68
  14.4 4.7 %collective-permute-start.6 = (bf16[64,512]{1,0:T(8,128)(2,1)}, bf16[64,512]{1,0:T(8,128)(2,1)S(1)}, u32[]{:S(2)}, u32[]{:S(2)}) collective-permute-start(bf16[64,512]{1,0:T(8,128)(2,1)} %get-tuple-element.52), channel_id=1, source_target_pairs={{0,7},{1,0},{2,1},{3,2},{4,3},{5,4},{6,5},{7,6},{8,15},{9,8},{10,9... | collective-permute-start | bytes 196616 | tf_op jit(solution)/shard_map/ppermute | solution.py:68
  19.2 0.8 copy-start.3
  22.4 7.6 %collective-permute-start.7 = (bf16[256,512]{1,0:T(8,128)(2,1)S(1)}, bf16[256,512]{1,0:T(8,128)(2,1)S(1)}, u32[]{:S(2)}, u32[]{:S(2)}) collective-permute-start(bf16[256,512]{1,0:T(8,128)(2,1)S(1)} %get-tuple-element.55), channel_id=1, source_target_pairs={{0,32},{1,9},{2,34},{3,11},{4,36},{5,13},{6,38},{7,15},{8,40},{9,1... | collective-permute-start | bytes 786440 | tf_op jit(solution)/shard_map/ppermute | solution.py:68
  24.2 9.9 %collective-permute-start.8 = (bf16[256,512]{1,0:T(8,128)(2,1)S(1)}, bf16[256,512]{1,0:T(8,128)(2,1)S(1)}, u32[]{:S(2)}, u32[]{:S(2)}) collective-permute-start(bf16[256,512]{1,0:T(8,128)(2,1)S(1)} %get-tuple-element.56), channel_id=1, source_target_pairs={{0,64},{1,17},{2,66},{3,19},{4,68},{5,21},{6,70},{7,23},{8,72},{9,... | collective-permute-start | bytes 786440 | tf_op jit(solution)/shard_map/ppermute | solution.py:68
  27.5 6.6 %collective-permute-start.9 = (bf16[256,512]{1,0:T(8,128)(2,1)S(1)}, bf16[256,512]{1,0:T(8,128)(2,1)S(1)}, u32[]{:S(2)}, u32[]{:S(2)}) collective-permute-start(bf16[256,512]{1,0:T(8,128)(2,1)S(1)} %get-tuple-element.57), channel_id=1, source_target_pairs={{0,96},{1,25},{2,98},{3,27},{4,100},{5,29},{6,102},{7,31},{8,104},... | collective-permute-start | bytes 786440 | tf_op jit(solution)/shard_map/ppermute | solution.py:68
  34.2 9.6 %collective-permute-start.13 = (bf16[1024,256]{1,0:T(8,128)(2,1)S(1)}, bf16[1024,256]{1,0:T(8,128)(2,1)S(1)}, u32[]{:S(2)}, u32[]{:S(2)}) collective-permute-start(bf16[1024,256]{1,0:T(8,128)(2,1)S(1)} %get-tuple-element.58.refs_3_), channel_id=1, source_target_pairs={{0,8},{1,33},{2,10},{3,35},{4,12},{5,37},{6,14},{7,39},{8,16},{9,4... | collective-permute-start | bytes 1572872 | tf_op jit(solution)/shard_map/ppermute | solution.py:68
  35.4 15.0 %collective-permute-start.14 = (bf16[1024,256]{1,0:T(8,128)(2,1)S(1)}, bf16[1024,256]{1,0:T(8,128)(2,1)S(1)}, u32[]{:S(2)}, u32[]{:S(2)}) collective-permute-start(bf16[1024,256]{1,0:T(8,128)(2,1)S(1)} %get-tuple-element.58.refs_3_), channel_id=1, source_target_pairs={{0,16},{1,65},{2,18},{3,67},{4,20},{5,69},{6,22},{7,71},{8,24},{9,... | collective-permute-start | bytes 1572872 | tf_op jit(solution)/shard_map/ppermute | solution.py:68
  37.9 12.5 %collective-permute-start.15 = (bf16[1024,256]{1,0:T(8,128)(2,1)S(1)}, bf16[1024,256]{1,0:T(8,128)(2,1)S(1)}, u32[]{:S(2)}, u32[]{:S(2)}) collective-permute-start(bf16[1024,256]{1,0:T(8,128)(2,1)S(1)} %get-tuple-element.58.refs_3_), channel_id=1, source_target_pairs={{0,24},{1,97},{2,26},{3,99},{4,28},{5,101},{6,30},{7,103},{8,0},{9... | collective-permute-start | bytes 1572872 | tf_op jit(solution)/shard_map/ppermute | solution.py:68
  39.0 18.1 %collective-permute-start.10 = (bf16[1024,128]{1,0:T(8,128)(2,1)S(1)}, bf16[1024,128]{1,0:T(8,128)(2,1)S(1)}, u32[]{:S(2)}, u32[]{:S(2)}) collective-permute-start(bf16[1024,128]{1,0:T(8,128)(2,1)S(1)} %get-tuple-element.59.refs_7_.refs_4_), channel_id=1, source_target_pairs={{0,8},{1,33},{2,10},{3,35},{4,12},{5,37},{6,14},{7,39},{8,16},{9,4... | collective-permute-start | bytes 786440 | tf_op jit(solution)/shard_map/ppermute | solution.py:68
  39.4 18.8 %collective-permute-start.11 = (bf16[1024,128]{1,0:T(8,128)(2,1)S(1)}, bf16[1024,128]{1,0:T(8,128)(2,1)S(1)}, u32[]{:S(2)}, u32[]{:S(2)}) collective-permute-start(bf16[1024,128]{1,0:T(8,128)(2,1)S(1)} %get-tuple-element.59.refs_7_.refs_4_), channel_id=1, source_target_pairs={{0,16},{1,65},{2,18},{3,67},{4,20},{5,69},{6,22},{7,71},{8,24},{9,... | collective-permute-start | bytes 786440 | tf_op jit(solution)/shard_map/ppermute | solution.py:68
  43.8 14.4 %collective-permute-start.12 = (bf16[1024,128]{1,0:T(8,128)(2,1)S(1)}, bf16[1024,128]{1,0:T(8,128)(2,1)S(1)}, u32[]{:S(2)}, u32[]{:S(2)}) collective-permute-start(bf16[1024,128]{1,0:T(8,128)(2,1)S(1)} %get-tuple-element.59.refs_7_.refs_4_), channel_id=1, source_target_pairs={{0,24},{1,97},{2,26},{3,99},{4,28},{5,101},{6,30},{7,103},{8,0},{9... | collective-permute-start | bytes 786440 | tf_op jit(solution)/shard_map/ppermute | solution.py:68
  54.0 4.1 %collective-permute-start.16 = (f32[8,1024]{1,0:T(8,128)S(1)}, f32[8,1024]{1,0:T(8,128)S(1)}, u32[]{:S(2)}, u32[]{:S(2)}) collective-permute-start(f32[8,1024]{1,0:T(8,128)S(1)} %get-tuple-element.64.s0), channel_id=1, source_target_pairs={{0,32},{1,9},{2,34},{3,11},{4,36},{5,13},{6,38},{7,15},{8,40},{9,1... | collective-permute-start | bytes 98312 | tf_op jit(solution)/shard_map/ppermute | solution.py:68
  54.8 4.3 %collective-permute-start.17 = (f32[8,1024]{1,0:T(8,128)S(1)}, f32[8,1024]{1,0:T(8,128)S(1)}, u32[]{:S(2)}, u32[]{:S(2)}) collective-permute-start(f32[8,1024]{1,0:T(8,128)S(1)} %get-tuple-element.64.s0), channel_id=1, source_target_pairs={{0,64},{1,17},{2,66},{3,19},{4,68},{5,21},{6,70},{7,23},{8,72},{9,... | collective-permute-start | bytes 98312 | tf_op jit(solution)/shard_map/ppermute | solution.py:68
  57.2 2.8 %collective-permute-start.18 = (f32[8,1024]{1,0:T(8,128)S(1)}, f32[8,1024]{1,0:T(8,128)S(1)}, u32[]{:S(2)}, u32[]{:S(2)}) collective-permute-start(f32[8,1024]{1,0:T(8,128)S(1)} %get-tuple-element.64.s0), channel_id=1, source_target_pairs={{0,96},{1,25},{2,98},{3,27},{4,100},{5,29},{6,102},{7,31},{8,104},... | collective-permute-start | bytes 98312 | tf_op jit(solution)/shard_map/ppermute | solution.py:68
  60.6 9.7 %collective-permute-start.19 = (bf16[1024,128]{1,0:T(8,128)(2,1)S(1)}, bf16[1024,128]{1,0:T(8,128)(2,1)S(1)}, u32[]{:S(2)}, u32[]{:S(2)}) collective-permute-start(bf16[1024,128]{1,0:T(8,128)(2,1)S(1)} %attn_grad.1.refs_5_.refs_8_), channel_id=1, source_target_pairs={{0,8},{1,33},{2,10},{3,35},{4,12},{5,37},{6,14},{7,39},{8,16},{9,4... | collective-permute-start | bytes 786440 | tf_op jit(solution)/shard_map/ppermute | solution.py:68
  62.6 11.8 %collective-permute-start.20 = (bf16[1024,128]{1,0:T(8,128)(2,1)S(1)}, bf16[1024,128]{1,0:T(8,128)(2,1)S(1)}, u32[]{:S(2)}, u32[]{:S(2)}) collective-permute-start(bf16[1024,128]{1,0:T(8,128)(2,1)S(1)} %attn_grad.1.refs_5_.refs_8_), channel_id=1, source_target_pairs={{0,16},{1,65},{2,18},{3,67},{4,20},{5,69},{6,22},{7,71},{8,24},{9,... | collective-permute-start | bytes 786440 | tf_op jit(solution)/shard_map/ppermute | solution.py:68
  67.5 6.9 %collective-permute-start.21 = (bf16[1024,128]{1,0:T(8,128)(2,1)S(1)}, bf16[1024,128]{1,0:T(8,128)(2,1)S(1)}, u32[]{:S(2)}, u32[]{:S(2)}) collective-permute-start(bf16[1024,128]{1,0:T(8,128)(2,1)S(1)} %attn_grad.1.refs_5_.refs_8_), channel_id=1, source_target_pairs={{0,24},{1,97},{2,26},{3,99},{4,28},{5,101},{6,30},{7,103},{8,0},{9... | collective-permute-start | bytes 786440 | tf_op jit(solution)/shard_map/ppermute | solution.py:68
  78.2 8.1 %collective-permute-start.22 = (bf16[256,512]{1,0:T(8,128)(2,1)S(1)}, bf16[256,512]{1,0:T(8,128)(2,1)S(1)}, u32[]{:S(2)}, u32[]{:S(2)}) collective-permute-start(bf16[256,512]{1,0:T(8,128)(2,1)S(1)} %get-tuple-element.68), channel_id=1, source_target_pairs={{32,0},{9,1},{34,2},{11,3},{36,4},{13,5},{38,6},{15,7},{40,8},{17,... | collective-permute-start | bytes 786440 | tf_op jit(solution)/shard_map/ppermute | solution.py:68
  80.1 6.8 %collective-permute-start.23 = (bf16[256,512]{1,0:T(8,128)(2,1)S(1)}, bf16[256,512]{1,0:T(8,128)(2,1)S(1)}, u32[]{:S(2)}, u32[]{:S(2)}) collective-permute-start(bf16[256,512]{1,0:T(8,128)(2,1)S(1)} %get-tuple-element.69), channel_id=1, source_target_pairs={{64,0},{17,1},{66,2},{19,3},{68,4},{21,5},{70,6},{23,7},{72,8},{25... | collective-permute-start | bytes 786440 | tf_op jit(solution)/shard_map/ppermute | solution.py:68
  80.1 9.2 %collective-permute-start.24 = (bf16[256,512]{1,0:T(8,128)(2,1)S(1)}, bf16[256,512]{1,0:T(8,128)(2,1)S(1)}, u32[]{:S(2)}, u32[]{:S(2)}) collective-permute-start(bf16[256,512]{1,0:T(8,128)(2,1)S(1)} %get-tuple-element.70), channel_id=1, source_target_pairs={{96,0},{25,1},{98,2},{27,3},{100,4},{29,5},{102,6},{31,7},{104,8},... | collective-permute-start | bytes 786440 | tf_op jit(solution)/shard_map/ppermute | solution.py:68
  89.4 22.4 %copy-start.7 = (s32[1,1,256]{2,1,0:T(1,128)S(1)}, s32[1,1,256]{2,1,0:T(1,128)}, u32[]{:S(2)}) copy-start(s32[1,1,256]{2,1,0:T(1,128)} %param.10) | copy-start | bytes 3076
  92.1 15.4 %collective-permute-start.25 = (bf16[64,512]{1,0:T(8,128)(2,1)S(1)}, bf16[64,512]{1,0:T(8,128)(2,1)S(1)}, u32[]{:S(2)}, u32[]{:S(2)}) collective-permute-start(bf16[64,512]{1,0:T(8,128)(2,1)S(1)} %get-tuple-element.75), channel_id=1, source_target_pairs={{1,0},{2,1},{3,2},{4,3},{5,4},{6,5},{7,6},{0,7},{9,8},{10,9},{11,1... | collective-permute-start | bytes 196616 | tf_op jit(solution)/shard_map/ppermute | solution.py:68
  99.9 7.5 %collective-permute-start.26 = (bf16[64,512]{1,0:T(8,128)(2,1)S(1)}, bf16[64,512]{1,0:T(8,128)(2,1)S(1)}, u32[]{:S(2)}, u32[]{:S(2)}) collective-permute-start(bf16[64,512]{1,0:T(8,128)(2,1)S(1)} %get-tuple-element.76), channel_id=1, source_target_pairs={{2,0},{3,1},{4,2},{5,3},{6,4},{7,5},{0,6},{1,7},{10,8},{11,9},{12,... | collective-permute-start | bytes 196616 | tf_op jit(solution)/shard_map/ppermute | solution.py:68
  102.0 6.5 %collective-permute-start.27 = (bf16[64,512]{1,0:T(8,128)(2,1)S(1)}, bf16[64,512]{1,0:T(8,128)(2,1)S(1)}, u32[]{:S(2)}, u32[]{:S(2)}) collective-permute-start(bf16[64,512]{1,0:T(8,128)(2,1)S(1)} %get-tuple-element.77), channel_id=1, source_target_pairs={{3,0},{4,1},{5,2},{6,3},{7,4},{0,5},{1,6},{2,7},{11,8},{12,9},{13,... | collective-permute-start | bytes 196616 | tf_op jit(solution)/shard_map/ppermute | solution.py:68
  103.3 5.2 %collective-permute-start.28 = (bf16[64,512]{1,0:T(8,128)(2,1)S(1)}, bf16[64,512]{1,0:T(8,128)(2,1)S(1)}, u32[]{:S(2)}, u32[]{:S(2)}) collective-permute-start(bf16[64,512]{1,0:T(8,128)(2,1)S(1)} %get-tuple-element.78), channel_id=1, source_target_pairs={{4,0},{5,1},{6,2},{7,3},{0,4},{1,5},{2,6},{3,7},{12,8},{13,9},{14,... | collective-permute-start | bytes 196616 | tf_op jit(solution)/shard_map/ppermute | solution.py:68
  103.9 6.0 %collective-permute-start.29 = (bf16[64,512]{1,0:T(8,128)(2,1)S(1)}, bf16[64,512]{1,0:T(8,128)(2,1)S(1)}, u32[]{:S(2)}, u32[]{:S(2)}) collective-permute-start(bf16[64,512]{1,0:T(8,128)(2,1)S(1)} %get-tuple-element.79), channel_id=1, source_target_pairs={{5,0},{6,1},{7,2},{0,3},{1,4},{2,5},{3,6},{4,7},{13,8},{14,9},{15,... | collective-permute-start | bytes 196616 | tf_op jit(solution)/shard_map/ppermute | solution.py:68
  107.4 4.3 %collective-permute-start.30 = (bf16[64,512]{1,0:T(8,128)(2,1)S(1)}, bf16[64,512]{1,0:T(8,128)(2,1)S(1)}, u32[]{:S(2)}, u32[]{:S(2)}) collective-permute-start(bf16[64,512]{1,0:T(8,128)(2,1)S(1)} %get-tuple-element.80), channel_id=1, source_target_pairs={{6,0},{7,1},{0,2},{1,3},{2,4},{3,5},{4,6},{5,7},{14,8},{15,9},{8,1... | collective-permute-start | bytes 196616 | tf_op jit(solution)/shard_map/ppermute | solution.py:68
  107.4 4.3 %collective-permute-start.31 = (bf16[64,512]{1,0:T(8,128)(2,1)S(1)}, bf16[64,512]{1,0:T(8,128)(2,1)S(1)}, u32[]{:S(2)}, u32[]{:S(2)}) collective-permute-start(bf16[64,512]{1,0:T(8,128)(2,1)S(1)} %get-tuple-element.81), channel_id=1, source_target_pairs={{7,0},{0,1},{1,2},{2,3},{3,4},{4,5},{5,6},{6,7},{15,8},{8,9},{9,10... | collective-permute-start | bytes 196616 | tf_op jit(solution)/shard_map/ppermute | solution.py:68

commit v5 on v4

--- a/solution.py
+++ b/solution.py
@@ -44,6 +44,14 @@
     return out
 
 
+def chip_pairs(step):
+    return [(device_id(x, z, y, c), device_id(x, z, (y + step) % 4, c)) for x, z, y, c in all_coords()]
+
+
+def core_pairs():
+    return [(device_id(x, z, y, c), device_id(x, z, y, 1 - c)) for x, z, y, c in all_coords()]
+
+
 def moved(axis, step):
     out = []
     for x, z, y, c in all_coords():
@@ -139,7 +147,7 @@
 
 
 def lookup_kernel(meta, dest, ids_ref, table, *rest):
-    outs, (buffer, total, column, arrived) = rest[:8], rest[8:]
+    outs, (buffer, total, column, arrived) = rest[:4], rest[4:]
     tile = buffer.shape[1]
     copies = [
         pltpu.make_async_copy(table.at[0, 0, pl.ds(n * tile, tile), :], buffer.at[n], arrived.at[n])
@@ -162,16 +170,21 @@
         else:
             total[...] += part
     own = meta[2] * 2 + meta[3]
-    for k in range(8):
-        outs[k][...] = jnp.zeros_like(outs[k])
-        for p in range(NBLK):
-
-            @pl.when(dest[p, own] == lax.rem(own + k, 8))
-            def _():
-                outs[k][...] = total[p * BROWS : (p + 1) * BROWS, :].astype(BF)
-
-
-def prepare_kernel(meta, lengths, tile_mask, incoming, w_out, key_work, query_work, starts, begins, key_pos, query_pos, dmixed, turned, bounds):
+    for k in range(4):
+        for core in range(2):
+            place = slice(core * BROWS, (core + 1) * BROWS)
+            outs[k][place, :] = jnp.zeros((BROWS, WIDTH), BF)
+            for p in range(NBLK):
+
+                @pl.when(dest[p, own] == lax.rem(meta[2] + k, 4) * 2 + core)
+                def _():
+                    outs[k][place, :] = total[p * BROWS : (p + 1) * BROWS, :].astype(BF)
+
+
+def prepare_kernel(
+    meta, lengths, tile_mask, piece, key_work, query_work, starts, begins, key_pos, query_pos, passed, turned, bounds
+):
+    passed[...] = piece[...]
     row, core = line(meta)[1], meta[3]
     ends, end = [], jnp.int32(0)
     for d in range(lengths.shape[0]):
@@ -226,6 +239,9 @@
         for end in ends:
             begin = jnp.where(spot >= end, end, begin)
         starts[:, cols] = begin.astype(F32)
+
+
+def mix_kernel(incoming, w_out, dmixed):
     dmixed[...] = dot_nt(incoming[...], w_out[...])
 
 
@@ -234,14 +250,15 @@
     hist, pre = rest[:2]
     outs = rest[2:6]
     act, grads = rest[6:]
-    own = meta[2] * 2 + meta[3]
+    core = meta[3]
+    own = meta[2] * 2 + core
     for k in range(8):
-        source = lax.rem(own - k + 8, 8)
+        source = lax.rem(meta[2] - k % 4 + 4, 4) * 2 + (core if k < 4 else 1 - core)
         for p in range(NBLK):
 
             @pl.when(dest[p, source] == own)
             def _():
-                hist[ds(slot[p, source] * BROWS, BROWS), :] = blocks[k][...]
+                hist[ds(slot[p, source] * BROWS, BROWS), :] = blocks[k][ds(core * BROWS, BROWS), :]
 
     hat, _ = row_statistics(hist[...].astype(F32))
     normed = hat.astype(BF)
@@ -474,7 +491,7 @@
 
 
 def input_grad_kernel(meta, dest, slot, p0, p1, p2, p3, pre, dmixed, hist, incoming, w_in, *rest):
-    outs, (mixed, attn, d_act, result) = rest[:8], rest[8:]
+    outs, (mixed, attn, d_act, result) = rest[:4], rest[4:]
     for j, part in enumerate((p0, p1, p2, p3)):
         head = lax.rem(line(meta)[0] + j, 4) * HD
         d_act[:, ds(2 * WIDTH + head, HD)] = part[:, 0:HD].astype(F32)
@@ -492,30 +509,35 @@
     hat, inverse = row_statistics(hist[...].astype(F32))
     result[...] = (incoming[...].astype(F32) + norm_backward(total, hat, inverse)).astype(BF)
     own = meta[2] * 2 + meta[3]
-    for k in range(8):
-        outs[k][...] = jnp.zeros_like(outs[k])
-        source = lax.rem(own - k + 8, 8)
-        for p in range(NBLK):
-
-            @pl.when(dest[p, source] == own)
-            def _():
-                outs[k][...] = result[ds(slot[p, source] * BROWS, BROWS), :]
-
-
-def output_kernel(mixed, hist, w_out, out):
+    for k in range(4):
+        for core in range(2):
+            place = slice(core * BROWS, (core + 1) * BROWS)
+            outs[k][place, :] = jnp.zeros((BROWS, WIDTH), BF)
+            source = lax.rem(meta[2] - k + 4, 4) * 2 + core
+            for p in range(NBLK):
+
+                @pl.when(dest[p, source] == own)
+                def _():
+                    outs[k][place, :] = result[ds(slot[p, source] * BROWS, BROWS), :]
+
+
+def output_kernel(mixed, hist, w_out, block, out, passed):
+    passed[...] = block[...]
     out[...] = (hist[...].astype(F32) + dot(mixed[...], w_out[...])).astype(BF)
 
 
 def table_grad_kernel(meta, dest, ids, *rest):
     blocks, out, rows, buffer, sent = rest[:8], rest[8], rest[9], rest[10], rest[11]
     tile = buffer.shape[1]
-    own = meta[2] * 2 + meta[3]
+    core = meta[3]
+    own = meta[2] * 2 + core
     for k in range(8):
+        owner = lax.rem(meta[2] + k % 4, 4) * 2 + (core if k < 4 else 1 - core)
         for p in range(NBLK):
 
-            @pl.when(dest[p, own] == lax.rem(own + k, 8))
+            @pl.when(dest[p, own] == owner)
             def _():
-                rows[p * BROWS : (p + 1) * BROWS, :] = blocks[k][...]
+                rows[p * BROWS : (p + 1) * BROWS, :] = blocks[k][ds(core * BROWS, BROWS), :]
 
     number = lax.broadcasted_iota(jnp.int32, (tile, ROWS), 0)
     copies = []
@@ -534,25 +556,6 @@
     slot = slots[0].T
     tab_rows = table.shape[2]
 
-    key_work, query_work, starts, begins, key_pos, query_pos, dmixed = call(
-        prepare_kernel,
-        [lengths[0], tile_mask[0], output_gradient[0], w_out],
-        [SMEM] + [VMEM] * 3,
-        [
-            shape((2 * ITEMS + 1,), jnp.int32),
-            shape((2 * ITEMS + 1,), jnp.int32),
-            shape((8, LENGTH), F32),
-            shape((LENGTH // 4, CHUNK), F32),
-            shape((16, LENGTH), F32),
-            shape((16, LENGTH), F32),
-            shape((ROWS, WIDTH), F32),
-        ],
-        [pltpu.VMEM((64, 64), F32), pltpu.SMEM((16,), jnp.int32)],
-        flops=2 * ROWS * WIDTH * WIDTH,
-        name="prepare",
-        out_specs=[SMEM] * 2 + [VMEM] * 5,
-    )
-
     tiles = 8
     tile = tab_rows // tiles
     block_shape = shape((BROWS, WIDTH), BF)
@@ -560,7 +563,7 @@
         lookup_kernel,
         [dest, row_ids.reshape(2, CHUNK), table],
         [SMEM, VMEM, pl.BlockSpec(memory_space=pltpu.HBM)],
-        [block_shape] * 8,
+        [shape((2 * BROWS, WIDTH), BF)] * 4,
         [
             pltpu.VMEM((tiles, tile, WIDTH), BF),
             pltpu.VMEM((ROWS, WIDTH), F32),
@@ -571,7 +574,18 @@
         name="lookup",
         limit=60,
     )
-    blocks = [outgoing[0]] + [send(outgoing[k], tab_pairs(k)) for k in range(1, 8)]
+    near = [outgoing[0]] + [send(outgoing[k], chip_pairs(k)) for k in range(1, 4)]
+    blocks = near + [send(v, core_pairs()) for v in near]
+
+    (dmixed,) = call(
+        mix_kernel,
+        [output_gradient[0], w_out],
+        [VMEM] * 2,
+        [shape((ROWS, WIDTH), F32)],
+        flops=10**9,
+        name="mix",
+        placed=False,
+    )
 
     four = shape((ROWS, 4 * HD), BF)
     two = shape((ROWS, 2 * HD), BF)
@@ -598,9 +612,28 @@
         flops=2 * ROWS * WIDTH * 4 * WIDTH,
         name="project",
     )
+    key_work, query_work, starts, begins, key_pos, query_pos, passed = call(
+        prepare_kernel,
+        [lengths[0], tile_mask[0], pieces[0]],
+        [SMEM] + [VMEM] * 2,
+        [
+            shape((2 * ITEMS + 1,), jnp.int32),
+            shape((2 * ITEMS + 1,), jnp.int32),
+            shape((8, LENGTH), F32),
+            shape((LENGTH // 4, CHUNK), F32),
+            shape((16, LENGTH), F32),
+            shape((16, LENGTH), F32),
+            four,
+        ],
+        [pltpu.VMEM((64, 64), F32), pltpu.SMEM((16,), jnp.int32)],
+        flops=3 * 10**9,
+        name="prepare",
+        out_specs=[SMEM] * 2 + [VMEM] * 5,
+    )
+
     own_keys, queries, grads = call(
         collect_kernel,
-        [*to_heads(pieces)],
+        [passed, *to_heads(pieces)[1:]],
         [VMEM] * 4,
         [rows_two, rows_one, rows_one],
         name="collect",
@@ -649,7 +682,7 @@
         input_grad_kernel,
         [dest, slot, *to_owners(back_parts), pre, dmixed, hist, incoming, w_in],
         [SMEM] * 2 + [VMEM] * 9,
-        [block_shape] * 8 + [shape((ROWS, WIDTH), BF)],
+        [shape((2 * BROWS, WIDTH), BF)] * 4 + [shape((ROWS, WIDTH), BF)],
         [
             pltpu.VMEM((ROWS, WIDTH), F32),
             pltpu.VMEM((ROWS, 3 * WIDTH), F32),
@@ -658,16 +691,17 @@
         flops=8 * ROWS * WIDTH * WIDTH,
         name="input_grad",
     )
-    (layer_out,) = call(
+    layer_out, passed = call(
         output_kernel,
-        [mixed, hist, w_out],
-        [VMEM] * 3,
-        [shape((ROWS, WIDTH), BF)],
+        [mixed, hist, w_out, returning[0]],
+        [VMEM] * 4,
+        [shape((ROWS, WIDTH), BF), shape((2 * BROWS, WIDTH), BF)],
         flops=2 * ROWS * WIDTH * WIDTH,
         name="output",
         placed=False,
     )
-    came_back = [returning[0]] + [send(returning[k], back(tab_pairs(k))) for k in range(1, 8)]
+    near = [passed] + [send(returning[k], back(chip_pairs(k))) for k in range(1, 4)]
+    came_back = near + [send(v, core_pairs()) for v in near]
     (table_grad,) = call(
         table_grad_kernel,
         [dest, row_ids.reshape(1, ROWS), *came_back],

time: 116 us -> 115 us (level)
  Pallas kernels: 27.9 us -> 33.5 us
  waiting for transfers between devices: 32.8 us -> 27.5 us
    pallas_call x11 -> x12, Pallas kernels: 27.9 us -> 33.5 us  [call(): pl.pallas_call(with_place(kernel) if placed else kernel, out_shape=outs,...]
    ppermute x32, waiting for transfers between devices: 32.8 us -> 27.5 us  [send(): return lax.ppermute(value, AXES, pairs)]
  transfers between devices with their start and end apart: 32 -> 32, of which waited for: 13 -> 13; matrix products, arithmetic and copies ran while one was open for 0% -> 0% of each run, Pallas kernels for 9% -> 14%
where the time goes in v5:
time: 115 us
  starting transfers between devices  53 us (46%)
  Pallas kernels  33.5 us (29%)
  waiting for transfers between devices  27.5 us (24%)
    ppermute x32, starting transfers between devices, send(): return lax.ppermute(value, AXES, pairs)  53 us
    pallas_call x12, Pallas kernels, call(): pl.pallas_call(with_place(kernel) if placed else kernel, out_shape=outs,...  33.5 us
    ppermute x32, waiting for transfers between devices, send(): return lax.ppermute(value, AXES, pairs)  27.5 us
  transfers between devices with their start and end apart: 32, of which 13 were waited for; matrix products, arithmetic and copies ran while one was open for 0% of the time, Pallas kernels for 14%

profile of v5, /device:TPU:1, one launch (start us, length us, event | category | flops | bytes accessed | tf_op | source)
XLA Modules:
  0.0 115.1 jit_solution(14834524262172531863)
XLA Ops:
  0.6 4.9 %lookup.1 = (bf16[128,512]{1,0:T(8,128)(2,1)}, bf16[128,512]{1,0:T(8,128)(2,1)}, bf16[128,512]{1,0:T(8,128)(2,1)}, bf16[128,512]{1,0:T(8,128)(2,1)}) custom-call(s32[4,8]{1,0:T(4,128)} %bitcast.14, s32[2,128]{1,0:T(2,128)} %bitcast.20, bf16[1,1,4096,512]{3,2,1,0:T(8,128)(2,1)} %refs_2_.1), custom_call_target="tpu_custom_call" | custom-call | flops 1073741824 | bytes 4719744 | tf_op jit(solution)/shard_map/lookup/pallas_call | solution.py:130
  5.5 0.0 copy-start
  5.6 0.0 copy-start.3
  5.6 0.0 copy-start.4
  5.6 0.0 copy-start.5
  5.6 2.2 %collective-permute-start = (bf16[128,512]{1,0:T(8,128)(2,1)}, bf16[128,512]{1,0:T(8,128)(2,1)S(1)}, u32[]{:S(2)}, u32[]{:S(2)}) collective-permute-start(bf16[128,512]{1,0:T(8,128)(2,1)} %get-tuple-element.37), channel_id=1, source_target_pairs={{0,2},{1,3},{2,4},{3,5},{4,6},{5,7},{6,0},{7,1},{8,10},{9,11},{10,... | collective-permute-start | bytes 393224 | tf_op jit(solution)/shard_map/ppermute | solution.py:76
  7.8 2.6 %collective-permute-start.1 = (bf16[128,512]{1,0:T(8,128)(2,1)}, bf16[128,512]{1,0:T(8,128)(2,1)S(1)}, u32[]{:S(2)}, u32[]{:S(2)}) collective-permute-start(bf16[128,512]{1,0:T(8,128)(2,1)} %get-tuple-element.38), channel_id=1, source_target_pairs={{0,4},{1,5},{2,6},{3,7},{4,0},{5,1},{6,2},{7,3},{8,12},{9,13},{10,... | collective-permute-start | bytes 393224 | tf_op jit(solution)/shard_map/ppermute | solution.py:76
  10.4 1.1 collective-permute-start.2
  11.5 1.5 %collective-permute-start.3 = (bf16[128,512]{1,0:T(8,128)(2,1)}, bf16[128,512]{1,0:T(8,128)(2,1)S(1)}, u32[]{:S(2)}, u32[]{:S(2)}) collective-permute-start(bf16[128,512]{1,0:T(8,128)(2,1)} %get-tuple-element.36.refs_2_), channel_id=1, source_target_pairs={{0,1},{1,0},{2,3},{3,2},{4,5},{5,4},{6,7},{7,6},{8,9},{9,8},{10,11... | collective-permute-start | bytes 393224 | tf_op jit(solution)/shard_map/ppermute | solution.py:76
  13.0 0.0 collective-permute-done.refs_3_
  13.0 0.9 collective-permute-start.4
  13.9 2.4 %collective-permute-done.1.refs_4_ = bf16[128,512]{1,0:T(8,128)(2,1)S(1)} collective-permute-done((bf16[128,512]{1,0:T(8,128)(2,1)}, bf16[128,512]{1,0:T(8,128)(2,1)S(1)}, u32[]{:S(2)}, u32[]{:S(2)}) %collective-permute-start.1) | collective-permute-done | bytes 131104 | tf_op jit(solution)/shard_map/ppermute | solution.py:76
  16.3 1.5 %collective-permute-start.5 = (bf16[128,512]{1,0:T(8,128)(2,1)S(1)}, bf16[128,512]{1,0:T(8,128)(2,1)S(1)}, u32[]{:S(2)}, u32[]{:S(2)}) collective-permute-start(bf16[128,512]{1,0:T(8,128)(2,1)S(1)} %collective-permute-done.1.refs_4_), channel_id=1, source_target_pairs={{0,1},{1,0},{2,3},{3,2},{4,5},{5,4},{6,7},{7,6},{8,9},{9,8},{10,11... | collective-permute-start | bytes 393224 | tf_op jit(solution)/shard_map/ppermute | solution.py:76
  17.9 0.0 collective-permute-done.2.refs_5_
  17.9 0.0 collective-permute-start.6
  17.9 0.3 mix.1.refs_11_.refs_7_
  18.2 0.0 copy-start.7
  18.2 0.0 copy-start.8
  18.3 0.6 collective-permute-done.5.refs_8_
  18.9 0.4 collective-permute-done.6.refs_9_
  19.2 2.4 %project.1 = (bf16[256,512]{1,0:T(8,128)(2,1)S(1)}, f32[256,2048]{1,0:T(8,128)S(1)}, bf16[256,512]{1,0:T(8,128)(2,1)S(1)}, bf16[256,512]{1,0:T(8,128)(2,1)S(1)},...) custom-call(s32[4,8]{1,0:T(4,128)S(1)} %bitcast.15, s32[4,8]{1,0:T(4,128)S(1)} %bitcast.18, ...), custom_call_target="tpu_custom_call" | custom-call | flops 536870912 | bytes 7078144 | tf_op jit(solution)/shard_map/project/pallas_call | solution.py:130
  21.7 1.7 %collective-permute-start.7 = (bf16[256,512]{1,0:T(8,128)(2,1)S(1)}, bf16[256,512]{1,0:T(8,128)(2,1)S(1)}, u32[]{:S(2)}, u32[]{:S(2)}) collective-permute-start(bf16[256,512]{1,0:T(8,128)(2,1)S(1)} %get-tuple-element.45), channel_id=1, source_target_pairs={{0,32},{1,9},{2,34},{3,11},{4,36},{5,13},{6,38},{7,15},{8,40},{9,1... | collective-permute-start | bytes 786440 | tf_op jit(solution)/shard_map/ppermute | solution.py:76
  23.4 3.3 %collective-permute-start.8 = (bf16[256,512]{1,0:T(8,128)(2,1)S(1)}, bf16[256,512]{1,0:T(8,128)(2,1)S(1)}, u32[]{:S(2)}, u32[]{:S(2)}) collective-permute-start(bf16[256,512]{1,0:T(8,128)(2,1)S(1)} %get-tuple-element.46), channel_id=1, source_target_pairs={{0,64},{1,17},{2,66},{3,19},{4,68},{5,21},{6,70},{7,23},{8,72},{9,... | collective-permute-start | bytes 786440 | tf_op jit(solution)/shard_map/ppermute | solution.py:76
  26.7 0.7 collective-permute-start.9
  27.4 2.7 %prepare.1 = (s32[257]{0:T(512)S(1)}, s32[257]{0:T(512)S(1)}, f32[8,4096]{1,0:T(8,128)S(1)}, f32[1024,128]{1,0:T(8,128)S(1)}, f32[16,4096]{1,0:T(8,128)S(1)}, /*...) custom-call(s32[16]{0:T(128)S(1)} %bitcast.23, s32[64,64]{1,0:T(8,128)S(1)} %bitcast.22, ...), custom_call_target="tpu_custom_call" | custom-call | flops 3000000000 | bytes 1722440 | tf_op jit(solution)/shard_map/prepare/pallas_call | solution.py:130
  30.2 3.1 %collective-permute-done.8.refs_2_ = bf16[256,512]{1,0:T(8,128)(2,1)S(1)} collective-permute-done((bf16[256,512]{1,0:T(8,128)(2,1)S(1)}, bf16[256,512]{1,0:T(8,128)(2,1)S(1)}, u32[]{:S(2)}, u32[]{:S(2)}) %collective-permute-start.8) | collective-permute-done | bytes 262176 | tf_op jit(solution)/shard_map/ppermute | solution.py:76
  33.3 0.1 collect.1
  33.4 1.3 %collective-permute-start.13 = (bf16[1024,256]{1,0:T(8,128)(2,1)S(1)}, bf16[1024,256]{1,0:T(8,128)(2,1)S(1)}, u32[]{:S(2)}, u32[]{:S(2)}) collective-permute-start(bf16[1024,256]{1,0:T(8,128)(2,1)S(1)} %get-tuple-element.48.refs_3_), channel_id=1, source_target_pairs={{0,8},{1,33},{2,10},{3,35},{4,12},{5,37},{6,14},{7,39},{8,16},{9,4... | collective-permute-start | bytes 1572872 | tf_op jit(solution)/shard_map/ppermute | solution.py:76
  34.7 2.5 %collective-permute-start.14 = (bf16[1024,256]{1,0:T(8,128)(2,1)S(1)}, bf16[1024,256]{1,0:T(8,128)(2,1)S(1)}, u32[]{:S(2)}, u32[]{:S(2)}) collective-permute-start(bf16[1024,256]{1,0:T(8,128)(2,1)S(1)} %get-tuple-element.48.refs_3_), channel_id=1, source_target_pairs={{0,16},{1,65},{2,18},{3,67},{4,20},{5,69},{6,22},{7,71},{8,24},{9,... | collective-permute-start | bytes 1572872 | tf_op jit(solution)/shard_map/ppermute | solution.py:76
  37.1 1.2 %collective-permute-start.15 = (bf16[1024,256]{1,0:T(8,128)(2,1)S(1)}, bf16[1024,256]{1,0:T(8,128)(2,1)S(1)}, u32[]{:S(2)}, u32[]{:S(2)}) collective-permute-start(bf16[1024,256]{1,0:T(8,128)(2,1)S(1)} %get-tuple-element.48.refs_3_), channel_id=1, source_target_pairs={{0,24},{1,97},{2,26},{3,99},{4,28},{5,101},{6,30},{7,103},{8,0},{9... | collective-permute-start | bytes 1572872 | tf_op jit(solution)/shard_map/ppermute | solution.py:76
  38.3 0.3 collective-permute-start.10
  38.6 0.9 collective-permute-start.11
  39.5 3.5 %collective-permute-done.13.refs_4_ = bf16[1024,256]{1,0:T(8,128)(2,1)S(1)} collective-permute-done((bf16[1024,256]{1,0:T(8,128)(2,1)S(1)}, bf16[1024,256]{1,0:T(8,128)(2,1)S(1)}, u32[]{:S(2)}, u32[]{:S(2)}) %collective-permute-start.13) | collective-permute-done | bytes 524320 | tf_op jit(solution)/shard_map/ppermute | solution.py:76
  43.0 1.3 %collective-permute-start.12 = (bf16[1024,128]{1,0:T(8,128)(2,1)S(1)}, bf16[1024,128]{1,0:T(8,128)(2,1)S(1)}, u32[]{:S(2)}, u32[]{:S(2)}) collective-permute-start(bf16[1024,128]{1,0:T(8,128)(2,1)S(1)} %get-tuple-element.49.refs_7_.refs_4_), channel_id=1, source_target_pairs={{0,24},{1,97},{2,26},{3,99},{4,28},{5,101},{6,30},{7,103},{8,0},{9... | collective-permute-start | bytes 786440 | tf_op jit(solution)/shard_map/ppermute | solution.py:76
  44.3 5.4 %collective-permute-done.14.refs_5_ = bf16[1024,256]{1,0:T(8,128)(2,1)S(1)} collective-permute-done((bf16[1024,256]{1,0:T(8,128)(2,1)S(1)}, bf16[1024,256]{1,0:T(8,128)(2,1)S(1)}, u32[]{:S(2)}, u32[]{:S(2)}) %collective-permute-start.14) | collective-permute-done | bytes 524320 | tf_op jit(solution)/shard_map/ppermute | solution.py:76
  49.6 5.7 %forward.1 = (bf16[4096,256]{1,0:T(8,128)(2,1)S(1)}, f32[1024,128]{1,0:T(8,128)S(1)}, f32[8,1024]{1,0:T(8,128)S(1)}) custom-call(s32[257]{0:T(512)S(1)} %get-tuple-element.50.refs_0_, f32[1024,128]{1,0:T(8,128)S(1)} %get-tuple-element.51.refs_1_, f32[16,4096]{1,0:T(8,128)S(1)} %get-tuple-element.52.refs_2_, bf16[1024,256]{1,0:T(8,128)(2,1)S(1)} %get-tuple-element.48.refs_3_, ...), custom_call_target="tpu_custom_call" | custom-call | flops 6000000000 | bytes 6063108 | tf_op jit(solution)/shard_map/forward/pallas_call | solution.py:130
  55.3 0.9 collective-permute-start.16
  56.2 2.3 %collective-permute-start.17 = (f32[8,1024]{1,0:T(8,128)S(1)}, f32[8,1024]{1,0:T(8,128)S(1)}, u32[]{:S(2)}, u32[]{:S(2)}) collective-permute-start(f32[8,1024]{1,0:T(8,128)S(1)} %get-tuple-element.54.s0), channel_id=1, source_target_pairs={{0,64},{1,17},{2,66},{3,19},{4,68},{5,21},{6,70},{7,23},{8,72},{9,... | collective-permute-start | bytes 98312 | tf_op jit(solution)/shard_map/ppermute | solution.py:76
  58.5 1.0 collective-permute-start.18
  59.5 1.0 collective-permute-done.17.s2
  60.5 1.1 collective-permute-done.18.s3
  61.5 0.6 attn_grad.1.refs_5_.refs_8_
  62.2 0.6 collective-permute-start.19
  62.8 1.1 collective-permute-start.20
  63.9 2.0 %collective-permute-start.21 = (bf16[1024,128]{1,0:T(8,128)(2,1)S(1)}, bf16[1024,128]{1,0:T(8,128)(2,1)S(1)}, u32[]{:S(2)}, u32[]{:S(2)}) collective-permute-start(bf16[1024,128]{1,0:T(8,128)(2,1)S(1)} %attn_grad.1.refs_5_.refs_8_), channel_id=1, source_target_pairs={{0,24},{1,97},{2,26},{3,99},{4,28},{5,101},{6,30},{7,103},{8,0},{9... | collective-permute-start | bytes 786440 | tf_op jit(solution)/shard_map/ppermute | solution.py:76
  65.9 6.0 %query_grad.1.refs_12_ = bf16[1024,128]{1,0:T(8,128)(2,1)S(1)} custom-call(s32[257]{0:T(512)S(1)} %get-tuple-element.50.refs_0_, f32[1024,128]{1,0:T(8,128)S(1)} %get-tuple-element.51.refs_1_, f32[16,4096]{1,0:T(8,128)S(1)} %get-tuple-element.52.refs_2_, bf16[4096,256]{1,0:T(8,128)(2,1)S(1)} %get-tuple-element.56.refs_3_, ...), custom_call_target="tpu_custom_call" | custom-call | flops 6000000000 | bytes 3671044 | tf_op jit(solution)/shard_map/query_grad/pallas_call | solution.py:130
  72.0 0.4 collective-permute-done.21.refs_11_
  72.4 3.8 %key_grad.1 = (bf16[256,512]{1,0:T(8,128)(2,1)S(1)}, bf16[256,512]{1,0:T(8,128)(2,1)S(1)}, bf16[256,512]{1,0:T(8,128)(2,1)S(1)}, bf16[256,512]{1,0:T(8,128)(2,1)S(1)}) custom-call(s32[257]{0:T(512)S(1)} %get-tuple-element.41.refs_0_, f32[8,4096]{1,0:T(8,128)S(1)} %get-tuple-element.42.refs_1_, f32[16,4096]{1,0:T(8,128)S(1)} %get-tuple-element.43.refs_2_, ...), custom_call_target="tpu_custom_call" | custom-call | flops 7000000000 | bytes 4850692 | tf_op jit(solution)/shard_map/key_grad/pallas_call | solution.py:130
  76.2 2.0 %collective-permute-start.22 = (bf16[256,512]{1,0:T(8,128)(2,1)S(1)}, bf16[256,512]{1,0:T(8,128)(2,1)S(1)}, u32[]{:S(2)}, u32[]{:S(2)}) collective-permute-start(bf16[256,512]{1,0:T(8,128)(2,1)S(1)} %get-tuple-element.58), channel_id=1, source_target_pairs={{32,0},{9,1},{34,2},{11,3},{36,4},{13,5},{38,6},{15,7},{40,8},{17,... | collective-permute-start | bytes 786440 | tf_op jit(solution)/shard_map/ppermute | solution.py:76
  78.2 0.0 collective-permute-start.23
  78.2 0.7 collective-permute-start.24
  78.8 5.5 %collective-permute-done.22.refs_3_ = bf16[256,512]{1,0:T(8,128)(2,1)S(1)} collective-permute-done((bf16[256,512]{1,0:T(8,128)(2,1)S(1)}, bf16[256,512]{1,0:T(8,128)(2,1)S(1)}, u32[]{:S(2)}, u32[]{:S(2)}) %collective-permute-start.22) | collective-permute-done | bytes 262176 | tf_op jit(solution)/shard_map/ppermute | solution.py:76
  84.3 0.7 collective-permute-done.23.refs_4_
  85.0 2.4 %collective-permute-done.24.refs_5_ = bf16[256,512]{1,0:T(8,128)(2,1)S(1)} collective-permute-done((bf16[256,512]{1,0:T(8,128)(2,1)S(1)}, bf16[256,512]{1,0:T(8,128)(2,1)S(1)}, u32[]{:S(2)}, u32[]{:S(2)}) %collective-permute-start.24) | collective-permute-done | bytes 262176 | tf_op jit(solution)/shard_map/ppermute | solution.py:76
  87.4 2.7 %input_grad.1 = (bf16[128,512]{1,0:T(8,128)(2,1)S(1)}, bf16[128,512]{1,0:T(8,128)(2,1)S(1)}, bf16[128,512]{1,0:T(8,128)(2,1)S(1)}, bf16[128,512]{1,0:T(8,128)(2,1)S(1)}, bf16[256,512]{1,0:T(8,128)(2,1)S(1)}) custom-call(s32[4,8]{1,0:T(4,128)S(1)} %bitcast.16, s32[4,8]{1,0:T(4,128)S(1)} %bitcast.19, bf16[256,512]{1,0:T(8,128)(2,1)S(1)} %get-tuple-element.57.refs_2_, ...), custom_call_target="tpu_custom_call" | custom-call | flops 536870912 | bytes 7078144 | tf_op jit(solution)/shard_map/input_grad/pallas_call | solution.py:130
  90.1 5.3 %collective-permute-start.25 = (bf16[128,512]{1,0:T(8,128)(2,1)S(1)}, bf16[128,512]{1,0:T(8,128)(2,1)S(1)}, u32[]{:S(2)}, u32[]{:S(2)}) collective-permute-start(bf16[128,512]{1,0:T(8,128)(2,1)S(1)} %get-tuple-element.67), channel_id=1, source_target_pairs={{2,0},{3,1},{4,2},{5,3},{6,4},{7,5},{0,6},{1,7},{10,8},{11,9},{12,... | collective-permute-start | bytes 393224 | tf_op jit(solution)/shard_map/ppermute | solution.py:76
  95.4 0.7 collective-permute-start.27
  96.0 1.0 output.1
  97.1 8.0 %collective-permute-start.28 = (bf16[128,512]{1,0:T(8,128)(2,1)S(1)}, bf16[128,512]{1,0:T(8,128)(2,1)S(1)}, u32[]{:S(2)}, u32[]{:S(2)}) collective-permute-start(bf16[128,512]{1,0:T(8,128)(2,1)S(1)} %get-tuple-element.66.refs_2_), channel_id=1, source_target_pairs={{0,1},{1,0},{2,3},{3,2},{4,5},{5,4},{6,7},{7,6},{8,9},{9,8},{10,11... | collective-permute-start | bytes 393224 | tf_op jit(solution)/shard_map/ppermute | solution.py:76
  105.0 2.0 %collective-permute-start.29 = (bf16[128,512]{1,0:T(8,128)(2,1)S(1)}, bf16[128,512]{1,0:T(8,128)(2,1)S(1)}, u32[]{:S(2)}, u32[]{:S(2)}) collective-permute-start(bf16[128,512]{1,0:T(8,128)(2,1)S(1)} %collective-permute-done.25.refs_3_), channel_id=1, source_target_pairs={{0,1},{1,0},{2,3},{3,2},{4,5},{5,4},{6,7},{7,6},{8,9},{9,8},{10,11... | collective-permute-start | bytes 393224 | tf_op jit(solution)/shard_map/ppermute | solution.py:76
  107.0 2.6 %collective-permute-start.30 = (bf16[128,512]{1,0:T(8,128)(2,1)S(1)}, bf16[128,512]{1,0:T(8,128)(2,1)S(1)}, u32[]{:S(2)}, u32[]{:S(2)}) collective-permute-start(bf16[128,512]{1,0:T(8,128)(2,1)S(1)} %collective-permute-done.26.refs_4_), channel_id=1, source_target_pairs={{0,1},{1,0},{2,3},{3,2},{4,5},{5,4},{6,7},{7,6},{8,9},{9,8},{10,11... | collective-permute-start | bytes 393224 | tf_op jit(solution)/shard_map/ppermute | solution.py:76
  109.6 1.0 collective-permute-start.31
  110.7 1.0 collective-permute-done.31.refs_9_
  111.6 3.2 %table_grad.1 = bf16[1,1,4096,512]{3,2,1,0:T(8,128)(2,1)} custom-call(s32[4,8]{1,0:T(4,128)S(1)} %bitcast.17, s32[1,256]{1,0:T(1,128)S(1)} %bitcast.21, bf16[128,512]{1,0:T(8,128)(2,1)S(1)} %get-tuple-element.66.refs_2_, bf16[128,512]{1,0:T(8,128)(2,1)S(1)} %collective-permute-done.25.refs_3_, bf16[128,512]{1,0:T(8,128)(2,1)S(1)} %collective-permute-done.26.refs_4_, ...), custom_call_target="tpu_custom_call" | custom-call | flops 1073741824 | bytes 5244032 | tf_op jit(solution)/shard_map/table_grad/pallas_call | solution.py:130
  (30 shorter events, 0.1 us)
Async XLA Ops:
  0.6 17.2 %copy-start.1 = (bf16[512,512]{1,0:T(8,128)(2,1)S(1)}, bf16[512,512]{1,0:T(8,128)(2,1)}, u32[]{:S(2)}) copy-start(bf16[512,512]{1,0:T(8,128)(2,1)} %w_out.3) | copy-start | bytes 1572868
  0.6 17.2 %copy-start.2 = (bf16[1,256,512]{2,1,0:T(8,128)(2,1)S(1)}, bf16[1,256,512]{2,1,0:T(8,128)(2,1)}, u32[]{:S(2)}) copy-start(bf16[1,256,512]{2,1,0:T(8,128)(2,1)} %param.17) | copy-start | bytes 786436
  5.5 13.7 %copy-start = (bf16[512,2048]{1,0:T(8,128)(2,1)S(1)}, bf16[512,2048]{1,0:T(8,128)(2,1)}, u32[]{:S(2)}) copy-start(bf16[512,2048]{1,0:T(8,128)(2,1)} %refs_10_.3) | copy-start | bytes 6291460
  5.6 13.7 %copy-start.3 = (bf16[128,512]{1,0:T(8,128)(2,1)S(1)}, bf16[128,512]{1,0:T(8,128)(2,1)}, u32[]{:S(2)}) copy-start(bf16[128,512]{1,0:T(8,128)(2,1)} %get-tuple-element.36.refs_2_) | copy-start | bytes 393220
  5.6 13.7 %copy-start.4 = (s32[1,8,4]{1,2,0:T(4,128)S(1)}, s32[1,8,4]{1,2,0:T(4,128)}, u32[]{:S(2)}) copy-start(s32[1,8,4]{1,2,0:T(4,128)} %param.11) | copy-start | bytes 388
  5.6 13.7 %copy-start.5 = (s32[1,8,4]{1,2,0:T(4,128)S(1)}, s32[1,8,4]{1,2,0:T(4,128)}, u32[]{:S(2)}) copy-start(s32[1,8,4]{1,2,0:T(4,128)} %param.12) | copy-start | bytes 388
  5.6 7.4 %collective-permute-start = (bf16[128,512]{1,0:T(8,128)(2,1)}, bf16[128,512]{1,0:T(8,128)(2,1)S(1)}, u32[]{:S(2)}, u32[]{:S(2)}) collective-permute-start(bf16[128,512]{1,0:T(8,128)(2,1)} %get-tuple-element.37), channel_id=1, source_target_pairs={{0,2},{1,3},{2,4},{3,5},{4,6},{5,7},{6,0},{7,1},{8,10},{9,11},{10,... | collective-permute-start | bytes 393224 | tf_op jit(solution)/shard_map/ppermute | solution.py:76
  7.8 8.5 %collective-permute-start.1 = (bf16[128,512]{1,0:T(8,128)(2,1)}, bf16[128,512]{1,0:T(8,128)(2,1)S(1)}, u32[]{:S(2)}, u32[]{:S(2)}) collective-permute-start(bf16[128,512]{1,0:T(8,128)(2,1)} %get-tuple-element.38), channel_id=1, source_target_pairs={{0,4},{1,5},{2,6},{3,7},{4,0},{5,1},{6,2},{7,3},{8,12},{9,13},{10,... | collective-permute-start | bytes 393224 | tf_op jit(solution)/shard_map/ppermute | solution.py:76
  10.4 7.5 %collective-permute-start.2 = (bf16[128,512]{1,0:T(8,128)(2,1)}, bf16[128,512]{1,0:T(8,128)(2,1)S(1)}, u32[]{:S(2)}, u32[]{:S(2)}) collective-permute-start(bf16[128,512]{1,0:T(8,128)(2,1)} %get-tuple-element.39), channel_id=1, source_target_pairs={{0,6},{1,7},{2,0},{3,1},{4,2},{5,3},{6,4},{7,5},{8,14},{9,15},{10,... | collective-permute-start | bytes 393224 | tf_op jit(solution)/shard_map/ppermute | solution.py:76
  11.5 6.8 %collective-permute-start.3 = (bf16[128,512]{1,0:T(8,128)(2,1)}, bf16[128,512]{1,0:T(8,128)(2,1)S(1)}, u32[]{:S(2)}, u32[]{:S(2)}) collective-permute-start(bf16[128,512]{1,0:T(8,128)(2,1)} %get-tuple-element.36.refs_2_), channel_id=1, source_target_pairs={{0,1},{1,0},{2,3},{3,2},{4,5},{5,4},{6,7},{7,6},{8,9},{9,8},{10,11... | collective-permute-start | bytes 393224 | tf_op jit(solution)/shard_map/ppermute | solution.py:76
  13.0 5.3 %collective-permute-start.4 = (bf16[128,512]{1,0:T(8,128)(2,1)S(1)}, bf16[128,512]{1,0:T(8,128)(2,1)S(1)}, u32[]{:S(2)}, u32[]{:S(2)}) collective-permute-start(bf16[128,512]{1,0:T(8,128)(2,1)S(1)} %collective-permute-done.refs_3_), channel_id=1, source_target_pairs={{0,1},{1,0},{2,3},{3,2},{4,5},{5,4},{6,7},{7,6},{8,9},{9,8},{10,11... | collective-permute-start | bytes 393224 | tf_op jit(solution)/shard_map/ppermute | solution.py:76
  16.3 2.5 %collective-permute-start.5 = (bf16[128,512]{1,0:T(8,128)(2,1)S(1)}, bf16[128,512]{1,0:T(8,128)(2,1)S(1)}, u32[]{:S(2)}, u32[]{:S(2)}) collective-permute-start(bf16[128,512]{1,0:T(8,128)(2,1)S(1)} %collective-permute-done.1.refs_4_), channel_id=1, source_target_pairs={{0,1},{1,0},{2,3},{3,2},{4,5},{5,4},{6,7},{7,6},{8,9},{9,8},{10,11... | collective-permute-start | bytes 393224 | tf_op jit(solution)/shard_map/ppermute | solution.py:76
  17.9 1.3 %collective-permute-start.6 = (bf16[128,512]{1,0:T(8,128)(2,1)S(1)}, bf16[128,512]{1,0:T(8,128)(2,1)S(1)}, u32[]{:S(2)}, u32[]{:S(2)}) collective-permute-start(bf16[128,512]{1,0:T(8,128)(2,1)S(1)} %collective-permute-done.2.refs_5_), channel_id=1, source_target_pairs={{0,1},{1,0},{2,3},{3,2},{4,5},{5,4},{6,7},{7,6},{8,9},{9,8},{10,11... | collective-permute-start | bytes 393224 | tf_op jit(solution)/shard_map/ppermute | solution.py:76
  18.2 9.2 %copy-start.7 = (s32[1,64,64]{2,1,0:T(8,128)S(1)}, s32[1,64,64]{2,1,0:T(8,128)}, u32[]{:S(2)}) copy-start(s32[1,64,64]{2,1,0:T(8,128)} %param.14) | copy-start | bytes 49156
  18.2 9.2 %copy-start.8 = (s32[1,16]{1,0:T(1,128)S(1)}, s32[1,16]{1,0:T(1,128)}, u32[]{:S(2)}) copy-start(s32[1,16]{1,0:T(1,128)} %param.13) | copy-start | bytes 196
  21.7 8.5 %collective-permute-start.7 = (bf16[256,512]{1,0:T(8,128)(2,1)S(1)}, bf16[256,512]{1,0:T(8,128)(2,1)S(1)}, u32[]{:S(2)}, u32[]{:S(2)}) collective-permute-start(bf16[256,512]{1,0:T(8,128)(2,1)S(1)} %get-tuple-element.45), channel_id=1, source_target_pairs={{0,32},{1,9},{2,34},{3,11},{4,36},{5,13},{6,38},{7,15},{8,40},{9,1... | collective-permute-start | bytes 786440 | tf_op jit(solution)/shard_map/ppermute | solution.py:76
  23.4 9.9 %collective-permute-start.8 = (bf16[256,512]{1,0:T(8,128)(2,1)S(1)}, bf16[256,512]{1,0:T(8,128)(2,1)S(1)}, u32[]{:S(2)}, u32[]{:S(2)}) collective-permute-start(bf16[256,512]{1,0:T(8,128)(2,1)S(1)} %get-tuple-element.46), channel_id=1, source_target_pairs={{0,64},{1,17},{2,66},{3,19},{4,68},{5,21},{6,70},{7,23},{8,72},{9,... | collective-permute-start | bytes 786440 | tf_op jit(solution)/shard_map/ppermute | solution.py:76
  26.7 6.6 %collective-permute-start.9 = (bf16[256,512]{1,0:T(8,128)(2,1)S(1)}, bf16[256,512]{1,0:T(8,128)(2,1)S(1)}, u32[]{:S(2)}, u32[]{:S(2)}) collective-permute-start(bf16[256,512]{1,0:T(8,128)(2,1)S(1)} %get-tuple-element.47), channel_id=1, source_target_pairs={{0,96},{1,25},{2,98},{3,27},{4,100},{5,29},{6,102},{7,31},{8,104},... | collective-permute-start | bytes 786440 | tf_op jit(solution)/shard_map/ppermute | solution.py:76
  33.4 9.6 %collective-permute-start.13 = (bf16[1024,256]{1,0:T(8,128)(2,1)S(1)}, bf16[1024,256]{1,0:T(8,128)(2,1)S(1)}, u32[]{:S(2)}, u32[]{:S(2)}) collective-permute-start(bf16[1024,256]{1,0:T(8,128)(2,1)S(1)} %get-tuple-element.48.refs_3_), channel_id=1, source_target_pairs={{0,8},{1,33},{2,10},{3,35},{4,12},{5,37},{6,14},{7,39},{8,16},{9,4... | collective-permute-start | bytes 1572872 | tf_op jit(solution)/shard_map/ppermute | solution.py:76
  34.7 15.0 %collective-permute-start.14 = (bf16[1024,256]{1,0:T(8,128)(2,1)S(1)}, bf16[1024,256]{1,0:T(8,128)(2,1)S(1)}, u32[]{:S(2)}, u32[]{:S(2)}) collective-permute-start(bf16[1024,256]{1,0:T(8,128)(2,1)S(1)} %get-tuple-element.48.refs_3_), channel_id=1, source_target_pairs={{0,16},{1,65},{2,18},{3,67},{4,20},{5,69},{6,22},{7,71},{8,24},{9,... | collective-permute-start | bytes 1572872 | tf_op jit(solution)/shard_map/ppermute | solution.py:76
  37.1 12.5 %collective-permute-start.15 = (bf16[1024,256]{1,0:T(8,128)(2,1)S(1)}, bf16[1024,256]{1,0:T(8,128)(2,1)S(1)}, u32[]{:S(2)}, u32[]{:S(2)}) collective-permute-start(bf16[1024,256]{1,0:T(8,128)(2,1)S(1)} %get-tuple-element.48.refs_3_), channel_id=1, source_target_pairs={{0,24},{1,97},{2,26},{3,99},{4,28},{5,101},{6,30},{7,103},{8,0},{9... | collective-permute-start | bytes 1572872 | tf_op jit(solution)/shard_map/ppermute | solution.py:76
  38.3 20.2 %collective-permute-start.10 = (bf16[1024,128]{1,0:T(8,128)(2,1)S(1)}, bf16[1024,128]{1,0:T(8,128)(2,1)S(1)}, u32[]{:S(2)}, u32[]{:S(2)}) collective-permute-start(bf16[1024,128]{1,0:T(8,128)(2,1)S(1)} %get-tuple-element.49.refs_7_.refs_4_), channel_id=1, source_target_pairs={{0,8},{1,33},{2,10},{3,35},{4,12},{5,37},{6,14},{7,39},{8,16},{9,4... | collective-permute-start | bytes 786440 | tf_op jit(solution)/shard_map/ppermute | solution.py:76
  38.6 20.9 %collective-permute-start.11 = (bf16[1024,128]{1,0:T(8,128)(2,1)S(1)}, bf16[1024,128]{1,0:T(8,128)(2,1)S(1)}, u32[]{:S(2)}, u32[]{:S(2)}) collective-permute-start(bf16[1024,128]{1,0:T(8,128)(2,1)S(1)} %get-tuple-element.49.refs_7_.refs_4_), channel_id=1, source_target_pairs={{0,16},{1,65},{2,18},{3,67},{4,20},{5,69},{6,22},{7,71},{8,24},{9,... | collective-permute-start | bytes 786440 | tf_op jit(solution)/shard_map/ppermute | solution.py:76
  43.0 16.5 %collective-permute-start.12 = (bf16[1024,128]{1,0:T(8,128)(2,1)S(1)}, bf16[1024,128]{1,0:T(8,128)(2,1)S(1)}, u32[]{:S(2)}, u32[]{:S(2)}) collective-permute-start(bf16[1024,128]{1,0:T(8,128)(2,1)S(1)} %get-tuple-element.49.refs_7_.refs_4_), channel_id=1, source_target_pairs={{0,24},{1,97},{2,26},{3,99},{4,28},{5,101},{6,30},{7,103},{8,0},{9... | collective-permute-start | bytes 786440 | tf_op jit(solution)/shard_map/ppermute | solution.py:76
  55.3 4.2 %collective-permute-start.16 = (f32[8,1024]{1,0:T(8,128)S(1)}, f32[8,1024]{1,0:T(8,128)S(1)}, u32[]{:S(2)}, u32[]{:S(2)}) collective-permute-start(f32[8,1024]{1,0:T(8,128)S(1)} %get-tuple-element.54.s0), channel_id=1, source_target_pairs={{0,32},{1,9},{2,34},{3,11},{4,36},{5,13},{6,38},{7,15},{8,40},{9,1... | collective-permute-start | bytes 98312 | tf_op jit(solution)/shard_map/ppermute | solution.py:76
  56.2 4.3 %collective-permute-start.17 = (f32[8,1024]{1,0:T(8,128)S(1)}, f32[8,1024]{1,0:T(8,128)S(1)}, u32[]{:S(2)}, u32[]{:S(2)}) collective-permute-start(f32[8,1024]{1,0:T(8,128)S(1)} %get-tuple-element.54.s0), channel_id=1, source_target_pairs={{0,64},{1,17},{2,66},{3,19},{4,68},{5,21},{6,70},{7,23},{8,72},{9,... | collective-permute-start | bytes 98312 | tf_op jit(solution)/shard_map/ppermute | solution.py:76
  58.5 3.1 %collective-permute-start.18 = (f32[8,1024]{1,0:T(8,128)S(1)}, f32[8,1024]{1,0:T(8,128)S(1)}, u32[]{:S(2)}, u32[]{:S(2)}) collective-permute-start(f32[8,1024]{1,0:T(8,128)S(1)} %get-tuple-element.54.s0), channel_id=1, source_target_pairs={{0,96},{1,25},{2,98},{3,27},{4,100},{5,29},{6,102},{7,31},{8,104},... | collective-permute-start | bytes 98312 | tf_op jit(solution)/shard_map/ppermute | solution.py:76
  62.2 9.8 %collective-permute-start.19 = (bf16[1024,128]{1,0:T(8,128)(2,1)S(1)}, bf16[1024,128]{1,0:T(8,128)(2,1)S(1)}, u32[]{:S(2)}, u32[]{:S(2)}) collective-permute-start(bf16[1024,128]{1,0:T(8,128)(2,1)S(1)} %attn_grad.1.refs_5_.refs_8_), channel_id=1, source_target_pairs={{0,8},{1,33},{2,10},{3,35},{4,12},{5,37},{6,14},{7,39},{8,16},{9,4... | collective-permute-start | bytes 786440 | tf_op jit(solution)/shard_map/ppermute | solution.py:76
  62.8 9.2 %collective-permute-start.20 = (bf16[1024,128]{1,0:T(8,128)(2,1)S(1)}, bf16[1024,128]{1,0:T(8,128)(2,1)S(1)}, u32[]{:S(2)}, u32[]{:S(2)}) collective-permute-start(bf16[1024,128]{1,0:T(8,128)(2,1)S(1)} %attn_grad.1.refs_5_.refs_8_), channel_id=1, source_target_pairs={{0,16},{1,65},{2,18},{3,67},{4,20},{5,69},{6,22},{7,71},{8,24},{9,... | collective-permute-start | bytes 786440 | tf_op jit(solution)/shard_map/ppermute | solution.py:76
  63.9 8.5 %collective-permute-start.21 = (bf16[1024,128]{1,0:T(8,128)(2,1)S(1)}, bf16[1024,128]{1,0:T(8,128)(2,1)S(1)}, u32[]{:S(2)}, u32[]{:S(2)}) collective-permute-start(bf16[1024,128]{1,0:T(8,128)(2,1)S(1)} %attn_grad.1.refs_5_.refs_8_), channel_id=1, source_target_pairs={{0,24},{1,97},{2,26},{3,99},{4,28},{5,101},{6,30},{7,103},{8,0},{9... | collective-permute-start | bytes 786440 | tf_op jit(solution)/shard_map/ppermute | solution.py:76
  76.2 8.1 %collective-permute-start.22 = (bf16[256,512]{1,0:T(8,128)(2,1)S(1)}, bf16[256,512]{1,0:T(8,128)(2,1)S(1)}, u32[]{:S(2)}, u32[]{:S(2)}) collective-permute-start(bf16[256,512]{1,0:T(8,128)(2,1)S(1)} %get-tuple-element.58), channel_id=1, source_target_pairs={{32,0},{9,1},{34,2},{11,3},{36,4},{13,5},{38,6},{15,7},{40,8},{17,... | collective-permute-start | bytes 786440 | tf_op jit(solution)/shard_map/ppermute | solution.py:76
  78.2 6.8 %collective-permute-start.23 = (bf16[256,512]{1,0:T(8,128)(2,1)S(1)}, bf16[256,512]{1,0:T(8,128)(2,1)S(1)}, u32[]{:S(2)}, u32[]{:S(2)}) collective-permute-start(bf16[256,512]{1,0:T(8,128)(2,1)S(1)} %get-tuple-element.59), channel_id=1, source_target_pairs={{64,0},{17,1},{66,2},{19,3},{68,4},{21,5},{70,6},{23,7},{72,8},{25... | collective-permute-start | bytes 786440 | tf_op jit(solution)/shard_map/ppermute | solution.py:76
  78.2 9.2 %collective-permute-start.24 = (bf16[256,512]{1,0:T(8,128)(2,1)S(1)}, bf16[256,512]{1,0:T(8,128)(2,1)S(1)}, u32[]{:S(2)}, u32[]{:S(2)}) collective-permute-start(bf16[256,512]{1,0:T(8,128)(2,1)S(1)} %get-tuple-element.60), channel_id=1, source_target_pairs={{96,0},{25,1},{98,2},{27,3},{100,4},{29,5},{102,6},{31,7},{104,8},... | collective-permute-start | bytes 786440 | tf_op jit(solution)/shard_map/ppermute | solution.py:76
  87.4 24.2 %copy-start.6 = (s32[1,1,256]{2,1,0:T(1,128)S(1)}, s32[1,1,256]{2,1,0:T(1,128)}, u32[]{:S(2)}) copy-start(s32[1,1,256]{2,1,0:T(1,128)} %param.10) | copy-start | bytes 3076
  90.1 14.9 %collective-permute-start.25 = (bf16[128,512]{1,0:T(8,128)(2,1)S(1)}, bf16[128,512]{1,0:T(8,128)(2,1)S(1)}, u32[]{:S(2)}, u32[]{:S(2)}) collective-permute-start(bf16[128,512]{1,0:T(8,128)(2,1)S(1)} %get-tuple-element.67), channel_id=1, source_target_pairs={{2,0},{3,1},{4,2},{5,3},{6,4},{7,5},{0,6},{1,7},{10,8},{11,9},{12,... | collective-permute-start | bytes 393224 | tf_op jit(solution)/shard_map/ppermute | solution.py:76
  95.4 11.6 %collective-permute-start.26 = (bf16[128,512]{1,0:T(8,128)(2,1)S(1)}, bf16[128,512]{1,0:T(8,128)(2,1)S(1)}, u32[]{:S(2)}, u32[]{:S(2)}) collective-permute-start(bf16[128,512]{1,0:T(8,128)(2,1)S(1)} %get-tuple-element.68), channel_id=1, source_target_pairs={{4,0},{5,1},{6,2},{7,3},{0,4},{1,5},{2,6},{3,7},{12,8},{13,9},{14,... | collective-permute-start | bytes 393224 | tf_op jit(solution)/shard_map/ppermute | solution.py:76
  95.4 14.3 %collective-permute-start.27 = (bf16[128,512]{1,0:T(8,128)(2,1)S(1)}, bf16[128,512]{1,0:T(8,128)(2,1)S(1)}, u32[]{:S(2)}, u32[]{:S(2)}) collective-permute-start(bf16[128,512]{1,0:T(8,128)(2,1)S(1)} %get-tuple-element.69), channel_id=1, source_target_pairs={{6,0},{7,1},{0,2},{1,3},{2,4},{3,5},{4,6},{5,7},{14,8},{15,9},{8,1... | collective-permute-start | bytes 393224 | tf_op jit(solution)/shard_map/ppermute | solution.py:76
  97.1 13.6 %collective-permute-start.28 = (bf16[128,512]{1,0:T(8,128)(2,1)S(1)}, bf16[128,512]{1,0:T(8,128)(2,1)S(1)}, u32[]{:S(2)}, u32[]{:S(2)}) collective-permute-start(bf16[128,512]{1,0:T(8,128)(2,1)S(1)} %get-tuple-element.66.refs_2_), channel_id=1, source_target_pairs={{0,1},{1,0},{2,3},{3,2},{4,5},{5,4},{6,7},{7,6},{8,9},{9,8},{10,11... | collective-permute-start | bytes 393224 | tf_op jit(solution)/shard_map/ppermute | solution.py:76
  105.0 5.6 %collective-permute-start.29 = (bf16[128,512]{1,0:T(8,128)(2,1)S(1)}, bf16[128,512]{1,0:T(8,128)(2,1)S(1)}, u32[]{:S(2)}, u32[]{:S(2)}) collective-permute-start(bf16[128,512]{1,0:T(8,128)(2,1)S(1)} %collective-permute-done.25.refs_3_), channel_id=1, source_target_pairs={{0,1},{1,0},{2,3},{3,2},{4,5},{5,4},{6,7},{7,6},{8,9},{9,8},{10,11... | collective-permute-start | bytes 393224 | tf_op jit(solution)/shard_map/ppermute | solution.py:76
  107.0 3.7 %collective-permute-start.30 = (bf16[128,512]{1,0:T(8,128)(2,1)S(1)}, bf16[128,512]{1,0:T(8,128)(2,1)S(1)}, u32[]{:S(2)}, u32[]{:S(2)}) collective-permute-start(bf16[128,512]{1,0:T(8,128)(2,1)S(1)} %collective-permute-done.26.refs_4_), channel_id=1, source_target_pairs={{0,1},{1,0},{2,3},{3,2},{4,5},{5,4},{6,7},{7,6},{8,9},{9,8},{10,11... | collective-permute-start | bytes 393224 | tf_op jit(solution)/shard_map/ppermute | solution.py:76
  109.6 2.0 %collective-permute-start.31 = (bf16[128,512]{1,0:T(8,128)(2,1)S(1)}, bf16[128,512]{1,0:T(8,128)(2,1)S(1)}, u32[]{:S(2)}, u32[]{:S(2)}) collective-permute-start(bf16[128,512]{1,0:T(8,128)(2,1)S(1)} %collective-permute-done.27.refs_5_), channel_id=1, source_target_pairs={{0,1},{1,0},{2,3},{3,2},{4,5},{5,4},{6,7},{7,6},{8,9},{9,8},{10,11... | collective-permute-start | bytes 393224 | tf_op jit(solution)/shard_map/ppermute | solution.py:76

commit v6 on v5

--- a/solution.py
+++ b/solution.py
@@ -66,6 +66,10 @@
 
 def row_pairs(step):
     return moved(1, step)
+
+
+def crossed(values):
+    return [values[0], values[2], values[1], values[3]]
 
 
 def back(pairs):
@@ -295,7 +299,7 @@
         yield j, CHUNK, 7 - source
 
 
-def collect_kernel(meta, p0, p1, p2, p3, keys, queries, grads):
+def collect_kernel(meta, p0, p2, p1, p3, keys, queries, grads):
     pieces = (p0, p1, p2, p3)
     for j, low, t in pieces_of(meta):
         rows, part = ds(t * CHUNK, CHUNK), pieces[j]
@@ -392,7 +396,7 @@
 
 
 def forward_kernel(
-    meta, work, begins, key_pos, k0, k1, k2, k3, queries, grads, keys, attn, stats, total
+    meta, work, begins, key_pos, k0, k2, k1, k3, queries, grads, keys, attn, stats, total
 ):
     place_rows(meta, (k0, k1, k2, k3), keys)
     total[...] = jnp.zeros_like(total)
@@ -455,7 +459,7 @@
 
 
 def key_grad_kernel(
-    meta, work, starts, query_pos, keys, q0, q1, q2, q3, g0, g1, g2, g3, d_query, attn,
+    meta, work, starts, query_pos, keys, q0, q2, q1, q3, g0, g2, g1, g3, d_query, attn,
     r0, r1, r2, r3, queries, grads, total,
 ):
     outs = (r0, r1, r2, r3)
@@ -490,7 +494,7 @@
         outs[j][low : low + CHUNK, 3 * HD : 4 * HD] = attn[rows, :].astype(BF)
 
 
-def input_grad_kernel(meta, dest, slot, p0, p1, p2, p3, pre, dmixed, hist, incoming, w_in, *rest):
+def input_grad_kernel(meta, dest, slot, p0, p2, p1, p3, pre, dmixed, hist, incoming, w_in, *rest):
     outs, (mixed, attn, d_act, result) = rest[:4], rest[4:]
     for j, part in enumerate((p0, p1, p2, p3)):
         head = lax.rem(line(meta)[0] + j, 4) * HD
@@ -633,14 +637,14 @@
 
     own_keys, queries, grads = call(
         collect_kernel,
-        [passed, *to_heads(pieces)[1:]],
+        crossed([passed, *to_heads(pieces)[1:]]),
         [VMEM] * 4,
         [rows_two, rows_one, rows_one],
         name="collect",
     )
     keys, attn, stats = call(
         forward_kernel,
-        [key_work, begins, key_pos, *over_rows(own_keys), queries, grads],
+        [key_work, begins, key_pos, *crossed(over_rows(own_keys)), queries, grads],
         [SMEM] + [VMEM] * 8,
         [shape((LENGTH, 2 * HD), BF), shape((quarter, HD), F32), shape((8, quarter), F32)],
         [pltpu.VMEM((quarter + ROWS, HD), F32)],
@@ -650,7 +654,7 @@
     all_queries = over_rows(queries)
     (d_attn,) = call(
         attn_grad_kernel,
-        [*to_heads([stats] * 4), attn, grads, *all_queries[1:]],
+        [*crossed(to_heads([stats] * 4)), attn, grads, *all_queries[1:]],
         [VMEM] * 6 + [pl.BlockSpec(memory_space=pl.ANY)] * 3,
         [rows_one],
         flops=10**9,
@@ -669,7 +673,7 @@
     )
     back_parts = call(
         key_grad_kernel,
-        [query_work, starts, query_pos, own_keys, *all_queries, *all_d_attn, d_query, attn],
+        [query_work, starts, query_pos, own_keys, *crossed(all_queries), *crossed(all_d_attn), d_query, attn],
         [SMEM] + [VMEM] * 13,
         [four] * 4,
         [pltpu.VMEM((LENGTH, HD), BF), pltpu.VMEM((LENGTH, HD), BF), pltpu.VMEM((quarter + ROWS, 2 * HD), F32)]
@@ -680,7 +684,7 @@
     incoming = output_gradient[0]
     *returning, mixed = call(
         input_grad_kernel,
-        [dest, slot, *to_owners(back_parts), pre, dmixed, hist, incoming, w_in],
+        [dest, slot, *crossed(to_owners(back_parts)), pre, dmixed, hist, incoming, w_in],
         [SMEM] * 2 + [VMEM] * 9,
         [shape((2 * BROWS, WIDTH), BF)] * 4 + [shape((ROWS, WIDTH), BF)],
         [

time: 115 us -> 111 us (0.965)
  waiting for transfers between devices: 27.5 us -> 22.3 us
  starting transfers between devices: 53 us -> 55.9 us
  Pallas kernels: 33.5 us -> 31.7 us
    ppermute x32, waiting for transfers between devices: 27.5 us -> 22.3 us  [send(): return lax.ppermute(value, AXES, pairs)]
    ppermute x32, starting transfers between devices: 53 us -> 55.9 us  [send(): return lax.ppermute(value, AXES, pairs)]
    pallas_call x12, Pallas kernels: 33.5 us -> 31.7 us  [call(): pl.pallas_call(with_place(kernel) if placed else kernel, out_shape=outs,...]
  transfers between devices with their start and end apart: 32 -> 32, of which waited for: 13 -> 14; matrix products, arithmetic and copies ran while one was open for 0% -> 0% of each run, Pallas kernels for 14% -> 13%
where the time goes in v6:
time: 111 us
  starting transfers between devices  55.9 us (50%)
  Pallas kernels  31.7 us (29%)
  waiting for transfers between devices  22.3 us (20%)
    ppermute x32, starting transfers between devices, send(): return lax.ppermute(value, AXES, pairs)  55.9 us
    pallas_call x12, Pallas kernels, call(): pl.pallas_call(with_place(kernel) if placed else kernel, out_shape=outs,...  31.7 us
    ppermute x32, waiting for transfers between devices, send(): return lax.ppermute(value, AXES, pairs)  22.3 us
  transfers between devices with their start and end apart: 32, of which 14 were waited for; matrix products, arithmetic and copies ran while one was open for 0% of the time, Pallas kernels for 13%

profile of v6, /device:TPU:1, one launch (start us, length us, event | category | flops | bytes accessed | tf_op | source)
XLA Modules:
  0.0 110.9 jit_solution(10328274245388207151)
XLA Ops:
  0.6 4.9 %lookup.1 = (bf16[128,512]{1,0:T(8,128)(2,1)}, bf16[128,512]{1,0:T(8,128)(2,1)}, bf16[128,512]{1,0:T(8,128)(2,1)}, bf16[128,512]{1,0:T(8,128)(2,1)}) custom-call(s32[4,8]{1,0:T(4,128)} %bitcast.14, s32[2,128]{1,0:T(2,128)} %bitcast.20, bf16[1,1,4096,512]{3,2,1,0:T(8,128)(2,1)} %refs_2_.1), custom_call_target="tpu_custom_call" | custom-call | flops 1073741824 | bytes 4719744 | tf_op jit(solution)/shard_map/lookup/pallas_call | solution.py:134
  5.5 0.0 copy-start
  5.6 0.0 copy-start.3
  5.6 0.0 copy-start.4
  5.6 0.0 copy-start.5
  5.6 2.2 %collective-permute-start = (bf16[128,512]{1,0:T(8,128)(2,1)}, bf16[128,512]{1,0:T(8,128)(2,1)S(1)}, u32[]{:S(2)}, u32[]{:S(2)}) collective-permute-start(bf16[128,512]{1,0:T(8,128)(2,1)} %get-tuple-element.37), channel_id=1, source_target_pairs={{0,2},{1,3},{2,4},{3,5},{4,6},{5,7},{6,0},{7,1},{8,10},{9,11},{10,... | collective-permute-start | bytes 393224 | tf_op jit(solution)/shard_map/ppermute | solution.py:80
  7.8 2.6 %collective-permute-start.1 = (bf16[128,512]{1,0:T(8,128)(2,1)}, bf16[128,512]{1,0:T(8,128)(2,1)S(1)}, u32[]{:S(2)}, u32[]{:S(2)}) collective-permute-start(bf16[128,512]{1,0:T(8,128)(2,1)} %get-tuple-element.38), channel_id=1, source_target_pairs={{0,4},{1,5},{2,6},{3,7},{4,0},{5,1},{6,2},{7,3},{8,12},{9,13},{10,... | collective-permute-start | bytes 393224 | tf_op jit(solution)/shard_map/ppermute | solution.py:80
  10.4 1.1 collective-permute-start.2
  11.5 1.5 %collective-permute-start.3 = (bf16[128,512]{1,0:T(8,128)(2,1)}, bf16[128,512]{1,0:T(8,128)(2,1)S(1)}, u32[]{:S(2)}, u32[]{:S(2)}) collective-permute-start(bf16[128,512]{1,0:T(8,128)(2,1)} %get-tuple-element.36.refs_2_), channel_id=1, source_target_pairs={{0,1},{1,0},{2,3},{3,2},{4,5},{5,4},{6,7},{7,6},{8,9},{9,8},{10,11... | collective-permute-start | bytes 393224 | tf_op jit(solution)/shard_map/ppermute | solution.py:80
  13.0 0.0 collective-permute-done.refs_3_
  13.0 0.9 collective-permute-start.4
  13.9 2.4 %collective-permute-done.1.refs_4_ = bf16[128,512]{1,0:T(8,128)(2,1)S(1)} collective-permute-done((bf16[128,512]{1,0:T(8,128)(2,1)}, bf16[128,512]{1,0:T(8,128)(2,1)S(1)}, u32[]{:S(2)}, u32[]{:S(2)}) %collective-permute-start.1) | collective-permute-done | bytes 131104 | tf_op jit(solution)/shard_map/ppermute | solution.py:80
  16.3 1.5 %collective-permute-start.5 = (bf16[128,512]{1,0:T(8,128)(2,1)S(1)}, bf16[128,512]{1,0:T(8,128)(2,1)S(1)}, u32[]{:S(2)}, u32[]{:S(2)}) collective-permute-start(bf16[128,512]{1,0:T(8,128)(2,1)S(1)} %collective-permute-done.1.refs_4_), channel_id=1, source_target_pairs={{0,1},{1,0},{2,3},{3,2},{4,5},{5,4},{6,7},{7,6},{8,9},{9,8},{10,11... | collective-permute-start | bytes 393224 | tf_op jit(solution)/shard_map/ppermute | solution.py:80
  17.9 0.0 collective-permute-start.6
  17.9 0.3 mix.1.refs_11_.refs_7_
  18.2 0.0 copy-start.7
  18.2 0.0 copy-start.8
  18.3 0.6 collective-permute-done.5.refs_8_
  18.9 0.4 collective-permute-done.6.refs_9_
  19.2 2.4 %project.1 = (bf16[256,512]{1,0:T(8,128)(2,1)S(1)}, f32[256,2048]{1,0:T(8,128)S(1)}, bf16[256,512]{1,0:T(8,128)(2,1)S(1)}, bf16[256,512]{1,0:T(8,128)(2,1)S(1)},...) custom-call(s32[4,8]{1,0:T(4,128)S(1)} %bitcast.15, s32[4,8]{1,0:T(4,128)S(1)} %bitcast.18, ...), custom_call_target="tpu_custom_call" | custom-call | flops 536870912 | bytes 7078144 | tf_op jit(solution)/shard_map/project/pallas_call | solution.py:134
  21.7 3.7 %collective-permute-start.7 = (bf16[256,512]{1,0:T(8,128)(2,1)S(1)}, bf16[256,512]{1,0:T(8,128)(2,1)S(1)}, u32[]{:S(2)}, u32[]{:S(2)}) collective-permute-start(bf16[256,512]{1,0:T(8,128)(2,1)S(1)} %get-tuple-element.45), channel_id=1, source_target_pairs={{0,64},{1,17},{2,66},{3,19},{4,68},{5,21},{6,70},{7,23},{8,72},{9,... | collective-permute-start | bytes 786440 | tf_op jit(solution)/shard_map/ppermute | solution.py:80
  25.4 0.7 collective-permute-start.8
  26.1 1.9 %collective-permute-start.9 = (bf16[256,512]{1,0:T(8,128)(2,1)S(1)}, bf16[256,512]{1,0:T(8,128)(2,1)S(1)}, u32[]{:S(2)}, u32[]{:S(2)}) collective-permute-start(bf16[256,512]{1,0:T(8,128)(2,1)S(1)} %get-tuple-element.47), channel_id=1, source_target_pairs={{0,96},{1,25},{2,98},{3,27},{4,100},{5,29},{6,102},{7,31},{8,104},... | collective-permute-start | bytes 786440 | tf_op jit(solution)/shard_map/ppermute | solution.py:80
  28.0 2.7 %prepare.1 = (s32[257]{0:T(512)S(1)}, s32[257]{0:T(512)S(1)}, f32[8,4096]{1,0:T(8,128)S(1)}, f32[1024,128]{1,0:T(8,128)S(1)}, f32[16,4096]{1,0:T(8,128)S(1)}, /*...) custom-call(s32[16]{0:T(128)S(1)} %bitcast.23, s32[64,64]{1,0:T(8,128)S(1)} %bitcast.22, ...), custom_call_target="tpu_custom_call" | custom-call | flops 3000000000 | bytes 1722440 | tf_op jit(solution)/shard_map/prepare/pallas_call | solution.py:134
  30.7 1.5 %collective-permute-done.8.refs_2_ = bf16[256,512]{1,0:T(8,128)(2,1)S(1)} collective-permute-done((bf16[256,512]{1,0:T(8,128)(2,1)S(1)}, bf16[256,512]{1,0:T(8,128)(2,1)S(1)}, u32[]{:S(2)}, u32[]{:S(2)}) %collective-permute-start.8) | collective-permute-done | bytes 262176 | tf_op jit(solution)/shard_map/ppermute | solution.py:80
  32.2 0.4 collective-permute-done.9.refs_3_
  32.7 0.1 collect.1
  32.8 2.8 %collective-permute-start.13 = (bf16[1024,256]{1,0:T(8,128)(2,1)S(1)}, bf16[1024,256]{1,0:T(8,128)(2,1)S(1)}, u32[]{:S(2)}, u32[]{:S(2)}) collective-permute-start(bf16[1024,256]{1,0:T(8,128)(2,1)S(1)} %get-tuple-element.48.refs_3_), channel_id=1, source_target_pairs={{0,16},{1,65},{2,18},{3,67},{4,20},{5,69},{6,22},{7,71},{8,24},{9,... | collective-permute-start | bytes 1572872 | tf_op jit(solution)/shard_map/ppermute | solution.py:80
  35.6 0.3 collective-permute-start.14
  35.9 2.4 %collective-permute-start.15 = (bf16[1024,256]{1,0:T(8,128)(2,1)S(1)}, bf16[1024,256]{1,0:T(8,128)(2,1)S(1)}, u32[]{:S(2)}, u32[]{:S(2)}) collective-permute-start(bf16[1024,256]{1,0:T(8,128)(2,1)S(1)} %get-tuple-element.48.refs_3_), channel_id=1, source_target_pairs={{0,24},{1,97},{2,26},{3,99},{4,28},{5,101},{6,30},{7,103},{8,0},{9... | collective-permute-start | bytes 1572872 | tf_op jit(solution)/shard_map/ppermute | solution.py:80
  38.3 0.6 collective-permute-start.11
  38.9 3.9 %collective-permute-done.13.refs_4_ = bf16[1024,256]{1,0:T(8,128)(2,1)S(1)} collective-permute-done((bf16[1024,256]{1,0:T(8,128)(2,1)S(1)}, bf16[1024,256]{1,0:T(8,128)(2,1)S(1)}, u32[]{:S(2)}, u32[]{:S(2)}) %collective-permute-start.13) | collective-permute-done | bytes 524320 | tf_op jit(solution)/shard_map/ppermute | solution.py:80
  42.7 2.5 %collective-permute-start.12 = (bf16[1024,128]{1,0:T(8,128)(2,1)S(1)}, bf16[1024,128]{1,0:T(8,128)(2,1)S(1)}, u32[]{:S(2)}, u32[]{:S(2)}) collective-permute-start(bf16[1024,128]{1,0:T(8,128)(2,1)S(1)} %get-tuple-element.49.refs_7_.refs_4_), channel_id=1, source_target_pairs={{0,24},{1,97},{2,26},{3,99},{4,28},{5,101},{6,30},{7,103},{8,0},{9... | collective-permute-start | bytes 786440 | tf_op jit(solution)/shard_map/ppermute | solution.py:80
  45.2 3.1 %collective-permute-done.14.refs_5_ = bf16[1024,256]{1,0:T(8,128)(2,1)S(1)} collective-permute-done((bf16[1024,256]{1,0:T(8,128)(2,1)S(1)}, bf16[1024,256]{1,0:T(8,128)(2,1)S(1)}, u32[]{:S(2)}, u32[]{:S(2)}) %collective-permute-start.14) | collective-permute-done | bytes 524320 | tf_op jit(solution)/shard_map/ppermute | solution.py:80
  48.3 0.1 collective-permute-done.15.refs_6_
  48.5 5.0 %forward.1 = (bf16[4096,256]{1,0:T(8,128)(2,1)S(1)}, f32[1024,128]{1,0:T(8,128)S(1)}, f32[8,1024]{1,0:T(8,128)S(1)}) custom-call(s32[257]{0:T(512)S(1)} %get-tuple-element.50.refs_0_, f32[1024,128]{1,0:T(8,128)S(1)} %get-tuple-element.51.refs_1_, f32[16,4096]{1,0:T(8,128)S(1)} %get-tuple-element.52.refs_2_, bf16[1024,256]{1,0:T(8,128)(2,1)S(1)} %get-tuple-element.48.refs_3_, ...), custom_call_target="tpu_custom_call" | custom-call | flops 6000000000 | bytes 6063108 | tf_op jit(solution)/shard_map/forward/pallas_call | solution.py:134
  53.4 2.1 %collective-permute-start.16 = (f32[8,1024]{1,0:T(8,128)S(1)}, f32[8,1024]{1,0:T(8,128)S(1)}, u32[]{:S(2)}, u32[]{:S(2)}) collective-permute-start(f32[8,1024]{1,0:T(8,128)S(1)} %get-tuple-element.54.s0), channel_id=1, source_target_pairs={{0,64},{1,17},{2,66},{3,19},{4,68},{5,21},{6,70},{7,23},{8,72},{9,... | collective-permute-start | bytes 98312 | tf_op jit(solution)/shard_map/ppermute | solution.py:80
  55.6 1.2 %collective-permute-start.17 = (f32[8,1024]{1,0:T(8,128)S(1)}, f32[8,1024]{1,0:T(8,128)S(1)}, u32[]{:S(2)}, u32[]{:S(2)}) collective-permute-start(f32[8,1024]{1,0:T(8,128)S(1)} %get-tuple-element.54.s0), channel_id=1, source_target_pairs={{0,32},{1,9},{2,34},{3,11},{4,36},{5,13},{6,38},{7,15},{8,40},{9,1... | collective-permute-start | bytes 98312 | tf_op jit(solution)/shard_map/ppermute | solution.py:80
  56.7 1.5 %collective-permute-start.18 = (f32[8,1024]{1,0:T(8,128)S(1)}, f32[8,1024]{1,0:T(8,128)S(1)}, u32[]{:S(2)}, u32[]{:S(2)}) collective-permute-start(f32[8,1024]{1,0:T(8,128)S(1)} %get-tuple-element.54.s0), channel_id=1, source_target_pairs={{0,96},{1,25},{2,98},{3,27},{4,100},{5,29},{6,102},{7,31},{8,104},... | collective-permute-start | bytes 98312 | tf_op jit(solution)/shard_map/ppermute | solution.py:80
  58.3 1.3 %collective-permute-done.17.s2 = f32[8,1024]{1,0:T(8,128)S(1)} collective-permute-done((f32[8,1024]{1,0:T(8,128)S(1)}, f32[8,1024]{1,0:T(8,128)S(1)}, u32[]{:S(2)}, u32[]{:S(2)}) %collective-permute-start.17) | collective-permute-done | bytes 32800 | tf_op jit(solution)/shard_map/ppermute | solution.py:80
  59.5 0.3 collective-permute-done.18.s3
  59.8 0.6 attn_grad.1.refs_5_.refs_8_
  60.4 1.6 %collective-permute-start.19 = (bf16[1024,128]{1,0:T(8,128)(2,1)S(1)}, bf16[1024,128]{1,0:T(8,128)(2,1)S(1)}, u32[]{:S(2)}, u32[]{:S(2)}) collective-permute-start(bf16[1024,128]{1,0:T(8,128)(2,1)S(1)} %attn_grad.1.refs_5_.refs_8_), channel_id=1, source_target_pairs={{0,16},{1,65},{2,18},{3,67},{4,20},{5,69},{6,22},{7,71},{8,24},{9,... | collective-permute-start | bytes 786440 | tf_op jit(solution)/shard_map/ppermute | solution.py:80
  62.0 0.4 collective-permute-start.20
  62.5 2.2 %collective-permute-start.21 = (bf16[1024,128]{1,0:T(8,128)(2,1)S(1)}, bf16[1024,128]{1,0:T(8,128)(2,1)S(1)}, u32[]{:S(2)}, u32[]{:S(2)}) collective-permute-start(bf16[1024,128]{1,0:T(8,128)(2,1)S(1)} %attn_grad.1.refs_5_.refs_8_), channel_id=1, source_target_pairs={{0,24},{1,97},{2,26},{3,99},{4,28},{5,101},{6,30},{7,103},{8,0},{9... | collective-permute-start | bytes 786440 | tf_op jit(solution)/shard_map/ppermute | solution.py:80
  64.7 4.9 %query_grad.1.refs_12_ = bf16[1024,128]{1,0:T(8,128)(2,1)S(1)} custom-call(s32[257]{0:T(512)S(1)} %get-tuple-element.50.refs_0_, f32[1024,128]{1,0:T(8,128)S(1)} %get-tuple-element.51.refs_1_, f32[16,4096]{1,0:T(8,128)S(1)} %get-tuple-element.52.refs_2_, bf16[4096,256]{1,0:T(8,128)(2,1)S(1)} %get-tuple-element.56.refs_3_, ...), custom_call_target="tpu_custom_call" | custom-call | flops 6000000000 | bytes 3671044 | tf_op jit(solution)/shard_map/query_grad/pallas_call | solution.py:134
  69.7 0.7 collective-permute-done.20.refs_10_
  70.4 3.8 %key_grad.1 = (bf16[256,512]{1,0:T(8,128)(2,1)S(1)}, bf16[256,512]{1,0:T(8,128)(2,1)S(1)}, bf16[256,512]{1,0:T(8,128)(2,1)S(1)}, bf16[256,512]{1,0:T(8,128)(2,1)S(1)}) custom-call(s32[257]{0:T(512)S(1)} %get-tuple-element.41.refs_0_, f32[8,4096]{1,0:T(8,128)S(1)} %get-tuple-element.42.refs_1_, f32[16,4096]{1,0:T(8,128)S(1)} %get-tuple-element.43.refs_2_, ...), custom_call_target="tpu_custom_call" | custom-call | flops 7000000000 | bytes 4850692 | tf_op jit(solution)/shard_map/key_grad/pallas_call | solution.py:134
  74.1 0.9 collective-permute-start.22
  75.0 1.7 %collective-permute-start.23 = (bf16[256,512]{1,0:T(8,128)(2,1)S(1)}, bf16[256,512]{1,0:T(8,128)(2,1)S(1)}, u32[]{:S(2)}, u32[]{:S(2)}) collective-permute-start(bf16[256,512]{1,0:T(8,128)(2,1)S(1)} %get-tuple-element.59), channel_id=1, source_target_pairs={{32,0},{9,1},{34,2},{11,3},{36,4},{13,5},{38,6},{15,7},{40,8},{17,... | collective-permute-start | bytes 786440 | tf_op jit(solution)/shard_map/ppermute | solution.py:80
  76.7 0.5 collective-permute-start.24
  77.2 3.8 %collective-permute-done.22.refs_3_ = bf16[256,512]{1,0:T(8,128)(2,1)S(1)} collective-permute-done((bf16[256,512]{1,0:T(8,128)(2,1)S(1)}, bf16[256,512]{1,0:T(8,128)(2,1)S(1)}, u32[]{:S(2)}, u32[]{:S(2)}) %collective-permute-start.22) | collective-permute-done | bytes 262176 | tf_op jit(solution)/shard_map/ppermute | solution.py:80
  81.0 2.8 %collective-permute-done.23.refs_4_ = bf16[256,512]{1,0:T(8,128)(2,1)S(1)} collective-permute-done((bf16[256,512]{1,0:T(8,128)(2,1)S(1)}, bf16[256,512]{1,0:T(8,128)(2,1)S(1)}, u32[]{:S(2)}, u32[]{:S(2)}) %collective-permute-start.23) | collective-permute-done | bytes 262176 | tf_op jit(solution)/shard_map/ppermute | solution.py:80
  83.8 2.7 %input_grad.1 = (bf16[128,512]{1,0:T(8,128)(2,1)S(1)}, bf16[128,512]{1,0:T(8,128)(2,1)S(1)}, bf16[128,512]{1,0:T(8,128)(2,1)S(1)}, bf16[128,512]{1,0:T(8,128)(2,1)S(1)}, bf16[256,512]{1,0:T(8,128)(2,1)S(1)}) custom-call(s32[4,8]{1,0:T(4,128)S(1)} %bitcast.16, s32[4,8]{1,0:T(4,128)S(1)} %bitcast.19, bf16[256,512]{1,0:T(8,128)(2,1)S(1)} %get-tuple-element.57.refs_2_, ...), custom_call_target="tpu_custom_call" | custom-call | flops 536870912 | bytes 7078144 | tf_op jit(solution)/shard_map/input_grad/pallas_call | solution.py:134
  86.5 2.6 %collective-permute-start.25 = (bf16[128,512]{1,0:T(8,128)(2,1)S(1)}, bf16[128,512]{1,0:T(8,128)(2,1)S(1)}, u32[]{:S(2)}, u32[]{:S(2)}) collective-permute-start(bf16[128,512]{1,0:T(8,128)(2,1)S(1)} %get-tuple-element.67), channel_id=1, source_target_pairs={{2,0},{3,1},{4,2},{5,3},{6,4},{7,5},{0,6},{1,7},{10,8},{11,9},{12,... | collective-permute-start | bytes 393224 | tf_op jit(solution)/shard_map/ppermute | solution.py:80
  89.1 1.2 %collective-permute-start.26 = (bf16[128,512]{1,0:T(8,128)(2,1)S(1)}, bf16[128,512]{1,0:T(8,128)(2,1)S(1)}, u32[]{:S(2)}, u32[]{:S(2)}) collective-permute-start(bf16[128,512]{1,0:T(8,128)(2,1)S(1)} %get-tuple-element.68), channel_id=1, source_target_pairs={{4,0},{5,1},{6,2},{7,3},{0,4},{1,5},{2,6},{3,7},{12,8},{13,9},{14,... | collective-permute-start | bytes 393224 | tf_op jit(solution)/shard_map/ppermute | solution.py:80
  90.3 0.1 collective-permute-start.27
  90.3 1.0 output.1
  91.4 11.3 %collective-permute-start.28 = (bf16[128,512]{1,0:T(8,128)(2,1)S(1)}, bf16[128,512]{1,0:T(8,128)(2,1)S(1)}, u32[]{:S(2)}, u32[]{:S(2)}) collective-permute-start(bf16[128,512]{1,0:T(8,128)(2,1)S(1)} %get-tuple-element.66.refs_2_), channel_id=1, source_target_pairs={{0,1},{1,0},{2,3},{3,2},{4,5},{5,4},{6,7},{7,6},{8,9},{9,8},{10,11... | collective-permute-start | bytes 393224 | tf_op jit(solution)/shard_map/ppermute | solution.py:80
  102.7 0.0 collective-permute-start.29
  102.7 1.9 %collective-permute-start.30 = (bf16[128,512]{1,0:T(8,128)(2,1)S(1)}, bf16[128,512]{1,0:T(8,128)(2,1)S(1)}, u32[]{:S(2)}, u32[]{:S(2)}) collective-permute-start(bf16[128,512]{1,0:T(8,128)(2,1)S(1)} %collective-permute-done.26.refs_4_), channel_id=1, source_target_pairs={{0,1},{1,0},{2,3},{3,2},{4,5},{5,4},{6,7},{7,6},{8,9},{9,8},{10,11... | collective-permute-start | bytes 393224 | tf_op jit(solution)/shard_map/ppermute | solution.py:80
  104.6 1.9 %collective-permute-start.31 = (bf16[128,512]{1,0:T(8,128)(2,1)S(1)}, bf16[128,512]{1,0:T(8,128)(2,1)S(1)}, u32[]{:S(2)}, u32[]{:S(2)}) collective-permute-start(bf16[128,512]{1,0:T(8,128)(2,1)S(1)} %collective-permute-done.27.refs_5_), channel_id=1, source_target_pairs={{0,1},{1,0},{2,3},{3,2},{4,5},{5,4},{6,7},{7,6},{8,9},{9,8},{10,11... | collective-permute-start | bytes 393224 | tf_op jit(solution)/shard_map/ppermute | solution.py:80
  106.5 1.0 collective-permute-done.31.refs_9_
  107.5 3.2 %table_grad.1 = bf16[1,1,4096,512]{3,2,1,0:T(8,128)(2,1)} custom-call(s32[4,8]{1,0:T(4,128)S(1)} %bitcast.17, s32[1,256]{1,0:T(1,128)S(1)} %bitcast.21, bf16[128,512]{1,0:T(8,128)(2,1)S(1)} %get-tuple-element.66.refs_2_, bf16[128,512]{1,0:T(8,128)(2,1)S(1)} %collective-permute-done.25.refs_3_, bf16[128,512]{1,0:T(8,128)(2,1)S(1)} %collective-permute-done.26.refs_4_, ...), custom_call_target="tpu_custom_call" | custom-call | flops 1073741824 | bytes 5244032 | tf_op jit(solution)/shard_map/table_grad/pallas_call | solution.py:134
  (30 shorter events, 0.1 us)
Async XLA Ops:
  0.6 17.2 %copy-start.1 = (bf16[512,512]{1,0:T(8,128)(2,1)S(1)}, bf16[512,512]{1,0:T(8,128)(2,1)}, u32[]{:S(2)}) copy-start(bf16[512,512]{1,0:T(8,128)(2,1)} %w_out.3) | copy-start | bytes 1572868
  0.6 17.2 %copy-start.2 = (bf16[1,256,512]{2,1,0:T(8,128)(2,1)S(1)}, bf16[1,256,512]{2,1,0:T(8,128)(2,1)}, u32[]{:S(2)}) copy-start(bf16[1,256,512]{2,1,0:T(8,128)(2,1)} %param.17) | copy-start | bytes 786436
  5.5 13.7 %copy-start = (bf16[512,2048]{1,0:T(8,128)(2,1)S(1)}, bf16[512,2048]{1,0:T(8,128)(2,1)}, u32[]{:S(2)}) copy-start(bf16[512,2048]{1,0:T(8,128)(2,1)} %refs_10_.3) | copy-start | bytes 6291460
  5.6 13.7 %copy-start.3 = (bf16[128,512]{1,0:T(8,128)(2,1)S(1)}, bf16[128,512]{1,0:T(8,128)(2,1)}, u32[]{:S(2)}) copy-start(bf16[128,512]{1,0:T(8,128)(2,1)} %get-tuple-element.36.refs_2_) | copy-start | bytes 393220
  5.6 13.7 %copy-start.4 = (s32[1,8,4]{1,2,0:T(4,128)S(1)}, s32[1,8,4]{1,2,0:T(4,128)}, u32[]{:S(2)}) copy-start(s32[1,8,4]{1,2,0:T(4,128)} %param.11) | copy-start | bytes 388
  5.6 13.7 %copy-start.5 = (s32[1,8,4]{1,2,0:T(4,128)S(1)}, s32[1,8,4]{1,2,0:T(4,128)}, u32[]{:S(2)}) copy-start(s32[1,8,4]{1,2,0:T(4,128)} %param.12) | copy-start | bytes 388
  5.6 7.4 %collective-permute-start = (bf16[128,512]{1,0:T(8,128)(2,1)}, bf16[128,512]{1,0:T(8,128)(2,1)S(1)}, u32[]{:S(2)}, u32[]{:S(2)}) collective-permute-start(bf16[128,512]{1,0:T(8,128)(2,1)} %get-tuple-element.37), channel_id=1, source_target_pairs={{0,2},{1,3},{2,4},{3,5},{4,6},{5,7},{6,0},{7,1},{8,10},{9,11},{10,... | collective-permute-start | bytes 393224 | tf_op jit(solution)/shard_map/ppermute | solution.py:80
  7.8 8.5 %collective-permute-start.1 = (bf16[128,512]{1,0:T(8,128)(2,1)}, bf16[128,512]{1,0:T(8,128)(2,1)S(1)}, u32[]{:S(2)}, u32[]{:S(2)}) collective-permute-start(bf16[128,512]{1,0:T(8,128)(2,1)} %get-tuple-element.38), channel_id=1, source_target_pairs={{0,4},{1,5},{2,6},{3,7},{4,0},{5,1},{6,2},{7,3},{8,12},{9,13},{10,... | collective-permute-start | bytes 393224 | tf_op jit(solution)/shard_map/ppermute | solution.py:80
  10.4 7.5 %collective-permute-start.2 = (bf16[128,512]{1,0:T(8,128)(2,1)}, bf16[128,512]{1,0:T(8,128)(2,1)S(1)}, u32[]{:S(2)}, u32[]{:S(2)}) collective-permute-start(bf16[128,512]{1,0:T(8,128)(2,1)} %get-tuple-element.39), channel_id=1, source_target_pairs={{0,6},{1,7},{2,0},{3,1},{4,2},{5,3},{6,4},{7,5},{8,14},{9,15},{10,... | collective-permute-start | bytes 393224 | tf_op jit(solution)/shard_map/ppermute | solution.py:80
  11.5 6.8 %collective-permute-start.3 = (bf16[128,512]{1,0:T(8,128)(2,1)}, bf16[128,512]{1,0:T(8,128)(2,1)S(1)}, u32[]{:S(2)}, u32[]{:S(2)}) collective-permute-start(bf16[128,512]{1,0:T(8,128)(2,1)} %get-tuple-element.36.refs_2_), channel_id=1, source_target_pairs={{0,1},{1,0},{2,3},{3,2},{4,5},{5,4},{6,7},{7,6},{8,9},{9,8},{10,11... | collective-permute-start | bytes 393224 | tf_op jit(solution)/shard_map/ppermute | solution.py:80
  13.0 5.3 %collective-permute-start.4 = (bf16[128,512]{1,0:T(8,128)(2,1)S(1)}, bf16[128,512]{1,0:T(8,128)(2,1)S(1)}, u32[]{:S(2)}, u32[]{:S(2)}) collective-permute-start(bf16[128,512]{1,0:T(8,128)(2,1)S(1)} %collective-permute-done.refs_3_), channel_id=1, source_target_pairs={{0,1},{1,0},{2,3},{3,2},{4,5},{5,4},{6,7},{7,6},{8,9},{9,8},{10,11... | collective-permute-start | bytes 393224 | tf_op jit(solution)/shard_map/ppermute | solution.py:80
  16.3 2.5 %collective-permute-start.5 = (bf16[128,512]{1,0:T(8,128)(2,1)S(1)}, bf16[128,512]{1,0:T(8,128)(2,1)S(1)}, u32[]{:S(2)}, u32[]{:S(2)}) collective-permute-start(bf16[128,512]{1,0:T(8,128)(2,1)S(1)} %collective-permute-done.1.refs_4_), channel_id=1, source_target_pairs={{0,1},{1,0},{2,3},{3,2},{4,5},{5,4},{6,7},{7,6},{8,9},{9,8},{10,11... | collective-permute-start | bytes 393224 | tf_op jit(solution)/shard_map/ppermute | solution.py:80
  17.9 1.3 %collective-permute-start.6 = (bf16[128,512]{1,0:T(8,128)(2,1)S(1)}, bf16[128,512]{1,0:T(8,128)(2,1)S(1)}, u32[]{:S(2)}, u32[]{:S(2)}) collective-permute-start(bf16[128,512]{1,0:T(8,128)(2,1)S(1)} %collective-permute-done.2.refs_5_), channel_id=1, source_target_pairs={{0,1},{1,0},{2,3},{3,2},{4,5},{5,4},{6,7},{7,6},{8,9},{9,8},{10,11... | collective-permute-start | bytes 393224 | tf_op jit(solution)/shard_map/ppermute | solution.py:80
  18.2 9.8 %copy-start.7 = (s32[1,64,64]{2,1,0:T(8,128)S(1)}, s32[1,64,64]{2,1,0:T(8,128)}, u32[]{:S(2)}) copy-start(s32[1,64,64]{2,1,0:T(8,128)} %param.14) | copy-start | bytes 49156
  18.2 9.8 %copy-start.8 = (s32[1,16]{1,0:T(1,128)S(1)}, s32[1,16]{1,0:T(1,128)}, u32[]{:S(2)}) copy-start(s32[1,16]{1,0:T(1,128)} %param.13) | copy-start | bytes 196
  21.7 9.1 %collective-permute-start.7 = (bf16[256,512]{1,0:T(8,128)(2,1)S(1)}, bf16[256,512]{1,0:T(8,128)(2,1)S(1)}, u32[]{:S(2)}, u32[]{:S(2)}) collective-permute-start(bf16[256,512]{1,0:T(8,128)(2,1)S(1)} %get-tuple-element.45), channel_id=1, source_target_pairs={{0,64},{1,17},{2,66},{3,19},{4,68},{5,21},{6,70},{7,23},{8,72},{9,... | collective-permute-start | bytes 786440 | tf_op jit(solution)/shard_map/ppermute | solution.py:80
  25.4 6.9 %collective-permute-start.8 = (bf16[256,512]{1,0:T(8,128)(2,1)S(1)}, bf16[256,512]{1,0:T(8,128)(2,1)S(1)}, u32[]{:S(2)}, u32[]{:S(2)}) collective-permute-start(bf16[256,512]{1,0:T(8,128)(2,1)S(1)} %get-tuple-element.46), channel_id=1, source_target_pairs={{0,32},{1,9},{2,34},{3,11},{4,36},{5,13},{6,38},{7,15},{8,40},{9,1... | collective-permute-start | bytes 786440 | tf_op jit(solution)/shard_map/ppermute | solution.py:80
  26.1 6.6 %collective-permute-start.9 = (bf16[256,512]{1,0:T(8,128)(2,1)S(1)}, bf16[256,512]{1,0:T(8,128)(2,1)S(1)}, u32[]{:S(2)}, u32[]{:S(2)}) collective-permute-start(bf16[256,512]{1,0:T(8,128)(2,1)S(1)} %get-tuple-element.47), channel_id=1, source_target_pairs={{0,96},{1,25},{2,98},{3,27},{4,100},{5,29},{6,102},{7,31},{8,104},... | collective-permute-start | bytes 786440 | tf_op jit(solution)/shard_map/ppermute | solution.py:80
  32.8 10.0 %collective-permute-start.13 = (bf16[1024,256]{1,0:T(8,128)(2,1)S(1)}, bf16[1024,256]{1,0:T(8,128)(2,1)S(1)}, u32[]{:S(2)}, u32[]{:S(2)}) collective-permute-start(bf16[1024,256]{1,0:T(8,128)(2,1)S(1)} %get-tuple-element.48.refs_3_), channel_id=1, source_target_pairs={{0,16},{1,65},{2,18},{3,67},{4,20},{5,69},{6,22},{7,71},{8,24},{9,... | collective-permute-start | bytes 1572872 | tf_op jit(solution)/shard_map/ppermute | solution.py:80
  35.6 12.7 %collective-permute-start.14 = (bf16[1024,256]{1,0:T(8,128)(2,1)S(1)}, bf16[1024,256]{1,0:T(8,128)(2,1)S(1)}, u32[]{:S(2)}, u32[]{:S(2)}) collective-permute-start(bf16[1024,256]{1,0:T(8,128)(2,1)S(1)} %get-tuple-element.48.refs_3_), channel_id=1, source_target_pairs={{0,8},{1,33},{2,10},{3,35},{4,12},{5,37},{6,14},{7,39},{8,16},{9,4... | collective-permute-start | bytes 1572872 | tf_op jit(solution)/shard_map/ppermute | solution.py:80
  35.9 12.5 %collective-permute-start.15 = (bf16[1024,256]{1,0:T(8,128)(2,1)S(1)}, bf16[1024,256]{1,0:T(8,128)(2,1)S(1)}, u32[]{:S(2)}, u32[]{:S(2)}) collective-permute-start(bf16[1024,256]{1,0:T(8,128)(2,1)S(1)} %get-tuple-element.48.refs_3_), channel_id=1, source_target_pairs={{0,24},{1,97},{2,26},{3,99},{4,28},{5,101},{6,30},{7,103},{8,0},{9... | collective-permute-start | bytes 1572872 | tf_op jit(solution)/shard_map/ppermute | solution.py:80
  38.3 18.4 %collective-permute-start.10 = (bf16[1024,128]{1,0:T(8,128)(2,1)S(1)}, bf16[1024,128]{1,0:T(8,128)(2,1)S(1)}, u32[]{:S(2)}, u32[]{:S(2)}) collective-permute-start(bf16[1024,128]{1,0:T(8,128)(2,1)S(1)} %get-tuple-element.49.refs_7_.refs_4_), channel_id=1, source_target_pairs={{0,16},{1,65},{2,18},{3,67},{4,20},{5,69},{6,22},{7,71},{8,24},{9,... | collective-permute-start | bytes 786440 | tf_op jit(solution)/shard_map/ppermute | solution.py:80
  38.3 19.9 %collective-permute-start.11 = (bf16[1024,128]{1,0:T(8,128)(2,1)S(1)}, bf16[1024,128]{1,0:T(8,128)(2,1)S(1)}, u32[]{:S(2)}, u32[]{:S(2)}) collective-permute-start(bf16[1024,128]{1,0:T(8,128)(2,1)S(1)} %get-tuple-element.49.refs_7_.refs_4_), channel_id=1, source_target_pairs={{0,8},{1,33},{2,10},{3,35},{4,12},{5,37},{6,14},{7,39},{8,16},{9,4... | collective-permute-start | bytes 786440 | tf_op jit(solution)/shard_map/ppermute | solution.py:80
  42.7 15.5 %collective-permute-start.12 = (bf16[1024,128]{1,0:T(8,128)(2,1)S(1)}, bf16[1024,128]{1,0:T(8,128)(2,1)S(1)}, u32[]{:S(2)}, u32[]{:S(2)}) collective-permute-start(bf16[1024,128]{1,0:T(8,128)(2,1)S(1)} %get-tuple-element.49.refs_7_.refs_4_), channel_id=1, source_target_pairs={{0,24},{1,97},{2,26},{3,99},{4,28},{5,101},{6,30},{7,103},{8,0},{9... | collective-permute-start | bytes 786440 | tf_op jit(solution)/shard_map/ppermute | solution.py:80
  53.4 4.8 %collective-permute-start.16 = (f32[8,1024]{1,0:T(8,128)S(1)}, f32[8,1024]{1,0:T(8,128)S(1)}, u32[]{:S(2)}, u32[]{:S(2)}) collective-permute-start(f32[8,1024]{1,0:T(8,128)S(1)} %get-tuple-element.54.s0), channel_id=1, source_target_pairs={{0,64},{1,17},{2,66},{3,19},{4,68},{5,21},{6,70},{7,23},{8,72},{9,... | collective-permute-start | bytes 98312 | tf_op jit(solution)/shard_map/ppermute | solution.py:80
  55.6 4.0 %collective-permute-start.17 = (f32[8,1024]{1,0:T(8,128)S(1)}, f32[8,1024]{1,0:T(8,128)S(1)}, u32[]{:S(2)}, u32[]{:S(2)}) collective-permute-start(f32[8,1024]{1,0:T(8,128)S(1)} %get-tuple-element.54.s0), channel_id=1, source_target_pairs={{0,32},{1,9},{2,34},{3,11},{4,36},{5,13},{6,38},{7,15},{8,40},{9,1... | collective-permute-start | bytes 98312 | tf_op jit(solution)/shard_map/ppermute | solution.py:80
  56.7 3.1 %collective-permute-start.18 = (f32[8,1024]{1,0:T(8,128)S(1)}, f32[8,1024]{1,0:T(8,128)S(1)}, u32[]{:S(2)}, u32[]{:S(2)}) collective-permute-start(f32[8,1024]{1,0:T(8,128)S(1)} %get-tuple-element.54.s0), channel_id=1, source_target_pairs={{0,96},{1,25},{2,98},{3,27},{4,100},{5,29},{6,102},{7,31},{8,104},... | collective-permute-start | bytes 98312 | tf_op jit(solution)/shard_map/ppermute | solution.py:80
  60.4 9.2 %collective-permute-start.19 = (bf16[1024,128]{1,0:T(8,128)(2,1)S(1)}, bf16[1024,128]{1,0:T(8,128)(2,1)S(1)}, u32[]{:S(2)}, u32[]{:S(2)}) collective-permute-start(bf16[1024,128]{1,0:T(8,128)(2,1)S(1)} %attn_grad.1.refs_5_.refs_8_), channel_id=1, source_target_pairs={{0,16},{1,65},{2,18},{3,67},{4,20},{5,69},{6,22},{7,71},{8,24},{9,... | collective-permute-start | bytes 786440 | tf_op jit(solution)/shard_map/ppermute | solution.py:80
  62.0 8.3 %collective-permute-start.20 = (bf16[1024,128]{1,0:T(8,128)(2,1)S(1)}, bf16[1024,128]{1,0:T(8,128)(2,1)S(1)}, u32[]{:S(2)}, u32[]{:S(2)}) collective-permute-start(bf16[1024,128]{1,0:T(8,128)(2,1)S(1)} %attn_grad.1.refs_5_.refs_8_), channel_id=1, source_target_pairs={{0,8},{1,33},{2,10},{3,35},{4,12},{5,37},{6,14},{7,39},{8,16},{9,4... | collective-permute-start | bytes 786440 | tf_op jit(solution)/shard_map/ppermute | solution.py:80
  62.5 7.9 %collective-permute-start.21 = (bf16[1024,128]{1,0:T(8,128)(2,1)S(1)}, bf16[1024,128]{1,0:T(8,128)(2,1)S(1)}, u32[]{:S(2)}, u32[]{:S(2)}) collective-permute-start(bf16[1024,128]{1,0:T(8,128)(2,1)S(1)} %attn_grad.1.refs_5_.refs_8_), channel_id=1, source_target_pairs={{0,24},{1,97},{2,26},{3,99},{4,28},{5,101},{6,30},{7,103},{8,0},{9... | collective-permute-start | bytes 786440 | tf_op jit(solution)/shard_map/ppermute | solution.py:80
  74.1 6.9 %collective-permute-start.22 = (bf16[256,512]{1,0:T(8,128)(2,1)S(1)}, bf16[256,512]{1,0:T(8,128)(2,1)S(1)}, u32[]{:S(2)}, u32[]{:S(2)}) collective-permute-start(bf16[256,512]{1,0:T(8,128)(2,1)S(1)} %get-tuple-element.58), channel_id=1, source_target_pairs={{64,0},{17,1},{66,2},{19,3},{68,4},{21,5},{70,6},{23,7},{72,8},{25... | collective-permute-start | bytes 786440 | tf_op jit(solution)/shard_map/ppermute | solution.py:80
  75.0 8.8 %collective-permute-start.23 = (bf16[256,512]{1,0:T(8,128)(2,1)S(1)}, bf16[256,512]{1,0:T(8,128)(2,1)S(1)}, u32[]{:S(2)}, u32[]{:S(2)}) collective-permute-start(bf16[256,512]{1,0:T(8,128)(2,1)S(1)} %get-tuple-element.59), channel_id=1, source_target_pairs={{32,0},{9,1},{34,2},{11,3},{36,4},{13,5},{38,6},{15,7},{40,8},{17,... | collective-permute-start | bytes 786440 | tf_op jit(solution)/shard_map/ppermute | solution.py:80
  76.7 7.1 %collective-permute-start.24 = (bf16[256,512]{1,0:T(8,128)(2,1)S(1)}, bf16[256,512]{1,0:T(8,128)(2,1)S(1)}, u32[]{:S(2)}, u32[]{:S(2)}) collective-permute-start(bf16[256,512]{1,0:T(8,128)(2,1)S(1)} %get-tuple-element.60), channel_id=1, source_target_pairs={{96,0},{25,1},{98,2},{27,3},{100,4},{29,5},{102,6},{31,7},{104,8},... | collective-permute-start | bytes 786440 | tf_op jit(solution)/shard_map/ppermute | solution.py:80
  83.8 23.7 %copy-start.6 = (s32[1,1,256]{2,1,0:T(1,128)S(1)}, s32[1,1,256]{2,1,0:T(1,128)}, u32[]{:S(2)}) copy-start(s32[1,1,256]{2,1,0:T(1,128)} %param.10) | copy-start | bytes 3076
  86.5 16.2 %collective-permute-start.25 = (bf16[128,512]{1,0:T(8,128)(2,1)S(1)}, bf16[128,512]{1,0:T(8,128)(2,1)S(1)}, u32[]{:S(2)}, u32[]{:S(2)}) collective-permute-start(bf16[128,512]{1,0:T(8,128)(2,1)S(1)} %get-tuple-element.67), channel_id=1, source_target_pairs={{2,0},{3,1},{4,2},{5,3},{6,4},{7,5},{0,6},{1,7},{10,8},{11,9},{12,... | collective-permute-start | bytes 393224 | tf_op jit(solution)/shard_map/ppermute | solution.py:80
  89.1 13.6 %collective-permute-start.26 = (bf16[128,512]{1,0:T(8,128)(2,1)S(1)}, bf16[128,512]{1,0:T(8,128)(2,1)S(1)}, u32[]{:S(2)}, u32[]{:S(2)}) collective-permute-start(bf16[128,512]{1,0:T(8,128)(2,1)S(1)} %get-tuple-element.68), channel_id=1, source_target_pairs={{4,0},{5,1},{6,2},{7,3},{0,4},{1,5},{2,6},{3,7},{12,8},{13,9},{14,... | collective-permute-start | bytes 393224 | tf_op jit(solution)/shard_map/ppermute | solution.py:80
  90.3 14.3 %collective-permute-start.27 = (bf16[128,512]{1,0:T(8,128)(2,1)S(1)}, bf16[128,512]{1,0:T(8,128)(2,1)S(1)}, u32[]{:S(2)}, u32[]{:S(2)}) collective-permute-start(bf16[128,512]{1,0:T(8,128)(2,1)S(1)} %get-tuple-element.69), channel_id=1, source_target_pairs={{6,0},{7,1},{0,2},{1,3},{2,4},{3,5},{4,6},{5,7},{14,8},{15,9},{8,1... | collective-permute-start | bytes 393224 | tf_op jit(solution)/shard_map/ppermute | solution.py:80
  91.4 15.2 %collective-permute-start.28 = (bf16[128,512]{1,0:T(8,128)(2,1)S(1)}, bf16[128,512]{1,0:T(8,128)(2,1)S(1)}, u32[]{:S(2)}, u32[]{:S(2)}) collective-permute-start(bf16[128,512]{1,0:T(8,128)(2,1)S(1)} %get-tuple-element.66.refs_2_), channel_id=1, source_target_pairs={{0,1},{1,0},{2,3},{3,2},{4,5},{5,4},{6,7},{7,6},{8,9},{9,8},{10,11... | collective-permute-start | bytes 393224 | tf_op jit(solution)/shard_map/ppermute | solution.py:80
  102.7 3.8 %collective-permute-start.29 = (bf16[128,512]{1,0:T(8,128)(2,1)S(1)}, bf16[128,512]{1,0:T(8,128)(2,1)S(1)}, u32[]{:S(2)}, u32[]{:S(2)}) collective-permute-start(bf16[128,512]{1,0:T(8,128)(2,1)S(1)} %collective-permute-done.25.refs_3_), channel_id=1, source_target_pairs={{0,1},{1,0},{2,3},{3,2},{4,5},{5,4},{6,7},{7,6},{8,9},{9,8},{10,11... | collective-permute-start | bytes 393224 | tf_op jit(solution)/shard_map/ppermute | solution.py:80
  102.7 3.8 %collective-permute-start.30 = (bf16[128,512]{1,0:T(8,128)(2,1)S(1)}, bf16[128,512]{1,0:T(8,128)(2,1)S(1)}, u32[]{:S(2)}, u32[]{:S(2)}) collective-permute-start(bf16[128,512]{1,0:T(8,128)(2,1)S(1)} %collective-permute-done.26.refs_4_), channel_id=1, source_target_pairs={{0,1},{1,0},{2,3},{3,2},{4,5},{5,4},{6,7},{7,6},{8,9},{9,8},{10,11... | collective-permute-start | bytes 393224 | tf_op jit(solution)/shard_map/ppermute | solution.py:80
  104.6 2.9 %collective-permute-start.31 = (bf16[128,512]{1,0:T(8,128)(2,1)S(1)}, bf16[128,512]{1,0:T(8,128)(2,1)S(1)}, u32[]{:S(2)}, u32[]{:S(2)}) collective-permute-start(bf16[128,512]{1,0:T(8,128)(2,1)S(1)} %collective-permute-done.27.refs_5_), channel_id=1, source_target_pairs={{0,1},{1,0},{2,3},{3,2},{4,5},{5,4},{6,7},{7,6},{8,9},{9,8},{10,11... | collective-permute-start | bytes 393224 | tf_op jit(solution)/shard_map/ppermute | solution.py:80
